TPU v7x, 32 devices: a whole 2x2x4 slice. The times are simulated.
32 devices in a mesh: blk: 8 (over y, x, core), dp: 4 (over z).
Axes of the slice: x: 2, y: 2, z: 4, core: 2. Of those that a mesh axis runs over, the one named last changes fastest.
Arguments:
- hidden_in: bfloat16 [16384, 8192], P(('blk', 'dp')), may hold values from -6 to 6
- segment_ids: int32 [64, 256], P(('blk', 'dp')), may hold values from 0 to 3, never falling along the last dimension, each value on 1 to 128 neighbouring positions
- key_weight: bfloat16 [8192, 512], P('blk'), may hold values from -0.0625 to 0.0625
- norm_gain: float32 [8192], replicated, may hold values from 0.5 to 1.5
- key_bias: float32 [512], replicated, may hold values from -6 to 6
- key_cotangent: bfloat16 [16384, 512], P(('blk', 'dp')), may hold values from -6 to 6
Outputs:
- keys: bfloat16 [16384, 512], P(('blk', 'dp'))
- grad_weight: float32 [8192, 512], P('blk')
- grad_bias: float32 [512], replicated
- grad_gain: float32 [8192], replicated
Inputs may be any that keep to these rules, and one draw needn't show every extreme that they name: `segment_ids`: segment ids never fall along a micro-batch; each segment has 1 to 128 tokens.
All inputs are finite; a program needn't handle non-finite values.
Results may differ from a plain program's by a relative error of at most 0.0048.
Values may be sent and summed in bfloat16 or wider, within the bound.
No kernel may reach another device: no remote copies, remote signals or barrier semaphores. Data moves between devices by JAX's collectives and lax.ppermute only.
A program may use at most 128 MiB of HBM per device.

v0:
```python
import jax
import jax.numpy as jnp
from jax import lax
from jax.sharding import PartitionSpec as P

KVH = 4
HEAD = 128
KW = 512


def positions_of(segs):
    same = segs[:, :, None] == segs[:, None, :]
    idx = jnp.arange(segs.shape[1], dtype=jnp.int32)
    earlier = idx[None, :] < idx[:, None]
    return jnp.sum((same & earlier[None]).astype(jnp.int32), axis=2)


def angles_of(pos, head):
    half = head // 2
    freq = jnp.arange(half, dtype=jnp.float32) * (2.0 / head)
    inv = jnp.power(jnp.float32(1000000.0), -freq)
    ang = pos.astype(jnp.float32)[:, None] * inv[None, :]
    return (jnp.cos(ang)[:, None, :], jnp.sin(ang)[:, None, :])


def rotate(values, cosine, sine, sign):
    rows = values.shape[0]
    heads = values.reshape(rows, KVH, HEAD)
    first = heads[:, :, : HEAD // 2]
    second = heads[:, :, HEAD // 2 :]
    out_a = first * cosine - sign * second * sine
    out_b = second * cosine + sign * first * sine
    return jnp.concatenate([out_a, out_b], axis=2).reshape(rows, KW)


def per_device(hidden_in, segment_ids, key_weight, norm_gain, key_bias, key_cotangent):
    tok_rows = hidden_in.shape[0]
    n_cycle = lax.axis_size("blk")
    n_rep = lax.axis_size("dp")
    positions = positions_of(segment_ids).reshape(tok_rows)
    xf = hidden_in.astype(jnp.float32)
    normed = xf * lax.rsqrt(jnp.mean(xf * xf, axis=1, keepdims=True) + 1e-06)
    scaled = (normed * norm_gain[None, :]).astype(jnp.bfloat16)
    cosine, sine = angles_of(positions, HEAD)
    dproj = rotate(key_cotangent.astype(jnp.float32), cosine, sine, -1.0).astype(jnp.bfloat16)
    full_weight = lax.all_gather(key_weight, "blk", axis=0, tiled=True)
    projected = jnp.dot(scaled, full_weight, preferred_element_type=jnp.float32)
    dscaled = lax.dot_general(
        dproj, full_weight, (((1,), (1,)), ((), ())), preferred_element_type=jnp.float32
    )
    projected = projected + key_bias[None, :]
    keys = rotate(projected, cosine, sine, 1.0).astype(jnp.bfloat16)
    cycle_part = lax.psum_scatter(
        lax.dot_general(
            scaled, dproj, (((0,), (0,)), ((), ())), preferred_element_type=jnp.float32
        ),
        "blk",
        scatter_dimension=0,
        tiled=True,
    )
    grad_weight = lax.psum(cycle_part, "dp")
    bias_part = jnp.sum(dproj.astype(jnp.float32), axis=0)
    gain_part = jnp.sum(dscaled * normed, axis=0)
    grad_bias, grad_gain = lax.psum((bias_part, gain_part), ("blk", "dp"))
    scale = 1.0 / jnp.sqrt(jnp.float32(tok_rows * n_cycle * n_rep))
    return (keys, grad_weight * scale, grad_bias * scale, grad_gain * scale)


def solution(mesh):
    return jax.shard_map(
        per_device,
        mesh=mesh,
        in_specs=(
            P(("blk", "dp"), None),
            P(("blk", "dp"), None),
            P("blk", None),
            P(),
            P(),
            P(("blk", "dp"), None),
        ),
        out_specs=(P(("blk", "dp"), None), P("blk", None), P(), P()),
        check_vma=False,
    )
```

profile of v0, /device:TPU:0, one launch (start us, length us, event | category | flops | bytes accessed | tf_op | source)
XLA Modules:
  0.0 301.2 jit_solution(16969954500867652314)
XLA Ops:
  7.2 0.0 copy-start.1
  7.2 0.0 copy-start
  7.2 0.0 copy-start.2
  7.2 0.0 reduce-scatter.2.cloned.1.call-start
  7.3 5.2 %fusion.4 = f32[512]{0:T(512)S(1)} fusion(bf16[512,8192]{1,0:T(8,128)(2,1)} %param.6), kind=kLoop, calls=%fused_computation.6 | loop fusion | flops 12582400 | bytes 8390656 | tf_op jit(solution)/shard_map/reduce_sum | solution.py:42
  12.5 0.0 copy-done.1
  12.5 0.2 convert_reduce_fusion.1
  12.7 0.0 copy-done
  12.8 0.2 copy.17
  13.0 0.5 broadcast_multiply_fusion.1
  13.5 0.2 multiply_subtract_fusion
  13.7 0.1 convert_reduce_fusion
  13.9 0.0 copy-done.2
  13.9 13.4 %fusion.5 = f32[8192,512]{1,0:T(8,128)} fusion(bf16[512,512]{0,1:T(8,128)(2,1)S(1)} %bitcast.15, bf16[512,8192]{1,0:T(8,128)(2,1)} %param.6, f32[8192]{0:T(1024)S(1)} %copy-done.2, f32[512]{0:T(512)S(1)} %add_rsqrt_fusion), kind=kOutput, calls=%fused_computation.7 | convolution fusion | flops 4311744512 | bytes 25724928 | tf_op jit(solution)/shard_map/dot_general | solution.py:54
  27.2 0.0 copy-start.3
  27.2 0.0 reduce-scatter.2.cloned.1.call-update
  27.3 0.0 all-gather.2.cloned.1.call-start
  27.3 0.7 all-gather.2.cloned.1.call-update
  28.0 0.2 all-reduce.3.cloned.1.call-start
  28.2 117.9 %reduce-scatter.2.cloned.1.call-done = f32[1024,512]{1,0:T(8,128)} async-done(((f32[8192,512]{1,0:T(8,128)}), f32[1024,512]{1,0:T(8,128)}) %reduce-scatter.2.cloned.1.call-update) | async-done | bytes 2097168 | tf_op jit(solution)/shard_map/reduce_scatter | solution.py:53
  146.1 0.0 all-reduce.3.cloned.1.call-update
  146.1 56.3 %all-gather.2.cloned.1.call-done = bf16[8192,512]{1,0:T(8,128)(2,1)} async-done(((bf16[1024,512]{1,0:T(8,128)(2,1)}), bf16[8192,512]{1,0:T(8,128)(2,1)}) %all-gather.2.cloned.1.call-update) | async-done | bytes 8388624 | tf_op jit(solution)/shard_map/all_gather | solution.py:46
  202.4 0.0 copy-done.3
  202.4 12.8 %fusion.9 = f32[512,512]{0,1:T(8,128)S(1)} fusion(bf16[8192,512]{1,0:T(8,128)(2,1)} %all-gather.2.cloned.1.call-done, bf16[512,8192]{1,0:T(8,128)(2,1)} %param.6, f32[8192]{0:T(1024)S(1)} %copy-done.2, f32[512]{0:T(512)S(1)} %add_rsqrt_fusion, f32[512]{0:T(512)S(1)} %copy-done.3), kind=kOutput, calls=%fused_computation.9 | convolution fusion | flops 4312006656 | bytes 17862656 | tf_op jit(solution)/shard_map/dot_general | solution.py:47
  215.2 0.2 subtract_convert_fusion
  215.5 1.0 copy.16
  216.5 12.0 %fusion.3 = f32[8192]{0:T(1024)S(1)} fusion(bf16[512,8192]{1,0:T(8,128)(2,1)} %param.6, bf16[512,512]{0,1:T(8,128)(2,1)S(1)} %bitcast.16, bf16[8192,512]{1,0:T(8,128)(2,1)} %all-gather.2.cloned.1.call-done, f32[512]{0:T(512)S(1)} %add_rsqrt_fusion), kind=kOutput, calls=%fused_computation.5 | convolution fusion | flops 4311736320 | bytes 17336320 | tf_op jit(solution)/shard_map/dot_general | solution.py:48
  228.5 39.9 %all-reduce = (f32[512]{0:T(512)S(1)}, f32[8192]{0:T(1024)S(1)}) all-reduce(f32[512]{0:T(512)S(1)} %bitcast.17, f32[8192]{0:T(1024)S(1)} %fusion.3), channel_id=1, replica_groups=mesh['blk'=8,'dp'=4] {'blk','dp'}, use_global_device_ids=true, to_apply=%region_5.0 | all-reduce | flops 8704 | bytes 69632 | tf_op jit(solution)/shard_map/psum | solution.py:64
  268.4 0.6 broadcast_multiply_fusion.3
  269.0 0.6 broadcast_multiply_fusion.2
  269.6 22.0 %all-reduce.3.cloned.1.call-done = f32[1024,512]{1,0:T(8,128)} async-done(((f32[1024,512]{1,0:T(8,128)}), f32[1024,512]{1,0:T(8,128)}) %all-reduce.3.cloned.1.call-update) | async-done | bytes 2097168 | tf_op jit(solution)/shard_map/psum | solution.py:61
  291.6 3.1 %broadcast_multiply_fusion = f32[1024,512]{1,0:T(8,128)} fusion(f32[1024,512]{1,0:T(8,128)} %all-reduce.3.cloned.1.call-done), kind=kLoop, calls=%fused_computation.12 | loop fusion | flops 524288 | bytes 4194304 | tf_op jit(solution)/shard_map/mul | solution.py:66
  (6 shorter events, 0.1 us)
Async XLA Ops:
  7.2 5.3 %copy-start.1 = (s32[2,256]{1,0:T(2,128)S(1)}, s32[2,256]{1,0:T(2,128)}, u32[]{:S(2)}) copy-start(s32[2,256]{1,0:T(2,128)} %param.7) | copy-start | bytes 6148
  7.2 5.6 %copy-start = (bf16[512,512]{1,0:T(8,128)(2,1)S(1)}, bf16[512,512]{1,0:T(8,128)(2,1)}, u32[]{:S(2)}) copy-start(bf16[512,512]{1,0:T(8,128)(2,1)} %param.11) | copy-start | bytes 1572868
  7.2 6.7 %copy-start.2 = (f32[8192]{0:T(1024)S(1)}, f32[8192]{0:T(1024)}, u32[]{:S(2)}) copy-start(f32[8192]{0:T(1024)} %param.9) | copy-start | bytes 98308
  7.2 138.9 %reduce-scatter.2.cloned.1.call-start = ((), (), s32[]{:S(2)}) async-start(), calls=%async_computation.2 | async-start | bytes 18874368 | tf_op jit(solution)/shard_map/reduce_scatter | solution.py:53
  27.2 175.2 %copy-start.3 = (f32[512]{0:T(512)S(1)}, f32[512]{0:T(512)}, u32[]{:S(2)}) copy-start(f32[512]{0:T(512)} %param.10) | copy-start | bytes 6148
  27.3 175.1 %all-gather.2.cloned.1.call-start = ((), (), s32[]{:S(2)}) async-start(), calls=%async_computation.1 | async-start | bytes 9437184 | tf_op jit(solution)/shard_map/all_gather | solution.py:46
  28.0 263.5 %all-reduce.3.cloned.1.call-start = ((), (), s32[]{:S(2)}) async-start(), calls=%async_computation.3 | async-start | bytes 4194304 | tf_op jit(solution)/shard_map/psum | solution.py:61
Sparse Core Ops, SparseCore 0:
  27.4 118.6 reduce-scatter.1
  148.0 54.3 all-gather.1
  204.8 86.7 all-reduce.2
where the time goes:
time: 302 us; the launch traced here: 301 us
  waiting for transfers between devices  197 us (65%)
  blocking collectives  39.9 us (13%)
  matrix products  38.2 us (13%)
  between operations  13.9 us (5%)
  other arithmetic  10.9 us (4%)
    reduce_scatter x1, waiting for transfers between devices, per_device(): lax.psum_scatter(lax.dot_general(scaled, dproj, (((0,), (0,)), ((), ())),...  118 us
    all_gather x1, waiting for transfers between devices, per_device(): full_weight = lax.all_gather(key_weight, 'blk', axis=0, tiled=True)  56.3 us
    psum x1, blocking collectives, per_device(): grad_bias, grad_gain = lax.psum((bias_part, gain_part), ('blk', 'dp'))  39.9 us
    psum x1, waiting for transfers between devices, per_device(): grad_weight = lax.psum(cycle_part, 'dp')  22 us
    dot_general x1, matrix products, per_device(): lax.dot_general(scaled, dproj, (((0,), (0,)), ((), ())), preferred_elemen...  13.4 us
    dot_general x1, matrix products, per_device(): projected = jnp.dot(scaled, full_weight, preferred_element_type=jnp.float32)  12.8 us
    dot_general x1, matrix products, per_device(): lax.dot_general(dproj, full_weight, (((1,), (1,)), ((), ())), preferred_e...  12 us
  transfers between devices with their start and end apart: 3, of which 3 were waited for; matrix products, arithmetic and copies ran while one was open for 9% of the time, Pallas kernels for 0%

commit v1 on v0

v1 whole, which is shorter than its diff:
```python
import functools

import jax
import jax.numpy as jnp
from jax import lax
from jax.experimental import pallas as pl
from jax.experimental.pallas import tpu as pltpu
from jax.sharding import PartitionSpec as P

KVH = 4
HEAD = 128
KW = 512
F32 = jnp.float32
BF16 = jnp.bfloat16


def positions_of(segs):
    same = segs[:, :, None] == segs[:, None, :]
    idx = jnp.arange(segs.shape[1], dtype=jnp.int32)
    earlier = idx[None, :] < idx[:, None]
    return jnp.sum((same & earlier[None]).astype(jnp.int32), axis=2)


def angles_of(pos, head):
    half = head // 2
    freq = jnp.arange(half, dtype=F32) * (2.0 / head)
    inv = jnp.power(F32(1000000.0), -freq)
    ang = pos.astype(F32)[:, None] * inv[None, :]
    return (jnp.cos(ang)[:, None, :], jnp.sin(ang)[:, None, :])


def rotate(values, cosine, sine, sign):
    rows = values.shape[0]
    heads = values.reshape(rows, KVH, HEAD)
    first = heads[:, :, : HEAD // 2]
    second = heads[:, :, HEAD // 2 :]
    out_a = first * cosine - sign * second * sine
    out_b = second * cosine + sign * first * sine
    return jnp.concatenate([out_a, out_b], axis=2).reshape(rows, KW)


def scale_body(n_blk, at_ref, x_ref, gain_ref, *outs):
    wide = x_ref.shape[1]
    part = wide // n_blk
    total = None
    for b in range(n_blk):
        xb = x_ref[:, b * part : (b + 1) * part].astype(F32)
        add = jnp.sum(xb * xb, axis=1, keepdims=True)
        total = add if total is None else total + add
    inv = lax.rsqrt(total * (1.0 / wide) + 1e-06)
    me = at_ref[0]
    for o, out in enumerate(outs):
        start = pl.multiple_of((me ^ o) * part, part)
        xb = x_ref[:, pl.ds(start, part)].astype(F32)
        out[...] = (xb * inv * gain_ref[:, pl.ds(start, part)]).astype(BF16)


def scaled_blocks(x, gain, n_blk, at):
    rows, wide = x.shape
    step = 64
    part = wide // n_blk
    return pl.pallas_call(
        functools.partial(scale_body, n_blk),
        grid_spec=pltpu.PrefetchScalarGridSpec(
            num_scalar_prefetch=1,
            grid=(rows // step,),
            in_specs=[
                pl.BlockSpec((step, wide), lambda r, at: (r, 0)),
                pl.BlockSpec((1, wide), lambda r, at: (0, 0)),
            ],
            out_specs=[pl.BlockSpec((step, part), lambda r, at: (r, 0))] * n_blk,
        ),
        out_shape=[jax.ShapeDtypeStruct((rows, part), BF16)] * n_blk,
        cost_estimate=pl.CostEstimate(
            flops=6 * rows * wide, bytes_accessed=4 * rows * wide, transcendentals=rows
        ),
        compiler_params=pltpu.CompilerParams(vmem_limit_bytes=16 * 1024 * 1024),
        name="scale_rows",
    )(at, x, gain[None, :])


def by_permutes(hidden_in, segment_ids, key_weight, norm_gain, key_bias, key_cotangent):
    tok = hidden_in.shape[0]
    me = lax.axis_index("blk")
    own = key_weight.shape[0]
    half = own // 2

    def over(bit):
        return lambda v: lax.ppermute(v, "blk", [(i, i ^ bit) for i in range(8)])

    core, px, py = over(1), over(2), over(4)

    def dot_t(a, b):
        return lax.dot_general(a, b, (((0,), (0,)), ((), ())), preferred_element_type=F32)

    def dot(a, b):
        return jnp.dot(a, b, preferred_element_type=F32)

    w_x, w_y = px(key_weight), py(key_weight)
    w_d = jnp.concatenate([px(w_y[:half]), py(w_x[half:])], axis=0)

    positions = positions_of(segment_ids).reshape(tok)
    cosine, sine = angles_of(positions, HEAD)
    dproj = rotate(key_cotangent.astype(F32), cosine, sine, -1.0).astype(BF16)
    dproj_sib = core(dproj)

    blocks = scaled_blocks(hidden_in, norm_gain, 8, me.reshape(1).astype(jnp.int32))
    mine = {j: blocks[j] for j in (0, 2, 4, 6)}
    sib = {j: core(blocks[j ^ 1]) for j in (6, 2, 4, 0)}

    def grad_rows(j):
        return dot_t(mine[j], dproj) + dot_t(sib[j], dproj_sib)

    g_d = grad_rows(6).astype(BF16)
    d_x, d_y = px(g_d[:half]), py(g_d[half:])
    g_x = grad_rows(2).astype(BF16)
    g_y = grad_rows(4).astype(BF16)
    x_low, y_high = px(g_x[:half]), py(g_y[half:])
    x_high = px((g_x[half:].astype(F32) + d_y.astype(F32)).astype(BF16))
    y_low = py((g_y[:half].astype(F32) + d_x.astype(F32)).astype(BF16))
    g_0 = grad_rows(0)

    n_z = lax.axis_index("dp")
    inner = (n_z == 1) | (n_z == 2)

    def along_z(g):
        into = lax.ppermute(g.astype(BF16), "dp", [(0, 1), (3, 2)])
        pair = (g + into.astype(F32)).astype(BF16)
        other = lax.ppermute(pair, "dp", [(1, 2), (2, 1)])
        total = (pair.astype(F32) + other.astype(F32)).astype(BF16)
        back = lax.ppermute(total, "dp", [(1, 0), (2, 3)])
        return jnp.where(inner, total, back).astype(F32)

    low = g_0[:half] + x_low.astype(F32) + y_low.astype(F32)
    high = g_0[half:] + x_high.astype(F32) + y_high.astype(F32)
    quarter = half // 2
    done = [along_z(v) for v in (low[:quarter], low[quarter:], high[:quarter], high[quarter:])]
    grad = jnp.concatenate(done, axis=0)

    here = dot(mine[0], key_weight) + dot(mine[2], w_x) + dot(mine[4], w_y) + dot(mine[6], w_d)
    there = dot(sib[0], key_weight) + dot(sib[2], w_x) + dot(sib[4], w_y) + dot(sib[6], w_d)
    projected = here + core(there) + key_bias[None, :]
    keys = rotate(projected, cosine, sine, 1.0).astype(BF16)

    scale = 1.0 / jnp.sqrt(F32(tok * 32))
    bias = jnp.sum(dproj.astype(F32), axis=0)
    for hop in (core, px, py):
        bias = bias + hop(bias)
    for bit in (1, 2):
        bias = bias + lax.ppermute(bias, "dp", [(i, i ^ bit) for i in range(4)])
    my_gain = lax.dynamic_slice(norm_gain, (me * own,), (own,))
    gain_rows = jnp.sum(grad * key_weight.astype(F32), axis=1) / my_gain
    grad_gain = lax.all_gather(gain_rows, "blk", axis=0, tiled=True)
    return (keys, grad * scale, bias * scale, grad_gain * scale)


def by_collectives(hidden_in, segment_ids, key_weight, norm_gain, key_bias, key_cotangent):
    tok_rows = hidden_in.shape[0]
    n_cycle = lax.axis_size("blk")
    n_rep = lax.axis_size("dp")
    positions = positions_of(segment_ids).reshape(tok_rows)
    xf = hidden_in.astype(F32)
    normed = xf * lax.rsqrt(jnp.mean(xf * xf, axis=1, keepdims=True) + 1e-06)
    scaled = (normed * norm_gain[None, :]).astype(BF16)
    cosine, sine = angles_of(positions, HEAD)
    dproj = rotate(key_cotangent.astype(F32), cosine, sine, -1.0).astype(BF16)
    full_weight = lax.all_gather(key_weight, "blk", axis=0, tiled=True)
    projected = jnp.dot(scaled, full_weight, preferred_element_type=F32)
    dscaled = lax.dot_general(
        dproj, full_weight, (((1,), (1,)), ((), ())), preferred_element_type=F32
    )
    projected = projected + key_bias[None, :]
    keys = rotate(projected, cosine, sine, 1.0).astype(BF16)
    cycle_part = lax.psum_scatter(
        lax.dot_general(scaled, dproj, (((0,), (0,)), ((), ())), preferred_element_type=F32),
        "blk",
        scatter_dimension=0,
        tiled=True,
    )
    grad_weight = lax.psum(cycle_part, "dp")
    bias_part = jnp.sum(dproj.astype(F32), axis=0)
    gain_part = jnp.sum(dscaled * normed, axis=0)
    grad_bias, grad_gain = lax.psum((bias_part, gain_part), ("blk", "dp"))
    scale = 1.0 / jnp.sqrt(F32(tok_rows * n_cycle * n_rep))
    return (keys, grad_weight * scale, grad_bias * scale, grad_gain * scale)


def solution(mesh):
    small = mesh.shape["blk"] == 8 and mesh.shape["dp"] == 4
    return jax.shard_map(
        by_permutes if small else by_collectives,
        mesh=mesh,
        in_specs=(
            P(("blk", "dp"), None),
            P(("blk", "dp"), None),
            P("blk", None),
            P(),
            P(),
            P(("blk", "dp"), None),
        ),
        out_specs=(P(("blk", "dp"), None), P("blk", None), P(), P()),
        check_vma=False,
    )
```

time: 302 us -> 194 us (0.64)
  waiting for transfers between devices: 197 us -> 85.3 us
  starting transfers between devices: 0.3 us -> 36.8 us
  blocking collectives: 39.9 us -> 9.07 us
  between operations: 13.9 us -> 1.19 us
  local copies, waits for them, and re-layouts: 1.23 us -> 7.15 us
  Pallas kernels: 0 us -> 5.38 us
    reduce_scatter x1 -> x0, waiting for transfers between devices: 118 us -> none  [per_device(): lax.psum_scatter(lax.dot_general(scaled, dproj, (((0,), (0,)), ((), ())),...]
    ppermute x0 -> x33, waiting for transfers between devices: none -> 85.3 us  [the longest x19 53.8 us: over(): return lambda v: lax.ppermute(v, 'blk', [(i, i ^ bit) for i in range(8)])]
    all_gather x1 -> x0, waiting for transfers between devices: 56.3 us -> none  [per_device(): full_weight = lax.all_gather(key_weight, 'blk', axis=0, tiled=True)]
    psum x1 -> x0, blocking collectives: 39.9 us -> none  [per_device(): grad_bias, grad_gain = lax.psum((bias_part, gain_part), ('blk', 'dp'))]
    ppermute x0 -> x33, starting transfers between devices: none -> 36.8 us  [the longest x19 18.2 us: over(): return lambda v: lax.ppermute(v, 'blk', [(i, i ^ bit) for i in range(8)])]
    psum x1 -> x0, waiting for transfers between devices: 22 us -> none  [per_device(): grad_weight = lax.psum(cycle_part, 'dp')]
    all_gather x0 -> x1, blocking collectives: none -> 9.07 us  [by_permutes(): grad_gain = lax.all_gather(gain_rows, 'blk', axis=0, tiled=True)]
    pallas_call x0 -> x1, Pallas kernels: none -> 5.38 us  [scaled_blocks(): pl.pallas_call(functools.partial(scale_body, n_blk), grid_spec=pltpu.Pref...]
  transfers between devices with their start and end apart: 3 -> 33, of which waited for: 3 -> 14; matrix products, arithmetic and copies ran while one was open for 9% -> 22% of each run, Pallas kernels for 0% -> 3%
where the time goes in v1:
time: 194 us; the launch traced here: 193 us
  waiting for transfers between devices  85.3 us (44%)
  starting transfers between devices  36.8 us (19%)
  matrix products  35.8 us (18%)
  other arithmetic  12.1 us (6%)
  blocking collectives  9.07 us (5%)
  local copies, waits for them, and re-layouts  7.15 us (4%)
  Pallas kernels  5.38 us (3%)
    ppermute x19, waiting for transfers between devices, over(): return lambda v: lax.ppermute(v, 'blk', [(i, i ^ bit) for i in range(8)])  53.8 us
    dot_general x8, matrix products, dot_t(): lax.dot_general(a, b, (((0,), (0,)), ((), ())), preferred_element_type=F32)  21.2 us
    ppermute x19, starting transfers between devices, over(): return lambda v: lax.ppermute(v, 'blk', [(i, i ^ bit) for i in range(8)])  18.2 us
    ppermute x4, waiting for transfers between devices, along_z(): back = lax.ppermute(total, 'dp', [(1, 0), (2, 3)])  17 us
    dot_general x8, matrix products, dot(): return jnp.dot(a, b, preferred_element_type=F32)  14.6 us
    ppermute x4, waiting for transfers between devices, along_z(): into = lax.ppermute(g.astype(BF16), 'dp', [(0, 1), (3, 2)])  14.6 us
    all_gather x1, blocking collectives, by_permutes(): grad_gain = lax.all_gather(gain_rows, 'blk', axis=0, tiled=True)  9.07 us
    ppermute x4, starting transfers between devices, along_z(): into = lax.ppermute(g.astype(BF16), 'dp', [(0, 1), (3, 2)])  6.29 us
  transfers between devices with their start and end apart: 33, of which 14 were waited for; matrix products, arithmetic and copies ran while one was open for 22% of the time, Pallas kernels for 3%

profile of v1, /device:TPU:0, one launch (start us, length us, event | category | flops | bytes accessed | tf_op | source)
XLA Modules:
  0.0 192.8 jit_solution(10073100523022517634)
XLA Ops:
  5.0 3.4 %copy-done = bf16[512,8192]{1,0:T(8,128)(2,1)S(1)} copy-done((bf16[512,8192]{1,0:T(8,128)(2,1)S(1)}, bf16[512,8192]{1,0:T(8,128)(2,1)}, u32[]{:S(2)}) %copy-start) | copy-done | bytes 8388632
  8.4 5.4 %scale_rows.1 = (bf16[512,1024]{1,0:T(8,128)(2,1)S(1)}, bf16[512,1024]{1,0:T(8,128)(2,1)S(1)}, bf16[512,1024]{1,0:T(8,128)(2,1)S(1)}, bf16[512,1024]{1,0:T(8,128...) custom-call(s32[1]{0:T(128)} %bitcast.at_ref, ...), custom_call_target="tpu_custom_call" | custom-call | flops 25165824 | bytes 16777216 | tf_op jit(solution)/shard_map/scale_rows/pallas_call | solution.py:62
  14.4 2.9 %collective-permute-start.1 = (bf16[1024,512]{1,0:T(8,128)(2,1)}, bf16[1024,512]{1,0:T(8,128)(2,1)}, u32[]{:S(2)}, u32[]{:S(2)}) collective-permute-start(bf16[1024,512]{1,0:T(8,128)(2,1)} %param.8), channel_id=1, source_target_pairs={{0,16},{4,20},{8,24},{12,28},{16,0},{20,4},{24,8},{28,12},{1,17},{... | collective-permute-start | bytes 3145736 | tf_op jit(solution)/shard_map/ppermute | solution.py:89
  17.3 3.2 %fusion.19 = f32[1024,512]{1,0:T(8,128)} fusion(bf16[512,1024]{1,0:T(8,128)(2,1)S(1)} %get-tuple-element.15, bf16[512,512]{0,1:T(8,128)(2,1)} %bitcast.4), kind=kOutput, calls=%fused_computation.69 | convolution fusion | flops 536870912 | bytes 3670016 | tf_op jit(solution)/shard_map/dot_general | solution.py:94
  20.5 1.5 collective-permute-start.29
  22.0 3.1 %fusion.17 = f32[1024,512]{1,0:T(8,128)} fusion(bf16[512,1024]{1,0:T(8,128)(2,1)S(1)} %get-tuple-element.13, bf16[512,512]{0,1:T(8,128)(2,1)} %bitcast.4), kind=kOutput, calls=%fused_computation.67 | convolution fusion | flops 536870912 | bytes 3670016 | tf_op jit(solution)/shard_map/dot_general | solution.py:94
  25.7 3.2 %fusion.18 = f32[1024,512]{1,0:T(8,128)} fusion(bf16[512,1024]{1,0:T(8,128)(2,1)S(1)} %get-tuple-element.14, bf16[512,512]{0,1:T(8,128)(2,1)} %bitcast.4), kind=kOutput, calls=%fused_computation.68 | convolution fusion | flops 536870912 | bytes 3670016 | tf_op jit(solution)/shard_map/dot_general | solution.py:94
  28.9 12.2 %collective-permute-done.30 = f32[512]{0:T(512)S(1)} collective-permute-done((f32[512]{0:T(512)S(1)}, f32[512]{0:T(512)S(1)}, u32[]{:S(2)}, u32[]{:S(2)}) %collective-permute-start.30) | collective-permute-done | bytes 2080 | tf_op jit(solution)/shard_map/ppermute | solution.py:89
  41.0 1.8 collective-permute-start.31
  42.8 3.1 %fusion.16 = f32[1024,512]{1,0:T(8,128)} fusion(bf16[512,1024]{1,0:T(8,128)(2,1)S(1)} %get-tuple-element.12, bf16[512,512]{0,1:T(8,128)(2,1)} %bitcast.4), kind=kOutput, calls=%fused_computation.66 | convolution fusion | flops 536870912 | bytes 3670016 | tf_op jit(solution)/shard_map/dot_general | solution.py:94
  46.0 2.6 %collective-permute-start.32 = (f32[512]{0:T(512)S(1)}, f32[512]{0:T(512)S(1)}, u32[]{:S(2)}, u32[]{:S(2)}) collective-permute-start(f32[512]{0:T(512)S(1)} %add.139), channel_id=1, source_target_pairs={{0,2},{1,3},{2,0},{3,1},{4,6},{5,7},{6,4},{7,5},{8,10},{9,11},{10,... | collective-permute-start | bytes 6152 | tf_op jit(solution)/shard_map/ppermute | solution.py:150
  48.6 2.9 %fusion.11 = f32[512,512]{0,1:T(8,128)} fusion(bf16[512,1024]{1,0:T(8,128)(2,1)S(1)} %get-tuple-element.12, bf16[1024,512]{1,0:T(8,128)(2,1)} %param.8), kind=kOutput, calls=%fused_computation.61 | convolution fusion | flops 536870912 | bytes 3145728 | tf_op jit(solution)/shard_map/dot_general | solution.py:97
  52.1 1.5 collective-permute-start
  53.8 2.8 %add_convert_fusion = bf16[1024,512]{1,0:T(8,128)(2,1)S(1)} fusion(f32[1024,512]{1,0:T(8,128)} %fusion.19, bf16[512,1024]{1,0:T(8,128)(2,1)} %collective-permute-done.7, bf16[512,512]{0,1:T(8,128)(2,1)} %collective-permute-done.9), kind=kOutput, calls=%fused_computation.3 | convolution fusion | flops 537919488 | bytes 4718592 | tf_op jit(solution)/shard_map/dot_general | solution.py:94
  56.8 1.6 collective-permute-start.19
  58.4 2.1 %add_convert_fusion.2 = bf16[1024,512]{1,0:T(8,128)(2,1)S(1)} fusion(f32[1024,512]{1,0:T(8,128)S(1)} %copy-done.5, bf16[512,1024]{1,0:T(8,128)(2,1)} %collective-permute-done.5, bf16[512,512]{0,1:T(8,128)(2,1)} %collective-permute-done.9), kind=kOutput, calls=%fused_computation.5 | convolution fusion | flops 537919488 | bytes 4718592 | tf_op jit(solution)/shard_map/dot_general | solution.py:94
  61.2 1.8 add_convert_fusion.1
  63.0 1.6 collective-permute-start.10
  65.7 12.6 %collective-permute-done = bf16[1024,512]{1,0:T(8,128)(2,1)S(1)} collective-permute-done((bf16[1024,512]{1,0:T(8,128)(2,1)}, bf16[1024,512]{1,0:T(8,128)(2,1)S(1)}, u32[]{:S(2)}, u32[]{:S(2)}) %collective-permute-start) | collective-permute-done | bytes 1048608 | tf_op jit(solution)/shard_map/ppermute | solution.py:89
  78.3 1.5 collective-permute-start.21
  80.6 1.6 collective-permute-start.2
  82.2 1.8 convolution_add_fusion
  84.0 2.0 %fusion.13 = f32[512,512]{0,1:T(8,128)S(1)} fusion(bf16[512,1024]{1,0:T(8,128)(2,1)} %collective-permute-done.5, bf16[1024,512]{1,0:T(8,128)(2,1)S(1)} %collective-permute-done), kind=kOutput, calls=%fused_computation.63 | convolution fusion | flops 536870912 | bytes 3145728 | tf_op jit(solution)/shard_map/dot_general | solution.py:97
  86.0 2.0 %fusion.14 = f32[512,512]{0,1:T(8,128)S(1)} fusion(bf16[512,1024]{1,0:T(8,128)(2,1)S(1)} %collective-permute-done.6, bf16[1024,512]{1,0:T(8,128)(2,1)} %collective-permute-done.1), kind=kOutput, calls=%fused_computation.64 | convolution fusion | flops 536870912 | bytes 3145728 | tf_op jit(solution)/shard_map/dot_general | solution.py:97
  89.5 1.5 collective-permute-start.20
  91.1 20.8 %collective-permute-done.2 = bf16[512,512]{1,0:T(8,128)(2,1)S(1)} collective-permute-done((bf16[512,512]{1,0:T(8,128)(2,1)S(1)}, bf16[512,512]{1,0:T(8,128)(2,1)S(1)}, u32[]{:S(2)}, u32[]{:S(2)}) %collective-permute-start.2) | collective-permute-done | bytes 524320 | tf_op jit(solution)/shard_map/ppermute | solution.py:89
  112.0 1.5 collective-permute-start.12
  113.6 2.0 %fusion.15 = f32[512,512]{0,1:T(8,128)S(1)} fusion(bf16[512,1024]{1,0:T(8,128)(2,1)} %collective-permute-done.7, bf16[1024,512]{1,0:T(8,128)(2,1)S(1)} %constant_dynamic-update-slice_fusion), kind=kOutput, calls=%fused_computation.65 | convolution fusion | flops 536870912 | bytes 3145728 | tf_op jit(solution)/shard_map/dot_general | solution.py:97
  115.6 2.2 %fusion.5 = f32[512,512]{0,1:T(8,128)S(1)} fusion(f32[512,512]{0,1:T(8,128)S(1)} %fusion.15, f32[512,512]{0,1:T(8,128)S(1)} %fusion.14, f32[512,512]{0,1:T(8,128)S(1)} %fusion.13, bf16[512,1024]{1,0:T(8,128)(2,1)S(1)} %collective-permute-done.4, bf16[1024,512]{1,0:T(8,128)(2,1)} %param.8), kind=kOutput, calls=%fused_computation.14 | convolution fusion | flops 537657344 | bytes 6291456 | tf_op jit(solution)/shard_map/dot_general | solution.py:97
  117.8 5.0 %collective-permute-done.20 = bf16[512,512]{1,0:T(8,128)(2,1)S(1)} collective-permute-done((bf16[512,512]{1,0:T(8,128)(2,1)S(1)}, bf16[512,512]{1,0:T(8,128)(2,1)S(1)}, u32[]{:S(2)}, u32[]{:S(2)}) %collective-permute-start.20) | collective-permute-done | bytes 524320 | tf_op jit(solution)/shard_map/ppermute | solution.py:89
  122.8 2.3 %collective-permute-done.12 = bf16[512,512]{1,0:T(8,128)(2,1)S(1)} collective-permute-done((bf16[512,512]{1,0:T(8,128)(2,1)S(1)}, bf16[512,512]{1,0:T(8,128)(2,1)S(1)}, u32[]{:S(2)}, u32[]{:S(2)}) %collective-permute-start.12) | collective-permute-done | bytes 524320 | tf_op jit(solution)/shard_map/ppermute | solution.py:89
  125.7 2.4 %collective-permute-start.13 = (bf16[256,512]{1,0:T(8,128)(2,1)S(1)}, bf16[256,512]{1,0:T(8,128)(2,1)S(1)}, u32[]{:S(2)}, u32[]{:S(2)}) collective-permute-start(bf16[256,512]{1,0:T(8,128)(2,1)S(1)} %get-tuple-element.32), channel_id=1, source_target_pairs={{0,1},{3,2},{4,5},{7,6},{8,9},{11,10},{12,13},{15,14},{16,17},{19,... | collective-permute-start | bytes 786440 | tf_op jit(solution)/shard_map/ppermute | solution.py:127
  128.0 1.3 collective-permute-start.16
  130.3 1.3 collective-permute-start.22
  131.6 1.3 collective-permute-start.25
  132.9 1.9 collective-permute-done.13
  134.8 5.6 %collective-permute-done.16 = bf16[256,512]{1,0:T(8,128)(2,1)S(1)} collective-permute-done((bf16[256,512]{1,0:T(8,128)(2,1)S(1)}, bf16[256,512]{1,0:T(8,128)(2,1)S(1)}, u32[]{:S(2)}, u32[]{:S(2)}) %collective-permute-start.16) | collective-permute-done | bytes 262176 | tf_op jit(solution)/shard_map/ppermute | solution.py:127
  141.9 4.1 %collective-permute-done.22 = bf16[256,512]{1,0:T(8,128)(2,1)S(1)} collective-permute-done((bf16[256,512]{1,0:T(8,128)(2,1)S(1)}, bf16[256,512]{1,0:T(8,128)(2,1)S(1)}, u32[]{:S(2)}, u32[]{:S(2)}) %collective-permute-start.22) | collective-permute-done | bytes 262176 | tf_op jit(solution)/shard_map/ppermute | solution.py:127
  146.0 3.0 %collective-permute-done.25 = bf16[256,512]{1,0:T(8,128)(2,1)S(1)} collective-permute-done((bf16[256,512]{1,0:T(8,128)(2,1)S(1)}, bf16[256,512]{1,0:T(8,128)(2,1)S(1)}, u32[]{:S(2)}, u32[]{:S(2)}) %collective-permute-start.25) | collective-permute-done | bytes 262176 | tf_op jit(solution)/shard_map/ppermute | solution.py:127
  150.6 1.3 collective-permute-start.15
  152.0 1.3 collective-permute-start.18
  156.1 2.0 %fusion.4 = f32[512,512]{0,1:T(8,128)S(1)} fusion(f32[512,512]{0,1:T(8,128)S(1)} %collective-permute-done.8, f32[512,512]{0,1:T(8,128)S(1)} %fusion.12, f32[512,512]{0,1:T(8,128)S(1)} %convolution_add_fusion.3, bf16[512,1024]{1,0:T(8,128)(2,1)S(1)} %get-tuple-element.14, bf16[1024,512]{1,0:T(8,128)(2,1)} %collective-permute-done.1, f32[512]{0:T(512)S(1)} %copy-done.8), kind=kOutput, calls=%fused_computation.13 | convolution fusion | flops 537919488 | bytes 6293504 | tf_op jit(solution)/shard_map/dot_general | solution.py:97
  159.3 6.9 %collective-permute-done.15 = bf16[256,512]{1,0:T(8,128)(2,1)} collective-permute-done((bf16[256,512]{1,0:T(8,128)(2,1)S(1)}, bf16[256,512]{1,0:T(8,128)(2,1)}, u32[]{:S(2)}, u32[]{:S(2)}) %collective-permute-start.15) | collective-permute-done | bytes 262176 | tf_op jit(solution)/shard_map/ppermute | solution.py:131
  167.2 4.6 %collective-permute-done.18 = bf16[256,512]{1,0:T(8,128)(2,1)} collective-permute-done((bf16[256,512]{1,0:T(8,128)(2,1)S(1)}, bf16[256,512]{1,0:T(8,128)(2,1)}, u32[]{:S(2)}, u32[]{:S(2)}) %collective-permute-start.18) | collective-permute-done | bytes 262176 | tf_op jit(solution)/shard_map/ppermute | solution.py:131
  172.8 3.6 %collective-permute-done.24 = bf16[256,512]{1,0:T(8,128)(2,1)} collective-permute-done((bf16[256,512]{1,0:T(8,128)(2,1)S(1)}, bf16[256,512]{1,0:T(8,128)(2,1)}, u32[]{:S(2)}, u32[]{:S(2)}) %collective-permute-start.24) | collective-permute-done | bytes 262176 | tf_op jit(solution)/shard_map/ppermute | solution.py:131
  177.4 1.8 collective-permute-done.27
  180.2 2.9 %fusion = (f32[1024]{0:T(1024)S(1)}, f32[1024,512]{1,0:T(8,128)}) fusion(bf16[1024,512]{1,0:T(8,128)(2,1)} %param.8, bf16[256,512]{1,0:T(8,128)(2,1)S(1)} %broadcast_select_fusion, bf16[256,512]{1,0:T(8,128)(2,1)S(1)} %broadcast_select_fusion.1, bf16[256,512]{1,0:T(8,128)(2,1)S(1)} %broadcast_select_fusion.2, bf16[256,512]{1,0:T(8,128)(2,1)S(1)} %broadcast_select_fusion.3), kind=kLoop, calls=%fused_computation.2 | loop fusion | flops 6290432 | bytes 4198400 | tf_op jit(solution)/shard_map/reduce_sum | solution.py:152
  183.1 9.1 %all_gather.3 = f32[8192]{0:T(1024)S(1)} all-gather(f32[1024]{0:T(1024)S(1)} %dynamic-slice_divide_fusion), channel_id=1, replica_groups=mesh['blk'=8,'dp'=4] {'blk'}, dimensions={0}, use_global_device_ids=true | all-gather | bytes 36864 | tf_op jit(solution)/shard_map/all_gather | solution.py:153
  (96 shorter events, 23.8 us)
Async XLA Ops:
  1.7 3.3 %copy-start.1 = (f32[8192]{0:T(1024)S(1)}, f32[8192]{0:T(1024)}, u32[]{:S(2)}) copy-start(f32[8192]{0:T(1024)} %param.9) | copy-start | bytes 98308
  4.6 47.5 %collective-permute-start.9 = (bf16[512,512]{0,1:T(8,128)(2,1)}, bf16[512,512]{0,1:T(8,128)(2,1)}, u32[]{:S(2)}, u32[]{:S(2)}) collective-permute-start(bf16[512,512]{0,1:T(8,128)(2,1)} %bitcast.4), channel_id=1, source_target_pairs={{0,4},{4,0},{8,12},{12,8},{16,20},{20,16},{24,28},{28,24},{1,5},{5... | collective-permute-start | bytes 1572872 | tf_op jit(solution)/shard_map/ppermute | solution.py:89
  5.0 3.4 %copy-start = (bf16[512,8192]{1,0:T(8,128)(2,1)S(1)}, bf16[512,8192]{1,0:T(8,128)(2,1)}, u32[]{:S(2)}) copy-start(bf16[512,8192]{1,0:T(8,128)(2,1)} %x_ref.1) | copy-start | bytes 25165828
  13.8 11.3 %copy-start.2 = (bf16[512,1024]{1,0:T(8,128)(2,1)}, bf16[512,1024]{1,0:T(8,128)(2,1)S(1)}, u32[]{:S(2)}) copy-start(bf16[512,1024]{1,0:T(8,128)(2,1)S(1)} %get-tuple-element.16) | copy-start | bytes 3145732
  13.8 11.3 %copy-start.3 = (bf16[512,1024]{1,0:T(8,128)(2,1)}, bf16[512,1024]{1,0:T(8,128)(2,1)S(1)}, u32[]{:S(2)}) copy-start(bf16[512,1024]{1,0:T(8,128)(2,1)S(1)} %get-tuple-element.18) | copy-start | bytes 3145732
  13.8 39.8 %collective-permute-start.7 = (bf16[512,1024]{1,0:T(8,128)(2,1)}, bf16[512,1024]{1,0:T(8,128)(2,1)}, u32[]{:S(2)}, u32[]{:S(2)}) collective-permute-start(bf16[512,1024]{1,0:T(8,128)(2,1)} %get-tuple-element.19), channel_id=1, source_target_pairs={{0,4},{4,0},{8,12},{12,8},{16,20},{20,16},{24,28},{28,24},{1,5},{5... | collective-permute-start | bytes 3145736 | tf_op jit(solution)/shard_map/ppermute | solution.py:89
  13.8 42.9 %collective-permute-start.5 = (bf16[512,1024]{1,0:T(8,128)(2,1)}, bf16[512,1024]{1,0:T(8,128)(2,1)}, u32[]{:S(2)}, u32[]{:S(2)}) collective-permute-start(bf16[512,1024]{1,0:T(8,128)(2,1)} %get-tuple-element.17), channel_id=1, source_target_pairs={{0,4},{4,0},{8,12},{12,8},{16,20},{20,16},{24,28},{28,24},{1,5},{5... | collective-permute-start | bytes 3145736 | tf_op jit(solution)/shard_map/ppermute | solution.py:89
  14.3 6.2 %collective-permute-start.28 = (f32[512]{0:T(512)S(1)}, f32[512]{0:T(512)S(1)}, u32[]{:S(2)}, u32[]{:S(2)}) collective-permute-start(f32[512]{0:T(512)S(1)} %bitcast.47), channel_id=1, source_target_pairs={{0,4},{4,0},{8,12},{12,8},{16,20},{20,16},{24,28},{28,24},{1,5},{5... | collective-permute-start | bytes 6152 | tf_op jit(solution)/shard_map/ppermute | solution.py:89
  14.4 48.7 %collective-permute-start.1 = (bf16[1024,512]{1,0:T(8,128)(2,1)}, bf16[1024,512]{1,0:T(8,128)(2,1)}, u32[]{:S(2)}, u32[]{:S(2)}) collective-permute-start(bf16[1024,512]{1,0:T(8,128)(2,1)} %param.8), channel_id=1, source_target_pairs={{0,16},{4,20},{8,24},{12,28},{16,0},{20,4},{24,8},{28,12},{1,17},{... | collective-permute-start | bytes 3145736 | tf_op jit(solution)/shard_map/ppermute | solution.py:89
  20.5 4.6 %collective-permute-start.29 = (f32[512]{0:T(512)S(1)}, f32[512]{0:T(512)S(1)}, u32[]{:S(2)}, u32[]{:S(2)}) collective-permute-start(f32[512]{0:T(512)S(1)} %bitcast_add_fusion), channel_id=1, source_target_pairs={{0,8},{4,12},{8,0},{12,4},{16,24},{20,28},{24,16},{28,20},{1,9},{5... | collective-permute-start | bytes 6152 | tf_op jit(solution)/shard_map/ppermute | solution.py:89
  25.1 15.9 %collective-permute-start.30 = (f32[512]{0:T(512)S(1)}, f32[512]{0:T(512)S(1)}, u32[]{:S(2)}, u32[]{:S(2)}) collective-permute-start(f32[512]{0:T(512)S(1)} %add.137), channel_id=1, source_target_pairs={{0,16},{4,20},{8,24},{12,28},{16,0},{20,4},{24,8},{28,12},{1,17},{... | collective-permute-start | bytes 6152 | tf_op jit(solution)/shard_map/ppermute | solution.py:89
  41.0 4.9 %collective-permute-start.31 = (f32[512]{0:T(512)S(1)}, f32[512]{0:T(512)S(1)}, u32[]{:S(2)}, u32[]{:S(2)}) collective-permute-start(f32[512]{0:T(512)S(1)} %add.138), channel_id=1, source_target_pairs={{0,1},{1,0},{2,3},{3,2},{4,5},{5,4},{6,7},{7,6},{8,9},{9,8},{10,11... | collective-permute-start | bytes 6152 | tf_op jit(solution)/shard_map/ppermute | solution.py:150
  46.0 5.5 %collective-permute-start.32 = (f32[512]{0:T(512)S(1)}, f32[512]{0:T(512)S(1)}, u32[]{:S(2)}, u32[]{:S(2)}) collective-permute-start(f32[512]{0:T(512)S(1)} %add.139), channel_id=1, source_target_pairs={{0,2},{1,3},{2,0},{3,1},{4,6},{5,7},{6,4},{7,5},{8,10},{9,11},{10,... | collective-permute-start | bytes 6152 | tf_op jit(solution)/shard_map/ppermute | solution.py:150
  51.5 9.0 %collective-permute-start.6 = (bf16[512,1024]{1,0:T(8,128)(2,1)}, bf16[512,1024]{1,0:T(8,128)(2,1)S(1)}, u32[]{:S(2)}, u32[]{:S(2)}) collective-permute-start(bf16[512,1024]{1,0:T(8,128)(2,1)} %copy-done.3), channel_id=1, source_target_pairs={{0,4},{4,0},{8,12},{12,8},{16,20},{20,16},{24,28},{28,24},{1,5},{5... | collective-permute-start | bytes 3145736 | tf_op jit(solution)/shard_map/ppermute | solution.py:89
  52.1 26.2 %collective-permute-start = (bf16[1024,512]{1,0:T(8,128)(2,1)}, bf16[1024,512]{1,0:T(8,128)(2,1)S(1)}, u32[]{:S(2)}, u32[]{:S(2)}) collective-permute-start(bf16[1024,512]{1,0:T(8,128)(2,1)} %param.8), channel_id=1, source_target_pairs={{0,8},{4,12},{8,0},{12,4},{16,24},{20,28},{24,16},{28,20},{1,9},{5... | collective-permute-start | bytes 3145736 | tf_op jit(solution)/shard_map/ppermute | solution.py:89
  53.6 27.0 %collective-permute-start.4 = (bf16[512,1024]{1,0:T(8,128)(2,1)}, bf16[512,1024]{1,0:T(8,128)(2,1)S(1)}, u32[]{:S(2)}, u32[]{:S(2)}) collective-permute-start(bf16[512,1024]{1,0:T(8,128)(2,1)} %copy-done.2), channel_id=1, source_target_pairs={{0,4},{4,0},{8,12},{12,8},{16,20},{20,16},{24,28},{28,24},{1,5},{5... | collective-permute-start | bytes 3145736 | tf_op jit(solution)/shard_map/ppermute | solution.py:89
  56.7 1.7 copy-start.5
  56.8 4.4 %copy-start.4 = (f32[1024,512]{1,0:T(8,128)S(1)}, f32[1024,512]{1,0:T(8,128)}, u32[]{:S(2)}) copy-start(f32[1024,512]{1,0:T(8,128)} %fusion.18) | copy-start | bytes 6291460
  56.8 31.2 %collective-permute-start.19 = (bf16[512,512]{1,0:T(8,128)(2,1)S(1)}, bf16[512,512]{1,0:T(8,128)(2,1)S(1)}, u32[]{:S(2)}, u32[]{:S(2)}) collective-permute-start(bf16[512,512]{1,0:T(8,128)(2,1)S(1)} %get-tuple-element.35), channel_id=1, source_target_pairs={{0,16},{4,20},{8,24},{12,28},{16,0},{20,4},{24,8},{28,12},{1,17},{... | collective-permute-start | bytes 1572872 | tf_op jit(solution)/shard_map/ppermute | solution.py:89
  60.6 29.0 %collective-permute-start.11 = (bf16[512,512]{1,0:T(8,128)(2,1)S(1)}, bf16[512,512]{1,0:T(8,128)(2,1)S(1)}, u32[]{:S(2)}, u32[]{:S(2)}) collective-permute-start(bf16[512,512]{1,0:T(8,128)(2,1)S(1)} %get-tuple-element.34), channel_id=1, source_target_pairs={{0,8},{4,12},{8,0},{12,4},{16,24},{20,28},{24,16},{28,20},{1,9},{5... | collective-permute-start | bytes 1572872 | tf_op jit(solution)/shard_map/ppermute | solution.py:89
  63.0 16.9 %copy-start.7 = (f32[512,512]{0,1:T(8,128)S(1)}, f32[512,512]{0,1:T(8,128)}, u32[]{:S(2)}) copy-start(f32[512,512]{0,1:T(8,128)} %fusion.11) | copy-start | bytes 3145732
  63.0 54.8 %collective-permute-start.10 = (bf16[512,512]{1,0:T(8,128)(2,1)S(1)}, bf16[512,512]{1,0:T(8,128)(2,1)S(1)}, u32[]{:S(2)}, u32[]{:S(2)}) collective-permute-start(bf16[512,512]{1,0:T(8,128)(2,1)S(1)} %slice.79), channel_id=1, source_target_pairs={{0,8},{4,12},{8,0},{12,4},{16,24},{20,28},{24,16},{28,20},{1,9},{5... | collective-permute-start | bytes 1572872 | tf_op jit(solution)/shard_map/ppermute | solution.py:89
  78.3 39.5 %collective-permute-start.21 = (bf16[512,512]{1,0:T(8,128)(2,1)S(1)}, bf16[512,512]{1,0:T(8,128)(2,1)S(1)}, u32[]{:S(2)}, u32[]{:S(2)}) collective-permute-start(bf16[512,512]{1,0:T(8,128)(2,1)S(1)} %slice.87), channel_id=1, source_target_pairs={{0,16},{4,20},{8,24},{12,28},{16,0},{20,4},{24,8},{28,12},{1,17},{... | collective-permute-start | bytes 1572872 | tf_op jit(solution)/shard_map/ppermute | solution.py:89
  79.8 2.4 %copy-start.6 = (f32[1024,512]{1,0:T(8,128)S(1)}, f32[1024,512]{1,0:T(8,128)}, u32[]{:S(2)}) copy-start(f32[1024,512]{1,0:T(8,128)} %fusion.16) | copy-start | bytes 6291460
  80.6 31.3 %collective-permute-start.2 = (bf16[512,512]{1,0:T(8,128)(2,1)S(1)}, bf16[512,512]{1,0:T(8,128)(2,1)S(1)}, u32[]{:S(2)}, u32[]{:S(2)}) collective-permute-start(bf16[512,512]{1,0:T(8,128)(2,1)S(1)} %slice.72), channel_id=1, source_target_pairs={{0,8},{4,12},{8,0},{12,4},{16,24},{20,28},{24,16},{28,20},{1,9},{5... | collective-permute-start | bytes 1572872 | tf_op jit(solution)/shard_map/ppermute | solution.py:89
  88.0 25.5 %collective-permute-start.3 = (bf16[512,512]{1,0:T(8,128)(2,1)S(1)}, bf16[512,512]{1,0:T(8,128)(2,1)S(1)}, u32[]{:S(2)}, u32[]{:S(2)}) collective-permute-start(bf16[512,512]{1,0:T(8,128)(2,1)S(1)} %slice.73), channel_id=1, source_target_pairs={{0,16},{4,20},{8,24},{12,28},{16,0},{20,4},{24,8},{28,12},{1,17},{... | collective-permute-start | bytes 1572872 | tf_op jit(solution)/shard_map/ppermute | solution.py:89
  89.5 33.3 %collective-permute-start.20 = (bf16[512,512]{1,0:T(8,128)(2,1)S(1)}, bf16[512,512]{1,0:T(8,128)(2,1)S(1)}, u32[]{:S(2)}, u32[]{:S(2)}) collective-permute-start(bf16[512,512]{1,0:T(8,128)(2,1)S(1)} %add_convert_fusion.3), channel_id=1, source_target_pairs={{0,8},{4,12},{8,0},{12,4},{16,24},{20,28},{24,16},{28,20},{1,9},{5... | collective-permute-start | bytes 1572872 | tf_op jit(solution)/shard_map/ppermute | solution.py:89
  112.0 13.2 %collective-permute-start.12 = (bf16[512,512]{1,0:T(8,128)(2,1)S(1)}, bf16[512,512]{1,0:T(8,128)(2,1)S(1)}, u32[]{:S(2)}, u32[]{:S(2)}) collective-permute-start(bf16[512,512]{1,0:T(8,128)(2,1)S(1)} %add_convert_fusion.4), channel_id=1, source_target_pairs={{0,16},{4,20},{8,24},{12,28},{16,0},{20,4},{24,8},{28,12},{1,17},{... | collective-permute-start | bytes 1572872 | tf_op jit(solution)/shard_map/ppermute | solution.py:89
  125.7 9.1 %collective-permute-start.13 = (bf16[256,512]{1,0:T(8,128)(2,1)S(1)}, bf16[256,512]{1,0:T(8,128)(2,1)S(1)}, u32[]{:S(2)}, u32[]{:S(2)}) collective-permute-start(bf16[256,512]{1,0:T(8,128)(2,1)S(1)} %get-tuple-element.32), channel_id=1, source_target_pairs={{0,1},{3,2},{4,5},{7,6},{8,9},{11,10},{12,13},{15,14},{16,17},{19,... | collective-permute-start | bytes 786440 | tf_op jit(solution)/shard_map/ppermute | solution.py:127
  128.0 12.3 %collective-permute-start.16 = (bf16[256,512]{1,0:T(8,128)(2,1)S(1)}, bf16[256,512]{1,0:T(8,128)(2,1)S(1)}, u32[]{:S(2)}, u32[]{:S(2)}) collective-permute-start(bf16[256,512]{1,0:T(8,128)(2,1)S(1)} %get-tuple-element.33), channel_id=1, source_target_pairs={{0,1},{3,2},{4,5},{7,6},{8,9},{11,10},{12,13},{15,14},{16,17},{19,... | collective-permute-start | bytes 786440 | tf_op jit(solution)/shard_map/ppermute | solution.py:127
  130.1 26.0 %collective-permute-start.8 = (f32[512,512]{0,1:T(8,128)S(1)}, f32[512,512]{0,1:T(8,128)S(1)}, u32[]{:S(2)}, u32[]{:S(2)}) collective-permute-start(f32[512,512]{0,1:T(8,128)S(1)} %fusion.5), channel_id=1, source_target_pairs={{0,4},{4,0},{8,12},{12,8},{16,20},{20,16},{24,28},{28,24},{1,5},{5... | collective-permute-start | bytes 3145736 | tf_op jit(solution)/shard_map/ppermute | solution.py:89
  130.3 15.7 %collective-permute-start.22 = (bf16[256,512]{1,0:T(8,128)(2,1)S(1)}, bf16[256,512]{1,0:T(8,128)(2,1)S(1)}, u32[]{:S(2)}, u32[]{:S(2)}) collective-permute-start(bf16[256,512]{1,0:T(8,128)(2,1)S(1)} %get-tuple-element.38), channel_id=1, source_target_pairs={{0,1},{3,2},{4,5},{7,6},{8,9},{11,10},{12,13},{15,14},{16,17},{19,... | collective-permute-start | bytes 786440 | tf_op jit(solution)/shard_map/ppermute | solution.py:127
  131.6 17.4 %collective-permute-start.25 = (bf16[256,512]{1,0:T(8,128)(2,1)S(1)}, bf16[256,512]{1,0:T(8,128)(2,1)S(1)}, u32[]{:S(2)}, u32[]{:S(2)}) collective-permute-start(bf16[256,512]{1,0:T(8,128)(2,1)S(1)} %get-tuple-element.39), channel_id=1, source_target_pairs={{0,1},{3,2},{4,5},{7,6},{8,9},{11,10},{12,13},{15,14},{16,17},{19,... | collective-permute-start | bytes 786440 | tf_op jit(solution)/shard_map/ppermute | solution.py:127
  140.6 10.0 %collective-permute-start.14 = (bf16[256,512]{1,0:T(8,128)(2,1)S(1)}, bf16[256,512]{1,0:T(8,128)(2,1)S(1)}, u32[]{:S(2)}, u32[]{:S(2)}) collective-permute-start(bf16[256,512]{1,0:T(8,128)(2,1)S(1)} %get-tuple-element.30), channel_id=1, source_target_pairs={{1,2},{2,1},{5,6},{6,5},{9,10},{10,9},{13,14},{14,13},{17,18},{18,... | collective-permute-start | bytes 786440 | tf_op jit(solution)/shard_map/ppermute | solution.py:129
  141.2 10.7 %collective-permute-start.17 = (bf16[256,512]{1,0:T(8,128)(2,1)S(1)}, bf16[256,512]{1,0:T(8,128)(2,1)S(1)}, u32[]{:S(2)}, u32[]{:S(2)}) collective-permute-start(bf16[256,512]{1,0:T(8,128)(2,1)S(1)} %get-tuple-element.31), channel_id=1, source_target_pairs={{1,2},{2,1},{5,6},{6,5},{9,10},{10,9},{13,14},{14,13},{17,18},{18,... | collective-permute-start | bytes 786440 | tf_op jit(solution)/shard_map/ppermute | solution.py:129
  149.2 6.9 %copy-start.8 = (f32[512]{0:T(512)S(1)}, f32[512]{0:T(512)}, u32[]{:S(2)}) copy-start(f32[512]{0:T(512)} %param.10) | copy-start | bytes 6148
  149.2 4.1 %collective-permute-start.23 = (bf16[256,512]{1,0:T(8,128)(2,1)S(1)}, bf16[256,512]{1,0:T(8,128)(2,1)S(1)}, u32[]{:S(2)}, u32[]{:S(2)}) collective-permute-start(bf16[256,512]{1,0:T(8,128)(2,1)S(1)} %get-tuple-element.36), channel_id=1, source_target_pairs={{1,2},{2,1},{5,6},{6,5},{9,10},{10,9},{13,14},{14,13},{17,18},{18,... | collective-permute-start | bytes 786440 | tf_op jit(solution)/shard_map/ppermute | solution.py:129
  149.9 4.8 %collective-permute-start.26 = (bf16[256,512]{1,0:T(8,128)(2,1)S(1)}, bf16[256,512]{1,0:T(8,128)(2,1)S(1)}, u32[]{:S(2)}, u32[]{:S(2)}) collective-permute-start(bf16[256,512]{1,0:T(8,128)(2,1)S(1)} %get-tuple-element.37), channel_id=1, source_target_pairs={{1,2},{2,1},{5,6},{6,5},{9,10},{10,9},{13,14},{14,13},{17,18},{18,... | collective-permute-start | bytes 786440 | tf_op jit(solution)/shard_map/ppermute | solution.py:129
  150.6 15.6 %collective-permute-start.15 = (bf16[256,512]{1,0:T(8,128)(2,1)S(1)}, bf16[256,512]{1,0:T(8,128)(2,1)}, u32[]{:S(2)}, u32[]{:S(2)}) collective-permute-start(bf16[256,512]{1,0:T(8,128)(2,1)S(1)} %add_convert_fusion.11), channel_id=1, source_target_pairs={{1,0},{2,3},{5,4},{6,7},{9,8},{10,11},{13,12},{14,15},{17,16},{18,... | collective-permute-start | bytes 786440 | tf_op jit(solution)/shard_map/ppermute | solution.py:131
  152.0 19.8 %collective-permute-start.18 = (bf16[256,512]{1,0:T(8,128)(2,1)S(1)}, bf16[256,512]{1,0:T(8,128)(2,1)}, u32[]{:S(2)}, u32[]{:S(2)}) collective-permute-start(bf16[256,512]{1,0:T(8,128)(2,1)S(1)} %add_convert_fusion.9), channel_id=1, source_target_pairs={{1,0},{2,3},{5,4},{6,7},{9,8},{10,11},{13,12},{14,15},{17,16},{18,... | collective-permute-start | bytes 786440 | tf_op jit(solution)/shard_map/ppermute | solution.py:131
  153.4 23.0 %collective-permute-start.24 = (bf16[256,512]{1,0:T(8,128)(2,1)S(1)}, bf16[256,512]{1,0:T(8,128)(2,1)}, u32[]{:S(2)}, u32[]{:S(2)}) collective-permute-start(bf16[256,512]{1,0:T(8,128)(2,1)S(1)} %add_convert_fusion.7), channel_id=1, source_target_pairs={{1,0},{2,3},{5,4},{6,7},{9,8},{10,11},{13,12},{14,15},{17,16},{18,... | collective-permute-start | bytes 786440 | tf_op jit(solution)/shard_map/ppermute | solution.py:131
  154.8 24.5 %collective-permute-start.27 = (bf16[256,512]{1,0:T(8,128)(2,1)S(1)}, bf16[256,512]{1,0:T(8,128)(2,1)}, u32[]{:S(2)}, u32[]{:S(2)}) collective-permute-start(bf16[256,512]{1,0:T(8,128)(2,1)S(1)} %add_convert_fusion.5), channel_id=1, source_target_pairs={{1,0},{2,3},{5,4},{6,7},{9,8},{10,11},{13,12},{14,15},{17,16},{18,... | collective-permute-start | bytes 786440 | tf_op jit(solution)/shard_map/ppermute | solution.py:131

commit v2 on v1

--- a/solution.py
+++ b/solution.py
@@ -39,28 +39,47 @@
     return jnp.concatenate([out_a, out_b], axis=2).reshape(rows, KW)
 
 
-def scale_body(n_blk, at_ref, x_ref, gain_ref, *outs):
+def call(body, out_shape, flops, nbytes, name):
+    return pl.pallas_call(
+        body,
+        out_shape=out_shape,
+        cost_estimate=pl.CostEstimate(flops=flops, bytes_accessed=nbytes, transcendentals=0),
+        compiler_params=pltpu.CompilerParams(vmem_limit_bytes=16 * 1024 * 1024),
+        name=name,
+    )
+
+
+def after(value, *others):
+    return lax.optimization_barrier((value, *others))[0]
+
+
+def scale_body(at_ref, x_ref, gain_ref, mine_a, mine_b, sib_a, sib_b):
     wide = x_ref.shape[1]
-    part = wide // n_blk
+    part = wide // 8
+    quarter = part // 4
     total = None
-    for b in range(n_blk):
+    for b in range(8):
         xb = x_ref[:, b * part : (b + 1) * part].astype(F32)
         add = jnp.sum(xb * xb, axis=1, keepdims=True)
         total = add if total is None else total + add
     inv = lax.rsqrt(total * (1.0 / wide) + 1e-06)
     me = at_ref[0]
-    for o, out in enumerate(outs):
+    for o in range(8):
         start = pl.multiple_of((me ^ o) * part, part)
-        xb = x_ref[:, pl.ds(start, part)].astype(F32)
-        out[...] = (xb * inv * gain_ref[:, pl.ds(start, part)]).astype(BF16)
-
-
-def scaled_blocks(x, gain, n_blk, at):
+        outs = (sib_a, sib_b) if o & 1 else (mine_a, mine_b)
+        for q in range(4):
+            cols = pl.ds(start + q * quarter, quarter)
+            xb = x_ref[:, cols].astype(F32)
+            to = (o // 2 * 2 + q // 2) * quarter
+            outs[q % 2][:, to : to + quarter] = (xb * inv * gain_ref[:, cols]).astype(BF16)
+
+
+def scaled_parts(x, gain, at):
     rows, wide = x.shape
     step = 64
-    part = wide // n_blk
+    part = wide // 4
     return pl.pallas_call(
-        functools.partial(scale_body, n_blk),
+        scale_body,
         grid_spec=pltpu.PrefetchScalarGridSpec(
             num_scalar_prefetch=1,
             grid=(rows // step,),
@@ -68,15 +87,88 @@
                 pl.BlockSpec((step, wide), lambda r, at: (r, 0)),
                 pl.BlockSpec((1, wide), lambda r, at: (0, 0)),
             ],
-            out_specs=[pl.BlockSpec((step, part), lambda r, at: (r, 0))] * n_blk,
+            out_specs=[pl.BlockSpec((step, part), lambda r, at: (r, 0))] * 4,
         ),
-        out_shape=[jax.ShapeDtypeStruct((rows, part), BF16)] * n_blk,
+        out_shape=[jax.ShapeDtypeStruct((rows, part), BF16)] * 4,
         cost_estimate=pl.CostEstimate(
             flops=6 * rows * wide, bytes_accessed=4 * rows * wide, transcendentals=rows
         ),
-        compiler_params=pltpu.CompilerParams(vmem_limit_bytes=16 * 1024 * 1024),
+        compiler_params=pltpu.CompilerParams(vmem_limit_bytes=44 * 1024 * 1024),
         name="scale_rows",
     )(at, x, gain[None, :])
+
+
+def grad_body(mine, sib, dproj, dproj_sib, to_x, to_y, keep_y, keep_x, own_low, own_high):
+    quarter = mine.shape[1] // 8
+    extra = own_low.shape[0] - quarter
+
+    def rows(chip, high):
+        at = (2 * chip + high) * quarter
+        dims = (((0,), (0,)), ((), ()))
+        return lax.dot_general(
+            mine[:, at : at + quarter], dproj[...], dims, preferred_element_type=F32
+        ) + lax.dot_general(
+            sib[:, at : at + quarter], dproj_sib[...], dims, preferred_element_type=F32
+        )
+
+    if extra:
+        bias = jnp.sum(dproj[...].astype(F32), axis=0, keepdims=True) + jnp.sum(
+            dproj_sib[...].astype(F32), axis=0, keepdims=True
+        )
+        first = lax.broadcasted_iota(jnp.int32, (extra, 1), 0) == 0
+        below = jnp.where(first, bias, 0.0)
+    low = quarter + extra
+    for chip, ref, at in ((1, to_x, 0), (3, to_x, low), (2, keep_y, 0), (0, own_low, 0)):
+        ref[at : at + quarter] = rows(chip, 0).astype(ref.dtype)
+        if extra:
+            ref[at + quarter : at + low] = below.astype(ref.dtype)
+    for chip, ref, at in ((2, to_y, 0), (3, to_y, quarter), (1, keep_x, 0), (0, own_high, 0)):
+        ref[at : at + quarter] = rows(chip, 1).astype(ref.dtype)
+
+
+def grad_parts(mine, sib, dproj, dproj_sib, extra):
+    tok, wide = mine.shape
+    q = wide // 8
+    low = q + extra
+    kw = dproj.shape[1]
+    shapes = ((2 * low, BF16), (2 * q, BF16), (low, BF16), (q, BF16), (low, F32), (q, F32))
+    return call(
+        grad_body,
+        [jax.ShapeDtypeStruct((r, kw), t) for r, t in shapes],
+        4 * tok * wide * kw,
+        4 * tok * wide + 2 * wide * kw,
+        "grad_rows",
+    )(mine, sib, dproj, dproj_sib)
+
+
+def forward_body(places, n_init, *refs):
+    acts, refs = refs[:4], refs[4:]
+    init, weights, outs = refs[:n_init], refs[n_init:-2], refs[-2:]
+    quarter = acts[0].shape[1] // 8
+    for side, out in enumerate(outs):
+        total = init[side][...] if n_init else None
+        for (chip, high), w in zip(places, weights, strict=True):
+            for chunk in (0, 1):
+                at = (2 * chip + high) * quarter
+                add = jnp.dot(
+                    acts[2 * side + chunk][:, at : at + quarter],
+                    w[chunk * quarter : (chunk + 1) * quarter],
+                    preferred_element_type=F32,
+                )
+                total = add if total is None else total + add
+        out[...] = total
+
+
+def forward(acts, places, weights, init=()):
+    tok = acts[0].shape[0]
+    rows, kw = weights[0].shape
+    return call(
+        functools.partial(forward_body, places, len(init)),
+        [jax.ShapeDtypeStruct((tok, kw), F32)] * 2,
+        4 * tok * rows * kw * len(weights),
+        4 * tok * rows * len(weights) + 8 * tok * kw,
+        "forward",
+    )(*acts, *init, *weights)
 
 
 def by_permutes(hidden_in, segment_ids, key_weight, norm_gain, key_bias, key_cotangent):
@@ -84,72 +176,76 @@
     me = lax.axis_index("blk")
     own = key_weight.shape[0]
     half = own // 2
+    quarter = own // 4
 
     def over(bit):
         return lambda v: lax.ppermute(v, "blk", [(i, i ^ bit) for i in range(8)])
 
     core, px, py = over(1), over(2), over(4)
 
-    def dot_t(a, b):
-        return lax.dot_general(a, b, (((0,), (0,)), ((), ())), preferred_element_type=F32)
-
-    def dot(a, b):
-        return jnp.dot(a, b, preferred_element_type=F32)
-
-    w_x, w_y = px(key_weight), py(key_weight)
-    w_d = jnp.concatenate([px(w_y[:half]), py(w_x[half:])], axis=0)
+    w_low, w_high = key_weight[:half], key_weight[half:]
+    wy_low, wx_high = py(w_low), px(w_high)
 
     positions = positions_of(segment_ids).reshape(tok)
     cosine, sine = angles_of(positions, HEAD)
     dproj = rotate(key_cotangent.astype(F32), cosine, sine, -1.0).astype(BF16)
     dproj_sib = core(dproj)
 
-    blocks = scaled_blocks(hidden_in, norm_gain, 8, me.reshape(1).astype(jnp.int32))
-    mine = {j: blocks[j] for j in (0, 2, 4, 6)}
-    sib = {j: core(blocks[j ^ 1]) for j in (6, 2, 4, 0)}
-
-    def grad_rows(j):
-        return dot_t(mine[j], dproj) + dot_t(sib[j], dproj_sib)
-
-    g_d = grad_rows(6).astype(BF16)
-    d_x, d_y = px(g_d[:half]), py(g_d[half:])
-    g_x = grad_rows(2).astype(BF16)
-    g_y = grad_rows(4).astype(BF16)
-    x_low, y_high = px(g_x[:half]), py(g_y[half:])
-    x_high = px((g_x[half:].astype(F32) + d_y.astype(F32)).astype(BF16))
-    y_low = py((g_y[:half].astype(F32) + d_x.astype(F32)).astype(BF16))
-    g_0 = grad_rows(0)
+    mine_a, mine_b, send_a, send_b = scaled_parts(
+        hidden_in, norm_gain, me.reshape(1).astype(jnp.int32)
+    )
+    sib_a, sib_b = core(send_a), core(send_b)
+    acts = (mine_a, mine_b, sib_a, sib_b)
+
+    def widen(v):
+        return v.astype(F32)
+
+    def phase_one(parts):
+        to_x, to_y, keep_y, keep_x, own_low, own_high = parts
+        from_x, from_y = px(to_x), py(to_y)
+        low = own_low.shape[0]
+        more_y = (widen(keep_y) + widen(from_x[low:])).astype(BF16)
+        more_x = (widen(keep_x) + widen(from_y[quarter:])).astype(BF16)
+        return more_y, more_x, own_low + widen(from_x[:low]), own_high + widen(from_y[:quarter])
 
     n_z = lax.axis_index("dp")
     inner = (n_z == 1) | (n_z == 2)
 
     def along_z(g):
         into = lax.ppermute(g.astype(BF16), "dp", [(0, 1), (3, 2)])
-        pair = (g + into.astype(F32)).astype(BF16)
+        pair = (g + widen(into)).astype(BF16)
         other = lax.ppermute(pair, "dp", [(1, 2), (2, 1)])
-        total = (pair.astype(F32) + other.astype(F32)).astype(BF16)
+        total = (widen(pair) + widen(other)).astype(BF16)
         back = lax.ppermute(total, "dp", [(1, 0), (2, 3)])
-        return jnp.where(inner, total, back).astype(F32)
-
-    low = g_0[:half] + x_low.astype(F32) + y_low.astype(F32)
-    high = g_0[half:] + x_high.astype(F32) + y_high.astype(F32)
-    quarter = half // 2
-    done = [along_z(v) for v in (low[:quarter], low[quarter:], high[:quarter], high[quarter:])]
-    grad = jnp.concatenate(done, axis=0)
-
-    here = dot(mine[0], key_weight) + dot(mine[2], w_x) + dot(mine[4], w_y) + dot(mine[6], w_d)
-    there = dot(sib[0], key_weight) + dot(sib[2], w_x) + dot(sib[4], w_y) + dot(sib[6], w_d)
+        return widen(jnp.where(inner, total, back))
+
+    def phase_two(more_y, more_x, low, high):
+        return along_z(low + widen(py(more_y))), along_z(high + widen(px(more_x)))
+
+    part_a = grad_parts(mine_a, sib_a, dproj, dproj_sib, 16)
+    one_a = phase_one(part_a)
+    part_b = grad_parts(after(mine_b, part_a), sib_b, dproj, dproj_sib, 0)
+    one_b = phase_one(part_b)
+
+    own_w = after((w_low, w_high), part_b)
+    here = forward(acts, ((0, 0), (0, 1), (2, 0), (1, 1)), (*own_w, wy_low, wx_high))
+    low_a, high_a = phase_two(*one_a)
+    later = after((w_low, w_high, wy_low, wx_high), one_a)
+    wx_low, wy_high = px(later[0]), py(later[1])
+    wd_low, wd_high = px(later[2]), py(later[3])
+    low_b, high_b = phase_two(*one_b)
+
+    here, there = forward(
+        acts, ((1, 0), (2, 1), (3, 0), (3, 1)), (wx_low, wy_high, wd_low, wd_high), here
+    )
     projected = here + core(there) + key_bias[None, :]
     keys = rotate(projected, cosine, sine, 1.0).astype(BF16)
 
     scale = 1.0 / jnp.sqrt(F32(tok * 32))
-    bias = jnp.sum(dproj.astype(F32), axis=0)
-    for hop in (core, px, py):
-        bias = bias + hop(bias)
-    for bit in (1, 2):
-        bias = bias + lax.ppermute(bias, "dp", [(i, i ^ bit) for i in range(4)])
+    grad = jnp.concatenate([low_a[:quarter], low_b, high_a, high_b], axis=0)
+    bias = low_a[quarter]
     my_gain = lax.dynamic_slice(norm_gain, (me * own,), (own,))
-    gain_rows = jnp.sum(grad * key_weight.astype(F32), axis=1) / my_gain
+    gain_rows = jnp.sum(grad * widen(key_weight), axis=1) / my_gain
     grad_gain = lax.all_gather(gain_rows, "blk", axis=0, tiled=True)
     return (keys, grad * scale, bias * scale, grad_gain * scale)
 

time: 194 us -> 151 us (0.78)
  matrix products: 35.8 us -> 0 us
  waiting for transfers between devices: 85.3 us -> 52.6 us
  Pallas kernels: 5.38 us -> 28.5 us
  starting transfers between devices: 36.8 us -> 32.3 us
  local copies, waits for them, and re-layouts: 7.15 us -> 11 us
  other arithmetic: 12.1 us -> 15.2 us
    dot_general x16 -> x0, matrix products: 35.8 us -> none  [the longest x8 21.2 us: dot_t(): lax.dot_general(a, b, (((0,), (0,)), ((), ())), preferred_element_type=F32)]
    ppermute x19 -> x18, waiting for transfers between devices: 53.8 us -> 20 us  [over(): return lambda v: lax.ppermute(v, 'blk', [(i, i ^ bit) for i in range(8)])]
    pallas_call x1 -> x5, Pallas kernels: 5.38 us -> 28.5 us  [the longest x2 9.77 us: grad_parts(): call(grad_body, [jax.ShapeDtypeStruct((r, kw), t) for r, t in shapes], 4...]
    ppermute x4, waiting for transfers between devices: 17 us -> 23.2 us  [along_z(): back = lax.ppermute(total, 'dp', [(1, 0), (2, 3)])]
    convert_element_type x8 -> x20, other arithmetic: 0.87 us -> 6.38 us  [the longest x4 2.33 us: along_z(): into = lax.ppermute(g.astype(BF16), 'dp', [(0, 1), (3, 2)])]
    ppermute x4, waiting for transfers between devices: 14.6 us -> 9.39 us  [along_z(): into = lax.ppermute(g.astype(BF16), 'dp', [(0, 1), (3, 2)])]
    unnamed x20 -> x49, local copies, waits for them, and re-layouts: 3.46 us -> 8.18 us
    ppermute x2 -> x0, starting transfers between devices: 4.39 us -> none  [by_permutes(): bias = bias + lax.ppermute(bias, 'dp', [(i, i ^ bit) for i in range(4)])]
  transfers between devices with their start and end apart: 33 -> 30, of which waited for: 14 -> 13; matrix products, arithmetic and copies ran while one was open for 22% -> 11% of each run, Pallas kernels for 3% -> 13%
where the time goes in v2:
time: 151 us; the launch traced here: 150 us
  waiting for transfers between devices  52.6 us (35%)
  starting transfers between devices  32.3 us (21%)
  Pallas kernels  28.5 us (19%)
  other arithmetic  15.2 us (10%)
  local copies, waits for them, and re-layouts  11 us (7%)
  blocking collectives  9.6 us (6%)
    ppermute x4, waiting for transfers between devices, along_z(): back = lax.ppermute(total, 'dp', [(1, 0), (2, 3)])  23.2 us
    ppermute x18, waiting for transfers between devices, over(): return lambda v: lax.ppermute(v, 'blk', [(i, i ^ bit) for i in range(8)])  20 us
    ppermute x18, starting transfers between devices, over(): return lambda v: lax.ppermute(v, 'blk', [(i, i ^ bit) for i in range(8)])  16.8 us
    pallas_call x2, Pallas kernels, grad_parts(): call(grad_body, [jax.ShapeDtypeStruct((r, kw), t) for r, t in shapes], 4...  9.77 us
    pallas_call x2, Pallas kernels, forward(): call(functools.partial(forward_body, places, len(init)), [jax.ShapeDtypeS...  9.71 us
    all_gather x1, blocking collectives, by_permutes(): grad_gain = lax.all_gather(gain_rows, 'blk', axis=0, tiled=True)  9.6 us
    ppermute x4, waiting for transfers between devices, along_z(): into = lax.ppermute(g.astype(BF16), 'dp', [(0, 1), (3, 2)])  9.39 us
    pallas_call x1, Pallas kernels, scaled_parts(): pl.pallas_call(scale_body, grid_spec=pltpu.PrefetchScalarGridSpec(num_sca...  8.97 us
  transfers between devices with their start and end apart: 30, of which 13 were waited for; matrix products, arithmetic and copies ran while one was open for 11% of the time, Pallas kernels for 13%

profile of v2, /device:TPU:0, one launch (start us, length us, event | category | flops | bytes accessed | tf_op | source)
XLA Modules:
  0.0 150.2 jit_solution(12709377260666766517)
XLA Ops:
  1.4 9.0 %scale_rows.1 = (bf16[512,2048]{1,0:T(8,128)(2,1)S(1)}, bf16[512,2048]{1,0:T(8,128)(2,1)S(1)}, bf16[512,2048]{1,0:T(8,128)(2,1)}, bf16[512,2048]{1,0:T(8,128)(2,1)}) custom-call(s32[1]{0:T(128)} %bitcast.at_ref, bf16[512,8192]{1,0:T(8,128)(2,1)} %x_ref.1, f32[1,8192]{1,0:T(1,128)S(1)} %bitcast.17), custom_call_target="tpu_custom_call" | custom-call | flops 25165824 | bytes 16777216 | tf_op jit(solution)/shard_map/scale_rows/pallas_call | solution.py:81
  10.4 1.3 copy-done
  12.5 1.4 reshape.106
  13.9 1.8 %multiply_sine_fusion = (f32[512,64]{1,0:T(8,128)}, f32[512,64]{1,0:T(8,128)S(1)}, f32[512,64]{1,0:T(8,128)S(1)}) fusion(f32[64]{0:T(128)S(1)} %negate_power_fusion, f32[512]{0:T(512)S(1)} %bitcast.21), kind=kLoop, calls=%fused_computation.32 | loop fusion | flops 65536 | bytes 395520 | tf_op jit(solution)/shard_map/sin | solution.py:29
  15.7 0.9 subtract_convert_fusion.1
  17.9 1.0 fusion.5
  18.9 2.8 %collective-permute-start.3 = (bf16[512,512]{1,0:T(8,128)(2,1)}, bf16[512,512]{1,0:T(8,128)(2,1)}, u32[]{:S(2)}, u32[]{:S(2)}) collective-permute-start(bf16[512,512]{1,0:T(8,128)(2,1)} %get-tuple-element.52.refs_4_), channel_id=1, source_target_pairs={{0,16},{4,20},{8,24},{12,28},{16,0},{20,4},{24,8},{28,12},{1,17},{... | collective-permute-start | bytes 1572872 | tf_op jit(solution)/shard_map/ppermute | solution.py:182
  21.8 1.5 collective-permute-start.4
  23.3 4.7 %grad_rows.2 = (bf16[544,512]{1,0:T(8,128)(2,1)S(1)}, bf16[512,512]{1,0:T(8,128)(2,1)}, bf16[272,512]{1,0:T(8,128)(2,1)S(1)}, bf16[256,512]{1,0:T(8,128)(2,1)S(1...) custom-call(bf16[512,2048]{1,0:T(8,128)(2,1)S(1)} %get-tuple-element.31.mine.refs_0_, ...), custom_call_target="tpu_custom_call" | custom-call | flops 2147483648 | bytes 6291456 | tf_op jit(solution)/shard_map/grad_rows/pallas_call | solution.py:135
  28.8 5.1 %grad_rows.3 = (bf16[512,512]{1,0:T(8,128)(2,1)}, bf16[512,512]{1,0:T(8,128)(2,1)S(1)}, bf16[256,512]{1,0:T(8,128)(2,1)S(1)}, bf16[256,512]{1,0:T(8,128)(2,1)S(1...) custom-call(bf16[512,2048]{1,0:T(8,128)(2,1)S(1)} %copy-done.1, bf16[512,2048]{1,0:T(8,128)(2,1)} %collective-permute-done.1.sib.refs_3_, ...), custom_call_target="tpu_custom_call" | custom-call | flops 2147483648 | bytes 6291456 | tf_op jit(solution)/shard_map/grad_rows/pallas_call | solution.py:135
  35.3 0.8 copy-done.15
  37.0 1.7 %collective-permute-start.5 = (bf16[544,512]{1,0:T(8,128)(2,1)}, bf16[544,512]{1,0:T(8,128)(2,1)S(1)}, u32[]{:S(2)}, u32[]{:S(2)}) collective-permute-start(bf16[544,512]{1,0:T(8,128)(2,1)} %copy-done.14), channel_id=1, source_target_pairs={{0,8},{4,12},{8,0},{12,4},{16,24},{20,28},{24,16},{28,20},{1,9},{5... | collective-permute-start | bytes 1671176 | tf_op jit(solution)/shard_map/ppermute | solution.py:182
  38.7 1.5 %collective-permute-start.25 = (bf16[512,512]{1,0:T(8,128)(2,1)}, bf16[512,512]{1,0:T(8,128)(2,1)S(1)}, u32[]{:S(2)}, u32[]{:S(2)}) collective-permute-start(bf16[512,512]{1,0:T(8,128)(2,1)} %copy-done.15), channel_id=1, source_target_pairs={{0,16},{4,20},{8,24},{12,28},{16,0},{20,4},{24,8},{28,12},{1,17},{... | collective-permute-start | bytes 1572872 | tf_op jit(solution)/shard_map/ppermute | solution.py:182
  40.2 1.6 %copy-done.2 = bf16[512,2048]{1,0:T(8,128)(2,1)S(1)} copy-done((bf16[512,2048]{1,0:T(8,128)(2,1)S(1)}, bf16[512,2048]{1,0:T(8,128)(2,1)}, u32[]{:S(2)}) %copy-start.2) | copy-done | bytes 2097176
  41.8 5.2 %forward.2 = (f32[512,512]{1,0:T(8,128)S(1)}, f32[512,512]{1,0:T(8,128)S(1)}) custom-call(bf16[512,2048]{1,0:T(8,128)(2,1)S(1)} %get-tuple-element.31.mine.refs_0_, bf16[512,2048]{1,0:T(8,128)(2,1)S(1)} %copy-done.2, bf16[512,2048]{1,0:T(8,128)(2,1)} %collective-permute-done.sib.refs_2_, bf16[512,2048]{1,0:T(8,128)(2,1)} %collective-permute-done.1.sib.refs_3_, ...), custom_call_target="tpu_custom_call" | custom-call | flops 2147483648 | bytes 6291456 | tf_op jit(solution)/shard_map/forward/pallas_call | solution.py:165
  47.0 4.3 %collective-permute-done.16 = bf16[512,512]{1,0:T(8,128)(2,1)} collective-permute-done((bf16[512,512]{1,0:T(8,128)(2,1)}, bf16[512,512]{1,0:T(8,128)(2,1)}, u32[]{:S(2)}, u32[]{:S(2)}) %collective-permute-start.16) | collective-permute-done | bytes 524320 | tf_op jit(solution)/shard_map/ppermute | solution.py:182
  51.3 1.0 add_convert_fusion.12
  52.9 1.0 add_convert_fusion.13
  54.5 8.5 %collective-permute-done.25 = bf16[512,512]{1,0:T(8,128)(2,1)S(1)} collective-permute-done((bf16[512,512]{1,0:T(8,128)(2,1)}, bf16[512,512]{1,0:T(8,128)(2,1)S(1)}, u32[]{:S(2)}, u32[]{:S(2)}) %collective-permute-start.25) | collective-permute-done | bytes 524320 | tf_op jit(solution)/shard_map/ppermute | solution.py:182
  63.1 1.6 %collective-permute-start.26 = (bf16[256,512]{1,0:T(8,128)(2,1)S(1)}, bf16[256,512]{1,0:T(8,128)(2,1)S(1)}, u32[]{:S(2)}, u32[]{:S(2)}) collective-permute-start(bf16[256,512]{1,0:T(8,128)(2,1)S(1)} %add_convert_fusion.7), channel_id=1, source_target_pairs={{0,8},{4,12},{8,0},{12,4},{16,24},{20,28},{24,16},{28,20},{1,9},{5... | collective-permute-start | bytes 786440 | tf_op jit(solution)/shard_map/ppermute | solution.py:182
  65.3 3.3 %collective-permute-done.17 = bf16[256,512]{1,0:T(8,128)(2,1)S(1)} collective-permute-done((bf16[256,512]{1,0:T(8,128)(2,1)S(1)}, bf16[256,512]{1,0:T(8,128)(2,1)S(1)}, u32[]{:S(2)}, u32[]{:S(2)}) %collective-permute-start.17) | collective-permute-done | bytes 262176 | tf_op jit(solution)/shard_map/ppermute | solution.py:182
  68.6 1.1 fusion.3
  69.7 3.5 %collective-permute-start.18 = (bf16[256,512]{1,0:T(8,128)(2,1)S(1)}, bf16[256,512]{1,0:T(8,128)(2,1)S(1)}, u32[]{:S(2)}, u32[]{:S(2)}) collective-permute-start(bf16[256,512]{1,0:T(8,128)(2,1)S(1)} %fusion.3), channel_id=1, source_target_pairs={{0,1},{3,2},{4,5},{7,6},{8,9},{11,10},{12,13},{15,14},{16,17},{19,... | collective-permute-start | bytes 786440 | tf_op jit(solution)/shard_map/ppermute | solution.py:215
  73.2 1.1 fusion.2
  74.3 1.3 collective-permute-start.22
  75.7 1.3 collective-permute-start.27
  77.2 1.3 collective-permute-start.13
  79.0 0.9 collective-permute-done.18
  79.9 1.5 collective-permute-start.7
  81.4 1.1 add_convert_fusion.11
  82.5 3.0 %collective-permute-done.22 = bf16[256,512]{1,0:T(8,128)(2,1)S(1)} collective-permute-done((bf16[256,512]{1,0:T(8,128)(2,1)S(1)}, bf16[256,512]{1,0:T(8,128)(2,1)S(1)}, u32[]{:S(2)}, u32[]{:S(2)}) %collective-permute-start.22) | collective-permute-done | bytes 262176 | tf_op jit(solution)/shard_map/ppermute | solution.py:215
  86.3 3.5 %collective-permute-done.27 = bf16[256,512]{1,0:T(8,128)(2,1)S(1)} collective-permute-done((bf16[256,512]{1,0:T(8,128)(2,1)S(1)}, bf16[256,512]{1,0:T(8,128)(2,1)S(1)}, u32[]{:S(2)}, u32[]{:S(2)}) %collective-permute-start.27) | collective-permute-done | bytes 262176 | tf_op jit(solution)/shard_map/ppermute | solution.py:215
  90.8 2.0 %collective-permute-done.13 = bf16[272,512]{1,0:T(8,128)(2,1)S(1)} collective-permute-done((bf16[272,512]{1,0:T(8,128)(2,1)S(1)}, bf16[272,512]{1,0:T(8,128)(2,1)S(1)}, u32[]{:S(2)}, u32[]{:S(2)}) %collective-permute-start.13) | collective-permute-done | bytes 278560 | tf_op jit(solution)/shard_map/ppermute | solution.py:215
  92.8 1.1 collective-permute-start.8
  94.0 1.0 collective-permute-start.9
  96.6 1.3 collective-permute-start.20
  97.9 1.3 collective-permute-start.24
  99.2 3.4 %collective-permute-done.8.refs_7_ = bf16[512,512]{1,0:T(8,128)(2,1)S(1)} collective-permute-done((bf16[512,512]{1,0:T(8,128)(2,1)}, bf16[512,512]{1,0:T(8,128)(2,1)S(1)}, u32[]{:S(2)}, u32[]{:S(2)}) %collective-permute-start.8) | collective-permute-done | bytes 524320 | tf_op jit(solution)/shard_map/ppermute | solution.py:182
  102.6 1.3 collective-permute-start.29
  104.2 4.5 %forward.3 = (f32[512,512]{1,0:T(8,128)S(1)}, f32[512,512]{1,0:T(8,128)S(1)}) custom-call(bf16[512,2048]{1,0:T(8,128)(2,1)S(1)} %get-tuple-element.31.mine.refs_0_, bf16[512,2048]{1,0:T(8,128)(2,1)S(1)} %copy-done.2, bf16[512,2048]{1,0:T(8,128)(2,1)} %collective-permute-done.sib.refs_2_, bf16[512,2048]{1,0:T(8,128)(2,1)} %collective-permute-done.1.sib.refs_3_, ...), custom_call_target="tpu_custom_call" | custom-call | flops 2147483648 | bytes 6291456 | tf_op jit(solution)/shard_map/forward/pallas_call | solution.py:165
  109.0 1.3 collective-permute-start.15
  110.3 11.7 %collective-permute-done.20 = bf16[256,512]{1,0:T(8,128)(2,1)S(1)} collective-permute-done((bf16[256,512]{1,0:T(8,128)(2,1)S(1)}, bf16[256,512]{1,0:T(8,128)(2,1)S(1)}, u32[]{:S(2)}, u32[]{:S(2)}) %collective-permute-start.20) | collective-permute-done | bytes 262176 | tf_op jit(solution)/shard_map/ppermute | solution.py:219
  122.0 2.8 %collective-permute-done.24 = bf16[256,512]{1,0:T(8,128)(2,1)S(1)} collective-permute-done((bf16[256,512]{1,0:T(8,128)(2,1)S(1)}, bf16[256,512]{1,0:T(8,128)(2,1)S(1)}, u32[]{:S(2)}, u32[]{:S(2)}) %collective-permute-start.24) | collective-permute-done | bytes 262176 | tf_op jit(solution)/shard_map/ppermute | solution.py:219
  124.8 2.8 %collective-permute-done.29 = bf16[256,512]{1,0:T(8,128)(2,1)S(1)} collective-permute-done((bf16[256,512]{1,0:T(8,128)(2,1)S(1)}, bf16[256,512]{1,0:T(8,128)(2,1)S(1)}, u32[]{:S(2)}, u32[]{:S(2)}) %collective-permute-start.29) | collective-permute-done | bytes 262176 | tf_op jit(solution)/shard_map/ppermute | solution.py:219
  127.6 6.0 %collective-permute-done.15 = bf16[272,512]{1,0:T(8,128)(2,1)S(1)} collective-permute-done((bf16[272,512]{1,0:T(8,128)(2,1)S(1)}, bf16[272,512]{1,0:T(8,128)(2,1)S(1)}, u32[]{:S(2)}, u32[]{:S(2)}) %collective-permute-start.15) | collective-permute-done | bytes 278560 | tf_op jit(solution)/shard_map/ppermute | solution.py:219
  133.7 1.6 %multiply_reduce_fusion = (f32[1024]{0:T(1024)S(1)}, f32[1024,512]{1,0:T(8,128)}) fusion(bf16[1024,512]{1,0:T(8,128)(2,1)S(1)} %copy-done.17, f32[256,512]{1,0:T(8,128)S(1)} %select_convert_fusion.1, f32[256,512]{1,0:T(8,128)S(1)} %select_convert_fusion.2, f32[256,512]{1,0:T(8,128)S(1)} %select_convert_fusion.3, f32[256,512]{1,0:T(8,128)S(1)} %slice.72), kind=kLoop, calls=%fused_computation.1 | loop fusion | flops 3668992 | bytes 5246976 | tf_op jit(solution)/shard_map/reduce_sum | solution.py:248
  136.0 9.6 %all_gather.3 = f32[8192]{0:T(1024)S(1)} all-gather(f32[1024]{0:T(1024)S(1)} %dynamic-slice_divide_fusion), channel_id=1, replica_groups=mesh['blk'=8,'dp'=4] {'blk'}, dimensions={0}, use_global_device_ids=true | all-gather | bytes 36864 | tf_op jit(solution)/shard_map/all_gather | solution.py:249
  149.4 0.9 copy.15
  (105 shorter events, 17.0 us)
Async XLA Ops:
  1.4 10.9 %copy-start.21 = (s32[2,256]{1,0:T(2,128)S(1)}, s32[2,256]{1,0:T(2,128)}, u32[]{:S(2)}) copy-start(s32[2,256]{1,0:T(2,128)} %param.7) | copy-start | bytes 6148
  10.4 1.3 copy-start
  11.7 11.6 %collective-permute-start = (bf16[512,2048]{1,0:T(8,128)(2,1)}, bf16[512,2048]{1,0:T(8,128)(2,1)}, u32[]{:S(2)}, u32[]{:S(2)}) collective-permute-start(bf16[512,2048]{1,0:T(8,128)(2,1)} %get-tuple-element.33), channel_id=1, source_target_pairs={{0,4},{4,0},{8,12},{12,8},{16,20},{20,16},{24,28},{28,24},{1,5},{5... | collective-permute-start | bytes 6291464 | tf_op jit(solution)/shard_map/ppermute | solution.py:182
  12.2 16.6 %collective-permute-start.1 = (bf16[512,2048]{1,0:T(8,128)(2,1)}, bf16[512,2048]{1,0:T(8,128)(2,1)}, u32[]{:S(2)}, u32[]{:S(2)}) collective-permute-start(bf16[512,2048]{1,0:T(8,128)(2,1)} %get-tuple-element.34), channel_id=1, source_target_pairs={{0,4},{4,0},{8,12},{12,8},{16,20},{20,16},{24,28},{28,24},{1,5},{5... | collective-permute-start | bytes 6291464 | tf_op jit(solution)/shard_map/ppermute | solution.py:182
  15.7 1.6 %copy-start.18 = (f32[512,64]{1,0:T(8,128)}, f32[512,64]{1,0:T(8,128)S(1)}, u32[]{:S(2)}) copy-start(f32[512,64]{1,0:T(8,128)S(1)} %get-tuple-element.72) | copy-start | bytes 393220
  16.6 1.4 copy-start.16
  17.4 5.9 %collective-permute-start.2 = (bf16[512,512]{1,0:T(8,128)(2,1)S(1)}, bf16[512,512]{1,0:T(8,128)(2,1)S(1)}, u32[]{:S(2)}, u32[]{:S(2)}) collective-permute-start(bf16[512,512]{1,0:T(8,128)(2,1)S(1)} %bitcast.14), channel_id=1, source_target_pairs={{0,4},{4,0},{8,12},{12,8},{16,20},{20,16},{24,28},{28,24},{1,5},{5... | collective-permute-start | bytes 1572872 | tf_op jit(solution)/shard_map/ppermute | solution.py:182
  18.9 19.7 %collective-permute-start.3 = (bf16[512,512]{1,0:T(8,128)(2,1)}, bf16[512,512]{1,0:T(8,128)(2,1)}, u32[]{:S(2)}, u32[]{:S(2)}) collective-permute-start(bf16[512,512]{1,0:T(8,128)(2,1)} %get-tuple-element.52.refs_4_), channel_id=1, source_target_pairs={{0,16},{4,20},{8,24},{12,28},{16,0},{20,4},{24,8},{28,12},{1,17},{... | collective-permute-start | bytes 1572872 | tf_op jit(solution)/shard_map/ppermute | solution.py:182
  21.8 18.4 %collective-permute-start.4 = (bf16[512,512]{1,0:T(8,128)(2,1)}, bf16[512,512]{1,0:T(8,128)(2,1)}, u32[]{:S(2)}, u32[]{:S(2)}) collective-permute-start(bf16[512,512]{1,0:T(8,128)(2,1)} %get-tuple-element.53.refs_5_), channel_id=1, source_target_pairs={{0,8},{4,12},{8,0},{12,4},{16,24},{20,28},{24,16},{28,20},{1,9},{5... | collective-permute-start | bytes 1572872 | tf_op jit(solution)/shard_map/ppermute | solution.py:182
  23.3 5.5 %copy-start.1 = (bf16[512,2048]{1,0:T(8,128)(2,1)S(1)}, bf16[512,2048]{1,0:T(8,128)(2,1)}, u32[]{:S(2)}) copy-start(bf16[512,2048]{1,0:T(8,128)(2,1)} %copy-done) | copy-start | bytes 6291460
  28.8 5.1 %copy-start.3 = (f32[272,512]{1,0:T(8,128)}, f32[272,512]{1,0:T(8,128)S(1)}, u32[]{:S(2)}) copy-start(f32[272,512]{1,0:T(8,128)S(1)} %get-tuple-element.39) | copy-start | bytes 1671172
  28.8 5.1 %copy-start.5 = (f32[256,512]{1,0:T(8,128)}, f32[256,512]{1,0:T(8,128)S(1)}, u32[]{:S(2)}) copy-start(f32[256,512]{1,0:T(8,128)S(1)} %get-tuple-element.40) | copy-start | bytes 1572868
  28.8 5.1 %copy-start.7 = (bf16[256,512]{1,0:T(8,128)(2,1)}, bf16[256,512]{1,0:T(8,128)(2,1)S(1)}, u32[]{:S(2)}) copy-start(bf16[256,512]{1,0:T(8,128)(2,1)S(1)} %get-tuple-element.38) | copy-start | bytes 786436
  36.1 15.2 %collective-permute-start.16 = (bf16[512,512]{1,0:T(8,128)(2,1)}, bf16[512,512]{1,0:T(8,128)(2,1)}, u32[]{:S(2)}, u32[]{:S(2)}) collective-permute-start(bf16[512,512]{1,0:T(8,128)(2,1)} %get-tuple-element.42), channel_id=1, source_target_pairs={{0,8},{4,12},{8,0},{12,4},{16,24},{20,28},{24,16},{28,20},{1,9},{5... | collective-permute-start | bytes 1572872 | tf_op jit(solution)/shard_map/ppermute | solution.py:182
  36.7 16.2 %collective-permute-start.6 = (bf16[512,512]{1,0:T(8,128)(2,1)}, bf16[512,512]{1,0:T(8,128)(2,1)}, u32[]{:S(2)}, u32[]{:S(2)}) collective-permute-start(bf16[512,512]{1,0:T(8,128)(2,1)} %get-tuple-element.36), channel_id=1, source_target_pairs={{0,16},{4,20},{8,24},{12,28},{16,0},{20,4},{24,8},{28,12},{1,17},{... | collective-permute-start | bytes 1572872 | tf_op jit(solution)/shard_map/ppermute | solution.py:182
  37.0 27.7 %collective-permute-start.5 = (bf16[544,512]{1,0:T(8,128)(2,1)}, bf16[544,512]{1,0:T(8,128)(2,1)S(1)}, u32[]{:S(2)}, u32[]{:S(2)}) collective-permute-start(bf16[544,512]{1,0:T(8,128)(2,1)} %copy-done.14), channel_id=1, source_target_pairs={{0,8},{4,12},{8,0},{12,4},{16,24},{20,28},{24,16},{28,20},{1,9},{5... | collective-permute-start | bytes 1671176 | tf_op jit(solution)/shard_map/ppermute | solution.py:182
  38.7 24.3 %collective-permute-start.25 = (bf16[512,512]{1,0:T(8,128)(2,1)}, bf16[512,512]{1,0:T(8,128)(2,1)S(1)}, u32[]{:S(2)}, u32[]{:S(2)}) collective-permute-start(bf16[512,512]{1,0:T(8,128)(2,1)} %copy-done.15), channel_id=1, source_target_pairs={{0,16},{4,20},{8,24},{12,28},{16,0},{20,4},{24,8},{28,12},{1,17},{... | collective-permute-start | bytes 1572872 | tf_op jit(solution)/shard_map/ppermute | solution.py:182
  40.2 1.6 %copy-start.2 = (bf16[512,2048]{1,0:T(8,128)(2,1)S(1)}, bf16[512,2048]{1,0:T(8,128)(2,1)}, u32[]{:S(2)}) copy-start(bf16[512,2048]{1,0:T(8,128)(2,1)} %copy-done) | copy-start | bytes 6291460
  41.8 9.5 %copy-start.12 = (bf16[256,512]{1,0:T(8,128)(2,1)S(1)}, bf16[256,512]{1,0:T(8,128)(2,1)}, u32[]{:S(2)}) copy-start(bf16[256,512]{1,0:T(8,128)(2,1)} %copy-done.11) | copy-start | bytes 786436
  41.8 11.1 %copy-start.8 = (bf16[256,512]{1,0:T(8,128)(2,1)S(1)}, bf16[256,512]{1,0:T(8,128)(2,1)}, u32[]{:S(2)}) copy-start(bf16[256,512]{1,0:T(8,128)(2,1)} %copy-done.7) | copy-start | bytes 786436
  41.8 21.2 %copy-start.10 = (bf16[256,512]{1,0:T(8,128)(2,1)S(1)}, bf16[256,512]{1,0:T(8,128)(2,1)}, u32[]{:S(2)}) copy-start(bf16[256,512]{1,0:T(8,128)(2,1)} %copy-done.9) | copy-start | bytes 786436
  47.0 26.2 %copy-start.6 = (f32[256,512]{1,0:T(8,128)S(1)}, f32[256,512]{1,0:T(8,128)}, u32[]{:S(2)}) copy-start(f32[256,512]{1,0:T(8,128)} %copy-done.5) | copy-start | bytes 1572868
  52.3 16.3 %collective-permute-start.17 = (bf16[256,512]{1,0:T(8,128)(2,1)S(1)}, bf16[256,512]{1,0:T(8,128)(2,1)S(1)}, u32[]{:S(2)}, u32[]{:S(2)}) collective-permute-start(bf16[256,512]{1,0:T(8,128)(2,1)S(1)} %add_convert_fusion.12), channel_id=1, source_target_pairs={{0,16},{4,20},{8,24},{12,28},{16,0},{20,4},{24,8},{28,12},{1,17},{... | collective-permute-start | bytes 786440 | tf_op jit(solution)/shard_map/ppermute | solution.py:182
  53.9 19.2 %collective-permute-start.21 = (bf16[256,512]{1,0:T(8,128)(2,1)S(1)}, bf16[256,512]{1,0:T(8,128)(2,1)S(1)}, u32[]{:S(2)}, u32[]{:S(2)}) collective-permute-start(bf16[256,512]{1,0:T(8,128)(2,1)S(1)} %add_convert_fusion.13), channel_id=1, source_target_pairs={{0,8},{4,12},{8,0},{12,4},{16,24},{20,28},{24,16},{28,20},{1,9},{5... | collective-permute-start | bytes 786440 | tf_op jit(solution)/shard_map/ppermute | solution.py:182
  63.1 12.5 %collective-permute-start.26 = (bf16[256,512]{1,0:T(8,128)(2,1)S(1)}, bf16[256,512]{1,0:T(8,128)(2,1)S(1)}, u32[]{:S(2)}, u32[]{:S(2)}) collective-permute-start(bf16[256,512]{1,0:T(8,128)(2,1)S(1)} %add_convert_fusion.7), channel_id=1, source_target_pairs={{0,8},{4,12},{8,0},{12,4},{16,24},{20,28},{24,16},{28,20},{1,9},{5... | collective-permute-start | bytes 786440 | tf_op jit(solution)/shard_map/ppermute | solution.py:182
  64.7 12.3 %copy-start.4 = (f32[272,512]{1,0:T(8,128)S(1)}, f32[272,512]{1,0:T(8,128)}, u32[]{:S(2)}) copy-start(f32[272,512]{1,0:T(8,128)} %copy-done.3) | copy-start | bytes 1671172
  64.7 12.3 %collective-permute-start.12 = (bf16[272,512]{1,0:T(8,128)(2,1)S(1)}, bf16[272,512]{1,0:T(8,128)(2,1)S(1)}, u32[]{:S(2)}, u32[]{:S(2)}) collective-permute-start(bf16[272,512]{1,0:T(8,128)(2,1)S(1)} %add_convert_fusion.4), channel_id=1, source_target_pairs={{0,16},{4,20},{8,24},{12,28},{16,0},{20,4},{24,8},{28,12},{1,17},{... | collective-permute-start | bytes 835592 | tf_op jit(solution)/shard_map/ppermute | solution.py:182
  69.7 10.2 %collective-permute-start.18 = (bf16[256,512]{1,0:T(8,128)(2,1)S(1)}, bf16[256,512]{1,0:T(8,128)(2,1)S(1)}, u32[]{:S(2)}, u32[]{:S(2)}) collective-permute-start(bf16[256,512]{1,0:T(8,128)(2,1)S(1)} %fusion.3), channel_id=1, source_target_pairs={{0,1},{3,2},{4,5},{7,6},{8,9},{11,10},{12,13},{15,14},{16,17},{19,... | collective-permute-start | bytes 786440 | tf_op jit(solution)/shard_map/ppermute | solution.py:215
  74.3 11.3 %collective-permute-start.22 = (bf16[256,512]{1,0:T(8,128)(2,1)S(1)}, bf16[256,512]{1,0:T(8,128)(2,1)S(1)}, u32[]{:S(2)}, u32[]{:S(2)}) collective-permute-start(bf16[256,512]{1,0:T(8,128)(2,1)S(1)} %get-tuple-element.60), channel_id=1, source_target_pairs={{0,1},{3,2},{4,5},{7,6},{8,9},{11,10},{12,13},{15,14},{16,17},{19,... | collective-permute-start | bytes 786440 | tf_op jit(solution)/shard_map/ppermute | solution.py:215
  75.7 14.1 %collective-permute-start.27 = (bf16[256,512]{1,0:T(8,128)(2,1)S(1)}, bf16[256,512]{1,0:T(8,128)(2,1)S(1)}, u32[]{:S(2)}, u32[]{:S(2)}) collective-permute-start(bf16[256,512]{1,0:T(8,128)(2,1)S(1)} %fusion.4), channel_id=1, source_target_pairs={{0,1},{3,2},{4,5},{7,6},{8,9},{11,10},{12,13},{15,14},{16,17},{19,... | collective-permute-start | bytes 786440 | tf_op jit(solution)/shard_map/ppermute | solution.py:215
  77.2 15.6 %collective-permute-start.13 = (bf16[272,512]{1,0:T(8,128)(2,1)S(1)}, bf16[272,512]{1,0:T(8,128)(2,1)S(1)}, u32[]{:S(2)}, u32[]{:S(2)}) collective-permute-start(bf16[272,512]{1,0:T(8,128)(2,1)S(1)} %get-tuple-element.58), channel_id=1, source_target_pairs={{0,1},{3,2},{4,5},{7,6},{8,9},{11,10},{12,13},{15,14},{16,17},{19,... | collective-permute-start | bytes 835592 | tf_op jit(solution)/shard_map/ppermute | solution.py:215
  78.5 18.1 %collective-permute-start.10 = (bf16[512,512]{1,0:T(8,128)(2,1)}, bf16[512,512]{1,0:T(8,128)(2,1)S(1)}, u32[]{:S(2)}, u32[]{:S(2)}) collective-permute-start(bf16[512,512]{1,0:T(8,128)(2,1)} %collective-permute-done.4.refs_7_), channel_id=1, source_target_pairs={{0,16},{4,20},{8,24},{12,28},{16,0},{20,4},{24,8},{28,12},{1,17},{... | collective-permute-start | bytes 1572872 | tf_op jit(solution)/shard_map/ppermute | solution.py:182
  79.9 18.0 %collective-permute-start.7 = (bf16[512,512]{1,0:T(8,128)(2,1)}, bf16[512,512]{1,0:T(8,128)(2,1)S(1)}, u32[]{:S(2)}, u32[]{:S(2)}) collective-permute-start(bf16[512,512]{1,0:T(8,128)(2,1)} %get-tuple-element.52.refs_4_), channel_id=1, source_target_pairs={{0,8},{4,12},{8,0},{12,4},{16,24},{20,28},{24,16},{28,20},{1,9},{5... | collective-permute-start | bytes 1572872 | tf_op jit(solution)/shard_map/ppermute | solution.py:182
  85.5 8.5 %collective-permute-start.19 = (bf16[256,512]{1,0:T(8,128)(2,1)S(1)}, bf16[256,512]{1,0:T(8,128)(2,1)S(1)}, u32[]{:S(2)}, u32[]{:S(2)}) collective-permute-start(bf16[256,512]{1,0:T(8,128)(2,1)S(1)} %add_convert_fusion.11), channel_id=1, source_target_pairs={{1,2},{2,1},{5,6},{6,5},{9,10},{10,9},{13,14},{14,13},{17,18},{18,... | collective-permute-start | bytes 786440 | tf_op jit(solution)/shard_map/ppermute | solution.py:217
  89.8 5.2 %collective-permute-start.23 = (bf16[256,512]{1,0:T(8,128)(2,1)S(1)}, bf16[256,512]{1,0:T(8,128)(2,1)S(1)}, u32[]{:S(2)}, u32[]{:S(2)}) collective-permute-start(bf16[256,512]{1,0:T(8,128)(2,1)S(1)} %add_convert_fusion.9), channel_id=1, source_target_pairs={{1,2},{2,1},{5,6},{6,5},{9,10},{10,9},{13,14},{14,13},{17,18},{18,... | collective-permute-start | bytes 786440 | tf_op jit(solution)/shard_map/ppermute | solution.py:217
  92.8 9.8 %collective-permute-start.8 = (bf16[512,512]{1,0:T(8,128)(2,1)}, bf16[512,512]{1,0:T(8,128)(2,1)S(1)}, u32[]{:S(2)}, u32[]{:S(2)}) collective-permute-start(bf16[512,512]{1,0:T(8,128)(2,1)} %get-tuple-element.53.refs_5_), channel_id=1, source_target_pairs={{0,16},{4,20},{8,24},{12,28},{16,0},{20,4},{24,8},{28,12},{1,17},{... | collective-permute-start | bytes 1572872 | tf_op jit(solution)/shard_map/ppermute | solution.py:182
  94.0 10.2 %collective-permute-start.9 = (bf16[512,512]{1,0:T(8,128)(2,1)}, bf16[512,512]{1,0:T(8,128)(2,1)S(1)}, u32[]{:S(2)}, u32[]{:S(2)}) collective-permute-start(bf16[512,512]{1,0:T(8,128)(2,1)} %collective-permute-done.3.refs_6_), channel_id=1, source_target_pairs={{0,8},{4,12},{8,0},{12,4},{16,24},{20,28},{24,16},{28,20},{1,9},{5... | collective-permute-start | bytes 1572872 | tf_op jit(solution)/shard_map/ppermute | solution.py:182
  95.0 0.8 collective-permute-start.28
  95.8 13.1 %collective-permute-start.14 = (bf16[272,512]{1,0:T(8,128)(2,1)S(1)}, bf16[272,512]{1,0:T(8,128)(2,1)S(1)}, u32[]{:S(2)}, u32[]{:S(2)}) collective-permute-start(bf16[272,512]{1,0:T(8,128)(2,1)S(1)} %add_convert_fusion.3), channel_id=1, source_target_pairs={{1,2},{2,1},{5,6},{6,5},{9,10},{10,9},{13,14},{14,13},{17,18},{18,... | collective-permute-start | bytes 835592 | tf_op jit(solution)/shard_map/ppermute | solution.py:217
  96.6 25.4 %collective-permute-start.20 = (bf16[256,512]{1,0:T(8,128)(2,1)S(1)}, bf16[256,512]{1,0:T(8,128)(2,1)S(1)}, u32[]{:S(2)}, u32[]{:S(2)}) collective-permute-start(bf16[256,512]{1,0:T(8,128)(2,1)S(1)} %add_convert_fusion.10), channel_id=1, source_target_pairs={{1,0},{2,3},{5,4},{6,7},{9,8},{10,11},{13,12},{14,15},{17,16},{18,... | collective-permute-start | bytes 786440 | tf_op jit(solution)/shard_map/ppermute | solution.py:219
  97.9 26.9 %collective-permute-start.24 = (bf16[256,512]{1,0:T(8,128)(2,1)S(1)}, bf16[256,512]{1,0:T(8,128)(2,1)S(1)}, u32[]{:S(2)}, u32[]{:S(2)}) collective-permute-start(bf16[256,512]{1,0:T(8,128)(2,1)S(1)} %add_convert_fusion.8), channel_id=1, source_target_pairs={{1,0},{2,3},{5,4},{6,7},{9,8},{10,11},{13,12},{14,15},{17,16},{18,... | collective-permute-start | bytes 786440 | tf_op jit(solution)/shard_map/ppermute | solution.py:219
  102.6 25.0 %collective-permute-start.29 = (bf16[256,512]{1,0:T(8,128)(2,1)S(1)}, bf16[256,512]{1,0:T(8,128)(2,1)S(1)}, u32[]{:S(2)}, u32[]{:S(2)}) collective-permute-start(bf16[256,512]{1,0:T(8,128)(2,1)S(1)} %add_convert_fusion.5), channel_id=1, source_target_pairs={{1,0},{2,3},{5,4},{6,7},{9,8},{10,11},{13,12},{14,15},{17,16},{18,... | collective-permute-start | bytes 786440 | tf_op jit(solution)/shard_map/ppermute | solution.py:219
  108.8 38.0 %collective-permute-start.11 = (f32[512,512]{1,0:T(8,128)S(1)}, f32[512,512]{1,0:T(8,128)S(1)}, u32[]{:S(2)}, u32[]{:S(2)}) collective-permute-start(f32[512,512]{1,0:T(8,128)S(1)} %get-tuple-element.57), channel_id=1, source_target_pairs={{0,4},{4,0},{8,12},{12,8},{16,20},{20,16},{24,28},{28,24},{1,5},{5... | collective-permute-start | bytes 3145736 | tf_op jit(solution)/shard_map/ppermute | solution.py:182
  109.0 24.7 %collective-permute-start.15 = (bf16[272,512]{1,0:T(8,128)(2,1)S(1)}, bf16[272,512]{1,0:T(8,128)(2,1)S(1)}, u32[]{:S(2)}, u32[]{:S(2)}) collective-permute-start(bf16[272,512]{1,0:T(8,128)(2,1)S(1)} %add_convert_fusion.2), channel_id=1, source_target_pairs={{1,0},{2,3},{5,4},{6,7},{9,8},{10,11},{13,12},{14,15},{17,16},{18,... | collective-permute-start | bytes 835592 | tf_op jit(solution)/shard_map/ppermute | solution.py:219
  122.0 11.7 %copy-start.17 = (bf16[1024,512]{1,0:T(8,128)(2,1)S(1)}, bf16[1024,512]{1,0:T(8,128)(2,1)}, u32[]{:S(2)}) copy-start(bf16[1024,512]{1,0:T(8,128)(2,1)} %param.8) | copy-start | bytes 3145732
  133.7 13.1 %copy-start.22 = (f32[512]{0:T(512)S(1)}, f32[512]{0:T(512)}, u32[]{:S(2)}) copy-start(f32[512]{0:T(512)} %param.10) | copy-start | bytes 6148
  146.8 1.0 copy-start.19
  146.8 1.0 copy-start.20
  (5 other events, 3.8 us)

commit v3 on v1

v3 whole, which is shorter than its diff:
```python
import functools

import jax
import jax.numpy as jnp
from jax import lax
from jax.experimental import pallas as pl
from jax.experimental.pallas import tpu as pltpu
from jax.sharding import PartitionSpec as P

KVH = 4
HEAD = 128
KW = 512
F32 = jnp.float32
BF16 = jnp.bfloat16


def positions_of(segs):
    same = segs[:, :, None] == segs[:, None, :]
    idx = jnp.arange(segs.shape[1], dtype=jnp.int32)
    earlier = idx[None, :] < idx[:, None]
    return jnp.sum((same & earlier[None]).astype(jnp.int32), axis=2)


def angles_of(pos, head):
    half = head // 2
    freq = jnp.arange(half, dtype=F32) * (2.0 / head)
    inv = jnp.power(F32(1000000.0), -freq)
    ang = pos.astype(F32)[:, None] * inv[None, :]
    return (jnp.cos(ang)[:, None, :], jnp.sin(ang)[:, None, :])


def rotate(values, cosine, sine, sign):
    rows = values.shape[0]
    heads = values.reshape(rows, KVH, HEAD)
    first = heads[:, :, : HEAD // 2]
    second = heads[:, :, HEAD // 2 :]
    out_a = first * cosine - sign * second * sine
    out_b = second * cosine + sign * first * sine
    return jnp.concatenate([out_a, out_b], axis=2).reshape(rows, KW)


def after(value, *others):
    return lax.optimization_barrier((value, *others))[0]


def call(body, out_shape, name):
    return pl.pallas_call(
        body,
        out_shape=out_shape,
        cost_estimate=pl.CostEstimate(flops=1, bytes_accessed=1, transcendentals=0),
        compiler_params=pltpu.CompilerParams(vmem_limit_bytes=10 * 1024 * 1024),
        name=name,
    )


def scale_body(at_ref, x_ref, gain_ref, *outs):
    wide = x_ref.shape[1]
    part = wide // 8
    half = part // 2
    total = None
    for b in range(8):
        xb = x_ref[:, b * part : (b + 1) * part].astype(F32)
        add = jnp.sum(xb * xb, axis=1, keepdims=True)
        total = add if total is None else total + add
    inv = lax.rsqrt(total * (1.0 / wide) + 1e-06)
    me = at_ref[0]
    mine, sib, rest = outs[:8], outs[8:12], outs[12]
    places = {8 + 3: 0, 8 + 1: 1, 8 + 2: 2, 12 + 3: 3}
    for o in range(8):
        start = pl.multiple_of((me ^ o) * part, part)
        for chunk in range(2):
            cols = pl.ds(start + chunk * half, half)
            xb = x_ref[:, cols].astype(F32)
            done = (xb * inv * gain_ref[:, cols]).astype(BF16)
            at = 4 * chunk + o // 2
            if not o & 1:
                mine[at][...] = done
            elif 8 + at in places:
                sib[places[8 + at]][...] = done
            else:
                at = max(at - 3, 0) * half
                rest[:, at : at + half] = done


def scaled_parts(x, gain, at):
    rows, wide = x.shape
    step = 64
    widths = [wide // 16] * 12 + [wide // 4]
    return pl.pallas_call(
        scale_body,
        grid_spec=pltpu.PrefetchScalarGridSpec(
            num_scalar_prefetch=1,
            grid=(rows // step,),
            in_specs=[
                pl.BlockSpec((step, wide), lambda r, at: (r, 0)),
                pl.BlockSpec((1, wide), lambda r, at: (0, 0)),
            ],
            out_specs=[pl.BlockSpec((step, n), lambda r, at: (r, 0)) for n in widths],
        ),
        out_shape=[jax.ShapeDtypeStruct((rows, n), BF16) for n in widths],
        cost_estimate=pl.CostEstimate(flops=1, bytes_accessed=1, transcendentals=0),
        compiler_params=pltpu.CompilerParams(vmem_limit_bytes=12 * 1024 * 1024),
        name="scale_rows",
    )(at, x, gain[None, :])


def turn(v, cosine, sine):
    return v * cosine + pltpu.roll(v, HEAD // 2, 1) * sine


def turn_body(v_ref, cos_ref, sin_ref, out_ref):
    for h in range(KVH):
        cols = slice(h * HEAD, (h + 1) * HEAD)
        out_ref[:, cols] = turn(v_ref[:, cols].astype(F32), cos_ref[...], sin_ref[...]).astype(BF16)


def keys_body(here, there, bias, cos_ref, sin_ref, out_ref):
    for h in range(KVH):
        cols = slice(h * HEAD, (h + 1) * HEAD)
        v = here[:, cols] + there[:, cols] + bias[:, cols]
        out_ref[:, cols] = turn(v, cos_ref[...], -sin_ref[...]).astype(BF16)


def product(mine, sib, dproj, dproj_sib):
    dims = (((0,), (0,)), ((), ()))
    return lax.dot_general(mine, dproj, dims, preferred_element_type=F32) + lax.dot_general(
        sib, dproj_sib, dims, preferred_element_type=F32
    )


def spread(rows, chip, outs):
    to_x, to_y, keep_y, keep_x = outs
    half = rows.shape[0] // 2
    low = {1: (to_x, 0), 3: (to_x, half), 2: (keep_y, 0)}[chip]
    high = {2: (to_y, 0), 3: (to_y, half), 1: (keep_x, 0)}[chip]
    for (ref, at), part in ((low, rows[:half]), (high, rows[half:])):
        ref[at : at + half] = part.astype(ref.dtype)


def first_grad_body(m1, m2, m3, s1, s2, s3, dproj, dproj_sib, *outs):
    for chip, mine, sib in ((3, m3, s3), (1, m1, s1), (2, m2, s2)):
        spread(product(mine[...], sib[...], dproj[...], dproj_sib[...]), chip, outs)


def second_grad_body(m_a0, m0, m1, m2, m3, s3, rest, dproj, dproj_sib, own_a, own_b, *outs):
    half = m0.shape[1]
    own_a[...] = product(m_a0[...], rest[:, :half], dproj[...], dproj_sib[...])
    for chip, mine in ((3, m3), (1, m1), (2, m2), (0, m0)):
        sib = s3[...] if chip == 3 else rest[:, (chip + 1) * half : (chip + 2) * half]
        rows = product(mine[...], sib, dproj[...], dproj_sib[...])
        if chip:
            spread(rows, chip, outs)
        else:
            own_b[...] = rows


def forward_body(weights_of, *refs):
    places, n_acts, n_init = weights_of
    acts, init, weights, outs = (
        refs[:n_acts],
        refs[n_acts : n_acts + n_init],
        refs[n_acts + n_init : -2],
        refs[-2:],
    )
    for side, out in enumerate(outs):
        total = init[side][...] if n_init else None
        for mine, sib, col, w, row in places:
            half = acts[0].shape[1]
            rows = acts[sib][:, col * half : (col + 1) * half] if side else acts[mine][...]
            add = jnp.dot(
                rows, weights[w][row * half : (row + 1) * half], preferred_element_type=F32
            )
            total = add if total is None else total + add
        out[...] = total


def forward(acts, places, weights, init=()):
    tok, kw = acts[0].shape[0], weights[0].shape[1]
    return call(
        functools.partial(forward_body, (places, len(acts), len(init))),
        [jax.ShapeDtypeStruct((tok, kw), F32)] * 2,
        "forward",
    )(*acts, *init, *weights)


def by_permutes(hidden_in, segment_ids, key_weight, norm_gain, key_bias, key_cotangent):
    tok = hidden_in.shape[0]
    me = lax.axis_index("blk")
    own, kw = key_weight.shape
    half = own // 2
    quarter = own // 4

    def over(bit):
        return lambda v: lax.ppermute(v, "blk", [(i, i ^ bit) for i in range(8)])

    core, px, py = over(1), over(2), over(4)

    def widen(v):
        return v.astype(F32)

    w_x, w_y = px(key_weight), py(key_weight)

    positions = positions_of(segment_ids).reshape(tok)
    lane = jnp.arange(HEAD, dtype=jnp.int32)
    freq = (lane % (HEAD // 2)).astype(F32) * (2.0 / HEAD)
    angle = positions.astype(F32)[:, None] * jnp.power(F32(1000000.0), -freq)[None, :]
    cosine = jnp.cos(angle)
    sine = jnp.sin(angle) * jnp.where(lane < HEAD // 2, 1.0, -1.0)[None, :]
    dproj = call(turn_body, jax.ShapeDtypeStruct((tok, kw), BF16), "turn_back")(
        key_cotangent, cosine, sine
    )
    n = tok // 2
    dproj_sib = jnp.concatenate([core(dproj[:n]), core(dproj[n:])], axis=0)

    parts = scaled_parts(
        after(hidden_in, dproj_sib), norm_gain, me.reshape(1).astype(jnp.int32)
    )
    mine_a, mine_b, (s_a3, s_a1, s_a2, s_b3, rest) = parts[:4], parts[4:8], parts[8:]
    s_a3, s_a1, s_a2 = core(s_a3), core(s_a1), core(s_a2)

    def part_shapes(h):
        shapes = ((2 * h, BF16), (2 * h, BF16), (h, BF16), (h, BF16))
        return [jax.ShapeDtypeStruct((r, kw), t) for r, t in shapes]

    def add_up(part, from_x, from_y):
        _, _, keep_y, keep_x = part
        more_y = (widen(keep_y) + widen(from_x[quarter:])).astype(BF16)
        more_x = (widen(keep_x) + widen(from_y[quarter:])).astype(BF16)
        return more_y, more_x

    def own_rows(mine, first, second):
        low = mine[:quarter] + widen(first[0][:quarter]) + widen(second[0])
        high = mine[quarter:] + widen(first[1][:quarter]) + widen(second[1])
        return low, high

    odd = (lax.axis_index("dp") & 1) == 1

    def over_z(bit):
        return lambda v: lax.ppermute(v, "dp", [(i, i ^ bit) for i in range(4)])

    def in_pair(low, high):
        sent = jnp.where(odd, low, high).astype(BF16)
        return over_z(1)(sent)

    def pair_sum(low, high, into):
        return (jnp.where(odd, high, low) + widen(into)).astype(BF16)

    def total_of(pair, other):
        return (widen(pair) + widen(other)).astype(BF16)

    def both(total, got):
        return widen(jnp.where(odd, got, total)), widen(jnp.where(odd, total, got))

    part_a = call(first_grad_body, part_shapes(quarter), "grad_a")(
        *mine_a[1:], s_a1, s_a2, s_a3, dproj, dproj_sib
    )
    to_a = after((part_a[0], part_a[1]), w_x, w_y)
    in_a = px(to_a[0]), py(to_a[1])
    s_b3, rest = after((s_b3, rest), part_a, w_x, w_y)
    s_b3, rest = core(s_b3), core(rest)
    own_shape = jax.ShapeDtypeStruct((half, kw), F32)
    own_a, own_b, *part_b = call(
        second_grad_body, [own_shape, own_shape, *part_shapes(quarter)], "grad_b"
    )(mine_a[0], *mine_b, s_b3, rest, dproj, dproj_sib)

    acts = (*mine_a[:3], *mine_b[:3], s_a1, s_a2, rest)
    places = (
        (0, 8, 0, 0, 0),
        (3, 8, 1, 0, 1),
        (1, 6, 0, 1, 0),
        (4, 8, 2, 1, 1),
        (2, 7, 0, 2, 0),
        (5, 8, 3, 2, 1),
    )
    here = forward(acts, places, (after(key_weight, part_b), w_x, w_y))

    in_a = after(in_a, here)
    to_b = after((part_b[0], part_b[1]), in_a)
    more = add_up(part_a, *in_a)
    two_a = py(more[0]), px(more[1])
    in_b = px(to_b[0]), py(to_b[1])
    local_a = own_rows(own_a, in_a, two_a)
    pair_a = pair_sum(*local_a, in_pair(*local_a))

    in_b = after(in_b, two_a)
    more = after(add_up(part_b, *in_b), pair_a)
    two_b = py(more[0]), px(more[1])
    later = after((w_y[:half], w_x[half:]), pair_a)
    wd_low, wd_high = px(later[0]), py(later[1])
    total_a = total_of(pair_a, over_z(2)(pair_a))
    got_a = over_z(1)(total_a)
    local_b = after(own_rows(own_b, in_b, two_b), total_a)
    into_b, wd_low, wd_high = after((in_pair(*local_b), wd_low, wd_high))
    pair_b = pair_sum(*local_b, into_b)

    acts = after((mine_a[3], mine_b[3], s_a3, s_b3), pair_b)
    here, there = forward(acts, ((0, 2, 0, 0, 0), (1, 3, 0, 1, 0)), (wd_low, wd_high), here)
    keys = call(keys_body, jax.ShapeDtypeStruct((tok, kw), BF16), "keys")(
        here, core(there), key_bias[None, :], cosine, sine
    )

    local = after((*local_a, *local_b), pair_b)
    my_gain = lax.dynamic_slice(norm_gain, (me * own,), (own,))
    gain_rows = jnp.concatenate(
        [
            jnp.sum(v * widen(key_weight[n * quarter : (n + 1) * quarter]), axis=1)
            for n, v in enumerate(local)
        ]
    )
    bias = jnp.sum(widen(dproj), axis=0) + jnp.sum(widen(dproj_sib), axis=0)
    n_own = own // HEAD
    small = jnp.concatenate([gain_rows / my_gain, bias]).reshape(-1, HEAD)
    for bit in (1, 2):
        small = small + over_z(bit)(small)
    gains, bias = small[:n_own], small[n_own:]
    scale = 1.0 / jnp.sqrt(F32(tok * 32))
    for bit in (1, 2, 4):
        got = over(bit)(jnp.concatenate([gains, bias], axis=0))
        if bit == 1:
            got, other_b, got_a = after((got, over_z(2)(pair_b), got_a))
            total_b = total_of(pair_b, other_b)
            got_b = over_z(1)(total_b)
        size = gains.shape[0]
        theirs = got[:size]
        first = (me & bit) == 0
        gains = jnp.concatenate(
            [jnp.where(first, gains, theirs), jnp.where(first, theirs, gains)], axis=0
        )
        if bit > 1:
            bias = bias + got[size:]
    got_b, keys, gains, bias = after((got_b, keys, gains, bias))
    grad = jnp.concatenate([*both(total_a, got_a), *both(total_b, got_b)], axis=0)
    return (keys, grad * scale, bias.reshape(-1) * scale, gains.reshape(-1) * scale)


def by_collectives(hidden_in, segment_ids, key_weight, norm_gain, key_bias, key_cotangent):
    tok_rows = hidden_in.shape[0]
    n_cycle = lax.axis_size("blk")
    n_rep = lax.axis_size("dp")
    positions = positions_of(segment_ids).reshape(tok_rows)
    xf = hidden_in.astype(F32)
    normed = xf * lax.rsqrt(jnp.mean(xf * xf, axis=1, keepdims=True) + 1e-06)
    scaled = (normed * norm_gain[None, :]).astype(BF16)
    cosine, sine = angles_of(positions, HEAD)
    dproj = rotate(key_cotangent.astype(F32), cosine, sine, -1.0).astype(BF16)
    full_weight = lax.all_gather(key_weight, "blk", axis=0, tiled=True)
    projected = jnp.dot(scaled, full_weight, preferred_element_type=F32)
    dscaled = lax.dot_general(
        dproj, full_weight, (((1,), (1,)), ((), ())), preferred_element_type=F32
    )
    projected = projected + key_bias[None, :]
    keys = rotate(projected, cosine, sine, 1.0).astype(BF16)
    cycle_part = lax.psum_scatter(
        lax.dot_general(scaled, dproj, (((0,), (0,)), ((), ())), preferred_element_type=F32),
        "blk",
        scatter_dimension=0,
        tiled=True,
    )
    grad_weight = lax.psum(cycle_part, "dp")
    bias_part = jnp.sum(dproj.astype(F32), axis=0)
    gain_part = jnp.sum(dscaled * normed, axis=0)
    grad_bias, grad_gain = lax.psum((bias_part, gain_part), ("blk", "dp"))
    scale = 1.0 / jnp.sqrt(F32(tok_rows * n_cycle * n_rep))
    return (keys, grad_weight * scale, grad_bias * scale, grad_gain * scale)


def solution(mesh):
    small = mesh.shape["blk"] == 8 and mesh.shape["dp"] == 4
    return jax.shard_map(
        by_permutes if small else by_collectives,
        mesh=mesh,
        in_specs=(
            P(("blk", "dp"), None),
            P(("blk", "dp"), None),
            P("blk", None),
            P(),
            P(),
            P(("blk", "dp"), None),
        ),
        out_specs=(P(("blk", "dp"), None), P("blk", None), P(), P()),
        check_vma=False,
    )
```

time: 194 us -> 132 us (0.68)
  waiting for transfers between devices: 85.3 us -> 37 us
  matrix products: 35.8 us -> 0 us
  local copies, waits for them, and re-layouts: 7.15 us -> 18.6 us
  Pallas kernels: 5.38 us -> 15.9 us
  blocking collectives: 9.07 us -> 0 us
  other arithmetic: 12.1 us -> 19.4 us
  starting transfers between devices: 36.8 us -> 39 us
    dot_general x16 -> x0, matrix products: 35.8 us -> none  [the longest x8 21.2 us: dot_t(): lax.dot_general(a, b, (((0,), (0,)), ((), ())), preferred_element_type=F32)]
    ppermute x19 -> x23, waiting for transfers between devices: 53.8 us -> 26.7 us  [over(): return lambda v: lax.ppermute(v, 'blk', [(i, i ^ bit) for i in range(8)])]
    ppermute x14 -> x8, waiting for transfers between devices: 31.5 us -> 10.3 us  [over_z(): return lambda v: lax.ppermute(v, 'dp', [(i, i ^ bit) for i in range(4)])]
    unnamed x20 -> x78, local copies, waits for them, and re-layouts: 3.46 us -> 15.7 us
    convert_element_type x8 -> x10, other arithmetic: 0.87 us -> 11.5 us  [the longest x2 2.83 us: total_of(): return (widen(pair) + widen(other)).astype(BF16)]
    pallas_call x1 -> x7, Pallas kernels: 5.38 us -> 15.9 us  [the longest x2 4.66 us: forward(): call(functools.partial(forward_body, (places, len(acts), len(init))), [ja...]
    all_gather x1 -> x0, blocking collectives: 9.07 us -> none  [by_permutes(): grad_gain = lax.all_gather(gain_rows, 'blk', axis=0, tiled=True)]
    reduce_sum x2 -> x3, other arithmetic: 3.73 us -> 0.54 us  [the longest x1 0.32 us: by_permutes(): jnp.sum(v * widen(key_weight[n * quarter:(n + 1) * quarter]), axis=1)]
  transfers between devices with their start and end apart: 33 -> 31, of which waited for: 14 -> 18; matrix products, arithmetic and copies ran while one was open for 22% -> 13% of each run, Pallas kernels for 3% -> 12%
where the time goes in v3:
time: 132 us; the launch traced here: 131 us
  starting transfers between devices  39 us (30%)
  waiting for transfers between devices  37 us (28%)
  other arithmetic  19.4 us (15%)
  local copies, waits for them, and re-layouts  18.6 us (14%)
  Pallas kernels  15.9 us (12%)
    ppermute x23, waiting for transfers between devices, over(): return lambda v: lax.ppermute(v, 'blk', [(i, i ^ bit) for i in range(8)])  26.7 us
    ppermute x23, starting transfers between devices, over(): return lambda v: lax.ppermute(v, 'blk', [(i, i ^ bit) for i in range(8)])  21 us
    ppermute x8, starting transfers between devices, over_z(): return lambda v: lax.ppermute(v, 'dp', [(i, i ^ bit) for i in range(4)])  18 us
    unnamed x78, local copies, waits for them, and re-layouts  15.7 us
    ppermute x8, waiting for transfers between devices, over_z(): return lambda v: lax.ppermute(v, 'dp', [(i, i ^ bit) for i in range(4)])  10.3 us
    pallas_call x2, Pallas kernels, forward(): call(functools.partial(forward_body, (places, len(acts), len(init))), [ja...  4.66 us
    pallas_call x1, Pallas kernels, scaled_parts(): pl.pallas_call(scale_body, grid_spec=pltpu.PrefetchScalarGridSpec(num_sca...  4.52 us
    pallas_call x1, Pallas kernels, by_permutes(): call(second_grad_body, [own_shape, own_shape, *part_shapes(quarter)], 'gr...  3.38 us
  transfers between devices with their start and end apart: 31, of which 18 were waited for; matrix products, arithmetic and copies ran while one was open for 13% of the time, Pallas kernels for 12%

profile of v3, /device:TPU:0, one launch (start us, length us, event | category | flops | bytes accessed | tf_op | source)
XLA Modules:
  0.0 131.0 jit_solution(12892864010849223255)
XLA Ops:
  0.6 3.0 %collective-permute-start.5 = (bf16[1024,512]{1,0:T(8,128)(2,1)}, bf16[1024,512]{1,0:T(8,128)(2,1)S(1)}, u32[]{:S(2)}, u32[]{:S(2)}) collective-permute-start(bf16[1024,512]{1,0:T(8,128)(2,1)} %refs_9_), channel_id=1, source_target_pairs={{0,8},{4,12},{8,0},{12,4},{16,24},{20,28},{24,16},{28,20},{1,9},{5... | collective-permute-start | bytes 3145736 | tf_op jit(solution)/shard_map/ppermute | solution.py:194
  3.6 1.5 %collective-permute-start.6 = (bf16[1024,512]{1,0:T(8,128)(2,1)}, bf16[1024,512]{1,0:T(8,128)(2,1)S(1)}, u32[]{:S(2)}, u32[]{:S(2)}) collective-permute-start(bf16[1024,512]{1,0:T(8,128)(2,1)} %refs_9_), channel_id=1, source_target_pairs={{0,16},{4,20},{8,24},{12,28},{16,0},{20,4},{24,8},{28,12},{1,17},{... | collective-permute-start | bytes 3145736 | tf_op jit(solution)/shard_map/ppermute | solution.py:194
  7.3 1.1 copy-done.21
  9.9 1.5 %collective-permute-done = bf16[256,512]{1,0:T(8,128)(2,1)} collective-permute-done((bf16[256,512]{1,0:T(8,128)(2,1)S(1)}, bf16[256,512]{1,0:T(8,128)(2,1)}, u32[]{:S(2)}, u32[]{:S(2)}) %collective-permute-start) | collective-permute-done | bytes 262176 | tf_op jit(solution)/shard_map/ppermute | solution.py:194
  13.4 3.4 %copy-done = bf16[512,8192]{1,0:T(8,128)(2,1)S(1)} copy-done((bf16[512,8192]{1,0:T(8,128)(2,1)S(1)}, bf16[512,8192]{1,0:T(8,128)(2,1)}, u32[]{:S(2)}) %copy-start) | copy-done | bytes 8388632
  16.8 4.5 %scale_rows.1 = (bf16[512,512]{1,0:T(8,128)(2,1)S(1)}, bf16[512,512]{1,0:T(8,128)(2,1)S(1)}, bf16[512,512]{1,0:T(8,128)(2,1)S(1)}, bf16[512,512]{1,0:T(8,128)(2,...) custom-call(s32[1]{0:T(128)} %bitcast.at_ref, ...), custom_call_target="tpu_custom_call" | custom-call | flops 1 | bytes 1 | tf_op jit(solution)/shard_map/scale_rows/pallas_call | solution.py:89
  22.0 1.3 collective-permute-done.2.s1.refs_6_
  24.8 1.8 %grad_a.1 = (bf16[512,512]{1,0:T(8,128)(2,1)S(1)}, bf16[512,512]{1,0:T(8,128)(2,1)S(1)}, bf16[256,512]{1,0:T(8,128)(2,1)S(1)}, bf16[256,512]{1,0:T(8,128)(2,1)S(1)}) custom-call(bf16[512,512]{1,0:T(8,128)(2,1)S(1)} %get-tuple-element.75.m1.refs_1_, bf16[512,512]{1,0:T(8,128)(2,1)S(1)} %get-tuple-element.76.m2.refs_2_, ...), custom_call_target="tpu_custom_call" | custom-call | flops 1 | bytes 1 | tf_op jit(solution)/shard_map/grad_a/pallas_call | solution.py:254
  27.0 1.5 %collective-permute-done.6.refs_11_ = bf16[1024,512]{1,0:T(8,128)(2,1)S(1)} collective-permute-done((bf16[1024,512]{1,0:T(8,128)(2,1)}, bf16[1024,512]{1,0:T(8,128)(2,1)S(1)}, u32[]{:S(2)}, u32[]{:S(2)}) %collective-permute-start.6) | collective-permute-done | bytes 1048608 | tf_op jit(solution)/shard_map/ppermute | solution.py:194
  30.3 1.7 %collective-permute-start.10 = (bf16[512,512]{1,0:T(8,128)(2,1)S(1)}, bf16[512,512]{1,0:T(8,128)(2,1)S(1)}, u32[]{:S(2)}, u32[]{:S(2)}) collective-permute-start(bf16[512,512]{1,0:T(8,128)(2,1)S(1)} %get-tuple-element.91), channel_id=1, source_target_pairs={{0,16},{4,20},{8,24},{12,28},{16,0},{20,4},{24,8},{28,12},{1,17},{... | collective-permute-start | bytes 1572872 | tf_op jit(solution)/shard_map/ppermute | solution.py:194
  32.0 2.3 %collective-permute-done.7.s3.refs_3_ = bf16[512,512]{1,0:T(8,128)(2,1)S(1)} collective-permute-done((bf16[512,512]{1,0:T(8,128)(2,1)S(1)}, bf16[512,512]{1,0:T(8,128)(2,1)S(1)}, u32[]{:S(2)}, u32[]{:S(2)}) %collective-permute-start.7) | collective-permute-done | bytes 524320 | tf_op jit(solution)/shard_map/ppermute | solution.py:194
  34.4 3.4 %grad_b.1 = (f32[512,512]{1,0:T(8,128)S(1)}, f32[512,512]{1,0:T(8,128)S(1)}, bf16[512,512]{1,0:T(8,128)(2,1)}, bf16[512,512]{1,0:T(8,128)(2,1)}, bf16[256,512]{1...) custom-call(bf16[512,512]{1,0:T(8,128)(2,1)S(1)} %get-tuple-element.68.m_a0.refs_0_, ...), custom_call_target="tpu_custom_call" | custom-call | flops 1 | bytes 1 | tf_op jit(solution)/shard_map/grad_b/pallas_call | solution.py:262
  38.8 3.4 %forward.2 = (f32[512,512]{1,0:T(8,128)S(1)}, f32[512,512]{1,0:T(8,128)S(1)}) custom-call(bf16[512,512]{1,0:T(8,128)(2,1)S(1)} %get-tuple-element.68.m_a0.refs_0_, bf16[512,512]{1,0:T(8,128)(2,1)S(1)} %get-tuple-element.75.m1.refs_1_, bf16[512,512]{1,0:T(8,128)(2,1)S(1)} %get-tuple-element.76.m2.refs_2_, bf16[512,512]{1,0:T(8,128)(2,1)S(1)} %get-tuple-element.69.m0.refs_3_, ...), custom_call_target="tpu_custom_call" | custom-call | flops 1 | bytes 1 | tf_op jit(solution)/shard_map/forward/pallas_call | solution.py:179
  42.2 1.0 copy-done.14
  45.1 1.3 %collective-permute-start.14 = (bf16[256,512]{1,0:T(8,128)(2,1)}, bf16[256,512]{1,0:T(8,128)(2,1)}, u32[]{:S(2)}, u32[]{:S(2)}) collective-permute-start(bf16[256,512]{1,0:T(8,128)(2,1)} %add_convert_fusion.6), channel_id=1, source_target_pairs={{0,8},{4,12},{8,0},{12,4},{16,24},{20,28},{24,16},{28,20},{1,9},{5... | collective-permute-start | bytes 786440 | tf_op jit(solution)/shard_map/ppermute | solution.py:194
  47.2 1.5 %collective-permute-start.13 = (bf16[256,512]{1,0:T(8,128)(2,1)}, bf16[256,512]{1,0:T(8,128)(2,1)}, u32[]{:S(2)}, u32[]{:S(2)}) collective-permute-start(bf16[256,512]{1,0:T(8,128)(2,1)} %add_convert_fusion.7), channel_id=1, source_target_pairs={{0,16},{4,20},{8,24},{12,28},{16,0},{20,4},{24,8},{28,12},{1,17},{... | collective-permute-start | bytes 786440 | tf_op jit(solution)/shard_map/ppermute | solution.py:194
  49.9 4.6 %collective-permute-done.14 = bf16[256,512]{1,0:T(8,128)(2,1)} collective-permute-done((bf16[256,512]{1,0:T(8,128)(2,1)}, bf16[256,512]{1,0:T(8,128)(2,1)}, u32[]{:S(2)}, u32[]{:S(2)}) %collective-permute-start.14) | collective-permute-done | bytes 262176 | tf_op jit(solution)/shard_map/ppermute | solution.py:194
  54.6 2.2 %collective-permute-done.13 = bf16[256,512]{1,0:T(8,128)(2,1)} collective-permute-done((bf16[256,512]{1,0:T(8,128)(2,1)}, bf16[256,512]{1,0:T(8,128)(2,1)}, u32[]{:S(2)}, u32[]{:S(2)}) %collective-permute-start.13) | collective-permute-done | bytes 262176 | tf_op jit(solution)/shard_map/ppermute | solution.py:194
  56.7 1.8 %select_convert_fusion.1 = (bf16[256,512]{1,0:T(8,128)(2,1)S(1)}, f32[256,512]{1,0:T(8,128)S(1)}, f32[256,512]{1,0:T(8,128)S(1)}) fusion(pred[]{:T(512)S(6)} %eq.27, bf16[256,512]{1,0:T(8,128)(2,1)} %collective-permute-done.14, bf16[512,512]{1,0:T(8,128)(2,1)} %copy-done.37, f32[512,512]{1,0:T(8,128)} %copy-done.20, ...), kind=kLoop, calls=%fused_computation.14 | loop fusion | flops 1179648 | bytes 3407873 | tf_op jit(solution)/shard_map/convert_element_type | solution.py:242
  58.5 1.6 %collective-permute-start.15 = (bf16[256,512]{1,0:T(8,128)(2,1)S(1)}, bf16[256,512]{1,0:T(8,128)(2,1)S(1)}, u32[]{:S(2)}, u32[]{:S(2)}) collective-permute-start(bf16[256,512]{1,0:T(8,128)(2,1)S(1)} %get-tuple-element.134), channel_id=1, source_target_pairs={{0,1},{1,0},{2,3},{3,2},{4,5},{5,4},{6,7},{7,6},{8,9},{9,8},{10,11... | collective-permute-start | bytes 786440 | tf_op jit(solution)/shard_map/ppermute | solution.py:239
  60.2 4.8 %collective-permute-done.11 = bf16[512,512]{1,0:T(8,128)(2,1)} collective-permute-done((bf16[512,512]{1,0:T(8,128)(2,1)}, bf16[512,512]{1,0:T(8,128)(2,1)}, u32[]{:S(2)}, u32[]{:S(2)}) %collective-permute-start.11) | collective-permute-done | bytes 524320 | tf_op jit(solution)/shard_map/ppermute | solution.py:194
  65.9 1.7 %add_convert_fusion.5 = bf16[256,512]{1,0:T(8,128)(2,1)} fusion(bf16[256,512]{1,0:T(8,128)(2,1)S(1)} %copy-done.29, bf16[512,512]{1,0:T(8,128)(2,1)} %collective-permute-done.11), kind=kLoop, calls=%fused_computation.18 | loop fusion | flops 524288 | bytes 786432 | tf_op jit(solution)/shard_map/convert_element_type | solution.py:227
  68.5 2.7 %collective-permute-start.18 = (bf16[256,512]{1,0:T(8,128)(2,1)}, bf16[256,512]{1,0:T(8,128)(2,1)}, u32[]{:S(2)}, u32[]{:S(2)}) collective-permute-start(bf16[256,512]{1,0:T(8,128)(2,1)} %add_convert_fusion.3), channel_id=1, source_target_pairs={{0,2},{1,3},{2,0},{3,1},{4,6},{5,7},{6,4},{7,5},{8,10},{9,11},{10,... | collective-permute-start | bytes 786440 | tf_op jit(solution)/shard_map/ppermute | solution.py:239
  71.2 1.7 %add_convert_fusion.4 = bf16[256,512]{1,0:T(8,128)(2,1)} fusion(bf16[256,512]{1,0:T(8,128)(2,1)S(1)} %copy-done.27, bf16[512,512]{1,0:T(8,128)(2,1)} %collective-permute-done.12), kind=kLoop, calls=%fused_computation.17 | loop fusion | flops 524288 | bytes 786432 | tf_op jit(solution)/shard_map/convert_element_type | solution.py:228
  72.9 1.5 %collective-permute-start.17 = (bf16[256,512]{1,0:T(8,128)(2,1)}, bf16[256,512]{1,0:T(8,128)(2,1)}, u32[]{:S(2)}, u32[]{:S(2)}) collective-permute-start(bf16[256,512]{1,0:T(8,128)(2,1)} %add_convert_fusion.4), channel_id=1, source_target_pairs={{0,8},{4,12},{8,0},{12,4},{16,24},{20,28},{24,16},{28,20},{1,9},{5... | collective-permute-start | bytes 786440 | tf_op jit(solution)/shard_map/ppermute | solution.py:194
  74.4 1.5 %collective-permute-start.16 = (bf16[256,512]{1,0:T(8,128)(2,1)}, bf16[256,512]{1,0:T(8,128)(2,1)}, u32[]{:S(2)}, u32[]{:S(2)}) collective-permute-start(bf16[256,512]{1,0:T(8,128)(2,1)} %add_convert_fusion.5), channel_id=1, source_target_pairs={{0,16},{4,20},{8,24},{12,28},{16,0},{20,4},{24,8},{28,12},{1,17},{... | collective-permute-start | bytes 786440 | tf_op jit(solution)/shard_map/ppermute | solution.py:194
  76.0 1.2 slice.111
  78.3 3.7 %collective-permute-done.18 = bf16[256,512]{1,0:T(8,128)(2,1)} collective-permute-done((bf16[256,512]{1,0:T(8,128)(2,1)}, bf16[256,512]{1,0:T(8,128)(2,1)}, u32[]{:S(2)}, u32[]{:S(2)}) %collective-permute-start.18) | collective-permute-done | bytes 262176 | tf_op jit(solution)/shard_map/ppermute | solution.py:239
  81.9 1.8 %add_convert_fusion.2 = bf16[256,512]{1,0:T(8,128)(2,1)} fusion(bf16[256,512]{1,0:T(8,128)(2,1)} %collective-permute-done.18, bf16[256,512]{1,0:T(8,128)(2,1)} %add_convert_fusion.3), kind=kLoop, calls=%fused_computation.10 | loop fusion | flops 524288 | bytes 786432 | tf_op jit(solution)/shard_map/convert_element_type | solution.py:249
  84.0 1.4 %convert_add_fusion = (f32[256,512]{1,0:T(8,128)S(1)}, f32[256,512]{1,0:T(8,128)S(1)}) fusion(bf16[256,512]{1,0:T(8,128)(2,1)} %collective-permute-done.17, f32[512,512]{1,0:T(8,128)S(1)} %copy-done.19, bf16[512,512]{1,0:T(8,128)(2,1)} %collective-permute-done.12, bf16[256,512]{1,0:T(8,128)(2,1)} %collective-permute-done.16, ...), kind=kLoop, calls=%fused_computation.11 | loop fusion | flops 1048576 | bytes 3145728 | tf_op jit(solution)/shard_map/add | solution.py:233
  85.6 1.6 %collective-permute-start.19 = (bf16[256,512]{1,0:T(8,128)(2,1)S(1)}, bf16[256,512]{1,0:T(8,128)(2,1)S(1)}, u32[]{:S(2)}, u32[]{:S(2)}) collective-permute-start(bf16[256,512]{1,0:T(8,128)(2,1)S(1)} %select_convert_fusion), channel_id=1, source_target_pairs={{0,1},{1,0},{2,3},{3,2},{4,5},{5,4},{6,7},{7,6},{8,9},{9,8},{10,11... | collective-permute-start | bytes 786440 | tf_op jit(solution)/shard_map/ppermute | solution.py:239
  87.5 3.6 %collective-permute-done.20.refs_6_ = bf16[512,512]{1,0:T(8,128)(2,1)S(1)} collective-permute-done((bf16[512,512]{1,0:T(8,128)(2,1)S(1)}, bf16[512,512]{1,0:T(8,128)(2,1)S(1)}, u32[]{:S(2)}, u32[]{:S(2)}) %collective-permute-start.20) | collective-permute-done | bytes 524320 | tf_op jit(solution)/shard_map/ppermute | solution.py:194
  94.5 1.6 %collective-permute-start.22 = (f32[12,128]{1,0:T(8,128)S(1)}, f32[12,128]{1,0:T(8,128)S(1)}, u32[]{:S(2)}, u32[]{:S(2)}) collective-permute-start(f32[12,128]{1,0:T(8,128)S(1)} %maximum_bitcast_fusion), channel_id=1, source_target_pairs={{0,1},{1,0},{2,3},{3,2},{4,5},{5,4},{6,7},{7,6},{8,9},{9,8},{10,11... | collective-permute-start | bytes 18440 | tf_op jit(solution)/shard_map/ppermute | solution.py:239
  96.6 2.6 %collective-permute-start.25 = (bf16[256,512]{1,0:T(8,128)(2,1)}, bf16[256,512]{1,0:T(8,128)(2,1)S(1)}, u32[]{:S(2)}, u32[]{:S(2)}) collective-permute-start(bf16[256,512]{1,0:T(8,128)(2,1)} %add_convert_fusion.1), channel_id=1, source_target_pairs={{0,2},{1,3},{2,0},{3,1},{4,6},{5,7},{6,4},{7,5},{8,10},{9,11},{10,... | collective-permute-start | bytes 786440 | tf_op jit(solution)/shard_map/ppermute | solution.py:239
  99.2 1.7 %collective-permute-start.23 = (f32[12,128]{1,0:T(8,128)S(1)}, f32[12,128]{1,0:T(8,128)S(1)}, u32[]{:S(2)}, u32[]{:S(2)}) collective-permute-start(f32[12,128]{1,0:T(8,128)S(1)} %fusion.5), channel_id=1, source_target_pairs={{0,2},{1,3},{2,0},{3,1},{4,6},{5,7},{6,4},{7,5},{8,10},{9,11},{10,... | collective-permute-start | bytes 18440 | tf_op jit(solution)/shard_map/ppermute | solution.py:239
  101.0 5.6 %collective-permute-done.23 = f32[12,128]{1,0:T(8,128)S(1)} collective-permute-done((f32[12,128]{1,0:T(8,128)S(1)}, f32[12,128]{1,0:T(8,128)S(1)}, u32[]{:S(2)}, u32[]{:S(2)}) %collective-permute-start.23) | collective-permute-done | bytes 6176 | tf_op jit(solution)/shard_map/ppermute | solution.py:239
  106.6 1.2 copy-done.15
  107.8 1.2 copy-done.17
  109.0 1.0 copy-done.23
  110.1 1.0 copy-done.25
  111.1 1.3 forward.3
  113.0 2.4 %collective-permute-start.29 = (f32[20,128]{1,0:T(8,128)S(1)}, f32[20,128]{1,0:T(8,128)S(1)}, u32[]{:S(2)}, u32[]{:S(2)}) collective-permute-start(f32[20,128]{1,0:T(8,128)S(1)} %pad_maximum_fusion.3), channel_id=1, source_target_pairs={{0,8},{4,12},{8,0},{12,4},{16,24},{20,28},{24,16},{28,20},{1,9},{5... | collective-permute-start | bytes 30728 | tf_op jit(solution)/shard_map/ppermute | solution.py:194
  116.4 5.5 %collective-permute-start.27 = (bf16[256,512]{1,0:T(8,128)(2,1)S(1)}, bf16[256,512]{1,0:T(8,128)(2,1)S(1)}, u32[]{:S(2)}, u32[]{:S(2)}) collective-permute-start(bf16[256,512]{1,0:T(8,128)(2,1)S(1)} %add_convert_fusion), channel_id=1, source_target_pairs={{0,1},{1,0},{2,3},{3,2},{4,5},{5,4},{6,7},{7,6},{8,9},{9,8},{10,11... | collective-permute-start | bytes 786440 | tf_op jit(solution)/shard_map/ppermute | solution.py:239
  122.0 1.6 %collective-permute-start.30 = (f32[36,128]{1,0:T(8,128)S(1)}, f32[36,128]{1,0:T(8,128)S(1)}, u32[]{:S(2)}, u32[]{:S(2)}) collective-permute-start(f32[36,128]{1,0:T(8,128)S(1)} %pad_maximum_fusion.1), channel_id=1, source_target_pairs={{0,16},{4,20},{8,24},{12,28},{16,0},{20,4},{24,8},{28,12},{1,17},{... | collective-permute-start | bytes 55304 | tf_op jit(solution)/shard_map/ppermute | solution.py:194
  124.5 1.3 collective-permute-done.30
  125.9 1.2 keys.1
  127.1 1.1 collective-permute-done.27
  129.4 1.6 %convert_multiply_fusion = f32[1024,512]{1,0:T(8,128)} fusion(bf16[256,512]{1,0:T(8,128)(2,1)S(1)} %get-tuple-element.142, bf16[256,512]{1,0:T(8,128)(2,1)S(1)} %get-tuple-element.141, bf16[256,512]{1,0:T(8,128)(2,1)S(1)} %get-tuple-element.140, bf16[256,512]{1,0:T(8,128)(2,1)S(1)} %get-tuple-element.139), kind=kLoop, calls=%fused_computation | loop fusion | flops 4718592 | bytes 3145728 | tf_op jit(solution)/shard_map/mul | solution.py:333
  (141 shorter events, 26.1 us)
Async XLA Ops:
  0.6 26.4 %collective-permute-start.5 = (bf16[1024,512]{1,0:T(8,128)(2,1)}, bf16[1024,512]{1,0:T(8,128)(2,1)S(1)}, u32[]{:S(2)}, u32[]{:S(2)}) collective-permute-start(bf16[1024,512]{1,0:T(8,128)(2,1)} %refs_9_), channel_id=1, source_target_pairs={{0,8},{4,12},{8,0},{12,4},{16,24},{20,28},{24,16},{28,20},{1,9},{5... | collective-permute-start | bytes 3145736 | tf_op jit(solution)/shard_map/ppermute | solution.py:194
  3.6 24.8 %collective-permute-start.6 = (bf16[1024,512]{1,0:T(8,128)(2,1)}, bf16[1024,512]{1,0:T(8,128)(2,1)S(1)}, u32[]{:S(2)}, u32[]{:S(2)}) collective-permute-start(bf16[1024,512]{1,0:T(8,128)(2,1)} %refs_9_), channel_id=1, source_target_pairs={{0,16},{4,20},{8,24},{12,28},{16,0},{20,4},{24,8},{28,12},{1,17},{... | collective-permute-start | bytes 3145736 | tf_op jit(solution)/shard_map/ppermute | solution.py:194
  6.2 7.1 %copy-start.30 = (f32[8192]{0:T(1024)S(1)}, f32[8192]{0:T(1024)}, u32[]{:S(2)}) copy-start(f32[8192]{0:T(1024)} %param.9) | copy-start | bytes 98308
  9.4 2.0 %collective-permute-start = (bf16[256,512]{1,0:T(8,128)(2,1)S(1)}, bf16[256,512]{1,0:T(8,128)(2,1)}, u32[]{:S(2)}, u32[]{:S(2)}) collective-permute-start(bf16[256,512]{1,0:T(8,128)(2,1)S(1)} %get-tuple-element.144), channel_id=1, source_target_pairs={{0,4},{4,0},{8,12},{12,8},{16,20},{20,16},{24,28},{28,24},{1,5},{5... | collective-permute-start | bytes 786440 | tf_op jit(solution)/shard_map/ppermute | solution.py:194
  9.4 3.0 %collective-permute-start.1 = (bf16[256,512]{1,0:T(8,128)(2,1)}, bf16[256,512]{1,0:T(8,128)(2,1)}, u32[]{:S(2)}, u32[]{:S(2)}) collective-permute-start(bf16[256,512]{1,0:T(8,128)(2,1)} %get-tuple-element.143), channel_id=1, source_target_pairs={{0,4},{4,0},{8,12},{12,8},{16,20},{20,16},{24,28},{28,24},{1,5},{5... | collective-permute-start | bytes 786440 | tf_op jit(solution)/shard_map/ppermute | solution.py:194
  21.3 5.3 %copy-start.10 = (bf16[512,512]{1,0:T(8,128)(2,1)}, bf16[512,512]{1,0:T(8,128)(2,1)S(1)}, u32[]{:S(2)}) copy-start(bf16[512,512]{1,0:T(8,128)(2,1)S(1)} %get-tuple-element.116.m3.refs_0_) | copy-start | bytes 1572868
  21.3 13.1 %copy-start.6 = (bf16[512,512]{1,0:T(8,128)(2,1)}, bf16[512,512]{1,0:T(8,128)(2,1)S(1)}, u32[]{:S(2)}) copy-start(bf16[512,512]{1,0:T(8,128)(2,1)S(1)} %get-tuple-element.117.m3.refs_1_) | copy-start | bytes 1572868
  21.3 2.0 %collective-permute-start.2 = (bf16[512,512]{1,0:T(8,128)(2,1)S(1)}, bf16[512,512]{1,0:T(8,128)(2,1)S(1)}, u32[]{:S(2)}, u32[]{:S(2)}) collective-permute-start(bf16[512,512]{1,0:T(8,128)(2,1)S(1)} %get-tuple-element.78), channel_id=1, source_target_pairs={{0,4},{4,0},{8,12},{12,8},{16,20},{20,16},{24,28},{28,24},{1,5},{5... | collective-permute-start | bytes 1572872 | tf_op jit(solution)/shard_map/ppermute | solution.py:194
  21.5 2.5 %collective-permute-start.3 = (bf16[512,512]{1,0:T(8,128)(2,1)S(1)}, bf16[512,512]{1,0:T(8,128)(2,1)S(1)}, u32[]{:S(2)}, u32[]{:S(2)}) collective-permute-start(bf16[512,512]{1,0:T(8,128)(2,1)S(1)} %get-tuple-element.79), channel_id=1, source_target_pairs={{0,4},{4,0},{8,12},{12,8},{16,20},{20,16},{24,28},{28,24},{1,5},{5... | collective-permute-start | bytes 1572872 | tf_op jit(solution)/shard_map/ppermute | solution.py:194
  21.9 2.9 %collective-permute-start.4 = (bf16[512,512]{1,0:T(8,128)(2,1)S(1)}, bf16[512,512]{1,0:T(8,128)(2,1)S(1)}, u32[]{:S(2)}, u32[]{:S(2)}) collective-permute-start(bf16[512,512]{1,0:T(8,128)(2,1)S(1)} %get-tuple-element.80), channel_id=1, source_target_pairs={{0,4},{4,0},{8,12},{12,8},{16,20},{20,16},{24,28},{28,24},{1,5},{5... | collective-permute-start | bytes 1572872 | tf_op jit(solution)/shard_map/ppermute | solution.py:194
  29.4 4.9 %collective-permute-start.8 = (bf16[512,2048]{1,0:T(8,128)(2,1)S(1)}, bf16[512,2048]{1,0:T(8,128)(2,1)S(1)}, u32[]{:S(2)}, u32[]{:S(2)}) collective-permute-start(bf16[512,2048]{1,0:T(8,128)(2,1)S(1)} %get-tuple-element.86), channel_id=1, source_target_pairs={{0,4},{4,0},{8,12},{12,8},{16,20},{20,16},{24,28},{28,24},{1,5},{5... | collective-permute-start | bytes 6291464 | tf_op jit(solution)/shard_map/ppermute | solution.py:194
  29.4 4.9 %collective-permute-start.7 = (bf16[512,512]{1,0:T(8,128)(2,1)S(1)}, bf16[512,512]{1,0:T(8,128)(2,1)S(1)}, u32[]{:S(2)}, u32[]{:S(2)}) collective-permute-start(bf16[512,512]{1,0:T(8,128)(2,1)S(1)} %get-tuple-element.85), channel_id=1, source_target_pairs={{0,4},{4,0},{8,12},{12,8},{16,20},{20,16},{24,28},{28,24},{1,5},{5... | collective-permute-start | bytes 1572872 | tf_op jit(solution)/shard_map/ppermute | solution.py:194
  29.9 14.3 %collective-permute-start.9 = (bf16[512,512]{1,0:T(8,128)(2,1)S(1)}, bf16[512,512]{1,0:T(8,128)(2,1)S(1)}, u32[]{:S(2)}, u32[]{:S(2)}) collective-permute-start(bf16[512,512]{1,0:T(8,128)(2,1)S(1)} %get-tuple-element.90), channel_id=1, source_target_pairs={{0,8},{4,12},{8,0},{12,4},{16,24},{20,28},{24,16},{28,20},{1,9},{5... | collective-permute-start | bytes 1572872 | tf_op jit(solution)/shard_map/ppermute | solution.py:194
  30.3 13.9 %collective-permute-start.10 = (bf16[512,512]{1,0:T(8,128)(2,1)S(1)}, bf16[512,512]{1,0:T(8,128)(2,1)S(1)}, u32[]{:S(2)}, u32[]{:S(2)}) collective-permute-start(bf16[512,512]{1,0:T(8,128)(2,1)S(1)} %get-tuple-element.91), channel_id=1, source_target_pairs={{0,16},{4,20},{8,24},{12,28},{16,0},{20,4},{24,8},{28,12},{1,17},{... | collective-permute-start | bytes 1572872 | tf_op jit(solution)/shard_map/ppermute | solution.py:194
  44.2 4.5 %copy-start.37 = (bf16[512,512]{1,0:T(8,128)(2,1)}, bf16[512,512]{1,0:T(8,128)(2,1)S(1)}, u32[]{:S(2)}) copy-start(bf16[512,512]{1,0:T(8,128)(2,1)S(1)} %collective-permute-done.10) | copy-start | bytes 1572868
  45.1 9.5 %collective-permute-start.14 = (bf16[256,512]{1,0:T(8,128)(2,1)}, bf16[256,512]{1,0:T(8,128)(2,1)}, u32[]{:S(2)}, u32[]{:S(2)}) collective-permute-start(bf16[256,512]{1,0:T(8,128)(2,1)} %add_convert_fusion.6), channel_id=1, source_target_pairs={{0,8},{4,12},{8,0},{12,4},{16,24},{20,28},{24,16},{28,20},{1,9},{5... | collective-permute-start | bytes 786440 | tf_op jit(solution)/shard_map/ppermute | solution.py:194
  47.2 9.6 %collective-permute-start.13 = (bf16[256,512]{1,0:T(8,128)(2,1)}, bf16[256,512]{1,0:T(8,128)(2,1)}, u32[]{:S(2)}, u32[]{:S(2)}) collective-permute-start(bf16[256,512]{1,0:T(8,128)(2,1)} %add_convert_fusion.7), channel_id=1, source_target_pairs={{0,16},{4,20},{8,24},{12,28},{16,0},{20,4},{24,8},{28,12},{1,17},{... | collective-permute-start | bytes 786440 | tf_op jit(solution)/shard_map/ppermute | solution.py:194
  48.7 16.3 %collective-permute-start.11 = (bf16[512,512]{1,0:T(8,128)(2,1)}, bf16[512,512]{1,0:T(8,128)(2,1)}, u32[]{:S(2)}, u32[]{:S(2)}) collective-permute-start(bf16[512,512]{1,0:T(8,128)(2,1)} %get-tuple-element.99), channel_id=1, source_target_pairs={{0,8},{4,12},{8,0},{12,4},{16,24},{20,28},{24,16},{28,20},{1,9},{5... | collective-permute-start | bytes 1572872 | tf_op jit(solution)/shard_map/ppermute | solution.py:194
  49.4 16.4 %collective-permute-start.12 = (bf16[512,512]{1,0:T(8,128)(2,1)}, bf16[512,512]{1,0:T(8,128)(2,1)}, u32[]{:S(2)}, u32[]{:S(2)}) collective-permute-start(bf16[512,512]{1,0:T(8,128)(2,1)} %get-tuple-element.100), channel_id=1, source_target_pairs={{0,16},{4,20},{8,24},{12,28},{16,0},{20,4},{24,8},{28,12},{1,17},{... | collective-permute-start | bytes 1572872 | tf_op jit(solution)/shard_map/ppermute | solution.py:194
  49.9 15.9 %copy-start.29 = (bf16[256,512]{1,0:T(8,128)(2,1)S(1)}, bf16[256,512]{1,0:T(8,128)(2,1)}, u32[]{:S(2)}) copy-start(bf16[256,512]{1,0:T(8,128)(2,1)} %copy-done.28) | copy-start | bytes 786436
  56.7 14.4 %copy-start.27 = (bf16[256,512]{1,0:T(8,128)(2,1)S(1)}, bf16[256,512]{1,0:T(8,128)(2,1)}, u32[]{:S(2)}) copy-start(bf16[256,512]{1,0:T(8,128)(2,1)} %copy-done.26) | copy-start | bytes 786436
  58.5 14.4 %copy-start.32 = (f32[256,512]{1,0:T(8,128)}, f32[256,512]{1,0:T(8,128)S(1)}, u32[]{:S(2)}) copy-start(f32[256,512]{1,0:T(8,128)S(1)} %get-tuple-element.112) | copy-start | bytes 1572868
  58.5 15.9 %copy-start.34 = (f32[256,512]{1,0:T(8,128)}, f32[256,512]{1,0:T(8,128)S(1)}, u32[]{:S(2)}) copy-start(f32[256,512]{1,0:T(8,128)S(1)} %get-tuple-element.111) | copy-start | bytes 1572868
  58.5 9.0 %collective-permute-start.15 = (bf16[256,512]{1,0:T(8,128)(2,1)S(1)}, bf16[256,512]{1,0:T(8,128)(2,1)S(1)}, u32[]{:S(2)}, u32[]{:S(2)}) collective-permute-start(bf16[256,512]{1,0:T(8,128)(2,1)S(1)} %get-tuple-element.134), channel_id=1, source_target_pairs={{0,1},{1,0},{2,3},{3,2},{4,5},{5,4},{6,7},{7,6},{8,9},{9,8},{10,11... | collective-permute-start | bytes 786440 | tf_op jit(solution)/shard_map/ppermute | solution.py:239
  68.5 13.5 %collective-permute-start.18 = (bf16[256,512]{1,0:T(8,128)(2,1)}, bf16[256,512]{1,0:T(8,128)(2,1)}, u32[]{:S(2)}, u32[]{:S(2)}) collective-permute-start(bf16[256,512]{1,0:T(8,128)(2,1)} %add_convert_fusion.3), channel_id=1, source_target_pairs={{0,2},{1,3},{2,0},{3,1},{4,6},{5,7},{6,4},{7,5},{8,10},{9,11},{10,... | collective-permute-start | bytes 786440 | tf_op jit(solution)/shard_map/ppermute | solution.py:239
  72.9 10.8 %collective-permute-start.17 = (bf16[256,512]{1,0:T(8,128)(2,1)}, bf16[256,512]{1,0:T(8,128)(2,1)}, u32[]{:S(2)}, u32[]{:S(2)}) collective-permute-start(bf16[256,512]{1,0:T(8,128)(2,1)} %add_convert_fusion.4), channel_id=1, source_target_pairs={{0,8},{4,12},{8,0},{12,4},{16,24},{20,28},{24,16},{28,20},{1,9},{5... | collective-permute-start | bytes 786440 | tf_op jit(solution)/shard_map/ppermute | solution.py:194
  74.4 9.6 %collective-permute-start.16 = (bf16[256,512]{1,0:T(8,128)(2,1)}, bf16[256,512]{1,0:T(8,128)(2,1)}, u32[]{:S(2)}, u32[]{:S(2)}) collective-permute-start(bf16[256,512]{1,0:T(8,128)(2,1)} %add_convert_fusion.5), channel_id=1, source_target_pairs={{0,16},{4,20},{8,24},{12,28},{16,0},{20,4},{24,8},{28,12},{1,17},{... | collective-permute-start | bytes 786440 | tf_op jit(solution)/shard_map/ppermute | solution.py:194
  76.0 8.0 %copy-start.19 = (f32[512,512]{1,0:T(8,128)S(1)}, f32[512,512]{1,0:T(8,128)}, u32[]{:S(2)}) copy-start(f32[512,512]{1,0:T(8,128)} %copy-done.18) | copy-start | bytes 3145732
  77.2 13.9 %collective-permute-start.20 = (bf16[512,512]{1,0:T(8,128)(2,1)S(1)}, bf16[512,512]{1,0:T(8,128)(2,1)S(1)}, u32[]{:S(2)}, u32[]{:S(2)}) collective-permute-start(bf16[512,512]{1,0:T(8,128)(2,1)S(1)} %slice.111), channel_id=1, source_target_pairs={{0,8},{4,12},{8,0},{12,4},{16,24},{20,28},{24,16},{28,20},{1,9},{5... | collective-permute-start | bytes 1572872 | tf_op jit(solution)/shard_map/ppermute | solution.py:194
  77.8 14.7 %collective-permute-start.21 = (bf16[512,512]{1,0:T(8,128)(2,1)S(1)}, bf16[512,512]{1,0:T(8,128)(2,1)S(1)}, u32[]{:S(2)}, u32[]{:S(2)}) collective-permute-start(bf16[512,512]{1,0:T(8,128)(2,1)S(1)} %slice.112), channel_id=1, source_target_pairs={{0,16},{4,20},{8,24},{12,28},{16,0},{20,4},{24,8},{28,12},{1,17},{... | collective-permute-start | bytes 1572872 | tf_op jit(solution)/shard_map/ppermute | solution.py:194
  85.4 8.7 %copy-start.33 = (f32[256,512]{1,0:T(8,128)S(1)}, f32[256,512]{1,0:T(8,128)}, u32[]{:S(2)}) copy-start(f32[256,512]{1,0:T(8,128)} %copy-done.32) | copy-start | bytes 1572868
  85.5 8.7 %copy-start.35 = (f32[256,512]{1,0:T(8,128)S(1)}, f32[256,512]{1,0:T(8,128)}, u32[]{:S(2)}) copy-start(f32[256,512]{1,0:T(8,128)} %copy-done.34) | copy-start | bytes 1572868
  85.6 7.7 %collective-permute-start.19 = (bf16[256,512]{1,0:T(8,128)(2,1)S(1)}, bf16[256,512]{1,0:T(8,128)(2,1)S(1)}, u32[]{:S(2)}, u32[]{:S(2)}) collective-permute-start(bf16[256,512]{1,0:T(8,128)(2,1)S(1)} %select_convert_fusion), channel_id=1, source_target_pairs={{0,1},{1,0},{2,3},{3,2},{4,5},{5,4},{6,7},{7,6},{8,9},{9,8},{10,11... | collective-permute-start | bytes 786440 | tf_op jit(solution)/shard_map/ppermute | solution.py:239
  87.4 19.1 %copy-start.7 = (bf16[512,512]{1,0:T(8,128)(2,1)S(1)}, bf16[512,512]{1,0:T(8,128)(2,1)}, u32[]{:S(2)}) copy-start(bf16[512,512]{1,0:T(8,128)(2,1)} %copy-done.6) | copy-start | bytes 1572868
  87.4 19.1 %copy-start.9 = (bf16[512,512]{1,0:T(8,128)(2,1)S(1)}, bf16[512,512]{1,0:T(8,128)(2,1)}, u32[]{:S(2)}) copy-start(bf16[512,512]{1,0:T(8,128)(2,1)} %copy-done.8) | copy-start | bytes 1572868
  87.5 19.1 %copy-start.11 = (bf16[512,512]{1,0:T(8,128)(2,1)S(1)}, bf16[512,512]{1,0:T(8,128)(2,1)}, u32[]{:S(2)}) copy-start(bf16[512,512]{1,0:T(8,128)(2,1)} %copy-done.10) | copy-start | bytes 1572868
  87.5 19.1 %copy-start.13 = (bf16[512,512]{1,0:T(8,128)(2,1)S(1)}, bf16[512,512]{1,0:T(8,128)(2,1)}, u32[]{:S(2)}) copy-start(bf16[512,512]{1,0:T(8,128)(2,1)} %copy-done.12) | copy-start | bytes 1572868
  94.5 4.7 %collective-permute-start.22 = (f32[12,128]{1,0:T(8,128)S(1)}, f32[12,128]{1,0:T(8,128)S(1)}, u32[]{:S(2)}, u32[]{:S(2)}) collective-permute-start(f32[12,128]{1,0:T(8,128)S(1)} %maximum_bitcast_fusion), channel_id=1, source_target_pairs={{0,1},{1,0},{2,3},{3,2},{4,5},{5,4},{6,7},{7,6},{8,9},{9,8},{10,11... | collective-permute-start | bytes 18440 | tf_op jit(solution)/shard_map/ppermute | solution.py:239
  96.1 16.8 %collective-permute-start.26 = (bf16[256,512]{1,0:T(8,128)(2,1)}, bf16[256,512]{1,0:T(8,128)(2,1)S(1)}, u32[]{:S(2)}, u32[]{:S(2)}) collective-permute-start(bf16[256,512]{1,0:T(8,128)(2,1)} %add_convert_fusion.2), channel_id=1, source_target_pairs={{0,1},{1,0},{2,3},{3,2},{4,5},{5,4},{6,7},{7,6},{8,9},{9,8},{10,11... | collective-permute-start | bytes 786440 | tf_op jit(solution)/shard_map/ppermute | solution.py:239
  96.6 16.3 %collective-permute-start.25 = (bf16[256,512]{1,0:T(8,128)(2,1)}, bf16[256,512]{1,0:T(8,128)(2,1)S(1)}, u32[]{:S(2)}, u32[]{:S(2)}) collective-permute-start(bf16[256,512]{1,0:T(8,128)(2,1)} %add_convert_fusion.1), channel_id=1, source_target_pairs={{0,2},{1,3},{2,0},{3,1},{4,6},{5,7},{6,4},{7,5},{8,10},{9,11},{10,... | collective-permute-start | bytes 786440 | tf_op jit(solution)/shard_map/ppermute | solution.py:239
  99.2 7.3 %collective-permute-start.23 = (f32[12,128]{1,0:T(8,128)S(1)}, f32[12,128]{1,0:T(8,128)S(1)}, u32[]{:S(2)}, u32[]{:S(2)}) collective-permute-start(f32[12,128]{1,0:T(8,128)S(1)} %fusion.5), channel_id=1, source_target_pairs={{0,2},{1,3},{2,0},{3,1},{4,6},{5,7},{6,4},{7,5},{8,10},{9,11},{10,... | collective-permute-start | bytes 18440 | tf_op jit(solution)/shard_map/ppermute | solution.py:239
  106.5 6.4 %collective-permute-start.24 = (f32[12,128]{1,0:T(8,128)S(1)}, f32[12,128]{1,0:T(8,128)S(1)}, u32[]{:S(2)}, u32[]{:S(2)}) collective-permute-start(f32[12,128]{1,0:T(8,128)S(1)} %fusion.7), channel_id=1, source_target_pairs={{0,4},{4,0},{8,12},{12,8},{16,20},{20,16},{24,28},{28,24},{1,5},{5... | collective-permute-start | bytes 18440 | tf_op jit(solution)/shard_map/ppermute | solution.py:194
  112.4 13.5 %copy-start.5 = (f32[512,128]{1,0:T(8,128)S(1)}, f32[512,128]{1,0:T(8,128)}, u32[]{:S(2)}) copy-start(f32[512,128]{1,0:T(8,128)} %copy-done.4) | copy-start | bytes 786436
  112.4 13.5 %copy-start.31 = (f32[512]{0:T(512)S(1)}, f32[512]{0:T(512)}, u32[]{:S(2)}) copy-start(f32[512]{0:T(512)} %param.10) | copy-start | bytes 6148
  112.4 13.5 %collective-permute-start.28 = (f32[512,512]{1,0:T(8,128)S(1)}, f32[512,512]{1,0:T(8,128)S(1)}, u32[]{:S(2)}, u32[]{:S(2)}) collective-permute-start(f32[512,512]{1,0:T(8,128)S(1)} %get-tuple-element.123), channel_id=1, source_target_pairs={{0,4},{4,0},{8,12},{12,8},{16,20},{20,16},{24,28},{28,24},{1,5},{5... | collective-permute-start | bytes 3145736 | tf_op jit(solution)/shard_map/ppermute | solution.py:194
  113.0 9.0 %collective-permute-start.29 = (f32[20,128]{1,0:T(8,128)S(1)}, f32[20,128]{1,0:T(8,128)S(1)}, u32[]{:S(2)}, u32[]{:S(2)}) collective-permute-start(f32[20,128]{1,0:T(8,128)S(1)} %pad_maximum_fusion.3), channel_id=1, source_target_pairs={{0,8},{4,12},{8,0},{12,4},{16,24},{20,28},{24,16},{28,20},{1,9},{5... | collective-permute-start | bytes 30728 | tf_op jit(solution)/shard_map/ppermute | solution.py:194
  116.4 11.7 %collective-permute-start.27 = (bf16[256,512]{1,0:T(8,128)(2,1)S(1)}, bf16[256,512]{1,0:T(8,128)(2,1)S(1)}, u32[]{:S(2)}, u32[]{:S(2)}) collective-permute-start(bf16[256,512]{1,0:T(8,128)(2,1)S(1)} %add_convert_fusion), channel_id=1, source_target_pairs={{0,1},{1,0},{2,3},{3,2},{4,5},{5,4},{6,7},{7,6},{8,9},{9,8},{10,11... | collective-permute-start | bytes 786440 | tf_op jit(solution)/shard_map/ppermute | solution.py:239
  122.0 3.8 %collective-permute-start.30 = (f32[36,128]{1,0:T(8,128)S(1)}, f32[36,128]{1,0:T(8,128)S(1)}, u32[]{:S(2)}, u32[]{:S(2)}) collective-permute-start(f32[36,128]{1,0:T(8,128)S(1)} %pad_maximum_fusion.1), channel_id=1, source_target_pairs={{0,16},{4,20},{8,24},{12,28},{16,0},{20,4},{24,8},{28,12},{1,17},{... | collective-permute-start | bytes 55304 | tf_op jit(solution)/shard_map/ppermute | solution.py:194
  (21 other events, 44.6 us)

commit v4 on v3

--- a/solution.py
+++ b/solution.py
@@ -2,6 +2,7 @@
 
 import jax
 import jax.numpy as jnp
+import numpy as np
 from jax import lax
 from jax.experimental import pallas as pl
 from jax.experimental.pallas import tpu as pltpu
@@ -53,8 +54,12 @@
     )
 
 
-def scale_body(at_ref, x_ref, gain_ref, *outs):
-    wide = x_ref.shape[1]
+def turn(v, cosine, sine):
+    return v * cosine + pltpu.roll(v, HEAD // 2, 1) * sine
+
+
+def prepare_body(per_batch, at_ref, x_ref, gain_ref, seg_ref, inv_ref, cot_ref, *outs):
+    step, wide = x_ref.shape
     part = wide // 8
     half = part // 2
     total = None
@@ -65,7 +70,8 @@
     inv = lax.rsqrt(total * (1.0 / wide) + 1e-06)
     me = at_ref[0]
     mine, sib, rest = outs[:8], outs[8:12], outs[12]
-    places = {8 + 3: 0, 8 + 1: 1, 8 + 2: 2, 12 + 3: 3}
+    cos_ref, sin_ref, dproj_ref = outs[13:]
+    places = {3: 0, 1: 1, 2: 2, 7: 3}
     for o in range(8):
         start = pl.multiple_of((me ^ o) * part, part)
         for chunk in range(2):
@@ -75,43 +81,60 @@
             at = 4 * chunk + o // 2
             if not o & 1:
                 mine[at][...] = done
-            elif 8 + at in places:
-                sib[places[8 + at]][...] = done
+            elif at in places:
+                sib[places[at]][...] = done
             else:
                 at = max(at - 3, 0) * half
                 rest[:, at : at + half] = done
 
-
-def scaled_parts(x, gain, at):
+    r = pl.program_id(0)
+    seq = seg_ref.shape[1]
+    segs = seg_ref[pl.ds(r // per_batch, 1), :]
+    row = lax.broadcasted_iota(jnp.int32, (step, seq), 0) + r % per_batch * step
+    col = lax.broadcasted_iota(jnp.int32, (step, seq), 1)
+    own = jnp.sum(jnp.where(row == col, segs, 0), axis=1, keepdims=True)
+    position = jnp.sum(
+        jnp.where((own == segs) & (col < row), 1, 0), axis=1, keepdims=True
+    )
+    angle = position.astype(F32) * inv_ref[...]
+    cosine, sine = jnp.cos(angle), jnp.sin(angle)
+    second = lax.broadcasted_iota(jnp.int32, sine.shape, 1) >= HEAD // 2
+    sine = jnp.where(second, -sine, sine)
+    cos_ref[...] = cosine
+    sin_ref[...] = sine
+    for h in range(KVH):
+        cols = slice(h * HEAD, (h + 1) * HEAD)
+        dproj_ref[:, cols] = turn(cot_ref[:, cols].astype(F32), cosine, sine).astype(BF16)
+
+
+def prepared(x, gain, segs, cotangent, at):
     rows, wide = x.shape
     step = 64
-    widths = [wide // 16] * 12 + [wide // 4]
+    half = wide // 16
+    outs = [(half, BF16)] * 12 + [(4 * half, BF16), (HEAD, F32), (HEAD, F32), (KW, BF16)]
+    freq = np.arange(HEAD) % (HEAD // 2) * (2.0 / HEAD)
+    inv = jnp.asarray(np.power(1000000.0, -freq)[None, :], F32)
+
+    def whole(v):
+        return pl.BlockSpec(v.shape, lambda r, at: (0, 0))
+
+    def some(n):
+        return pl.BlockSpec((step, n), lambda r, at: (r, 0))
+
+    gain = gain[None, :]
     return pl.pallas_call(
-        scale_body,
+        functools.partial(prepare_body, segs.shape[1] // step),
         grid_spec=pltpu.PrefetchScalarGridSpec(
             num_scalar_prefetch=1,
             grid=(rows // step,),
-            in_specs=[
-                pl.BlockSpec((step, wide), lambda r, at: (r, 0)),
-                pl.BlockSpec((1, wide), lambda r, at: (0, 0)),
-            ],
-            out_specs=[pl.BlockSpec((step, n), lambda r, at: (r, 0)) for n in widths],
+            in_specs=[some(wide), whole(gain), whole(segs), whole(inv), some(KW)],
+            out_specs=[some(n) for n, _ in outs],
         ),
-        out_shape=[jax.ShapeDtypeStruct((rows, n), BF16) for n in widths],
+        out_shape=[jax.ShapeDtypeStruct((rows, n), t) for n, t in outs],
         cost_estimate=pl.CostEstimate(flops=1, bytes_accessed=1, transcendentals=0),
-        compiler_params=pltpu.CompilerParams(vmem_limit_bytes=12 * 1024 * 1024),
-        name="scale_rows",
-    )(at, x, gain[None, :])
-
-
-def turn(v, cosine, sine):
-    return v * cosine + pltpu.roll(v, HEAD // 2, 1) * sine
-
-
-def turn_body(v_ref, cos_ref, sin_ref, out_ref):
-    for h in range(KVH):
-        cols = slice(h * HEAD, (h + 1) * HEAD)
-        out_ref[:, cols] = turn(v_ref[:, cols].astype(F32), cos_ref[...], sin_ref[...]).astype(BF16)
+        compiler_params=pltpu.CompilerParams(vmem_limit_bytes=14 * 1024 * 1024),
+        name="prepare",
+    )(at, x, gain, segs, inv, cotangent)
 
 
 def keys_body(here, there, bias, cos_ref, sin_ref, out_ref):
@@ -137,17 +160,19 @@
         ref[at : at + half] = part.astype(ref.dtype)
 
 
-def first_grad_body(m1, m2, m3, s1, s2, s3, dproj, dproj_sib, *outs):
+def first_grad_body(m1, m2, m3, s1, s2, s3, dproj, upper, lower, *outs):
+    dproj_sib = jnp.concatenate([upper[...], lower[...]], axis=0)
     for chip, mine, sib in ((3, m3, s3), (1, m1, s1), (2, m2, s2)):
-        spread(product(mine[...], sib[...], dproj[...], dproj_sib[...]), chip, outs)
-
-
-def second_grad_body(m_a0, m0, m1, m2, m3, s3, rest, dproj, dproj_sib, own_a, own_b, *outs):
+        spread(product(mine[...], sib[...], dproj[...], dproj_sib), chip, outs)
+
+
+def second_grad_body(m_a0, m0, m1, m2, m3, s3, rest, dproj, upper, lower, own_a, own_b, *outs):
+    dproj_sib = jnp.concatenate([upper[...], lower[...]], axis=0)
     half = m0.shape[1]
-    own_a[...] = product(m_a0[...], rest[:, :half], dproj[...], dproj_sib[...])
+    own_a[...] = product(m_a0[...], rest[:, :half], dproj[...], dproj_sib)
     for chip, mine in ((3, m3), (1, m1), (2, m2), (0, m0)):
         sib = s3[...] if chip == 3 else rest[:, (chip + 1) * half : (chip + 2) * half]
-        rows = product(mine[...], sib, dproj[...], dproj_sib[...])
+        rows = product(mine[...], sib, dproj[...], dproj_sib)
         if chip:
             spread(rows, chip, outs)
         else:
@@ -198,24 +223,20 @@
     def widen(v):
         return v.astype(F32)
 
+    odd = (lax.axis_index("dp") & 1) == 1
+    firsts = [(me & bit) == 0 for bit in (1, 2, 4)]
+    my_gain = lax.dynamic_slice(norm_gain, (me * own,), (own,))
+    at = me.reshape(1).astype(jnp.int32)
+    odd, firsts, my_gain, at, key_weight, hidden_in, key_cotangent, segment_ids = after(
+        (odd, firsts, my_gain, at, key_weight, hidden_in, key_cotangent, segment_ids)
+    )
     w_x, w_y = px(key_weight), py(key_weight)
 
-    positions = positions_of(segment_ids).reshape(tok)
-    lane = jnp.arange(HEAD, dtype=jnp.int32)
-    freq = (lane % (HEAD // 2)).astype(F32) * (2.0 / HEAD)
-    angle = positions.astype(F32)[:, None] * jnp.power(F32(1000000.0), -freq)[None, :]
-    cosine = jnp.cos(angle)
-    sine = jnp.sin(angle) * jnp.where(lane < HEAD // 2, 1.0, -1.0)[None, :]
-    dproj = call(turn_body, jax.ShapeDtypeStruct((tok, kw), BF16), "turn_back")(
-        key_cotangent, cosine, sine
-    )
+    parts = prepared(hidden_in, norm_gain, segment_ids, key_cotangent, at)
+    mine_a, mine_b, (s_a3, s_a1, s_a2, s_b3, rest) = parts[:4], parts[4:8], parts[8:13]
+    cosine, sine, dproj = parts[13:]
     n = tok // 2
-    dproj_sib = jnp.concatenate([core(dproj[:n]), core(dproj[n:])], axis=0)
-
-    parts = scaled_parts(
-        after(hidden_in, dproj_sib), norm_gain, me.reshape(1).astype(jnp.int32)
-    )
-    mine_a, mine_b, (s_a3, s_a1, s_a2, s_b3, rest) = parts[:4], parts[4:8], parts[8:]
+    dproj_sib = core(dproj[:n]), core(dproj[n:])
     s_a3, s_a1, s_a2 = core(s_a3), core(s_a1), core(s_a2)
 
     def part_shapes(h):
@@ -233,8 +254,6 @@
         high = mine[quarter:] + widen(first[1][:quarter]) + widen(second[1])
         return low, high
 
-    odd = (lax.axis_index("dp") & 1) == 1
-
     def over_z(bit):
         return lambda v: lax.ppermute(v, "dp", [(i, i ^ bit) for i in range(4)])
 
@@ -252,7 +271,7 @@
         return widen(jnp.where(odd, got, total)), widen(jnp.where(odd, total, got))
 
     part_a = call(first_grad_body, part_shapes(quarter), "grad_a")(
-        *mine_a[1:], s_a1, s_a2, s_a3, dproj, dproj_sib
+        *mine_a[1:], s_a1, s_a2, s_a3, dproj, *dproj_sib
     )
     to_a = after((part_a[0], part_a[1]), w_x, w_y)
     in_a = px(to_a[0]), py(to_a[1])
@@ -261,7 +280,7 @@
     own_shape = jax.ShapeDtypeStruct((half, kw), F32)
     own_a, own_b, *part_b = call(
         second_grad_body, [own_shape, own_shape, *part_shapes(quarter)], "grad_b"
-    )(mine_a[0], *mine_b, s_b3, rest, dproj, dproj_sib)
+    )(mine_a[0], *mine_b, s_b3, rest, dproj, *dproj_sib)
 
     acts = (*mine_a[:3], *mine_b[:3], s_a1, s_a2, rest)
     places = (
@@ -285,13 +304,29 @@
     in_b = after(in_b, two_a)
     more = after(add_up(part_b, *in_b), pair_a)
     two_b = py(more[0]), px(more[1])
-    later = after((w_y[:half], w_x[half:]), pair_a)
+    later = after((w_y[:half], w_x[half:]), two_b)
     wd_low, wd_high = px(later[0]), py(later[1])
     total_a = total_of(pair_a, over_z(2)(pair_a))
     got_a = over_z(1)(total_a)
     local_b = after(own_rows(own_b, in_b, two_b), total_a)
-    into_b, wd_low, wd_high = after((in_pair(*local_b), wd_low, wd_high))
+    into_b = in_pair(*local_b)
+
+    gain_rows = jnp.concatenate(
+        [
+            jnp.sum(v * widen(key_weight[n * quarter : (n + 1) * quarter]), axis=1)
+            for n, v in enumerate((*local_a, *local_b))
+        ]
+    )
+    bias = sum(jnp.sum(widen(v), axis=0) for v in (dproj, *dproj_sib))
+    n_own = own // HEAD
+    small = jnp.concatenate([gain_rows / my_gain, bias]).reshape(-1, HEAD)
+    small = small + over_z(1)(small)
+    into_b, small = after((into_b, small))
     pair_b = pair_sum(*local_b, into_b)
+    small = small + over_z(2)(small)
+    other_b, got_a, small = after((over_z(2)(pair_b), got_a, small))
+    total_b = total_of(pair_b, other_b)
+    got_b = over_z(1)(total_b)
 
     acts = after((mine_a[3], mine_b[3], s_a3, s_b3), pair_b)
     here, there = forward(acts, ((0, 2, 0, 0, 0), (1, 3, 0, 1, 0)), (wd_low, wd_high), here)
@@ -299,30 +334,12 @@
         here, core(there), key_bias[None, :], cosine, sine
     )
 
-    local = after((*local_a, *local_b), pair_b)
-    my_gain = lax.dynamic_slice(norm_gain, (me * own,), (own,))
-    gain_rows = jnp.concatenate(
-        [
-            jnp.sum(v * widen(key_weight[n * quarter : (n + 1) * quarter]), axis=1)
-            for n, v in enumerate(local)
-        ]
-    )
-    bias = jnp.sum(widen(dproj), axis=0) + jnp.sum(widen(dproj_sib), axis=0)
-    n_own = own // HEAD
-    small = jnp.concatenate([gain_rows / my_gain, bias]).reshape(-1, HEAD)
-    for bit in (1, 2):
-        small = small + over_z(bit)(small)
     gains, bias = small[:n_own], small[n_own:]
     scale = 1.0 / jnp.sqrt(F32(tok * 32))
-    for bit in (1, 2, 4):
+    for bit, first in zip((1, 2, 4), firsts, strict=True):
         got = over(bit)(jnp.concatenate([gains, bias], axis=0))
-        if bit == 1:
-            got, other_b, got_a = after((got, over_z(2)(pair_b), got_a))
-            total_b = total_of(pair_b, other_b)
-            got_b = over_z(1)(total_b)
         size = gains.shape[0]
         theirs = got[:size]
-        first = (me & bit) == 0
         gains = jnp.concatenate(
             [jnp.where(first, gains, theirs), jnp.where(first, theirs, gains)], axis=0
         )

time: 132 us -> 116 us (0.88)
  waiting for transfers between devices: 37 us -> 56.4 us
  other arithmetic: 19.4 us -> 5.08 us
  local copies, waits for them, and re-layouts: 18.6 us -> 7.33 us
  starting transfers between devices: 39 us -> 29.9 us
    ppermute x8, waiting for transfers between devices: 10.3 us -> 24.3 us  [over_z(): return lambda v: lax.ppermute(v, 'dp', [(i, i ^ bit) for i in range(4)])]
    unnamed x78 -> x14, local copies, waits for them, and re-layouts: 15.7 us -> 6.53 us
    ppermute x8, starting transfers between devices: 18 us -> 10.2 us  [over_z(): return lambda v: lax.ppermute(v, 'dp', [(i, i ^ bit) for i in range(4)])]
    ppermute x23, waiting for transfers between devices: 26.7 us -> 32.1 us  [over(): return lambda v: lax.ppermute(v, 'blk', [(i, i ^ bit) for i in range(8)])]
    convert_element_type x2, other arithmetic: 2.83 us -> 0.13 us  [total_of(): return (widen(pair) + widen(other)).astype(BF16)]
    convert_element_type x2 -> x1, other arithmetic: 2.48 us -> 0.07 us  [add_up(): more_y = (widen(keep_y) + widen(from_x[quarter:])).astype(BF16)]
    convert_element_type x2, other arithmetic: 2.59 us -> 0.2 us  [add_up(): more_x = (widen(keep_x) + widen(from_y[quarter:])).astype(BF16)]
    slice x3, local copies, waits for them, and re-layouts: 1.94 us -> 0.11 us  [the longest x2 0.07 us: by_permutes(): later = after((w_y[:half], w_x[half:]), two_b)]
  transfers between devices with their start and end apart: 31 -> 31, of which waited for: 18 -> 20; matrix products, arithmetic and copies ran while one was open for 13% -> 1% of each run, Pallas kernels for 12% -> 14%
where the time goes in v4:
time: 116 us
  waiting for transfers between devices  56.4 us (49%)
  starting transfers between devices  29.9 us (26%)
  Pallas kernels  16.4 us (14%)
  local copies, waits for them, and re-layouts  7.33 us (6%)
  other arithmetic  5.08 us (4%)
    ppermute x23, waiting for transfers between devices, over(): return lambda v: lax.ppermute(v, 'blk', [(i, i ^ bit) for i in range(8)])  32.1 us
    ppermute x8, waiting for transfers between devices, over_z(): return lambda v: lax.ppermute(v, 'dp', [(i, i ^ bit) for i in range(4)])  24.3 us
    ppermute x23, starting transfers between devices, over(): return lambda v: lax.ppermute(v, 'blk', [(i, i ^ bit) for i in range(8)])  19.6 us
    ppermute x8, starting transfers between devices, over_z(): return lambda v: lax.ppermute(v, 'dp', [(i, i ^ bit) for i in range(4)])  10.2 us
    unnamed x14, local copies, waits for them, and re-layouts  6.53 us
    pallas_call x1, Pallas kernels, prepared(): pl.pallas_call(functools.partial(prepare_body, segs.shape[1] // step), gr...  5.75 us
    pallas_call x2, Pallas kernels, forward(): call(functools.partial(forward_body, (places, len(acts), len(init))), [ja...  4.68 us
    pallas_call x1, Pallas kernels, by_permutes(): call(second_grad_body, [own_shape, own_shape, *part_shapes(quarter)], 'gr...  2.91 us
  transfers between devices with their start and end apart: 31, of which 20 were waited for; matrix products, arithmetic and copies ran while one was open for 1% of the time, Pallas kernels for 14%

profile of v4, /device:TPU:0, one launch (start us, length us, event | category | flops | bytes accessed | tf_op | source)
XLA Modules:
  0.0 116.0 jit_solution(13631866175164354718)
XLA Ops:
  0.6 0.7 dynamic_slice.3
  1.3 2.9 %collective-permute-start.5 = (bf16[1024,512]{1,0:T(8,128)(2,1)}, bf16[1024,512]{1,0:T(8,128)(2,1)S(1)}, u32[]{:S(2)}, u32[]{:S(2)}) collective-permute-start(bf16[1024,512]{1,0:T(8,128)(2,1)} %refs_9_), channel_id=1, source_target_pairs={{0,8},{4,12},{8,0},{12,4},{16,24},{20,28},{24,16},{28,20},{1,9},{5... | collective-permute-start | bytes 3145736 | tf_op jit(solution)/shard_map/ppermute | solution.py:219
  4.3 1.5 %collective-permute-start.6 = (bf16[1024,512]{1,0:T(8,128)(2,1)}, bf16[1024,512]{1,0:T(8,128)(2,1)S(1)}, u32[]{:S(2)}, u32[]{:S(2)}) collective-permute-start(bf16[1024,512]{1,0:T(8,128)(2,1)} %refs_9_), channel_id=1, source_target_pairs={{0,16},{4,20},{8,24},{12,28},{16,0},{20,4},{24,8},{28,12},{1,17},{... | collective-permute-start | bytes 3145736 | tf_op jit(solution)/shard_map/ppermute | solution.py:219
  5.8 3.4 %copy-done = bf16[512,8192]{1,0:T(8,128)(2,1)S(1)} copy-done((bf16[512,8192]{1,0:T(8,128)(2,1)S(1)}, bf16[512,8192]{1,0:T(8,128)(2,1)}, u32[]{:S(2)}) %copy-start) | copy-done | bytes 8388632
  9.2 1.0 copy-done.2
  10.2 0.8 copy-done.3
  11.0 0.7 copy-done.5
  11.7 0.7 copy-done.6
  12.3 5.8 %prepare.1 = (bf16[512,512]{1,0:T(8,128)(2,1)S(1)}, bf16[512,512]{1,0:T(8,128)(2,1)S(1)}, bf16[512,512]{1,0:T(8,128)(2,1)S(1)}, bf16[512,512]{1,0:T(8,128)(2,1)S...) custom-call(s32[1]{0:T(128)} %bitcast.at_ref, ...), custom_call_target="tpu_custom_call" | custom-call | flops 1 | bytes 1 | tf_op jit(solution)/shard_map/prepare/pallas_call | solution.py:125
  18.8 0.9 collective-permute-done.3.upper
  20.9 0.8 collective-permute-done.1.s2.refs_7_
  21.6 0.7 collective-permute-done.2.s3.refs_2_
  22.4 1.8 %grad_a.1 = (bf16[512,512]{1,0:T(8,128)(2,1)S(1)}, bf16[512,512]{1,0:T(8,128)(2,1)S(1)}, bf16[256,512]{1,0:T(8,128)(2,1)S(1)}, bf16[256,512]{1,0:T(8,128)(2,1)S(1)}) custom-call(bf16[512,512]{1,0:T(8,128)(2,1)S(1)} %get-tuple-element.86.m1.refs_1_, bf16[512,512]{1,0:T(8,128)(2,1)S(1)} %get-tuple-element.87.m2.refs_2_, ...), custom_call_target="tpu_custom_call" | custom-call | flops 1 | bytes 1 | tf_op jit(solution)/shard_map/grad_a/pallas_call | solution.py:273
  24.2 3.4 %collective-permute-done.5.refs_10_ = bf16[1024,512]{1,0:T(8,128)(2,1)S(1)} collective-permute-done((bf16[1024,512]{1,0:T(8,128)(2,1)}, bf16[1024,512]{1,0:T(8,128)(2,1)S(1)}, u32[]{:S(2)}, u32[]{:S(2)}) %collective-permute-start.5) | collective-permute-done | bytes 1048608 | tf_op jit(solution)/shard_map/ppermute | solution.py:219
  27.6 1.5 %collective-permute-done.6.refs_11_ = bf16[1024,512]{1,0:T(8,128)(2,1)S(1)} collective-permute-done((bf16[1024,512]{1,0:T(8,128)(2,1)}, bf16[1024,512]{1,0:T(8,128)(2,1)S(1)}, u32[]{:S(2)}, u32[]{:S(2)}) %collective-permute-start.6) | collective-permute-done | bytes 1048608 | tf_op jit(solution)/shard_map/ppermute | solution.py:219
  29.6 1.5 %collective-permute-start.10 = (bf16[512,512]{1,0:T(8,128)(2,1)S(1)}, bf16[512,512]{1,0:T(8,128)(2,1)S(1)}, u32[]{:S(2)}, u32[]{:S(2)}) collective-permute-start(bf16[512,512]{1,0:T(8,128)(2,1)S(1)} %get-tuple-element.104), channel_id=1, source_target_pairs={{0,16},{4,20},{8,24},{12,28},{16,0},{20,4},{24,8},{28,12},{1,17},{... | collective-permute-start | bytes 1572872 | tf_op jit(solution)/shard_map/ppermute | solution.py:219
  31.7 2.3 %collective-permute-done.7.s3.refs_3_ = bf16[512,512]{1,0:T(8,128)(2,1)S(1)} collective-permute-done((bf16[512,512]{1,0:T(8,128)(2,1)S(1)}, bf16[512,512]{1,0:T(8,128)(2,1)S(1)}, u32[]{:S(2)}, u32[]{:S(2)}) %collective-permute-start.7) | collective-permute-done | bytes 524320 | tf_op jit(solution)/shard_map/ppermute | solution.py:219
  34.0 2.9 %grad_b.1 = (f32[512,512]{1,0:T(8,128)S(1)}, f32[512,512]{1,0:T(8,128)S(1)}, bf16[512,512]{1,0:T(8,128)(2,1)S(1)}, bf16[512,512]{1,0:T(8,128)(2,1)S(1)}, bf16[25...) custom-call(bf16[512,512]{1,0:T(8,128)(2,1)S(1)} %get-tuple-element.79.m_a0.refs_0_, ...), custom_call_target="tpu_custom_call" | custom-call | flops 1 | bytes 1 | tf_op jit(solution)/shard_map/grad_b/pallas_call | solution.py:281
  36.9 3.4 %forward.2 = (f32[512,512]{1,0:T(8,128)S(1)}, f32[512,512]{1,0:T(8,128)S(1)}) custom-call(bf16[512,512]{1,0:T(8,128)(2,1)S(1)} %get-tuple-element.79.m_a0.refs_0_, bf16[512,512]{1,0:T(8,128)(2,1)S(1)} %get-tuple-element.86.m1.refs_1_, bf16[512,512]{1,0:T(8,128)(2,1)S(1)} %get-tuple-element.87.m2.refs_2_, bf16[512,512]{1,0:T(8,128)(2,1)S(1)} %get-tuple-element.80.m0.refs_3_, ...), custom_call_target="tpu_custom_call" | custom-call | flops 1 | bytes 1 | tf_op jit(solution)/shard_map/forward/pallas_call | solution.py:204
  40.4 3.1 %collective-permute-done.10 = bf16[512,512]{1,0:T(8,128)(2,1)S(1)} collective-permute-done((bf16[512,512]{1,0:T(8,128)(2,1)S(1)}, bf16[512,512]{1,0:T(8,128)(2,1)S(1)}, u32[]{:S(2)}, u32[]{:S(2)}) %collective-permute-start.10) | collective-permute-done | bytes 524320 | tf_op jit(solution)/shard_map/ppermute | solution.py:219
  43.5 1.2 %collective-permute-done.9 = bf16[512,512]{1,0:T(8,128)(2,1)S(1)} collective-permute-done((bf16[512,512]{1,0:T(8,128)(2,1)S(1)}, bf16[512,512]{1,0:T(8,128)(2,1)S(1)}, u32[]{:S(2)}, u32[]{:S(2)}) %collective-permute-start.9) | collective-permute-done | bytes 524320 | tf_op jit(solution)/shard_map/ppermute | solution.py:219
  45.8 1.7 %collective-permute-start.11 = (bf16[512,512]{1,0:T(8,128)(2,1)S(1)}, bf16[512,512]{1,0:T(8,128)(2,1)S(1)}, u32[]{:S(2)}, u32[]{:S(2)}) collective-permute-start(bf16[512,512]{1,0:T(8,128)(2,1)S(1)} %get-tuple-element.112), channel_id=1, source_target_pairs={{0,8},{4,12},{8,0},{12,4},{16,24},{20,28},{24,16},{28,20},{1,9},{5... | collective-permute-start | bytes 1572872 | tf_op jit(solution)/shard_map/ppermute | solution.py:219
  47.5 1.5 %collective-permute-start.12 = (bf16[512,512]{1,0:T(8,128)(2,1)S(1)}, bf16[512,512]{1,0:T(8,128)(2,1)S(1)}, u32[]{:S(2)}, u32[]{:S(2)}) collective-permute-start(bf16[512,512]{1,0:T(8,128)(2,1)S(1)} %get-tuple-element.113), channel_id=1, source_target_pairs={{0,16},{4,20},{8,24},{12,28},{16,0},{20,4},{24,8},{28,12},{1,17},{... | collective-permute-start | bytes 1572872 | tf_op jit(solution)/shard_map/ppermute | solution.py:219
  49.0 5.1 %collective-permute-done.14 = bf16[256,512]{1,0:T(8,128)(2,1)S(1)} collective-permute-done((bf16[256,512]{1,0:T(8,128)(2,1)S(1)}, bf16[256,512]{1,0:T(8,128)(2,1)S(1)}, u32[]{:S(2)}, u32[]{:S(2)}) %collective-permute-start.14) | collective-permute-done | bytes 262176 | tf_op jit(solution)/shard_map/ppermute | solution.py:219
  54.1 0.7 collective-permute-done.13
  55.0 1.6 %collective-permute-start.15 = (bf16[256,512]{1,0:T(8,128)(2,1)S(1)}, bf16[256,512]{1,0:T(8,128)(2,1)S(1)}, u32[]{:S(2)}, u32[]{:S(2)}) collective-permute-start(bf16[256,512]{1,0:T(8,128)(2,1)S(1)} %select_convert_fusion.1), channel_id=1, source_target_pairs={{0,1},{1,0},{2,3},{3,2},{4,5},{5,4},{6,7},{7,6},{8,9},{9,8},{10,11... | collective-permute-start | bytes 786440 | tf_op jit(solution)/shard_map/ppermute | solution.py:258
  56.9 6.2 %collective-permute-done.11 = bf16[512,512]{1,0:T(8,128)(2,1)S(1)} collective-permute-done((bf16[512,512]{1,0:T(8,128)(2,1)S(1)}, bf16[512,512]{1,0:T(8,128)(2,1)S(1)}, u32[]{:S(2)}, u32[]{:S(2)}) %collective-permute-start.11) | collective-permute-done | bytes 524320 | tf_op jit(solution)/shard_map/ppermute | solution.py:219
  63.8 2.7 %collective-permute-start.18 = (bf16[256,512]{1,0:T(8,128)(2,1)S(1)}, bf16[256,512]{1,0:T(8,128)(2,1)S(1)}, u32[]{:S(2)}, u32[]{:S(2)}) collective-permute-start(bf16[256,512]{1,0:T(8,128)(2,1)S(1)} %add_convert_fusion.3), channel_id=1, source_target_pairs={{0,2},{1,3},{2,0},{3,1},{4,6},{5,7},{6,4},{7,5},{8,10},{9,11},{10,... | collective-permute-start | bytes 786440 | tf_op jit(solution)/shard_map/ppermute | solution.py:258
  66.6 0.7 collective-permute-start.16
  67.3 1.5 %collective-permute-start.17 = (bf16[256,512]{1,0:T(8,128)(2,1)S(1)}, bf16[256,512]{1,0:T(8,128)(2,1)S(1)}, u32[]{:S(2)}, u32[]{:S(2)}) collective-permute-start(bf16[256,512]{1,0:T(8,128)(2,1)S(1)} %get-tuple-element.118), channel_id=1, source_target_pairs={{0,8},{4,12},{8,0},{12,4},{16,24},{20,28},{24,16},{28,20},{1,9},{5... | collective-permute-start | bytes 786440 | tf_op jit(solution)/shard_map/ppermute | solution.py:219
  68.8 7.5 %collective-permute-done.18 = bf16[256,512]{1,0:T(8,128)(2,1)S(1)} collective-permute-done((bf16[256,512]{1,0:T(8,128)(2,1)S(1)}, bf16[256,512]{1,0:T(8,128)(2,1)S(1)}, u32[]{:S(2)}, u32[]{:S(2)}) %collective-permute-start.18) | collective-permute-done | bytes 262176 | tf_op jit(solution)/shard_map/ppermute | solution.py:258
  76.7 0.7 collective-permute-start.19
  77.9 1.4 %collective-permute-start.20 = (f32[12,128]{1,0:T(8,128)S(1)}, f32[12,128]{1,0:T(8,128)S(1)}, u32[]{:S(2)}, u32[]{:S(2)}) collective-permute-start(f32[12,128]{1,0:T(8,128)S(1)} %maximum_bitcast_fusion), channel_id=1, source_target_pairs={{0,1},{1,0},{2,3},{3,2},{4,5},{5,4},{6,7},{7,6},{8,9},{9,8},{10,11... | collective-permute-start | bytes 18440 | tf_op jit(solution)/shard_map/ppermute | solution.py:258
  79.4 0.7 collective-permute-start.22
  80.1 1.5 %collective-permute-start.25 = (bf16[512,512]{1,0:T(8,128)(2,1)S(1)}, bf16[512,512]{1,0:T(8,128)(2,1)S(1)}, u32[]{:S(2)}, u32[]{:S(2)}) collective-permute-start(bf16[512,512]{1,0:T(8,128)(2,1)S(1)} %slice.109), channel_id=1, source_target_pairs={{0,8},{4,12},{8,0},{12,4},{16,24},{20,28},{24,16},{28,20},{1,9},{5... | collective-permute-start | bytes 1572872 | tf_op jit(solution)/shard_map/ppermute | solution.py:219
  81.6 0.7 collective-permute-start.26
  82.3 3.8 %collective-permute-done.20 = f32[12,128]{1,0:T(8,128)S(1)} collective-permute-done((f32[12,128]{1,0:T(8,128)S(1)}, f32[12,128]{1,0:T(8,128)S(1)}, u32[]{:S(2)}, u32[]{:S(2)}) %collective-permute-start.20) | collective-permute-done | bytes 6176 | tf_op jit(solution)/shard_map/ppermute | solution.py:258
  86.3 2.1 %collective-permute-start.21 = (bf16[256,512]{1,0:T(8,128)(2,1)S(1)}, bf16[256,512]{1,0:T(8,128)(2,1)S(1)}, u32[]{:S(2)}, u32[]{:S(2)}) collective-permute-start(bf16[256,512]{1,0:T(8,128)(2,1)S(1)} %add_convert_fusion.1), channel_id=1, source_target_pairs={{0,2},{1,3},{2,0},{3,1},{4,6},{5,7},{6,4},{7,5},{8,10},{9,11},{10,... | collective-permute-start | bytes 786440 | tf_op jit(solution)/shard_map/ppermute | solution.py:258
  88.3 0.9 collective-permute-start.23
  89.3 10.2 %collective-permute-done.23 = f32[12,128]{1,0:T(8,128)S(1)} collective-permute-done((f32[12,128]{1,0:T(8,128)S(1)}, f32[12,128]{1,0:T(8,128)S(1)}, u32[]{:S(2)}, u32[]{:S(2)}) %collective-permute-start.23) | collective-permute-done | bytes 6176 | tf_op jit(solution)/shard_map/ppermute | solution.py:258
  99.6 1.3 %forward.3 = (f32[512,512]{1,0:T(8,128)S(1)}, f32[512,512]{1,0:T(8,128)S(1)}) custom-call(bf16[512,512]{1,0:T(8,128)(2,1)S(1)} %get-tuple-element.125.m3.refs_0_, bf16[512,512]{1,0:T(8,128)(2,1)S(1)} %get-tuple-element.126.m3.refs_1_, bf16[512,512]{1,0:T(8,128)(2,1)S(1)} %collective-permute-done.2.s3.refs_2_, ...), custom_call_target="tpu_custom_call" | custom-call | flops 1 | bytes 1 | tf_op jit(solution)/shard_map/forward/pallas_call | solution.py:204
  101.5 1.6 %collective-permute-start.29 = (f32[20,128]{1,0:T(8,128)S(1)}, f32[20,128]{1,0:T(8,128)S(1)}, u32[]{:S(2)}, u32[]{:S(2)}) collective-permute-start(f32[20,128]{1,0:T(8,128)S(1)} %pad_maximum_fusion.3), channel_id=1, source_target_pairs={{0,8},{4,12},{8,0},{12,4},{16,24},{20,28},{24,16},{28,20},{1,9},{5... | collective-permute-start | bytes 30728 | tf_op jit(solution)/shard_map/ppermute | solution.py:219
  103.1 2.2 %collective-permute-done.29 = f32[20,128]{1,0:T(8,128)S(1)} collective-permute-done((f32[20,128]{1,0:T(8,128)S(1)}, f32[20,128]{1,0:T(8,128)S(1)}, u32[]{:S(2)}, u32[]{:S(2)}) %collective-permute-start.29) | collective-permute-done | bytes 10272 | tf_op jit(solution)/shard_map/ppermute | solution.py:219
  105.2 1.0 collective-permute-start.30
  106.4 2.7 %collective-permute-done.30 = f32[36,128]{1,0:T(8,128)S(1)} collective-permute-done((f32[36,128]{1,0:T(8,128)S(1)}, f32[36,128]{1,0:T(8,128)S(1)}, u32[]{:S(2)}, u32[]{:S(2)}) %collective-permute-start.30) | collective-permute-done | bytes 18464 | tf_op jit(solution)/shard_map/ppermute | solution.py:219
  109.1 1.3 %keys.1 = bf16[512,512]{1,0:T(8,128)(2,1)} custom-call(f32[512,512]{1,0:T(8,128)S(1)} %get-tuple-element.131.here, f32[512,512]{1,0:T(8,128)S(1)} %collective-permute-done.27.there, f32[1,512]{1,0:T(1,128)S(1)} %bitcast.12, f32[512,128]{1,0:T(8,128)S(1)} %get-tuple-element.133.cos_ref, f32[512,128]{1,0:T(8,128)S(1)} %get-tuple-element.134.sin_ref), custom_call_target="tpu_custom_call" | custom-call | flops 1 | bytes 1 | tf_op jit(solution)/shard_map/keys/pallas_call | solution.py:333
  110.4 2.8 %collective-permute-done.24 = bf16[256,512]{1,0:T(8,128)(2,1)S(1)} collective-permute-done((bf16[256,512]{1,0:T(8,128)(2,1)S(1)}, bf16[256,512]{1,0:T(8,128)(2,1)S(1)}, u32[]{:S(2)}, u32[]{:S(2)}) %collective-permute-start.24) | collective-permute-done | bytes 262176 | tf_op jit(solution)/shard_map/ppermute | solution.py:258
  114.4 1.6 %convert_multiply_fusion = f32[1024,512]{1,0:T(8,128)} fusion(bf16[256,512]{1,0:T(8,128)(2,1)S(1)} %get-tuple-element.153, bf16[256,512]{1,0:T(8,128)(2,1)S(1)} %get-tuple-element.152, bf16[256,512]{1,0:T(8,128)(2,1)S(1)} %get-tuple-element.151, bf16[256,512]{1,0:T(8,128)(2,1)S(1)} %get-tuple-element.150), kind=kLoop, calls=%fused_computation | loop fusion | flops 4718592 | bytes 3145728 | tf_op jit(solution)/shard_map/mul | solution.py:350
  (71 shorter events, 8.5 us)
Async XLA Ops:
  1.3 26.3 %collective-permute-start.5 = (bf16[1024,512]{1,0:T(8,128)(2,1)}, bf16[1024,512]{1,0:T(8,128)(2,1)S(1)}, u32[]{:S(2)}, u32[]{:S(2)}) collective-permute-start(bf16[1024,512]{1,0:T(8,128)(2,1)} %refs_9_), channel_id=1, source_target_pairs={{0,8},{4,12},{8,0},{12,4},{16,24},{20,28},{24,16},{28,20},{1,9},{5... | collective-permute-start | bytes 3145736 | tf_op jit(solution)/shard_map/ppermute | solution.py:219
  4.3 24.8 %collective-permute-start.6 = (bf16[1024,512]{1,0:T(8,128)(2,1)}, bf16[1024,512]{1,0:T(8,128)(2,1)S(1)}, u32[]{:S(2)}, u32[]{:S(2)}) collective-permute-start(bf16[1024,512]{1,0:T(8,128)(2,1)} %refs_9_), channel_id=1, source_target_pairs={{0,16},{4,20},{8,24},{12,28},{16,0},{20,4},{24,8},{28,12},{1,17},{... | collective-permute-start | bytes 3145736 | tf_op jit(solution)/shard_map/ppermute | solution.py:219
  5.8 3.4 %copy-start = (bf16[512,8192]{1,0:T(8,128)(2,1)S(1)}, bf16[512,8192]{1,0:T(8,128)(2,1)}, u32[]{:S(2)}) copy-start(bf16[512,8192]{1,0:T(8,128)(2,1)} %x_ref) | copy-start | bytes 25165828
  9.2 1.0 copy-start.2
  10.2 0.8 copy-start.3
  11.0 0.7 copy-start.5
  11.7 0.7 copy-start.6
  18.1 1.6 %collective-permute-start.3 = (bf16[256,512]{1,0:T(8,128)(2,1)S(1)}, bf16[256,512]{1,0:T(8,128)(2,1)S(1)}, u32[]{:S(2)}, u32[]{:S(2)}) collective-permute-start(bf16[256,512]{1,0:T(8,128)(2,1)S(1)} %get-tuple-element.155), channel_id=1, source_target_pairs={{0,4},{4,0},{8,12},{12,8},{16,20},{20,16},{24,28},{28,24},{1,5},{5... | collective-permute-start | bytes 786440 | tf_op jit(solution)/shard_map/ppermute | solution.py:219
  18.2 1.9 %collective-permute-start.4 = (bf16[256,512]{1,0:T(8,128)(2,1)S(1)}, bf16[256,512]{1,0:T(8,128)(2,1)S(1)}, u32[]{:S(2)}, u32[]{:S(2)}) collective-permute-start(bf16[256,512]{1,0:T(8,128)(2,1)S(1)} %get-tuple-element.154), channel_id=1, source_target_pairs={{0,4},{4,0},{8,12},{12,8},{16,20},{20,16},{24,28},{28,24},{1,5},{5... | collective-permute-start | bytes 786440 | tf_op jit(solution)/shard_map/ppermute | solution.py:219
  18.7 2.1 %collective-permute-start = (bf16[512,512]{1,0:T(8,128)(2,1)S(1)}, bf16[512,512]{1,0:T(8,128)(2,1)S(1)}, u32[]{:S(2)}, u32[]{:S(2)}) collective-permute-start(bf16[512,512]{1,0:T(8,128)(2,1)S(1)} %get-tuple-element.89), channel_id=1, source_target_pairs={{0,4},{4,0},{8,12},{12,8},{16,20},{20,16},{24,28},{28,24},{1,5},{5... | collective-permute-start | bytes 1572872 | tf_op jit(solution)/shard_map/ppermute | solution.py:219
  19.7 1.9 %collective-permute-start.1 = (bf16[512,512]{1,0:T(8,128)(2,1)S(1)}, bf16[512,512]{1,0:T(8,128)(2,1)S(1)}, u32[]{:S(2)}, u32[]{:S(2)}) collective-permute-start(bf16[512,512]{1,0:T(8,128)(2,1)S(1)} %get-tuple-element.90), channel_id=1, source_target_pairs={{0,4},{4,0},{8,12},{12,8},{16,20},{20,16},{24,28},{28,24},{1,5},{5... | collective-permute-start | bytes 1572872 | tf_op jit(solution)/shard_map/ppermute | solution.py:219
  20.1 2.3 %collective-permute-start.2 = (bf16[512,512]{1,0:T(8,128)(2,1)S(1)}, bf16[512,512]{1,0:T(8,128)(2,1)S(1)}, u32[]{:S(2)}, u32[]{:S(2)}) collective-permute-start(bf16[512,512]{1,0:T(8,128)(2,1)S(1)} %get-tuple-element.91), channel_id=1, source_target_pairs={{0,4},{4,0},{8,12},{12,8},{16,20},{20,16},{24,28},{28,24},{1,5},{5... | collective-permute-start | bytes 1572872 | tf_op jit(solution)/shard_map/ppermute | solution.py:219
  29.1 4.9 %collective-permute-start.8 = (bf16[512,2048]{1,0:T(8,128)(2,1)S(1)}, bf16[512,2048]{1,0:T(8,128)(2,1)S(1)}, u32[]{:S(2)}, u32[]{:S(2)}) collective-permute-start(bf16[512,2048]{1,0:T(8,128)(2,1)S(1)} %get-tuple-element.99), channel_id=1, source_target_pairs={{0,4},{4,0},{8,12},{12,8},{16,20},{20,16},{24,28},{28,24},{1,5},{5... | collective-permute-start | bytes 6291464 | tf_op jit(solution)/shard_map/ppermute | solution.py:219
  29.1 4.9 %collective-permute-start.7 = (bf16[512,512]{1,0:T(8,128)(2,1)S(1)}, bf16[512,512]{1,0:T(8,128)(2,1)S(1)}, u32[]{:S(2)}, u32[]{:S(2)}) collective-permute-start(bf16[512,512]{1,0:T(8,128)(2,1)S(1)} %get-tuple-element.98), channel_id=1, source_target_pairs={{0,4},{4,0},{8,12},{12,8},{16,20},{20,16},{24,28},{28,24},{1,5},{5... | collective-permute-start | bytes 1572872 | tf_op jit(solution)/shard_map/ppermute | solution.py:219
  29.6 13.8 %collective-permute-start.10 = (bf16[512,512]{1,0:T(8,128)(2,1)S(1)}, bf16[512,512]{1,0:T(8,128)(2,1)S(1)}, u32[]{:S(2)}, u32[]{:S(2)}) collective-permute-start(bf16[512,512]{1,0:T(8,128)(2,1)S(1)} %get-tuple-element.104), channel_id=1, source_target_pairs={{0,16},{4,20},{8,24},{12,28},{16,0},{20,4},{24,8},{28,12},{1,17},{... | collective-permute-start | bytes 1572872 | tf_op jit(solution)/shard_map/ppermute | solution.py:219
  31.1 13.6 %collective-permute-start.9 = (bf16[512,512]{1,0:T(8,128)(2,1)S(1)}, bf16[512,512]{1,0:T(8,128)(2,1)S(1)}, u32[]{:S(2)}, u32[]{:S(2)}) collective-permute-start(bf16[512,512]{1,0:T(8,128)(2,1)S(1)} %get-tuple-element.103), channel_id=1, source_target_pairs={{0,8},{4,12},{8,0},{12,4},{16,24},{20,28},{24,16},{28,20},{1,9},{5... | collective-permute-start | bytes 1572872 | tf_op jit(solution)/shard_map/ppermute | solution.py:219
  34.0 2.9 %copy-start.1 = (bf16[1024,512]{1,0:T(8,128)(2,1)S(1)}, bf16[1024,512]{1,0:T(8,128)(2,1)}, u32[]{:S(2)}) copy-start(bf16[1024,512]{1,0:T(8,128)(2,1)} %refs_9_) | copy-start | bytes 3145732
  44.8 9.3 %collective-permute-start.14 = (bf16[256,512]{1,0:T(8,128)(2,1)S(1)}, bf16[256,512]{1,0:T(8,128)(2,1)S(1)}, u32[]{:S(2)}, u32[]{:S(2)}) collective-permute-start(bf16[256,512]{1,0:T(8,128)(2,1)S(1)} %add_convert_fusion.6), channel_id=1, source_target_pairs={{0,8},{4,12},{8,0},{12,4},{16,24},{20,28},{24,16},{28,20},{1,9},{5... | collective-permute-start | bytes 786440 | tf_op jit(solution)/shard_map/ppermute | solution.py:219
  45.4 9.3 %collective-permute-start.13 = (bf16[256,512]{1,0:T(8,128)(2,1)S(1)}, bf16[256,512]{1,0:T(8,128)(2,1)S(1)}, u32[]{:S(2)}, u32[]{:S(2)}) collective-permute-start(bf16[256,512]{1,0:T(8,128)(2,1)S(1)} %add_convert_fusion.7), channel_id=1, source_target_pairs={{0,16},{4,20},{8,24},{12,28},{16,0},{20,4},{24,8},{28,12},{1,17},{... | collective-permute-start | bytes 786440 | tf_op jit(solution)/shard_map/ppermute | solution.py:219
  45.8 17.3 %collective-permute-start.11 = (bf16[512,512]{1,0:T(8,128)(2,1)S(1)}, bf16[512,512]{1,0:T(8,128)(2,1)S(1)}, u32[]{:S(2)}, u32[]{:S(2)}) collective-permute-start(bf16[512,512]{1,0:T(8,128)(2,1)S(1)} %get-tuple-element.112), channel_id=1, source_target_pairs={{0,8},{4,12},{8,0},{12,4},{16,24},{20,28},{24,16},{28,20},{1,9},{5... | collective-permute-start | bytes 1572872 | tf_op jit(solution)/shard_map/ppermute | solution.py:219
  47.5 16.0 %collective-permute-start.12 = (bf16[512,512]{1,0:T(8,128)(2,1)S(1)}, bf16[512,512]{1,0:T(8,128)(2,1)S(1)}, u32[]{:S(2)}, u32[]{:S(2)}) collective-permute-start(bf16[512,512]{1,0:T(8,128)(2,1)S(1)} %get-tuple-element.113), channel_id=1, source_target_pairs={{0,16},{4,20},{8,24},{12,28},{16,0},{20,4},{24,8},{28,12},{1,17},{... | collective-permute-start | bytes 1572872 | tf_op jit(solution)/shard_map/ppermute | solution.py:219
  55.0 8.5 %collective-permute-start.15 = (bf16[256,512]{1,0:T(8,128)(2,1)S(1)}, bf16[256,512]{1,0:T(8,128)(2,1)S(1)}, u32[]{:S(2)}, u32[]{:S(2)}) collective-permute-start(bf16[256,512]{1,0:T(8,128)(2,1)S(1)} %select_convert_fusion.1), channel_id=1, source_target_pairs={{0,1},{1,0},{2,3},{3,2},{4,5},{5,4},{6,7},{7,6},{8,9},{9,8},{10,11... | collective-permute-start | bytes 786440 | tf_op jit(solution)/shard_map/ppermute | solution.py:258
  63.8 12.4 %collective-permute-start.18 = (bf16[256,512]{1,0:T(8,128)(2,1)S(1)}, bf16[256,512]{1,0:T(8,128)(2,1)S(1)}, u32[]{:S(2)}, u32[]{:S(2)}) collective-permute-start(bf16[256,512]{1,0:T(8,128)(2,1)S(1)} %add_convert_fusion.3), channel_id=1, source_target_pairs={{0,2},{1,3},{2,0},{3,1},{4,6},{5,7},{6,4},{7,5},{8,10},{9,11},{10,... | collective-permute-start | bytes 786440 | tf_op jit(solution)/shard_map/ppermute | solution.py:258
  66.6 9.7 %collective-permute-start.16 = (bf16[256,512]{1,0:T(8,128)(2,1)S(1)}, bf16[256,512]{1,0:T(8,128)(2,1)S(1)}, u32[]{:S(2)}, u32[]{:S(2)}) collective-permute-start(bf16[256,512]{1,0:T(8,128)(2,1)S(1)} %get-tuple-element.117), channel_id=1, source_target_pairs={{0,16},{4,20},{8,24},{12,28},{16,0},{20,4},{24,8},{28,12},{1,17},{... | collective-permute-start | bytes 786440 | tf_op jit(solution)/shard_map/ppermute | solution.py:219
  67.3 9.0 %collective-permute-start.17 = (bf16[256,512]{1,0:T(8,128)(2,1)S(1)}, bf16[256,512]{1,0:T(8,128)(2,1)S(1)}, u32[]{:S(2)}, u32[]{:S(2)}) collective-permute-start(bf16[256,512]{1,0:T(8,128)(2,1)S(1)} %get-tuple-element.118), channel_id=1, source_target_pairs={{0,8},{4,12},{8,0},{12,4},{16,24},{20,28},{24,16},{28,20},{1,9},{5... | collective-permute-start | bytes 786440 | tf_op jit(solution)/shard_map/ppermute | solution.py:219
  76.7 9.5 %collective-permute-start.19 = (bf16[256,512]{1,0:T(8,128)(2,1)S(1)}, bf16[256,512]{1,0:T(8,128)(2,1)S(1)}, u32[]{:S(2)}, u32[]{:S(2)}) collective-permute-start(bf16[256,512]{1,0:T(8,128)(2,1)S(1)} %select_convert_fusion), channel_id=1, source_target_pairs={{0,1},{1,0},{2,3},{3,2},{4,5},{5,4},{6,7},{7,6},{8,9},{9,8},{10,11... | collective-permute-start | bytes 786440 | tf_op jit(solution)/shard_map/ppermute | solution.py:258
  77.9 8.2 %collective-permute-start.20 = (f32[12,128]{1,0:T(8,128)S(1)}, f32[12,128]{1,0:T(8,128)S(1)}, u32[]{:S(2)}, u32[]{:S(2)}) collective-permute-start(f32[12,128]{1,0:T(8,128)S(1)} %maximum_bitcast_fusion), channel_id=1, source_target_pairs={{0,1},{1,0},{2,3},{3,2},{4,5},{5,4},{6,7},{7,6},{8,9},{9,8},{10,11... | collective-permute-start | bytes 18440 | tf_op jit(solution)/shard_map/ppermute | solution.py:258
  79.4 20.1 %collective-permute-start.22 = (bf16[256,512]{1,0:T(8,128)(2,1)S(1)}, bf16[256,512]{1,0:T(8,128)(2,1)S(1)}, u32[]{:S(2)}, u32[]{:S(2)}) collective-permute-start(bf16[256,512]{1,0:T(8,128)(2,1)S(1)} %add_convert_fusion.2), channel_id=1, source_target_pairs={{0,1},{1,0},{2,3},{3,2},{4,5},{5,4},{6,7},{7,6},{8,9},{9,8},{10,11... | collective-permute-start | bytes 786440 | tf_op jit(solution)/shard_map/ppermute | solution.py:258
  80.1 19.5 %collective-permute-start.25 = (bf16[512,512]{1,0:T(8,128)(2,1)S(1)}, bf16[512,512]{1,0:T(8,128)(2,1)S(1)}, u32[]{:S(2)}, u32[]{:S(2)}) collective-permute-start(bf16[512,512]{1,0:T(8,128)(2,1)S(1)} %slice.109), channel_id=1, source_target_pairs={{0,8},{4,12},{8,0},{12,4},{16,24},{20,28},{24,16},{28,20},{1,9},{5... | collective-permute-start | bytes 1572872 | tf_op jit(solution)/shard_map/ppermute | solution.py:219
  81.6 18.0 %collective-permute-start.26 = (bf16[512,512]{1,0:T(8,128)(2,1)S(1)}, bf16[512,512]{1,0:T(8,128)(2,1)S(1)}, u32[]{:S(2)}, u32[]{:S(2)}) collective-permute-start(bf16[512,512]{1,0:T(8,128)(2,1)S(1)} %slice.110), channel_id=1, source_target_pairs={{0,16},{4,20},{8,24},{12,28},{16,0},{20,4},{24,8},{28,12},{1,17},{... | collective-permute-start | bytes 1572872 | tf_op jit(solution)/shard_map/ppermute | solution.py:219
  86.3 13.2 %collective-permute-start.21 = (bf16[256,512]{1,0:T(8,128)(2,1)S(1)}, bf16[256,512]{1,0:T(8,128)(2,1)S(1)}, u32[]{:S(2)}, u32[]{:S(2)}) collective-permute-start(bf16[256,512]{1,0:T(8,128)(2,1)S(1)} %add_convert_fusion.1), channel_id=1, source_target_pairs={{0,2},{1,3},{2,0},{3,1},{4,6},{5,7},{6,4},{7,5},{8,10},{9,11},{10,... | collective-permute-start | bytes 786440 | tf_op jit(solution)/shard_map/ppermute | solution.py:258
  88.3 11.2 %collective-permute-start.23 = (f32[12,128]{1,0:T(8,128)S(1)}, f32[12,128]{1,0:T(8,128)S(1)}, u32[]{:S(2)}, u32[]{:S(2)}) collective-permute-start(f32[12,128]{1,0:T(8,128)S(1)} %fusion), channel_id=1, source_target_pairs={{0,2},{1,3},{2,0},{3,1},{4,6},{5,7},{6,4},{7,5},{8,10},{9,11},{10,... | collective-permute-start | bytes 18440 | tf_op jit(solution)/shard_map/ppermute | solution.py:258
  99.5 1.9 %collective-permute-start.28 = (f32[12,128]{1,0:T(8,128)S(1)}, f32[12,128]{1,0:T(8,128)S(1)}, u32[]{:S(2)}, u32[]{:S(2)}) collective-permute-start(f32[12,128]{1,0:T(8,128)S(1)} %add.88), channel_id=1, source_target_pairs={{0,4},{4,0},{8,12},{12,8},{16,20},{20,16},{24,28},{28,24},{1,5},{5... | collective-permute-start | bytes 18440 | tf_op jit(solution)/shard_map/ppermute | solution.py:219
  100.9 8.2 %copy-start.4 = (f32[512]{0:T(512)S(1)}, f32[512]{0:T(512)}, u32[]{:S(2)}) copy-start(f32[512]{0:T(512)} %param.11) | copy-start | bytes 6148
  100.9 8.2 %collective-permute-start.27 = (f32[512,512]{1,0:T(8,128)S(1)}, f32[512,512]{1,0:T(8,128)S(1)}, u32[]{:S(2)}, u32[]{:S(2)}) collective-permute-start(f32[512,512]{1,0:T(8,128)S(1)} %get-tuple-element.132), channel_id=1, source_target_pairs={{0,4},{4,0},{8,12},{12,8},{16,20},{20,16},{24,28},{28,24},{1,5},{5... | collective-permute-start | bytes 3145736 | tf_op jit(solution)/shard_map/ppermute | solution.py:219
  101.5 3.8 %collective-permute-start.29 = (f32[20,128]{1,0:T(8,128)S(1)}, f32[20,128]{1,0:T(8,128)S(1)}, u32[]{:S(2)}, u32[]{:S(2)}) collective-permute-start(f32[20,128]{1,0:T(8,128)S(1)} %pad_maximum_fusion.3), channel_id=1, source_target_pairs={{0,8},{4,12},{8,0},{12,4},{16,24},{20,28},{24,16},{28,20},{1,9},{5... | collective-permute-start | bytes 30728 | tf_op jit(solution)/shard_map/ppermute | solution.py:219
  105.2 3.8 %collective-permute-start.30 = (f32[36,128]{1,0:T(8,128)S(1)}, f32[36,128]{1,0:T(8,128)S(1)}, u32[]{:S(2)}, u32[]{:S(2)}) collective-permute-start(f32[36,128]{1,0:T(8,128)S(1)} %pad_maximum_fusion.1), channel_id=1, source_target_pairs={{0,16},{4,20},{8,24},{12,28},{16,0},{20,4},{24,8},{28,12},{1,17},{... | collective-permute-start | bytes 55304 | tf_op jit(solution)/shard_map/ppermute | solution.py:219
  106.3 6.9 %collective-permute-start.24 = (bf16[256,512]{1,0:T(8,128)(2,1)S(1)}, bf16[256,512]{1,0:T(8,128)(2,1)S(1)}, u32[]{:S(2)}, u32[]{:S(2)}) collective-permute-start(bf16[256,512]{1,0:T(8,128)(2,1)S(1)} %add_convert_fusion), channel_id=1, source_target_pairs={{0,1},{1,0},{2,3},{3,2},{4,5},{5,4},{6,7},{7,6},{8,9},{9,8},{10,11... | collective-permute-start | bytes 786440 | tf_op jit(solution)/shard_map/ppermute | solution.py:258

commit v5 on v4

--- a/solution.py
+++ b/solution.py
@@ -1,8 +1,8 @@
 import functools
+import math
 
 import jax
 import jax.numpy as jnp
-import numpy as np
 from jax import lax
 from jax.experimental import pallas as pl
 from jax.experimental.pallas import tpu as pltpu
@@ -58,7 +58,7 @@
     return v * cosine + pltpu.roll(v, HEAD // 2, 1) * sine
 
 
-def prepare_body(per_batch, at_ref, x_ref, gain_ref, seg_ref, inv_ref, cot_ref, *outs):
+def prepare_body(per_batch, at_ref, x_ref, gain_ref, seg_ref, cot_ref, *outs):
     step, wide = x_ref.shape
     part = wide // 8
     half = part // 2
@@ -70,7 +70,8 @@
     inv = lax.rsqrt(total * (1.0 / wide) + 1e-06)
     me = at_ref[0]
     mine, sib, rest = outs[:8], outs[8:12], outs[12]
-    cos_ref, sin_ref, dproj_ref = outs[13:]
+    cos_ref, sin_ref, dproj_ref, own_gain_ref = outs[13:]
+    own_gain_ref[...] = gain_ref[:, pl.ds(pl.multiple_of(me * part, part), part)]
     places = {3: 0, 1: 1, 2: 2, 7: 3}
     for o in range(8):
         start = pl.multiple_of((me ^ o) * part, part)
@@ -96,10 +97,14 @@
     position = jnp.sum(
         jnp.where((own == segs) & (col < row), 1, 0), axis=1, keepdims=True
     )
-    angle = position.astype(F32) * inv_ref[...]
-    cosine, sine = jnp.cos(angle), jnp.sin(angle)
-    second = lax.broadcasted_iota(jnp.int32, sine.shape, 1) >= HEAD // 2
-    sine = jnp.where(second, -sine, sine)
+    lane = lax.broadcasted_iota(jnp.int32, (1, HEAD), 1)
+    second = lane >= HEAD // 2
+    freq = (lane % (HEAD // 2)).astype(F32)
+    angle = position.astype(F32) * jnp.exp(freq * (-2.0 * math.log(1000000.0) / HEAD))
+    pair = jnp.cos(angle - jnp.where(second, math.pi / 2, 0.0).astype(F32))
+    swapped = pltpu.roll(pair, HEAD // 2, 1)
+    cosine = jnp.where(second, swapped, pair)
+    sine = jnp.where(second, -pair, swapped)
     cos_ref[...] = cosine
     sin_ref[...] = sine
     for h in range(KVH):
@@ -112,35 +117,41 @@
     step = 64
     half = wide // 16
     outs = [(half, BF16)] * 12 + [(4 * half, BF16), (HEAD, F32), (HEAD, F32), (KW, BF16)]
-    freq = np.arange(HEAD) % (HEAD // 2) * (2.0 / HEAD)
-    inv = jnp.asarray(np.power(1000000.0, -freq)[None, :], F32)
-
     def whole(v):
         return pl.BlockSpec(v.shape, lambda r, at: (0, 0))
 
     def some(n):
         return pl.BlockSpec((step, n), lambda r, at: (r, 0))
 
-    gain = gain[None, :]
+    gain, segs, cotangent = (
+        pltpu.with_memory_space_constraint(v, pltpu.HBM) for v in (gain[None, :], segs, cotangent)
+    )
     return pl.pallas_call(
         functools.partial(prepare_body, segs.shape[1] // step),
         grid_spec=pltpu.PrefetchScalarGridSpec(
             num_scalar_prefetch=1,
             grid=(rows // step,),
-            in_specs=[some(wide), whole(gain), whole(segs), whole(inv), some(KW)],
-            out_specs=[some(n) for n, _ in outs],
+            in_specs=[some(wide), whole(gain), whole(segs), some(KW)],
+            out_specs=[
+                *(some(n) for n, _ in outs),
+                pl.BlockSpec((1, 2 * half), lambda r, at: (0, 0)),
+            ],
         ),
-        out_shape=[jax.ShapeDtypeStruct((rows, n), t) for n, t in outs],
+        out_shape=[
+            *(jax.ShapeDtypeStruct((rows, n), t) for n, t in outs),
+            jax.ShapeDtypeStruct((1, 2 * half), F32),
+        ],
         cost_estimate=pl.CostEstimate(flops=1, bytes_accessed=1, transcendentals=0),
         compiler_params=pltpu.CompilerParams(vmem_limit_bytes=14 * 1024 * 1024),
         name="prepare",
-    )(at, x, gain, segs, inv, cotangent)
-
-
-def keys_body(here, there, bias, cos_ref, sin_ref, out_ref):
+    )(at, x, gain, segs, cotangent)
+
+
+def keys_body(here, upper, lower, bias, cos_ref, sin_ref, out_ref):
     for h in range(KVH):
         cols = slice(h * HEAD, (h + 1) * HEAD)
-        v = here[:, cols] + there[:, cols] + bias[:, cols]
+        there = jnp.concatenate([upper[:, cols], lower[:, cols]], axis=0).astype(F32)
+        v = here[:, cols] + there + bias[:, cols]
         out_ref[:, cols] = turn(v, cos_ref[...], -sin_ref[...]).astype(BF16)
 
 
@@ -179,31 +190,34 @@
             own_b[...] = rows
 
 
-def forward_body(weights_of, *refs):
-    places, n_acts, n_init = weights_of
-    acts, init, weights, outs = (
-        refs[:n_acts],
-        refs[n_acts : n_acts + n_init],
-        refs[n_acts + n_init : -2],
-        refs[-2:],
-    )
-    for side, out in enumerate(outs):
-        total = init[side][...] if n_init else None
-        for mine, sib, col, w, row in places:
-            half = acts[0].shape[1]
+def forward_body(places, n_acts, n_init, *refs):
+    acts, init, refs = refs[:n_acts], refs[n_acts : n_acts + n_init], refs[n_acts + n_init :]
+    half = acts[0].shape[1]
+    n_outs = 3 if n_init else 2
+    weights, outs = refs[:-n_outs], refs[-n_outs:]
+    totals = [v[...] for v in init] if n_init else [None, None]
+    for side in (1, 0):
+        total = totals[side]
+        for mine, sib, col, pieces in places:
+            w = jnp.concatenate([weights[n][at : at + rows] for n, at, rows in pieces], axis=0)
             rows = acts[sib][:, col * half : (col + 1) * half] if side else acts[mine][...]
-            add = jnp.dot(
-                rows, weights[w][row * half : (row + 1) * half], preferred_element_type=F32
-            )
+            add = jnp.dot(rows, w, preferred_element_type=F32)
             total = add if total is None else total + add
-        out[...] = total
+        if side and n_init:
+            n = outs[1].shape[0]
+            outs[1][...] = total[:n].astype(BF16)
+            outs[2][...] = total[n:].astype(BF16)
+        else:
+            outs[side][...] = total
 
 
 def forward(acts, places, weights, init=()):
     tok, kw = acts[0].shape[0], weights[0].shape[1]
+    shape = jax.ShapeDtypeStruct((tok, kw), F32)
+    part = jax.ShapeDtypeStruct((tok // 2, kw), BF16)
     return call(
-        functools.partial(forward_body, (places, len(acts), len(init))),
-        [jax.ShapeDtypeStruct((tok, kw), F32)] * 2,
+        functools.partial(forward_body, places, len(acts), len(init)),
+        [shape, part, part] if init else [shape, shape],
         "forward",
     )(*acts, *init, *weights)
 
@@ -225,16 +239,18 @@
 
     odd = (lax.axis_index("dp") & 1) == 1
     firsts = [(me & bit) == 0 for bit in (1, 2, 4)]
-    my_gain = lax.dynamic_slice(norm_gain, (me * own,), (own,))
     at = me.reshape(1).astype(jnp.int32)
-    odd, firsts, my_gain, at, key_weight, hidden_in, key_cotangent, segment_ids = after(
-        (odd, firsts, my_gain, at, key_weight, hidden_in, key_cotangent, segment_ids)
-    )
-    w_x, w_y = px(key_weight), py(key_weight)
+    odd, firsts, at, key_weight, hidden_in, key_cotangent, segment_ids = after(
+        (odd, firsts, at, key_weight, hidden_in, key_cotangent, segment_ids)
+    )
+    early = half + own * 5 // 16
+    late = own - early
+    w_x, w_y = px(key_weight[late:]), py(key_weight[:early])
 
     parts = prepared(hidden_in, norm_gain, segment_ids, key_cotangent, at)
     mine_a, mine_b, (s_a3, s_a1, s_a2, s_b3, rest) = parts[:4], parts[4:8], parts[8:13]
-    cosine, sine, dproj = parts[13:]
+    cosine, sine, dproj, my_gain = parts[13:]
+    my_gain = my_gain.reshape(own)
     n = tok // 2
     dproj_sib = core(dproj[:n]), core(dproj[n:])
     s_a3, s_a1, s_a2 = core(s_a3), core(s_a1), core(s_a2)
@@ -282,16 +298,14 @@
         second_grad_body, [own_shape, own_shape, *part_shapes(quarter)], "grad_b"
     )(mine_a[0], *mine_b, s_b3, rest, dproj, *dproj_sib)
 
-    acts = (*mine_a[:3], *mine_b[:3], s_a1, s_a2, rest)
+    acts = (mine_a[0], mine_b[0], mine_a[2], mine_b[1], s_a2, rest)
     places = (
-        (0, 8, 0, 0, 0),
-        (3, 8, 1, 0, 1),
-        (1, 6, 0, 1, 0),
-        (4, 8, 2, 1, 1),
-        (2, 7, 0, 2, 0),
-        (5, 8, 3, 2, 1),
-    )
-    here = forward(acts, places, (after(key_weight, part_b), w_x, w_y))
+        (0, 5, 0, ((0, 0, half),)),
+        (1, 5, 1, ((0, half, half),)),
+        (2, 4, 0, ((1, 0, half),)),
+        (3, 5, 2, ((2, early - half, half),)),
+    )
+    here = forward(acts, places, (after(key_weight, part_b), w_y, w_x))
 
     in_a = after(in_a, here)
     to_b = after((part_b[0], part_b[1]), in_a)
@@ -304,8 +318,9 @@
     in_b = after(in_b, two_a)
     more = after(add_up(part_b, *in_b), pair_a)
     two_b = py(more[0]), px(more[1])
-    later = after((w_y[:half], w_x[half:]), two_b)
-    wd_low, wd_high = px(later[0]), py(later[1])
+    w_y, w_x, key_weight = after((w_y, w_x, key_weight), two_b)
+    more_wx = px(jnp.concatenate([key_weight[:late], w_y[:half]], axis=0))
+    more_wy = py(jnp.concatenate([key_weight[early:], w_x[early - half :]], axis=0))
     total_a = total_of(pair_a, over_z(2)(pair_a))
     got_a = over_z(1)(total_a)
     local_b = after(own_rows(own_b, in_b, two_b), total_a)
@@ -324,27 +339,37 @@
     into_b, small = after((into_b, small))
     pair_b = pair_sum(*local_b, into_b)
     small = small + over_z(2)(small)
-    other_b, got_a, small = after((over_z(2)(pair_b), got_a, small))
+    acts = (mine_a[3], mine_b[3], mine_a[1], mine_b[2], s_a3, s_b3, s_a1, rest)
+    places = (
+        (0, 4, 0, ((0, late, half),)),
+        (1, 5, 0, ((1, late, half),)),
+        (2, 6, 0, ((0, 0, late), (3, 0, half - late))),
+        (3, 7, 3, ((2, half, early - half), (1, 0, late))),
+    )
+    more_wx, more_wy = after((more_wx, more_wy), pair_b)
+    forwarded = forward(acts, places, (more_wx, more_wy, w_y, w_x), here)
+    other_b, got_a, small, forwarded = after((over_z(2)(pair_b), got_a, small, forwarded))
     total_b = total_of(pair_b, other_b)
     got_b = over_z(1)(total_b)
 
-    acts = after((mine_a[3], mine_b[3], s_a3, s_b3), pair_b)
-    here, there = forward(acts, ((0, 2, 0, 0, 0), (1, 3, 0, 1, 0)), (wd_low, wd_high), here)
+    here, *there = forwarded
     keys = call(keys_body, jax.ShapeDtypeStruct((tok, kw), BF16), "keys")(
-        here, core(there), key_bias[None, :], cosine, sine
-    )
+        here, *(core(v) for v in there), key_bias[None, :], cosine, sine
+    )
+
+    def ordered(first, one, two):
+        return jnp.concatenate([jnp.where(first, one, two), jnp.where(first, two, one)], axis=0)
 
     gains, bias = small[:n_own], small[n_own:]
+    gains = ordered(firsts[0], gains, core(gains))
+    packed = jnp.concatenate([gains, bias], axis=0)
+    n = gains.shape[0]
+    got_x, got_y, got_xy = px(packed), py(packed), over(6)(packed)
+    same = ordered(firsts[1], gains, got_x[:n])
+    gains = ordered(firsts[2], same, ordered(firsts[1], got_y[:n], got_xy[:n]))
+    bias = (bias + got_x[n:]) + (got_y[n:] + got_xy[n:])
+
     scale = 1.0 / jnp.sqrt(F32(tok * 32))
-    for bit, first in zip((1, 2, 4), firsts, strict=True):
-        got = over(bit)(jnp.concatenate([gains, bias], axis=0))
-        size = gains.shape[0]
-        theirs = got[:size]
-        gains = jnp.concatenate(
-            [jnp.where(first, gains, theirs), jnp.where(first, theirs, gains)], axis=0
-        )
-        if bit > 1:
-            bias = bias + got[size:]
     got_b, keys, gains, bias = after((got_b, keys, gains, bias))
     grad = jnp.concatenate([*both(total_a, got_a), *both(total_b, got_b)], axis=0)
     return (keys, grad * scale, bias.reshape(-1) * scale, gains.reshape(-1) * scale)

time: 116 us -> 109 us (0.940)
  waiting for transfers between devices: 56.4 us -> 50.7 us
  local copies, waits for them, and re-layouts: 7.33 us -> 5.1 us
    ppermute x8, waiting for transfers between devices: 24.3 us -> 17.3 us  [over_z(): return lambda v: lax.ppermute(v, 'dp', [(i, i ^ bit) for i in range(4)])]
    unnamed x14 -> x10, local copies, waits for them, and re-layouts: 6.53 us -> 3.4 us
    ppermute x23 -> x25, starting transfers between devices: 19.6 us -> 17.7 us  [over(): return lambda v: lax.ppermute(v, 'blk', [(i, i ^ bit) for i in range(8)])]
    slice x2 -> x5, local copies, waits for them, and re-layouts: 0.07 us -> 1.65 us  [the longest x1 1.59 us: by_permutes(): w_x, w_y = (px(key_weight[late:]), py(key_weight[:early]))]
    ppermute x8, starting transfers between devices: 10.2 us -> 11.5 us  [over_z(): return lambda v: lax.ppermute(v, 'dp', [(i, i ^ bit) for i in range(4)])]
    ppermute x23 -> x25, waiting for transfers between devices: 32.1 us -> 33.3 us  [over(): return lambda v: lax.ppermute(v, 'blk', [(i, i ^ bit) for i in range(8)])]
  transfers between devices with their start and end apart: 31 -> 33, of which waited for: 20 -> 25; matrix products, arithmetic and copies ran while one was open for 1% -> 2% of each run, Pallas kernels for 14% -> 16%
where the time goes in v5:
time: 109 us; the launch traced here: 108 us
  waiting for transfers between devices  50.7 us (47%)
  starting transfers between devices  29.1 us (27%)
  Pallas kernels  17.2 us (16%)
  other arithmetic  5.17 us (5%)
  local copies, waits for them, and re-layouts  5.1 us (5%)
    ppermute x25, waiting for transfers between devices, over(): return lambda v: lax.ppermute(v, 'blk', [(i, i ^ bit) for i in range(8)])  33.3 us
    ppermute x25, starting transfers between devices, over(): return lambda v: lax.ppermute(v, 'blk', [(i, i ^ bit) for i in range(8)])  17.7 us
    ppermute x8, waiting for transfers between devices, over_z(): return lambda v: lax.ppermute(v, 'dp', [(i, i ^ bit) for i in range(4)])  17.3 us
    ppermute x8, starting transfers between devices, over_z(): return lambda v: lax.ppermute(v, 'dp', [(i, i ^ bit) for i in range(4)])  11.5 us
    pallas_call x1, Pallas kernels, prepared(): pl.pallas_call(functools.partial(prepare_body, segs.shape[1] // step), gr...  6.62 us
    pallas_call x2, Pallas kernels, forward(): call(functools.partial(forward_body, places, len(acts), len(init)), [shap...  4.67 us
    unnamed x10, local copies, waits for them, and re-layouts  3.4 us
    pallas_call x1, Pallas kernels, by_permutes(): call(second_grad_body, [own_shape, own_shape, *part_shapes(quarter)], 'gr...  2.91 us
  transfers between devices with their start and end apart: 33, of which 25 were waited for; matrix products, arithmetic and copies ran while one was open for 2% of the time, Pallas kernels for 16%

profile of v5, /device:TPU:0, one launch (start us, length us, event | category | flops | bytes accessed | tf_op | source)
XLA Modules:
  0.0 108.3 jit_solution(12902153774684095253)
XLA Ops:
  0.6 1.6 %fusion.5 = (bf16[832,512]{1,0:T(8,128)(2,1)S(1)}, bf16[832,512]{1,0:T(8,128)(2,1)S(1)}) fusion(bf16[1024,512]{1,0:T(8,128)(2,1)} %refs_6_), kind=kLoop, calls=%fused_computation.51 | loop fusion | bytes 3407872 | tf_op jit(solution)/shard_map/slice | solution.py:248
  2.2 3.0 %collective-permute-start.6 = (bf16[832,512]{1,0:T(8,128)(2,1)S(1)}, bf16[832,512]{1,0:T(8,128)(2,1)S(1)}, u32[]{:S(2)}, u32[]{:S(2)}) collective-permute-start(bf16[832,512]{1,0:T(8,128)(2,1)S(1)} %get-tuple-element.158), channel_id=1, source_target_pairs={{0,16},{4,20},{8,24},{12,28},{16,0},{20,4},{24,8},{28,12},{1,17},{... | collective-permute-start | bytes 2555912 | tf_op jit(solution)/shard_map/ppermute | solution.py:233
  5.3 1.5 %collective-permute-start.5 = (bf16[832,512]{1,0:T(8,128)(2,1)S(1)}, bf16[832,512]{1,0:T(8,128)(2,1)S(1)}, u32[]{:S(2)}, u32[]{:S(2)}) collective-permute-start(bf16[832,512]{1,0:T(8,128)(2,1)S(1)} %get-tuple-element.159), channel_id=1, source_target_pairs={{0,8},{4,12},{8,0},{12,4},{16,24},{20,28},{24,16},{28,20},{1,9},{5... | collective-permute-start | bytes 2555912 | tf_op jit(solution)/shard_map/ppermute | solution.py:233
  6.8 3.4 %copy-done.1 = bf16[512,8192]{1,0:T(8,128)(2,1)S(1)} copy-done((bf16[512,8192]{1,0:T(8,128)(2,1)S(1)}, bf16[512,8192]{1,0:T(8,128)(2,1)}, u32[]{:S(2)}) %copy-start.1) | copy-done | bytes 8388632
  10.1 6.6 %prepare.1 = (bf16[512,512]{1,0:T(8,128)(2,1)S(1)}, bf16[512,512]{1,0:T(8,128)(2,1)S(1)}, bf16[512,512]{1,0:T(8,128)(2,1)S(1)}, bf16[512,512]{1,0:T(8,128)(2,1)S...) custom-call(s32[1]{0:T(128)} %bitcast.at_ref, ...), custom_call_target="tpu_custom_call" | custom-call | flops 1 | bytes 1 | tf_op jit(solution)/shard_map/prepare/pallas_call | solution.py:129
  17.5 0.9 collective-permute-done.4.lower
  18.9 0.6 collective-permute-done.s1.refs_6_
  19.5 0.8 collective-permute-done.1.s2.refs_4_
  20.3 0.7 collective-permute-done.2.s3.refs_4_
  21.1 1.8 %grad_a.1 = (bf16[512,512]{1,0:T(8,128)(2,1)S(1)}, bf16[512,512]{1,0:T(8,128)(2,1)S(1)}, bf16[256,512]{1,0:T(8,128)(2,1)S(1)}, bf16[256,512]{1,0:T(8,128)(2,1)S(1)}) custom-call(bf16[512,512]{1,0:T(8,128)(2,1)S(1)} %get-tuple-element.89.m1.refs_2_, bf16[512,512]{1,0:T(8,128)(2,1)S(1)} %get-tuple-element.90.m2.refs_2_, ...), custom_call_target="tpu_custom_call" | custom-call | flops 1 | bytes 1 | tf_op jit(solution)/shard_map/grad_a/pallas_call | solution.py:289
  22.9 1.3 %collective-permute-done.6.refs_7_.refs_12_ = bf16[832,512]{1,0:T(8,128)(2,1)S(1)} collective-permute-done((bf16[832,512]{1,0:T(8,128)(2,1)S(1)}, bf16[832,512]{1,0:T(8,128)(2,1)S(1)}, u32[]{:S(2)}, u32[]{:S(2)}) %collective-permute-start.6) | collective-permute-done | bytes 852000 | tf_op jit(solution)/shard_map/ppermute | solution.py:233
  24.2 1.5 %collective-permute-done.5.refs_8_.refs_13_ = bf16[832,512]{1,0:T(8,128)(2,1)S(1)} collective-permute-done((bf16[832,512]{1,0:T(8,128)(2,1)S(1)}, bf16[832,512]{1,0:T(8,128)(2,1)S(1)}, u32[]{:S(2)}, u32[]{:S(2)}) %collective-permute-start.5) | collective-permute-done | bytes 852000 | tf_op jit(solution)/shard_map/ppermute | solution.py:233
  26.2 1.5 %collective-permute-start.9 = (bf16[512,512]{1,0:T(8,128)(2,1)S(1)}, bf16[512,512]{1,0:T(8,128)(2,1)S(1)}, u32[]{:S(2)}, u32[]{:S(2)}) collective-permute-start(bf16[512,512]{1,0:T(8,128)(2,1)S(1)} %get-tuple-element.106), channel_id=1, source_target_pairs={{0,8},{4,12},{8,0},{12,4},{16,24},{20,28},{24,16},{28,20},{1,9},{5... | collective-permute-start | bytes 1572872 | tf_op jit(solution)/shard_map/ppermute | solution.py:233
  28.2 2.4 %collective-permute-done.7.s3.refs_5_ = bf16[512,512]{1,0:T(8,128)(2,1)S(1)} collective-permute-done((bf16[512,512]{1,0:T(8,128)(2,1)S(1)}, bf16[512,512]{1,0:T(8,128)(2,1)S(1)}, u32[]{:S(2)}, u32[]{:S(2)}) %collective-permute-start.7) | collective-permute-done | bytes 524320 | tf_op jit(solution)/shard_map/ppermute | solution.py:233
  30.6 2.9 %grad_b.1 = (f32[512,512]{1,0:T(8,128)S(1)}, f32[512,512]{1,0:T(8,128)S(1)}, bf16[512,512]{1,0:T(8,128)(2,1)S(1)}, bf16[512,512]{1,0:T(8,128)(2,1)S(1)}, bf16[25...) custom-call(bf16[512,512]{1,0:T(8,128)(2,1)S(1)} %get-tuple-element.82.m_a0.refs_0_, ...), custom_call_target="tpu_custom_call" | custom-call | flops 1 | bytes 1 | tf_op jit(solution)/shard_map/grad_b/pallas_call | solution.py:297
  33.5 2.3 %forward.2 = (f32[512,512]{1,0:T(8,128)S(1)}, f32[512,512]{1,0:T(8,128)S(1)}) custom-call(bf16[512,512]{1,0:T(8,128)(2,1)S(1)} %get-tuple-element.82.m_a0.refs_0_, bf16[512,512]{1,0:T(8,128)(2,1)S(1)} %get-tuple-element.83.m0.refs_1_, bf16[512,512]{1,0:T(8,128)(2,1)S(1)} %get-tuple-element.90.m2.refs_2_, bf16[512,512]{1,0:T(8,128)(2,1)S(1)} %get-tuple-element.84.m1.refs_3_, ...), custom_call_target="tpu_custom_call" | custom-call | flops 1 | bytes 1 | tf_op jit(solution)/shard_map/forward/pallas_call | solution.py:218
  35.8 4.2 %collective-permute-done.9 = bf16[512,512]{1,0:T(8,128)(2,1)S(1)} collective-permute-done((bf16[512,512]{1,0:T(8,128)(2,1)S(1)}, bf16[512,512]{1,0:T(8,128)(2,1)S(1)}, u32[]{:S(2)}, u32[]{:S(2)}) %collective-permute-start.9) | collective-permute-done | bytes 524320 | tf_op jit(solution)/shard_map/ppermute | solution.py:233
  40.0 1.2 %collective-permute-done.10 = bf16[512,512]{1,0:T(8,128)(2,1)S(1)} collective-permute-done((bf16[512,512]{1,0:T(8,128)(2,1)S(1)}, bf16[512,512]{1,0:T(8,128)(2,1)S(1)}, u32[]{:S(2)}, u32[]{:S(2)}) %collective-permute-start.10) | collective-permute-done | bytes 524320 | tf_op jit(solution)/shard_map/ppermute | solution.py:233
  41.4 0.6 collective-permute-start.14
  42.3 6.1 %collective-permute-done.14 = bf16[256,512]{1,0:T(8,128)(2,1)S(1)} collective-permute-done((bf16[256,512]{1,0:T(8,128)(2,1)S(1)}, bf16[256,512]{1,0:T(8,128)(2,1)S(1)}, u32[]{:S(2)}, u32[]{:S(2)}) %collective-permute-start.14) | collective-permute-done | bytes 262176 | tf_op jit(solution)/shard_map/ppermute | solution.py:233
  49.1 1.6 %collective-permute-start.15 = (bf16[256,512]{1,0:T(8,128)(2,1)S(1)}, bf16[256,512]{1,0:T(8,128)(2,1)S(1)}, u32[]{:S(2)}, u32[]{:S(2)}) collective-permute-start(bf16[256,512]{1,0:T(8,128)(2,1)S(1)} %select_convert_fusion.1), channel_id=1, source_target_pairs={{0,1},{1,0},{2,3},{3,2},{4,5},{5,4},{6,7},{7,6},{8,9},{9,8},{10,11... | collective-permute-start | bytes 786440 | tf_op jit(solution)/shard_map/ppermute | solution.py:274
  50.8 1.5 %collective-permute-start.11 = (bf16[512,512]{1,0:T(8,128)(2,1)S(1)}, bf16[512,512]{1,0:T(8,128)(2,1)S(1)}, u32[]{:S(2)}, u32[]{:S(2)}) collective-permute-start(bf16[512,512]{1,0:T(8,128)(2,1)S(1)} %get-tuple-element.115), channel_id=1, source_target_pairs={{0,8},{4,12},{8,0},{12,4},{16,24},{20,28},{24,16},{28,20},{1,9},{5... | collective-permute-start | bytes 1572872 | tf_op jit(solution)/shard_map/ppermute | solution.py:233
  52.9 2.6 %collective-permute-done.15 = bf16[256,512]{1,0:T(8,128)(2,1)S(1)} collective-permute-done((bf16[256,512]{1,0:T(8,128)(2,1)S(1)}, bf16[256,512]{1,0:T(8,128)(2,1)S(1)}, u32[]{:S(2)}, u32[]{:S(2)}) %collective-permute-start.15) | collective-permute-done | bytes 262176 | tf_op jit(solution)/shard_map/ppermute | solution.py:274
  55.8 3.2 %collective-permute-start.18 = (bf16[256,512]{1,0:T(8,128)(2,1)S(1)}, bf16[256,512]{1,0:T(8,128)(2,1)S(1)}, u32[]{:S(2)}, u32[]{:S(2)}) collective-permute-start(bf16[256,512]{1,0:T(8,128)(2,1)S(1)} %add_convert_fusion.3), channel_id=1, source_target_pairs={{0,2},{1,3},{2,0},{3,1},{4,6},{5,7},{6,4},{7,5},{8,10},{9,11},{10,... | collective-permute-start | bytes 786440 | tf_op jit(solution)/shard_map/ppermute | solution.py:274
  59.0 3.1 %collective-permute-done.11 = bf16[512,512]{1,0:T(8,128)(2,1)S(1)} collective-permute-done((bf16[512,512]{1,0:T(8,128)(2,1)S(1)}, bf16[512,512]{1,0:T(8,128)(2,1)S(1)}, u32[]{:S(2)}, u32[]{:S(2)}) %collective-permute-start.11) | collective-permute-done | bytes 524320 | tf_op jit(solution)/shard_map/ppermute | solution.py:233
  62.1 2.1 %collective-permute-done.12 = bf16[512,512]{1,0:T(8,128)(2,1)S(1)} collective-permute-done((bf16[512,512]{1,0:T(8,128)(2,1)S(1)}, bf16[512,512]{1,0:T(8,128)(2,1)S(1)}, u32[]{:S(2)}, u32[]{:S(2)}) %collective-permute-start.12) | collective-permute-done | bytes 524320 | tf_op jit(solution)/shard_map/ppermute | solution.py:233
  64.9 0.6 collective-permute-start.17
  65.5 1.6 %collective-permute-done.18 = bf16[256,512]{1,0:T(8,128)(2,1)S(1)} collective-permute-done((bf16[256,512]{1,0:T(8,128)(2,1)S(1)}, bf16[256,512]{1,0:T(8,128)(2,1)S(1)}, u32[]{:S(2)}, u32[]{:S(2)}) %collective-permute-start.18) | collective-permute-done | bytes 262176 | tf_op jit(solution)/shard_map/ppermute | solution.py:274
  67.2 0.7 collective-permute-start.22
  67.9 2.8 %collective-permute-done.16 = bf16[256,512]{1,0:T(8,128)(2,1)S(1)} collective-permute-done((bf16[256,512]{1,0:T(8,128)(2,1)S(1)}, bf16[256,512]{1,0:T(8,128)(2,1)S(1)}, u32[]{:S(2)}, u32[]{:S(2)}) %collective-permute-start.16) | collective-permute-done | bytes 262176 | tf_op jit(solution)/shard_map/ppermute | solution.py:233
  72.6 1.6 %collective-permute-start.19 = (bf16[256,512]{1,0:T(8,128)(2,1)S(1)}, bf16[256,512]{1,0:T(8,128)(2,1)S(1)}, u32[]{:S(2)}, u32[]{:S(2)}) collective-permute-start(bf16[256,512]{1,0:T(8,128)(2,1)S(1)} %select_convert_fusion), channel_id=1, source_target_pairs={{0,1},{1,0},{2,3},{3,2},{4,5},{5,4},{6,7},{7,6},{8,9},{9,8},{10,11... | collective-permute-start | bytes 786440 | tf_op jit(solution)/shard_map/ppermute | solution.py:274
  74.3 1.6 %collective-permute-start.25 = (bf16[704,512]{1,0:T(8,128)(2,1)S(1)}, bf16[704,512]{1,0:T(8,128)(2,1)S(1)}, u32[]{:S(2)}, u32[]{:S(2)}) collective-permute-start(bf16[704,512]{1,0:T(8,128)(2,1)S(1)} %pad_maximum_fusion.1), channel_id=1, source_target_pairs={{0,16},{4,20},{8,24},{12,28},{16,0},{20,4},{24,8},{28,12},{1,17},{... | collective-permute-start | bytes 2162696 | tf_op jit(solution)/shard_map/ppermute | solution.py:233
  76.0 0.7 collective-permute-start.24
  76.7 2.8 %collective-permute-done.19 = bf16[256,512]{1,0:T(8,128)(2,1)S(1)} collective-permute-done((bf16[256,512]{1,0:T(8,128)(2,1)S(1)}, bf16[256,512]{1,0:T(8,128)(2,1)S(1)}, u32[]{:S(2)}, u32[]{:S(2)}) %collective-permute-start.19) | collective-permute-done | bytes 262176 | tf_op jit(solution)/shard_map/ppermute | solution.py:274
  79.6 2.5 %collective-permute-start.21 = (bf16[256,512]{1,0:T(8,128)(2,1)S(1)}, bf16[256,512]{1,0:T(8,128)(2,1)S(1)}, u32[]{:S(2)}, u32[]{:S(2)}) collective-permute-start(bf16[256,512]{1,0:T(8,128)(2,1)S(1)} %add_convert_fusion.1), channel_id=1, source_target_pairs={{0,2},{1,3},{2,0},{3,1},{4,6},{5,7},{6,4},{7,5},{8,10},{9,11},{10,... | collective-permute-start | bytes 786440 | tf_op jit(solution)/shard_map/ppermute | solution.py:274
  82.6 9.5 %collective-permute-done.23 = f32[12,128]{1,0:T(8,128)S(1)} collective-permute-done((f32[12,128]{1,0:T(8,128)S(1)}, f32[12,128]{1,0:T(8,128)S(1)}, u32[]{:S(2)}, u32[]{:S(2)}) %collective-permute-start.23) | collective-permute-done | bytes 6176 | tf_op jit(solution)/shard_map/ppermute | solution.py:274
  92.1 2.3 %forward.3 = (f32[512,512]{1,0:T(8,128)S(1)}, bf16[256,512]{1,0:T(8,128)(2,1)S(1)}, bf16[256,512]{1,0:T(8,128)(2,1)S(1)}) custom-call(bf16[512,512]{1,0:T(8,128)(2,1)S(1)} %get-tuple-element.91.m3.refs_0_, bf16[512,512]{1,0:T(8,128)(2,1)S(1)} %get-tuple-element.86.m3.refs_1_, bf16[512,512]{1,0:T(8,128)(2,1)S(1)} %get-tuple-element.89.m1.refs_2_, ...), custom_call_target="tpu_custom_call" | custom-call | flops 1 | bytes 1 | tf_op jit(solution)/shard_map/forward/pallas_call | solution.py:218
  94.6 1.1 %collective-permute-done.29 = f32[8,128]{1,0:T(8,128)S(1)} collective-permute-done((f32[8,128]{1,0:T(8,128)S(1)}, f32[8,128]{1,0:T(8,128)S(1)}, u32[]{:S(2)}, u32[]{:S(2)}) %collective-permute-start.29) | collective-permute-done | bytes 4128 | tf_op jit(solution)/shard_map/ppermute | solution.py:233
  95.7 1.4 %collective-permute-start.30 = (f32[20,128]{1,0:T(8,128)S(1)}, f32[20,128]{1,0:T(8,128)S(1)}, u32[]{:S(2)}, u32[]{:S(2)}) collective-permute-start(f32[20,128]{1,0:T(8,128)S(1)} %pad_maximum_fusion.5), channel_id=1, source_target_pairs={{0,8},{4,12},{8,0},{12,4},{16,24},{20,28},{24,16},{28,20},{1,9},{5... | collective-permute-start | bytes 30728 | tf_op jit(solution)/shard_map/ppermute | solution.py:233
  97.2 0.8 collective-permute-start.26
  98.7 0.8 collective-permute-done.30
  99.5 1.2 %collective-permute-start.31 = (f32[20,128]{1,0:T(8,128)S(1)}, f32[20,128]{1,0:T(8,128)S(1)}, u32[]{:S(2)}, u32[]{:S(2)}) collective-permute-start(f32[20,128]{1,0:T(8,128)S(1)} %pad_maximum_fusion.5), channel_id=1, source_target_pairs={{0,16},{4,20},{8,24},{12,28},{16,0},{20,4},{24,8},{28,12},{1,17},{... | collective-permute-start | bytes 30728 | tf_op jit(solution)/shard_map/ppermute | solution.py:233
  100.6 2.5 %collective-permute-done.32 = f32[20,128]{1,0:T(8,128)S(1)} collective-permute-done((f32[20,128]{1,0:T(8,128)S(1)}, f32[20,128]{1,0:T(8,128)S(1)}, u32[]{:S(2)}, u32[]{:S(2)}) %collective-permute-start.32) | collective-permute-done | bytes 10272 | tf_op jit(solution)/shard_map/ppermute | solution.py:233
  103.3 1.2 %keys.1 = bf16[512,512]{1,0:T(8,128)(2,1)} custom-call(f32[512,512]{1,0:T(8,128)S(1)} %get-tuple-element.136.here, bf16[256,512]{1,0:T(8,128)(2,1)S(1)} %collective-permute-done.27.upper, bf16[256,512]{1,0:T(8,128)(2,1)S(1)} %collective-permute-done.28.lower, f32[1,512]{1,0:T(1,128)S(1)} %bitcast.13, f32[512,128]{1,0:T(8,128)S(1)} %get-tuple-element.139.cos_ref, ...), custom_call_target="tpu_custom_call" | custom-call | flops 1 | bytes 1 | tf_op jit(solution)/shard_map/keys/pallas_call | solution.py:356
  104.5 0.9 collective-permute-done.26
  105.4 0.6 multiply_bitcast_fusion.1
  106.0 0.6 multiply_bitcast_fusion
  106.6 1.6 %convert_multiply_fusion = f32[1024,512]{1,0:T(8,128)} fusion(bf16[256,512]{1,0:T(8,128)(2,1)S(1)} %get-tuple-element.163, bf16[256,512]{1,0:T(8,128)(2,1)S(1)} %get-tuple-element.162, bf16[256,512]{1,0:T(8,128)(2,1)S(1)} %get-tuple-element.161, bf16[256,512]{1,0:T(8,128)(2,1)S(1)} %get-tuple-element.160), kind=kLoop, calls=%fused_computation | loop fusion | flops 4718592 | bytes 3145728 | tf_op jit(solution)/shard_map/mul | solution.py:375
  (75 shorter events, 8.9 us)
Async XLA Ops:
  2.2 22.0 %collective-permute-start.6 = (bf16[832,512]{1,0:T(8,128)(2,1)S(1)}, bf16[832,512]{1,0:T(8,128)(2,1)S(1)}, u32[]{:S(2)}, u32[]{:S(2)}) collective-permute-start(bf16[832,512]{1,0:T(8,128)(2,1)S(1)} %get-tuple-element.158), channel_id=1, source_target_pairs={{0,16},{4,20},{8,24},{12,28},{16,0},{20,4},{24,8},{28,12},{1,17},{... | collective-permute-start | bytes 2555912 | tf_op jit(solution)/shard_map/ppermute | solution.py:233
  5.3 20.4 %collective-permute-start.5 = (bf16[832,512]{1,0:T(8,128)(2,1)S(1)}, bf16[832,512]{1,0:T(8,128)(2,1)S(1)}, u32[]{:S(2)}, u32[]{:S(2)}) collective-permute-start(bf16[832,512]{1,0:T(8,128)(2,1)S(1)} %get-tuple-element.159), channel_id=1, source_target_pairs={{0,8},{4,12},{8,0},{12,4},{16,24},{20,28},{24,16},{28,20},{1,9},{5... | collective-permute-start | bytes 2555912 | tf_op jit(solution)/shard_map/ppermute | solution.py:233
  6.8 3.4 %copy-start.1 = (bf16[512,8192]{1,0:T(8,128)(2,1)S(1)}, bf16[512,8192]{1,0:T(8,128)(2,1)}, u32[]{:S(2)}) copy-start(bf16[512,8192]{1,0:T(8,128)(2,1)} %x_ref) | copy-start | bytes 25165828
  16.8 1.6 %collective-permute-start.4 = (bf16[256,512]{1,0:T(8,128)(2,1)S(1)}, bf16[256,512]{1,0:T(8,128)(2,1)S(1)}, u32[]{:S(2)}, u32[]{:S(2)}) collective-permute-start(bf16[256,512]{1,0:T(8,128)(2,1)S(1)} %get-tuple-element.164), channel_id=1, source_target_pairs={{0,4},{4,0},{8,12},{12,8},{16,20},{20,16},{24,28},{28,24},{1,5},{5... | collective-permute-start | bytes 786440 | tf_op jit(solution)/shard_map/ppermute | solution.py:233
  16.9 1.9 %collective-permute-start.3 = (bf16[256,512]{1,0:T(8,128)(2,1)S(1)}, bf16[256,512]{1,0:T(8,128)(2,1)S(1)}, u32[]{:S(2)}, u32[]{:S(2)}) collective-permute-start(bf16[256,512]{1,0:T(8,128)(2,1)S(1)} %get-tuple-element.165), channel_id=1, source_target_pairs={{0,4},{4,0},{8,12},{12,8},{16,20},{20,16},{24,28},{28,24},{1,5},{5... | collective-permute-start | bytes 786440 | tf_op jit(solution)/shard_map/ppermute | solution.py:233
  17.4 2.1 %collective-permute-start = (bf16[512,512]{1,0:T(8,128)(2,1)S(1)}, bf16[512,512]{1,0:T(8,128)(2,1)S(1)}, u32[]{:S(2)}, u32[]{:S(2)}) collective-permute-start(bf16[512,512]{1,0:T(8,128)(2,1)S(1)} %get-tuple-element.92), channel_id=1, source_target_pairs={{0,4},{4,0},{8,12},{12,8},{16,20},{20,16},{24,28},{28,24},{1,5},{5... | collective-permute-start | bytes 1572872 | tf_op jit(solution)/shard_map/ppermute | solution.py:233
  18.4 1.9 %collective-permute-start.1 = (bf16[512,512]{1,0:T(8,128)(2,1)S(1)}, bf16[512,512]{1,0:T(8,128)(2,1)S(1)}, u32[]{:S(2)}, u32[]{:S(2)}) collective-permute-start(bf16[512,512]{1,0:T(8,128)(2,1)S(1)} %get-tuple-element.93), channel_id=1, source_target_pairs={{0,4},{4,0},{8,12},{12,8},{16,20},{20,16},{24,28},{28,24},{1,5},{5... | collective-permute-start | bytes 1572872 | tf_op jit(solution)/shard_map/ppermute | solution.py:233
  18.8 2.3 %collective-permute-start.2 = (bf16[512,512]{1,0:T(8,128)(2,1)S(1)}, bf16[512,512]{1,0:T(8,128)(2,1)S(1)}, u32[]{:S(2)}, u32[]{:S(2)}) collective-permute-start(bf16[512,512]{1,0:T(8,128)(2,1)S(1)} %get-tuple-element.94), channel_id=1, source_target_pairs={{0,4},{4,0},{8,12},{12,8},{16,20},{20,16},{24,28},{28,24},{1,5},{5... | collective-permute-start | bytes 1572872 | tf_op jit(solution)/shard_map/ppermute | solution.py:233
  24.2 50.0 %copy-start.2 = (bf16[832,512]{1,0:T(8,128)(2,1)}, bf16[832,512]{1,0:T(8,128)(2,1)S(1)}, u32[]{:S(2)}) copy-start(bf16[832,512]{1,0:T(8,128)(2,1)S(1)} %collective-permute-done.6.refs_7_.refs_12_) | copy-start | bytes 2555908
  25.7 4.9 %collective-permute-start.8 = (bf16[512,2048]{1,0:T(8,128)(2,1)S(1)}, bf16[512,2048]{1,0:T(8,128)(2,1)S(1)}, u32[]{:S(2)}, u32[]{:S(2)}) collective-permute-start(bf16[512,2048]{1,0:T(8,128)(2,1)S(1)} %get-tuple-element.102), channel_id=1, source_target_pairs={{0,4},{4,0},{8,12},{12,8},{16,20},{20,16},{24,28},{28,24},{1,5},{5... | collective-permute-start | bytes 6291464 | tf_op jit(solution)/shard_map/ppermute | solution.py:233
  25.7 4.9 %collective-permute-start.7 = (bf16[512,512]{1,0:T(8,128)(2,1)S(1)}, bf16[512,512]{1,0:T(8,128)(2,1)S(1)}, u32[]{:S(2)}, u32[]{:S(2)}) collective-permute-start(bf16[512,512]{1,0:T(8,128)(2,1)S(1)} %get-tuple-element.101), channel_id=1, source_target_pairs={{0,4},{4,0},{8,12},{12,8},{16,20},{20,16},{24,28},{28,24},{1,5},{5... | collective-permute-start | bytes 1572872 | tf_op jit(solution)/shard_map/ppermute | solution.py:233
  26.2 13.8 %collective-permute-start.9 = (bf16[512,512]{1,0:T(8,128)(2,1)S(1)}, bf16[512,512]{1,0:T(8,128)(2,1)S(1)}, u32[]{:S(2)}, u32[]{:S(2)}) collective-permute-start(bf16[512,512]{1,0:T(8,128)(2,1)S(1)} %get-tuple-element.106), channel_id=1, source_target_pairs={{0,8},{4,12},{8,0},{12,4},{16,24},{20,28},{24,16},{28,20},{1,9},{5... | collective-permute-start | bytes 1572872 | tf_op jit(solution)/shard_map/ppermute | solution.py:233
  27.7 13.6 %collective-permute-start.10 = (bf16[512,512]{1,0:T(8,128)(2,1)S(1)}, bf16[512,512]{1,0:T(8,128)(2,1)S(1)}, u32[]{:S(2)}, u32[]{:S(2)}) collective-permute-start(bf16[512,512]{1,0:T(8,128)(2,1)S(1)} %get-tuple-element.107), channel_id=1, source_target_pairs={{0,16},{4,20},{8,24},{12,28},{16,0},{20,4},{24,8},{28,12},{1,17},{... | collective-permute-start | bytes 1572872 | tf_op jit(solution)/shard_map/ppermute | solution.py:233
  30.6 2.9 %copy-start = (bf16[1024,512]{1,0:T(8,128)(2,1)S(1)}, bf16[1024,512]{1,0:T(8,128)(2,1)}, u32[]{:S(2)}) copy-start(bf16[1024,512]{1,0:T(8,128)(2,1)} %refs_6_) | copy-start | bytes 3145732
  41.4 7.1 %collective-permute-start.14 = (bf16[256,512]{1,0:T(8,128)(2,1)S(1)}, bf16[256,512]{1,0:T(8,128)(2,1)S(1)}, u32[]{:S(2)}, u32[]{:S(2)}) collective-permute-start(bf16[256,512]{1,0:T(8,128)(2,1)S(1)} %add_convert_fusion.6), channel_id=1, source_target_pairs={{0,8},{4,12},{8,0},{12,4},{16,24},{20,28},{24,16},{28,20},{1,9},{5... | collective-permute-start | bytes 786440 | tf_op jit(solution)/shard_map/ppermute | solution.py:233
  42.0 6.8 %collective-permute-start.13 = (bf16[256,512]{1,0:T(8,128)(2,1)S(1)}, bf16[256,512]{1,0:T(8,128)(2,1)S(1)}, u32[]{:S(2)}, u32[]{:S(2)}) collective-permute-start(bf16[256,512]{1,0:T(8,128)(2,1)S(1)} %add_convert_fusion.7), channel_id=1, source_target_pairs={{0,16},{4,20},{8,24},{12,28},{16,0},{20,4},{24,8},{28,12},{1,17},{... | collective-permute-start | bytes 786440 | tf_op jit(solution)/shard_map/ppermute | solution.py:233
  49.1 6.4 %collective-permute-start.15 = (bf16[256,512]{1,0:T(8,128)(2,1)S(1)}, bf16[256,512]{1,0:T(8,128)(2,1)S(1)}, u32[]{:S(2)}, u32[]{:S(2)}) collective-permute-start(bf16[256,512]{1,0:T(8,128)(2,1)S(1)} %select_convert_fusion.1), channel_id=1, source_target_pairs={{0,1},{1,0},{2,3},{3,2},{4,5},{5,4},{6,7},{7,6},{8,9},{9,8},{10,11... | collective-permute-start | bytes 786440 | tf_op jit(solution)/shard_map/ppermute | solution.py:274
  50.8 11.3 %collective-permute-start.11 = (bf16[512,512]{1,0:T(8,128)(2,1)S(1)}, bf16[512,512]{1,0:T(8,128)(2,1)S(1)}, u32[]{:S(2)}, u32[]{:S(2)}) collective-permute-start(bf16[512,512]{1,0:T(8,128)(2,1)S(1)} %get-tuple-element.115), channel_id=1, source_target_pairs={{0,8},{4,12},{8,0},{12,4},{16,24},{20,28},{24,16},{28,20},{1,9},{5... | collective-permute-start | bytes 1572872 | tf_op jit(solution)/shard_map/ppermute | solution.py:233
  52.3 11.9 %collective-permute-start.12 = (bf16[512,512]{1,0:T(8,128)(2,1)S(1)}, bf16[512,512]{1,0:T(8,128)(2,1)S(1)}, u32[]{:S(2)}, u32[]{:S(2)}) collective-permute-start(bf16[512,512]{1,0:T(8,128)(2,1)S(1)} %get-tuple-element.116), channel_id=1, source_target_pairs={{0,16},{4,20},{8,24},{12,28},{16,0},{20,4},{24,8},{28,12},{1,17},{... | collective-permute-start | bytes 1572872 | tf_op jit(solution)/shard_map/ppermute | solution.py:233
  55.8 11.3 %collective-permute-start.18 = (bf16[256,512]{1,0:T(8,128)(2,1)S(1)}, bf16[256,512]{1,0:T(8,128)(2,1)S(1)}, u32[]{:S(2)}, u32[]{:S(2)}) collective-permute-start(bf16[256,512]{1,0:T(8,128)(2,1)S(1)} %add_convert_fusion.3), channel_id=1, source_target_pairs={{0,2},{1,3},{2,0},{3,1},{4,6},{5,7},{6,4},{7,5},{8,10},{9,11},{10,... | collective-permute-start | bytes 786440 | tf_op jit(solution)/shard_map/ppermute | solution.py:274
  64.3 6.4 %collective-permute-start.16 = (bf16[256,512]{1,0:T(8,128)(2,1)S(1)}, bf16[256,512]{1,0:T(8,128)(2,1)S(1)}, u32[]{:S(2)}, u32[]{:S(2)}) collective-permute-start(bf16[256,512]{1,0:T(8,128)(2,1)S(1)} %get-tuple-element.120), channel_id=1, source_target_pairs={{0,16},{4,20},{8,24},{12,28},{16,0},{20,4},{24,8},{28,12},{1,17},{... | collective-permute-start | bytes 786440 | tf_op jit(solution)/shard_map/ppermute | solution.py:233
  64.9 6.4 %collective-permute-start.17 = (bf16[256,512]{1,0:T(8,128)(2,1)S(1)}, bf16[256,512]{1,0:T(8,128)(2,1)S(1)}, u32[]{:S(2)}, u32[]{:S(2)}) collective-permute-start(bf16[256,512]{1,0:T(8,128)(2,1)S(1)} %get-tuple-element.121), channel_id=1, source_target_pairs={{0,8},{4,12},{8,0},{12,4},{16,24},{20,28},{24,16},{28,20},{1,9},{5... | collective-permute-start | bytes 786440 | tf_op jit(solution)/shard_map/ppermute | solution.py:233
  67.2 27.3 %collective-permute-start.22 = (bf16[256,512]{1,0:T(8,128)(2,1)S(1)}, bf16[256,512]{1,0:T(8,128)(2,1)S(1)}, u32[]{:S(2)}, u32[]{:S(2)}) collective-permute-start(bf16[256,512]{1,0:T(8,128)(2,1)S(1)} %add_convert_fusion.2), channel_id=1, source_target_pairs={{0,1},{1,0},{2,3},{3,2},{4,5},{5,4},{6,7},{7,6},{8,9},{9,8},{10,11... | collective-permute-start | bytes 786440 | tf_op jit(solution)/shard_map/ppermute | solution.py:274
  72.1 4.5 %collective-permute-start.20 = (f32[12,128]{1,0:T(8,128)S(1)}, f32[12,128]{1,0:T(8,128)S(1)}, u32[]{:S(2)}, u32[]{:S(2)}) collective-permute-start(f32[12,128]{1,0:T(8,128)S(1)} %maximum_bitcast_fusion), channel_id=1, source_target_pairs={{0,1},{1,0},{2,3},{3,2},{4,5},{5,4},{6,7},{7,6},{8,9},{9,8},{10,11... | collective-permute-start | bytes 18440 | tf_op jit(solution)/shard_map/ppermute | solution.py:274
  72.6 6.8 %collective-permute-start.19 = (bf16[256,512]{1,0:T(8,128)(2,1)S(1)}, bf16[256,512]{1,0:T(8,128)(2,1)S(1)}, u32[]{:S(2)}, u32[]{:S(2)}) collective-permute-start(bf16[256,512]{1,0:T(8,128)(2,1)S(1)} %select_convert_fusion), channel_id=1, source_target_pairs={{0,1},{1,0},{2,3},{3,2},{4,5},{5,4},{6,7},{7,6},{8,9},{9,8},{10,11... | collective-permute-start | bytes 786440 | tf_op jit(solution)/shard_map/ppermute | solution.py:274
  74.2 1.7 %slice-start = ((bf16[832,512]{1,0:T(8,128)(2,1)}), bf16[512,512]{1,0:T(8,128)(2,1)S(1)}, s32[]{:S(2)}) async-start(bf16[832,512]{1,0:T(8,128)(2,1)} %copy-done.2), calls=%async_computation | async-start | bytes 1048576 | tf_op jit(solution)/shard_map/slice | solution.py:322
  74.3 17.8 %copy-start.3 = (bf16[832,512]{1,0:T(8,128)(2,1)S(1)}, bf16[832,512]{1,0:T(8,128)(2,1)}, u32[]{:S(2)}) copy-start(bf16[832,512]{1,0:T(8,128)(2,1)} %copy-done.2) | copy-start | bytes 2555908
  74.3 17.7 %collective-permute-start.25 = (bf16[704,512]{1,0:T(8,128)(2,1)S(1)}, bf16[704,512]{1,0:T(8,128)(2,1)S(1)}, u32[]{:S(2)}, u32[]{:S(2)}) collective-permute-start(bf16[704,512]{1,0:T(8,128)(2,1)S(1)} %pad_maximum_fusion.1), channel_id=1, source_target_pairs={{0,16},{4,20},{8,24},{12,28},{16,0},{20,4},{24,8},{28,12},{1,17},{... | collective-permute-start | bytes 2162696 | tf_op jit(solution)/shard_map/ppermute | solution.py:233
  76.0 16.1 %collective-permute-start.24 = (bf16[704,512]{1,0:T(8,128)(2,1)S(1)}, bf16[704,512]{1,0:T(8,128)(2,1)S(1)}, u32[]{:S(2)}, u32[]{:S(2)}) collective-permute-start(bf16[704,512]{1,0:T(8,128)(2,1)S(1)} %pad_maximum_fusion), channel_id=1, source_target_pairs={{0,8},{4,12},{8,0},{12,4},{16,24},{20,28},{24,16},{28,20},{1,9},{5... | collective-permute-start | bytes 2162696 | tf_op jit(solution)/shard_map/ppermute | solution.py:233
  79.6 14.8 %collective-permute-start.21 = (bf16[256,512]{1,0:T(8,128)(2,1)S(1)}, bf16[256,512]{1,0:T(8,128)(2,1)S(1)}, u32[]{:S(2)}, u32[]{:S(2)}) collective-permute-start(bf16[256,512]{1,0:T(8,128)(2,1)S(1)} %add_convert_fusion.1), channel_id=1, source_target_pairs={{0,2},{1,3},{2,0},{3,1},{4,6},{5,7},{6,4},{7,5},{8,10},{9,11},{10,... | collective-permute-start | bytes 786440 | tf_op jit(solution)/shard_map/ppermute | solution.py:274
  82.1 10.0 %collective-permute-start.23 = (f32[12,128]{1,0:T(8,128)S(1)}, f32[12,128]{1,0:T(8,128)S(1)}, u32[]{:S(2)}, u32[]{:S(2)}) collective-permute-start(f32[12,128]{1,0:T(8,128)S(1)} %fusion.3), channel_id=1, source_target_pairs={{0,2},{1,3},{2,0},{3,1},{4,6},{5,7},{6,4},{7,5},{8,10},{9,11},{10,... | collective-permute-start | bytes 18440 | tf_op jit(solution)/shard_map/ppermute | solution.py:274
  94.4 8.9 %copy-start.4 = (f32[512]{0:T(512)S(1)}, f32[512]{0:T(512)}, u32[]{:S(2)}) copy-start(f32[512]{0:T(512)} %param.10) | copy-start | bytes 6148
  94.5 1.2 %collective-permute-start.29 = (f32[8,128]{1,0:T(8,128)S(1)}, f32[8,128]{1,0:T(8,128)S(1)}, u32[]{:S(2)}, u32[]{:S(2)}) collective-permute-start(f32[8,128]{1,0:T(8,128)S(1)} %slice.120), channel_id=1, source_target_pairs={{0,4},{4,0},{8,12},{12,8},{16,20},{20,16},{24,28},{28,24},{1,5},{5... | collective-permute-start | bytes 12296 | tf_op jit(solution)/shard_map/ppermute | solution.py:233
  95.7 3.8 %collective-permute-start.30 = (f32[20,128]{1,0:T(8,128)S(1)}, f32[20,128]{1,0:T(8,128)S(1)}, u32[]{:S(2)}, u32[]{:S(2)}) collective-permute-start(f32[20,128]{1,0:T(8,128)S(1)} %pad_maximum_fusion.5), channel_id=1, source_target_pairs={{0,8},{4,12},{8,0},{12,4},{16,24},{20,28},{24,16},{28,20},{1,9},{5... | collective-permute-start | bytes 30728 | tf_op jit(solution)/shard_map/ppermute | solution.py:233
  97.2 8.2 %collective-permute-start.26 = (bf16[256,512]{1,0:T(8,128)(2,1)S(1)}, bf16[256,512]{1,0:T(8,128)(2,1)S(1)}, u32[]{:S(2)}, u32[]{:S(2)}) collective-permute-start(bf16[256,512]{1,0:T(8,128)(2,1)S(1)} %add_convert_fusion), channel_id=1, source_target_pairs={{0,1},{1,0},{2,3},{3,2},{4,5},{5,4},{6,7},{7,6},{8,9},{9,8},{10,11... | collective-permute-start | bytes 786440 | tf_op jit(solution)/shard_map/ppermute | solution.py:274
  98.0 5.3 %collective-permute-start.27 = (bf16[256,512]{1,0:T(8,128)(2,1)S(1)}, bf16[256,512]{1,0:T(8,128)(2,1)S(1)}, u32[]{:S(2)}, u32[]{:S(2)}) collective-permute-start(bf16[256,512]{1,0:T(8,128)(2,1)S(1)} %get-tuple-element.137), channel_id=1, source_target_pairs={{0,4},{4,0},{8,12},{12,8},{16,20},{20,16},{24,28},{28,24},{1,5},{5... | collective-permute-start | bytes 786440 | tf_op jit(solution)/shard_map/ppermute | solution.py:233
  98.0 5.3 %collective-permute-start.28 = (bf16[256,512]{1,0:T(8,128)(2,1)S(1)}, bf16[256,512]{1,0:T(8,128)(2,1)S(1)}, u32[]{:S(2)}, u32[]{:S(2)}) collective-permute-start(bf16[256,512]{1,0:T(8,128)(2,1)S(1)} %get-tuple-element.138), channel_id=1, source_target_pairs={{0,4},{4,0},{8,12},{12,8},{16,20},{20,16},{24,28},{28,24},{1,5},{5... | collective-permute-start | bytes 786440 | tf_op jit(solution)/shard_map/ppermute | solution.py:233
  98.5 4.6 %collective-permute-start.32 = (f32[20,128]{1,0:T(8,128)S(1)}, f32[20,128]{1,0:T(8,128)S(1)}, u32[]{:S(2)}, u32[]{:S(2)}) collective-permute-start(f32[20,128]{1,0:T(8,128)S(1)} %pad_maximum_fusion.5), channel_id=1, source_target_pairs={{0,24},{4,28},{8,16},{12,20},{16,8},{20,12},{24,0},{28,4},{1,25},{... | collective-permute-start | bytes 30728 | tf_op jit(solution)/shard_map/ppermute | solution.py:233
  99.5 3.8 %collective-permute-start.31 = (f32[20,128]{1,0:T(8,128)S(1)}, f32[20,128]{1,0:T(8,128)S(1)}, u32[]{:S(2)}, u32[]{:S(2)}) collective-permute-start(f32[20,128]{1,0:T(8,128)S(1)} %pad_maximum_fusion.5), channel_id=1, source_target_pairs={{0,16},{4,20},{8,24},{12,28},{16,0},{20,4},{24,8},{28,12},{1,17},{... | collective-permute-start | bytes 30728 | tf_op jit(solution)/shard_map/ppermute | solution.py:233

commit v6 on v5

--- a/solution.py
+++ b/solution.py
@@ -44,10 +44,11 @@
     return lax.optimization_barrier((value, *others))[0]
 
 
-def call(body, out_shape, name):
+def call(body, out_shape, name, in_specs=None):
     return pl.pallas_call(
         body,
         out_shape=out_shape,
+        **({} if in_specs is None else {"in_specs": in_specs}),
         cost_estimate=pl.CostEstimate(flops=1, bytes_accessed=1, transcendentals=0),
         compiler_params=pltpu.CompilerParams(vmem_limit_bytes=10 * 1024 * 1024),
         name=name,
@@ -114,7 +115,7 @@
 
 def prepared(x, gain, segs, cotangent, at):
     rows, wide = x.shape
-    step = 64
+    step = 128
     half = wide // 16
     outs = [(half, BF16)] * 12 + [(4 * half, BF16), (HEAD, F32), (HEAD, F32), (KW, BF16)]
     def whole(v):
@@ -123,8 +124,9 @@
     def some(n):
         return pl.BlockSpec((step, n), lambda r, at: (r, 0))
 
-    gain, segs, cotangent = (
-        pltpu.with_memory_space_constraint(v, pltpu.HBM) for v in (gain[None, :], segs, cotangent)
+    x, gain, segs, cotangent = (
+        pltpu.with_memory_space_constraint(v, pltpu.HBM)
+        for v in (x, gain[None, :], segs, cotangent)
     )
     return pl.pallas_call(
         functools.partial(prepare_body, segs.shape[1] // step),
@@ -147,10 +149,10 @@
     )(at, x, gain, segs, cotangent)
 
 
-def keys_body(here, upper, lower, bias, cos_ref, sin_ref, out_ref):
+def keys_body(here, upper, middle, lower, bias, cos_ref, sin_ref, out_ref):
     for h in range(KVH):
         cols = slice(h * HEAD, (h + 1) * HEAD)
-        there = jnp.concatenate([upper[:, cols], lower[:, cols]], axis=0).astype(F32)
+        there = jnp.concatenate([v[:, cols] for v in (upper, middle, lower)], axis=0).astype(F32)
         v = here[:, cols] + there + bias[:, cols]
         out_ref[:, cols] = turn(v, cos_ref[...], -sin_ref[...]).astype(BF16)
 
@@ -193,7 +195,7 @@
 def forward_body(places, n_acts, n_init, *refs):
     acts, init, refs = refs[:n_acts], refs[n_acts : n_acts + n_init], refs[n_acts + n_init :]
     half = acts[0].shape[1]
-    n_outs = 3 if n_init else 2
+    n_outs = 4 if n_init else 2
     weights, outs = refs[:-n_outs], refs[-n_outs:]
     totals = [v[...] for v in init] if n_init else [None, None]
     for side in (1, 0):
@@ -204,9 +206,11 @@
             add = jnp.dot(rows, w, preferred_element_type=F32)
             total = add if total is None else total + add
         if side and n_init:
-            n = outs[1].shape[0]
-            outs[1][...] = total[:n].astype(BF16)
-            outs[2][...] = total[n:].astype(BF16)
+            start = 0
+            for out in outs[1:]:
+                stop = start + out.shape[0]
+                out[...] = total[start:stop].astype(BF16)
+                start = stop
         else:
             outs[side][...] = total
 
@@ -214,12 +218,25 @@
 def forward(acts, places, weights, init=()):
     tok, kw = acts[0].shape[0], weights[0].shape[1]
     shape = jax.ShapeDtypeStruct((tok, kw), F32)
-    part = jax.ShapeDtypeStruct((tok // 2, kw), BF16)
+    third = tok // 48 * 16
+    parts = [jax.ShapeDtypeStruct((n, kw), BF16) for n in (third, third, tok - 2 * third)]
     return call(
         functools.partial(forward_body, places, len(acts), len(init)),
-        [shape, part, part] if init else [shape, shape],
+        [shape, *parts] if init else [shape, shape],
         "forward",
     )(*acts, *init, *weights)
+
+
+def collect_body(scale, at_ref, here, over_x, over_y, over_xy, gains_ref, bias_ref):
+    n = gains_ref.shape[0] // 8
+    chip, core = at_ref[0] // 2, at_ref[0] % 2
+    refs = (here, over_x, over_y, over_xy)
+    for away, ref in enumerate(refs):
+        first = (chip ^ away) * 2
+        gains_ref[pl.ds(pl.multiple_of((first + core) * n, n), n)] = ref[:n] * scale
+        gains_ref[pl.ds(pl.multiple_of((first + 1 - core) * n, n), n)] = ref[n : 2 * n] * scale
+    bias = [ref[2 * n :] for ref in refs]
+    bias_ref[...] = ((bias[0] + bias[1]) + (bias[2] + bias[3])) * scale
 
 
 def by_permutes(hidden_in, segment_ids, key_weight, norm_gain, key_bias, key_cotangent):
@@ -238,12 +255,11 @@
         return v.astype(F32)
 
     odd = (lax.axis_index("dp") & 1) == 1
-    firsts = [(me & bit) == 0 for bit in (1, 2, 4)]
     at = me.reshape(1).astype(jnp.int32)
-    odd, firsts, at, key_weight, hidden_in, key_cotangent, segment_ids = after(
-        (odd, firsts, at, key_weight, hidden_in, key_cotangent, segment_ids)
-    )
-    early = half + own * 5 // 16
+    odd, at, key_weight, hidden_in, key_cotangent, segment_ids = after(
+        (odd, at, key_weight, hidden_in, key_cotangent, segment_ids)
+    )
+    early = half + own*17//64
     late = own - early
     w_x, w_y = px(key_weight[late:]), py(key_weight[:early])
 
@@ -316,7 +332,7 @@
     pair_a = pair_sum(*local_a, in_pair(*local_a))
 
     in_b = after(in_b, two_a)
-    more = after(add_up(part_b, *in_b), pair_a)
+    more = add_up(part_b, *in_b)
     two_b = py(more[0]), px(more[1])
     w_y, w_x, key_weight = after((w_y, w_x, key_weight), two_b)
     more_wx = px(jnp.concatenate([key_weight[:late], w_y[:half]], axis=0))
@@ -346,33 +362,36 @@
         (2, 6, 0, ((0, 0, late), (3, 0, half - late))),
         (3, 7, 3, ((2, half, early - half), (1, 0, late))),
     )
-    more_wx, more_wy = after((more_wx, more_wy), pair_b)
-    forwarded = forward(acts, places, (more_wx, more_wy, w_y, w_x), here)
-    other_b, got_a, small, forwarded = after((over_z(2)(pair_b), got_a, small, forwarded))
+    gains, bias = small[:n_own], small[n_own:]
+    other_gains = core(gains)
+    other_b, got_a, gains, bias, other_gains, more_wx, more_wy = after(
+        (over_z(2)(pair_b), got_a, gains, bias, other_gains, more_wx, more_wy)
+    )
     total_b = total_of(pair_b, other_b)
     got_b = over_z(1)(total_b)
+    more_wx, more_wy = after((more_wx, more_wy), total_b)
+    forwarded = forward(acts, places, (more_wx, more_wy, w_y, w_x), here)
 
     here, *there = forwarded
     keys = call(keys_body, jax.ShapeDtypeStruct((tok, kw), BF16), "keys")(
         here, *(core(v) for v in there), key_bias[None, :], cosine, sine
     )
 
-    def ordered(first, one, two):
-        return jnp.concatenate([jnp.where(first, one, two), jnp.where(first, two, one)], axis=0)
-
-    gains, bias = small[:n_own], small[n_own:]
-    gains = ordered(firsts[0], gains, core(gains))
-    packed = jnp.concatenate([gains, bias], axis=0)
-    n = gains.shape[0]
-    got_x, got_y, got_xy = px(packed), py(packed), over(6)(packed)
-    same = ordered(firsts[1], gains, got_x[:n])
-    gains = ordered(firsts[2], same, ordered(firsts[1], got_y[:n], got_xy[:n]))
-    bias = (bias + got_x[n:]) + (got_y[n:] + got_xy[n:])
-
-    scale = 1.0 / jnp.sqrt(F32(tok * 32))
-    got_b, keys, gains, bias = after((got_b, keys, gains, bias))
+    scale = 1.0 / math.sqrt(tok * 32)
+    packed = jnp.concatenate([gains, other_gains, bias], axis=0)
+    gains, bias = call(
+        functools.partial(collect_body, scale),
+        [
+            jax.ShapeDtypeStruct((8 * n_own, HEAD), F32),
+            jax.ShapeDtypeStruct(bias.shape, F32),
+        ],
+        "collect",
+        [pl.BlockSpec(memory_space=pltpu.SMEM)] + [pl.BlockSpec(memory_space=pltpu.VMEM)] * 4,
+    )(at, packed, px(packed), py(packed), over(6)(packed))
+
+    got_b, keys = after((got_b, keys))
     grad = jnp.concatenate([*both(total_a, got_a), *both(total_b, got_b)], axis=0)
-    return (keys, grad * scale, bias.reshape(-1) * scale, gains.reshape(-1) * scale)
+    return (keys, grad * scale, bias.reshape(-1), gains.reshape(-1))
 
 
 def by_collectives(hidden_in, segment_ids, key_weight, norm_gain, key_bias, key_cotangent):

time: 109 us -> 103 us (0.945)
  local copies, waits for them, and re-layouts: 5.1 us -> 2 us
  waiting for transfers between devices: 50.7 us -> 48 us
  Pallas kernels: 17.2 us -> 18.9 us
  other arithmetic: 5.17 us -> 3.86 us
    unnamed x10, local copies, waits for them, and re-layouts: 3.4 us -> 0.02 us
    ppermute x8, waiting for transfers between devices: 17.3 us -> 15.3 us  [over_z(): return lambda v: lax.ppermute(v, 'dp', [(i, i ^ bit) for i in range(4)])]
    ppermute x25 -> x26, starting transfers between devices: 17.7 us -> 19 us  [over(): return lambda v: lax.ppermute(v, 'blk', [(i, i ^ bit) for i in range(8)])]
    mul x3 -> x1, other arithmetic: 2.81 us -> 1.61 us  [by_permutes(): return (keys, grad * scale, bias.reshape(-1), gains.reshape(-1))]
    ppermute x8, starting transfers between devices: 11.5 us -> 10.3 us  [over_z(): return lambda v: lax.ppermute(v, 'dp', [(i, i ^ bit) for i in range(4)])]
    pallas_call x1, Pallas kernels: 6.62 us -> 7.75 us  [prepared(): pl.pallas_call(functools.partial(prepare_body, segs.shape[1] // step), gr...]
    ppermute x25 -> x26, waiting for transfers between devices: 33.3 us -> 32.7 us  [over(): return lambda v: lax.ppermute(v, 'blk', [(i, i ^ bit) for i in range(8)])]
  transfers between devices with their start and end apart: 33 -> 34, of which waited for: 25 -> 24; matrix products, arithmetic and copies ran while one was open for 2% -> 2% of each run, Pallas kernels for 16% -> 18%
where the time goes in v6:
time: 103 us
  waiting for transfers between devices  48 us (47%)
  starting transfers between devices  29.3 us (28%)
  Pallas kernels  18.9 us (18%)
  other arithmetic  3.86 us (4%)
  local copies, waits for them, and re-layouts  2 us (2%)
    ppermute x26, waiting for transfers between devices, over(): return lambda v: lax.ppermute(v, 'blk', [(i, i ^ bit) for i in range(8)])  32.7 us
    ppermute x26, starting transfers between devices, over(): return lambda v: lax.ppermute(v, 'blk', [(i, i ^ bit) for i in range(8)])  19 us
    ppermute x8, waiting for transfers between devices, over_z(): return lambda v: lax.ppermute(v, 'dp', [(i, i ^ bit) for i in range(4)])  15.3 us
    ppermute x8, starting transfers between devices, over_z(): return lambda v: lax.ppermute(v, 'dp', [(i, i ^ bit) for i in range(4)])  10.3 us
    pallas_call x1, Pallas kernels, prepared(): pl.pallas_call(functools.partial(prepare_body, segs.shape[1] // step), gr...  7.75 us
    pallas_call x2, Pallas kernels, forward(): call(functools.partial(forward_body, places, len(acts), len(init)), [shap...  4.66 us
    pallas_call x1, Pallas kernels, by_permutes(): call(second_grad_body, [own_shape, own_shape, *part_shapes(quarter)], 'gr...  2.91 us
  transfers between devices with their start and end apart: 34, of which 24 were waited for; matrix products, arithmetic and copies ran while one was open for 2% of the time, Pallas kernels for 18%

profile of v6, /device:TPU:0, one launch (start us, length us, event | category | flops | bytes accessed | tf_op | source)
XLA Modules:
  0.0 103.1 jit_solution(17637770020528219626)
XLA Ops:
  0.6 1.5 %fusion.2 = (bf16[784,512]{1,0:T(8,128)(2,1)S(1)}, bf16[784,512]{1,0:T(8,128)(2,1)S(1)}) fusion(bf16[1024,512]{1,0:T(8,128)(2,1)} %refs_6_), kind=kLoop, calls=%fused_computation.36 | loop fusion | bytes 3211264 | tf_op jit(solution)/shard_map/slice | solution.py:264
  2.1 3.0 %collective-permute-start.6 = (bf16[784,512]{1,0:T(8,128)(2,1)S(1)}, bf16[784,512]{1,0:T(8,128)(2,1)S(1)}, u32[]{:S(2)}, u32[]{:S(2)}) collective-permute-start(bf16[784,512]{1,0:T(8,128)(2,1)S(1)} %get-tuple-element.152), channel_id=1, source_target_pairs={{0,16},{4,20},{8,24},{12,28},{16,0},{20,4},{24,8},{28,12},{1,17},{... | collective-permute-start | bytes 2408456 | tf_op jit(solution)/shard_map/ppermute | solution.py:250
  5.2 1.5 %collective-permute-start.5 = (bf16[784,512]{1,0:T(8,128)(2,1)S(1)}, bf16[784,512]{1,0:T(8,128)(2,1)S(1)}, u32[]{:S(2)}, u32[]{:S(2)}) collective-permute-start(bf16[784,512]{1,0:T(8,128)(2,1)S(1)} %get-tuple-element.153), channel_id=1, source_target_pairs={{0,8},{4,12},{8,0},{12,4},{16,24},{20,28},{24,16},{28,20},{1,9},{5... | collective-permute-start | bytes 2408456 | tf_op jit(solution)/shard_map/ppermute | solution.py:250
  6.7 7.7 %prepare.1 = (bf16[512,512]{1,0:T(8,128)(2,1)S(1)}, bf16[512,512]{1,0:T(8,128)(2,1)S(1)}, bf16[512,512]{1,0:T(8,128)(2,1)S(1)}, bf16[512,512]{1,0:T(8,128)(2,1)S...) custom-call(s32[1]{0:T(128)} %bitcast.at_ref, ...), custom_call_target="tpu_custom_call" | custom-call | flops 1 | bytes 1 | tf_op jit(solution)/shard_map/prepare/pallas_call | solution.py:131
  14.5 0.5 collective-permute-start.3
  15.1 0.9 collective-permute-done.4.lower
  16.6 0.6 collective-permute-done.s1.refs_6_
  17.2 0.8 collective-permute-done.1.s2.refs_4_
  18.0 0.7 collective-permute-done.2.s3.refs_4_
  18.7 1.8 %grad_a.1 = (bf16[512,512]{1,0:T(8,128)(2,1)S(1)}, bf16[512,512]{1,0:T(8,128)(2,1)S(1)}, bf16[256,512]{1,0:T(8,128)(2,1)S(1)}, bf16[256,512]{1,0:T(8,128)(2,1)S(1)}) custom-call(bf16[512,512]{1,0:T(8,128)(2,1)S(1)} %get-tuple-element.86.m1.refs_2_, bf16[512,512]{1,0:T(8,128)(2,1)S(1)} %get-tuple-element.87.m2.refs_2_, ...), custom_call_target="tpu_custom_call" | custom-call | flops 1 | bytes 1 | tf_op jit(solution)/shard_map/grad_a/pallas_call | solution.py:305
  20.5 2.5 %collective-permute-done.6.refs_7_.refs_12_ = bf16[784,512]{1,0:T(8,128)(2,1)S(1)} collective-permute-done((bf16[784,512]{1,0:T(8,128)(2,1)S(1)}, bf16[784,512]{1,0:T(8,128)(2,1)S(1)}, u32[]{:S(2)}, u32[]{:S(2)}) %collective-permute-start.6) | collective-permute-done | bytes 802848 | tf_op jit(solution)/shard_map/ppermute | solution.py:250
  23.1 1.5 %collective-permute-done.5.refs_8_.refs_13_ = bf16[784,512]{1,0:T(8,128)(2,1)S(1)} collective-permute-done((bf16[784,512]{1,0:T(8,128)(2,1)S(1)}, bf16[784,512]{1,0:T(8,128)(2,1)S(1)}, u32[]{:S(2)}, u32[]{:S(2)}) %collective-permute-start.5) | collective-permute-done | bytes 802848 | tf_op jit(solution)/shard_map/ppermute | solution.py:250
  24.5 0.5 collective-permute-start.7
  25.0 1.5 %collective-permute-start.9 = (bf16[512,512]{1,0:T(8,128)(2,1)S(1)}, bf16[512,512]{1,0:T(8,128)(2,1)S(1)}, u32[]{:S(2)}, u32[]{:S(2)}) collective-permute-start(bf16[512,512]{1,0:T(8,128)(2,1)S(1)} %get-tuple-element.103), channel_id=1, source_target_pairs={{0,8},{4,12},{8,0},{12,4},{16,24},{20,28},{24,16},{28,20},{1,9},{5... | collective-permute-start | bytes 1572872 | tf_op jit(solution)/shard_map/ppermute | solution.py:250
  26.5 0.5 collective-permute-start.10
  27.0 2.4 %collective-permute-done.7.s3.refs_5_ = bf16[512,512]{1,0:T(8,128)(2,1)S(1)} collective-permute-done((bf16[512,512]{1,0:T(8,128)(2,1)S(1)}, bf16[512,512]{1,0:T(8,128)(2,1)S(1)}, u32[]{:S(2)}, u32[]{:S(2)}) %collective-permute-start.7) | collective-permute-done | bytes 524320 | tf_op jit(solution)/shard_map/ppermute | solution.py:250
  29.4 2.9 %grad_b.1 = (f32[512,512]{1,0:T(8,128)S(1)}, f32[512,512]{1,0:T(8,128)S(1)}, bf16[512,512]{1,0:T(8,128)(2,1)S(1)}, bf16[512,512]{1,0:T(8,128)(2,1)S(1)}, bf16[25...) custom-call(bf16[512,512]{1,0:T(8,128)(2,1)S(1)} %get-tuple-element.79.m_a0.refs_0_, ...), custom_call_target="tpu_custom_call" | custom-call | flops 1 | bytes 1 | tf_op jit(solution)/shard_map/grad_b/pallas_call | solution.py:313
  32.4 2.3 %forward.2 = (f32[512,512]{1,0:T(8,128)S(1)}, f32[512,512]{1,0:T(8,128)S(1)}) custom-call(bf16[512,512]{1,0:T(8,128)(2,1)S(1)} %get-tuple-element.79.m_a0.refs_0_, bf16[512,512]{1,0:T(8,128)(2,1)S(1)} %get-tuple-element.80.m0.refs_1_, bf16[512,512]{1,0:T(8,128)(2,1)S(1)} %get-tuple-element.87.m2.refs_2_, bf16[512,512]{1,0:T(8,128)(2,1)S(1)} %get-tuple-element.81.m1.refs_3_, ...), custom_call_target="tpu_custom_call" | custom-call | flops 1 | bytes 1 | tf_op jit(solution)/shard_map/forward/pallas_call | solution.py:223
  34.7 4.2 %collective-permute-done.9 = bf16[512,512]{1,0:T(8,128)(2,1)S(1)} collective-permute-done((bf16[512,512]{1,0:T(8,128)(2,1)S(1)}, bf16[512,512]{1,0:T(8,128)(2,1)S(1)}, u32[]{:S(2)}, u32[]{:S(2)}) %collective-permute-start.9) | collective-permute-done | bytes 524320 | tf_op jit(solution)/shard_map/ppermute | solution.py:250
  38.9 1.2 %collective-permute-done.10 = bf16[512,512]{1,0:T(8,128)(2,1)S(1)} collective-permute-done((bf16[512,512]{1,0:T(8,128)(2,1)S(1)}, bf16[512,512]{1,0:T(8,128)(2,1)S(1)}, u32[]{:S(2)}, u32[]{:S(2)}) %collective-permute-start.10) | collective-permute-done | bytes 524320 | tf_op jit(solution)/shard_map/ppermute | solution.py:250
  40.2 0.6 collective-permute-start.14
  41.2 6.1 %collective-permute-done.14 = bf16[256,512]{1,0:T(8,128)(2,1)S(1)} collective-permute-done((bf16[256,512]{1,0:T(8,128)(2,1)S(1)}, bf16[256,512]{1,0:T(8,128)(2,1)S(1)}, u32[]{:S(2)}, u32[]{:S(2)}) %collective-permute-start.14) | collective-permute-done | bytes 262176 | tf_op jit(solution)/shard_map/ppermute | solution.py:250
  47.9 1.6 %collective-permute-start.17 = (bf16[256,512]{1,0:T(8,128)(2,1)S(1)}, bf16[256,512]{1,0:T(8,128)(2,1)S(1)}, u32[]{:S(2)}, u32[]{:S(2)}) collective-permute-start(bf16[256,512]{1,0:T(8,128)(2,1)S(1)} %select_convert_fusion.1), channel_id=1, source_target_pairs={{0,1},{1,0},{2,3},{3,2},{4,5},{5,4},{6,7},{7,6},{8,9},{9,8},{10,11... | collective-permute-start | bytes 786440 | tf_op jit(solution)/shard_map/ppermute | solution.py:290
  49.6 1.5 %collective-permute-start.11 = (bf16[512,512]{1,0:T(8,128)(2,1)S(1)}, bf16[512,512]{1,0:T(8,128)(2,1)S(1)}, u32[]{:S(2)}, u32[]{:S(2)}) collective-permute-start(bf16[512,512]{1,0:T(8,128)(2,1)S(1)} %get-tuple-element.112), channel_id=1, source_target_pairs={{0,8},{4,12},{8,0},{12,4},{16,24},{20,28},{24,16},{28,20},{1,9},{5... | collective-permute-start | bytes 1572872 | tf_op jit(solution)/shard_map/ppermute | solution.py:250
  51.1 0.5 collective-permute-start.12
  51.8 2.6 %collective-permute-done.17 = bf16[256,512]{1,0:T(8,128)(2,1)S(1)} collective-permute-done((bf16[256,512]{1,0:T(8,128)(2,1)S(1)}, bf16[256,512]{1,0:T(8,128)(2,1)S(1)}, u32[]{:S(2)}, u32[]{:S(2)}) %collective-permute-start.17) | collective-permute-done | bytes 262176 | tf_op jit(solution)/shard_map/ppermute | solution.py:290
  54.6 3.2 %collective-permute-start.18 = (bf16[256,512]{1,0:T(8,128)(2,1)S(1)}, bf16[256,512]{1,0:T(8,128)(2,1)S(1)}, u32[]{:S(2)}, u32[]{:S(2)}) collective-permute-start(bf16[256,512]{1,0:T(8,128)(2,1)S(1)} %add_convert_fusion.3), channel_id=1, source_target_pairs={{0,2},{1,3},{2,0},{3,1},{4,6},{5,7},{6,4},{7,5},{8,10},{9,11},{10,... | collective-permute-start | bytes 786440 | tf_op jit(solution)/shard_map/ppermute | solution.py:290
  57.8 3.1 %collective-permute-done.11 = bf16[512,512]{1,0:T(8,128)(2,1)S(1)} collective-permute-done((bf16[512,512]{1,0:T(8,128)(2,1)S(1)}, bf16[512,512]{1,0:T(8,128)(2,1)S(1)}, u32[]{:S(2)}, u32[]{:S(2)}) %collective-permute-start.11) | collective-permute-done | bytes 524320 | tf_op jit(solution)/shard_map/ppermute | solution.py:250
  60.9 1.6 %collective-permute-done.12 = bf16[512,512]{1,0:T(8,128)(2,1)S(1)} collective-permute-done((bf16[512,512]{1,0:T(8,128)(2,1)S(1)}, bf16[512,512]{1,0:T(8,128)(2,1)S(1)}, u32[]{:S(2)}, u32[]{:S(2)}) %collective-permute-start.12) | collective-permute-done | bytes 524320 | tf_op jit(solution)/shard_map/ppermute | solution.py:250
  63.0 0.5 collective-permute-start.15
  63.6 2.4 %collective-permute-done.18 = bf16[256,512]{1,0:T(8,128)(2,1)S(1)} collective-permute-done((bf16[256,512]{1,0:T(8,128)(2,1)S(1)}, bf16[256,512]{1,0:T(8,128)(2,1)S(1)}, u32[]{:S(2)}, u32[]{:S(2)}) %collective-permute-start.18) | collective-permute-done | bytes 262176 | tf_op jit(solution)/shard_map/ppermute | solution.py:290
  66.0 3.1 %collective-permute-done.16 = bf16[256,512]{1,0:T(8,128)(2,1)S(1)} collective-permute-done((bf16[256,512]{1,0:T(8,128)(2,1)S(1)}, bf16[256,512]{1,0:T(8,128)(2,1)S(1)}, u32[]{:S(2)}, u32[]{:S(2)}) %collective-permute-start.16) | collective-permute-done | bytes 262176 | tf_op jit(solution)/shard_map/ppermute | solution.py:250
  69.1 1.5 %collective-permute-done.15 = bf16[256,512]{1,0:T(8,128)(2,1)S(1)} collective-permute-done((bf16[256,512]{1,0:T(8,128)(2,1)S(1)}, bf16[256,512]{1,0:T(8,128)(2,1)S(1)}, u32[]{:S(2)}, u32[]{:S(2)}) %collective-permute-start.15) | collective-permute-done | bytes 262176 | tf_op jit(solution)/shard_map/ppermute | solution.py:250
  71.2 0.6 collective-permute-start.26
  72.1 2.6 %collective-permute-start.25 = (bf16[752,512]{1,0:T(8,128)(2,1)S(1)}, bf16[752,512]{1,0:T(8,128)(2,1)S(1)}, u32[]{:S(2)}, u32[]{:S(2)}) collective-permute-start(bf16[752,512]{1,0:T(8,128)(2,1)S(1)} %pad_maximum_fusion), channel_id=1, source_target_pairs={{0,8},{4,12},{8,0},{12,4},{16,24},{20,28},{24,16},{28,20},{1,9},{5... | collective-permute-start | bytes 2310152 | tf_op jit(solution)/shard_map/ppermute | solution.py:250
  75.2 2.1 %collective-permute-start.20 = (f32[12,128]{1,0:T(8,128)S(1)}, f32[12,128]{1,0:T(8,128)S(1)}, u32[]{:S(2)}, u32[]{:S(2)}) collective-permute-start(f32[12,128]{1,0:T(8,128)S(1)} %maximum_bitcast_fusion), channel_id=1, source_target_pairs={{0,1},{1,0},{2,3},{3,2},{4,5},{5,4},{6,7},{7,6},{8,9},{9,8},{10,11... | collective-permute-start | bytes 18440 | tf_op jit(solution)/shard_map/ppermute | solution.py:290
  77.3 3.0 %collective-permute-done.20 = f32[12,128]{1,0:T(8,128)S(1)} collective-permute-done((f32[12,128]{1,0:T(8,128)S(1)}, f32[12,128]{1,0:T(8,128)S(1)}, u32[]{:S(2)}, u32[]{:S(2)}) %collective-permute-start.20) | collective-permute-done | bytes 6176 | tf_op jit(solution)/shard_map/ppermute | solution.py:290
  80.5 2.1 %collective-permute-start.21 = (bf16[256,512]{1,0:T(8,128)(2,1)S(1)}, bf16[256,512]{1,0:T(8,128)(2,1)S(1)}, u32[]{:S(2)}, u32[]{:S(2)}) collective-permute-start(bf16[256,512]{1,0:T(8,128)(2,1)S(1)} %add_convert_fusion.1), channel_id=1, source_target_pairs={{0,2},{1,3},{2,0},{3,1},{4,6},{5,7},{6,4},{7,5},{8,10},{9,11},{10,... | collective-permute-start | bytes 786440 | tf_op jit(solution)/shard_map/ppermute | solution.py:290
  82.6 0.8 collective-permute-start.23
  83.5 7.3 %collective-permute-done.23 = f32[12,128]{1,0:T(8,128)S(1)} collective-permute-done((f32[12,128]{1,0:T(8,128)S(1)}, f32[12,128]{1,0:T(8,128)S(1)}, u32[]{:S(2)}, u32[]{:S(2)}) %collective-permute-start.23) | collective-permute-done | bytes 6176 | tf_op jit(solution)/shard_map/ppermute | solution.py:290
  90.8 1.1 %collective-permute-done.24 = f32[8,128]{1,0:T(8,128)S(1)} collective-permute-done((f32[8,128]{1,0:T(8,128)S(1)}, f32[8,128]{1,0:T(8,128)S(1)}, u32[]{:S(2)}, u32[]{:S(2)}) %collective-permute-start.24) | collective-permute-done | bytes 4128 | tf_op jit(solution)/shard_map/ppermute | solution.py:250
  92.3 1.4 %collective-permute-start.33 = (f32[20,128]{1,0:T(8,128)S(1)}, f32[20,128]{1,0:T(8,128)S(1)}, u32[]{:S(2)}, u32[]{:S(2)}) collective-permute-start(f32[20,128]{1,0:T(8,128)S(1)} %constant_dynamic-update-slice_fusion.here), channel_id=1, source_target_pairs={{0,24},{4,28},{8,16},{12,20},{16,8},{20,12},{24,0},{28,4},{1,25},{... | collective-permute-start | bytes 30728 | tf_op jit(solution)/shard_map/ppermute | solution.py:250
  93.8 1.3 %collective-permute-start.32 = (f32[20,128]{1,0:T(8,128)S(1)}, f32[20,128]{1,0:T(8,128)S(1)}, u32[]{:S(2)}, u32[]{:S(2)}) collective-permute-start(f32[20,128]{1,0:T(8,128)S(1)} %constant_dynamic-update-slice_fusion.here), channel_id=1, source_target_pairs={{0,16},{4,20},{8,24},{12,28},{16,0},{20,4},{24,8},{28,12},{1,17},{... | collective-permute-start | bytes 30728 | tf_op jit(solution)/shard_map/ppermute | solution.py:250
  95.1 0.8 collective-permute-start.31
  95.8 2.3 %forward.3 = (f32[512,512]{1,0:T(8,128)S(1)}, bf16[160,512]{1,0:T(8,128)(2,1)S(1)}, bf16[160,512]{1,0:T(8,128)(2,1)S(1)}, bf16[192,512]{1,0:T(8,128)(2,1)S(1)}) custom-call(bf16[512,512]{1,0:T(8,128)(2,1)S(1)} %get-tuple-element.88.m3.refs_0_, bf16[512,512]{1,0:T(8,128)(2,1)S(1)} %get-tuple-element.83.m3.refs_1_, ...), custom_call_target="tpu_custom_call" | custom-call | flops 1 | bytes 1 | tf_op jit(solution)/shard_map/forward/pallas_call | solution.py:223
  98.9 0.6 collect.1
  100.2 1.2 %keys.1 = bf16[512,512]{1,0:T(8,128)(2,1)} custom-call(f32[512,512]{1,0:T(8,128)S(1)} %get-tuple-element.130.here, bf16[160,512]{1,0:T(8,128)(2,1)S(1)} %collective-permute-done.28.upper, bf16[160,512]{1,0:T(8,128)(2,1)S(1)} %collective-permute-done.29.middle, bf16[192,512]{1,0:T(8,128)(2,1)S(1)} %collective-permute-done.30.lower, f32[1,512]{1,0:T(1,128)S(1)} %bitcast.11, ...), custom_call_target="tpu_custom_call" | custom-call | flops 1 | bytes 1 | tf_op jit(solution)/shard_map/keys/pallas_call | solution.py:376
  101.4 1.6 %convert_multiply_fusion = f32[1024,512]{1,0:T(8,128)} fusion(bf16[256,512]{1,0:T(8,128)(2,1)S(1)} %get-tuple-element.157, bf16[256,512]{1,0:T(8,128)(2,1)S(1)} %get-tuple-element.156, bf16[256,512]{1,0:T(8,128)(2,1)S(1)} %get-tuple-element.155, bf16[256,512]{1,0:T(8,128)(2,1)S(1)} %get-tuple-element.154), kind=kLoop, calls=%fused_computation | loop fusion | flops 4718592 | bytes 3145728 | tf_op jit(solution)/shard_map/mul | solution.py:394
  (71 shorter events, 6.2 us)
Async XLA Ops:
  2.1 20.9 %collective-permute-start.6 = (bf16[784,512]{1,0:T(8,128)(2,1)S(1)}, bf16[784,512]{1,0:T(8,128)(2,1)S(1)}, u32[]{:S(2)}, u32[]{:S(2)}) collective-permute-start(bf16[784,512]{1,0:T(8,128)(2,1)S(1)} %get-tuple-element.152), channel_id=1, source_target_pairs={{0,16},{4,20},{8,24},{12,28},{16,0},{20,4},{24,8},{28,12},{1,17},{... | collective-permute-start | bytes 2408456 | tf_op jit(solution)/shard_map/ppermute | solution.py:250
  5.2 19.4 %collective-permute-start.5 = (bf16[784,512]{1,0:T(8,128)(2,1)S(1)}, bf16[784,512]{1,0:T(8,128)(2,1)S(1)}, u32[]{:S(2)}, u32[]{:S(2)}) collective-permute-start(bf16[784,512]{1,0:T(8,128)(2,1)S(1)} %get-tuple-element.153), channel_id=1, source_target_pairs={{0,8},{4,12},{8,0},{12,4},{16,24},{20,28},{24,16},{28,20},{1,9},{5... | collective-permute-start | bytes 2408456 | tf_op jit(solution)/shard_map/ppermute | solution.py:250
  14.5 1.6 %collective-permute-start.4 = (bf16[256,512]{1,0:T(8,128)(2,1)S(1)}, bf16[256,512]{1,0:T(8,128)(2,1)S(1)}, u32[]{:S(2)}, u32[]{:S(2)}) collective-permute-start(bf16[256,512]{1,0:T(8,128)(2,1)S(1)} %get-tuple-element.158), channel_id=1, source_target_pairs={{0,4},{4,0},{8,12},{12,8},{16,20},{20,16},{24,28},{28,24},{1,5},{5... | collective-permute-start | bytes 786440 | tf_op jit(solution)/shard_map/ppermute | solution.py:250
  14.5 1.9 %collective-permute-start.3 = (bf16[256,512]{1,0:T(8,128)(2,1)S(1)}, bf16[256,512]{1,0:T(8,128)(2,1)S(1)}, u32[]{:S(2)}, u32[]{:S(2)}) collective-permute-start(bf16[256,512]{1,0:T(8,128)(2,1)S(1)} %get-tuple-element.159), channel_id=1, source_target_pairs={{0,4},{4,0},{8,12},{12,8},{16,20},{20,16},{24,28},{28,24},{1,5},{5... | collective-permute-start | bytes 786440 | tf_op jit(solution)/shard_map/ppermute | solution.py:250
  15.0 2.1 %collective-permute-start = (bf16[512,512]{1,0:T(8,128)(2,1)S(1)}, bf16[512,512]{1,0:T(8,128)(2,1)S(1)}, u32[]{:S(2)}, u32[]{:S(2)}) collective-permute-start(bf16[512,512]{1,0:T(8,128)(2,1)S(1)} %get-tuple-element.89), channel_id=1, source_target_pairs={{0,4},{4,0},{8,12},{12,8},{16,20},{20,16},{24,28},{28,24},{1,5},{5... | collective-permute-start | bytes 1572872 | tf_op jit(solution)/shard_map/ppermute | solution.py:250
  16.1 1.9 %collective-permute-start.1 = (bf16[512,512]{1,0:T(8,128)(2,1)S(1)}, bf16[512,512]{1,0:T(8,128)(2,1)S(1)}, u32[]{:S(2)}, u32[]{:S(2)}) collective-permute-start(bf16[512,512]{1,0:T(8,128)(2,1)S(1)} %get-tuple-element.90), channel_id=1, source_target_pairs={{0,4},{4,0},{8,12},{12,8},{16,20},{20,16},{24,28},{28,24},{1,5},{5... | collective-permute-start | bytes 1572872 | tf_op jit(solution)/shard_map/ppermute | solution.py:250
  16.4 2.3 %collective-permute-start.2 = (bf16[512,512]{1,0:T(8,128)(2,1)S(1)}, bf16[512,512]{1,0:T(8,128)(2,1)S(1)}, u32[]{:S(2)}, u32[]{:S(2)}) collective-permute-start(bf16[512,512]{1,0:T(8,128)(2,1)S(1)} %get-tuple-element.91), channel_id=1, source_target_pairs={{0,4},{4,0},{8,12},{12,8},{16,20},{20,16},{24,28},{28,24},{1,5},{5... | collective-permute-start | bytes 1572872 | tf_op jit(solution)/shard_map/ppermute | solution.py:250
  23.1 48.0 %copy-start.1 = (bf16[784,512]{1,0:T(8,128)(2,1)}, bf16[784,512]{1,0:T(8,128)(2,1)S(1)}, u32[]{:S(2)}) copy-start(bf16[784,512]{1,0:T(8,128)(2,1)S(1)} %collective-permute-done.6.refs_7_.refs_12_) | copy-start | bytes 2408452
  24.5 4.9 %collective-permute-start.8 = (bf16[512,2048]{1,0:T(8,128)(2,1)S(1)}, bf16[512,2048]{1,0:T(8,128)(2,1)S(1)}, u32[]{:S(2)}, u32[]{:S(2)}) collective-permute-start(bf16[512,2048]{1,0:T(8,128)(2,1)S(1)} %get-tuple-element.99), channel_id=1, source_target_pairs={{0,4},{4,0},{8,12},{12,8},{16,20},{20,16},{24,28},{28,24},{1,5},{5... | collective-permute-start | bytes 6291464 | tf_op jit(solution)/shard_map/ppermute | solution.py:250
  24.5 4.9 %collective-permute-start.7 = (bf16[512,512]{1,0:T(8,128)(2,1)S(1)}, bf16[512,512]{1,0:T(8,128)(2,1)S(1)}, u32[]{:S(2)}, u32[]{:S(2)}) collective-permute-start(bf16[512,512]{1,0:T(8,128)(2,1)S(1)} %get-tuple-element.98), channel_id=1, source_target_pairs={{0,4},{4,0},{8,12},{12,8},{16,20},{20,16},{24,28},{28,24},{1,5},{5... | collective-permute-start | bytes 1572872 | tf_op jit(solution)/shard_map/ppermute | solution.py:250
  25.0 13.8 %collective-permute-start.9 = (bf16[512,512]{1,0:T(8,128)(2,1)S(1)}, bf16[512,512]{1,0:T(8,128)(2,1)S(1)}, u32[]{:S(2)}, u32[]{:S(2)}) collective-permute-start(bf16[512,512]{1,0:T(8,128)(2,1)S(1)} %get-tuple-element.103), channel_id=1, source_target_pairs={{0,8},{4,12},{8,0},{12,4},{16,24},{20,28},{24,16},{28,20},{1,9},{5... | collective-permute-start | bytes 1572872 | tf_op jit(solution)/shard_map/ppermute | solution.py:250
  26.5 13.6 %collective-permute-start.10 = (bf16[512,512]{1,0:T(8,128)(2,1)S(1)}, bf16[512,512]{1,0:T(8,128)(2,1)S(1)}, u32[]{:S(2)}, u32[]{:S(2)}) collective-permute-start(bf16[512,512]{1,0:T(8,128)(2,1)S(1)} %get-tuple-element.104), channel_id=1, source_target_pairs={{0,16},{4,20},{8,24},{12,28},{16,0},{20,4},{24,8},{28,12},{1,17},{... | collective-permute-start | bytes 1572872 | tf_op jit(solution)/shard_map/ppermute | solution.py:250
  29.4 2.9 %copy-start = (bf16[1024,512]{1,0:T(8,128)(2,1)S(1)}, bf16[1024,512]{1,0:T(8,128)(2,1)}, u32[]{:S(2)}) copy-start(bf16[1024,512]{1,0:T(8,128)(2,1)} %refs_6_) | copy-start | bytes 3145732
  40.2 7.1 %collective-permute-start.14 = (bf16[256,512]{1,0:T(8,128)(2,1)S(1)}, bf16[256,512]{1,0:T(8,128)(2,1)S(1)}, u32[]{:S(2)}, u32[]{:S(2)}) collective-permute-start(bf16[256,512]{1,0:T(8,128)(2,1)S(1)} %add_convert_fusion.6), channel_id=1, source_target_pairs={{0,8},{4,12},{8,0},{12,4},{16,24},{20,28},{24,16},{28,20},{1,9},{5... | collective-permute-start | bytes 786440 | tf_op jit(solution)/shard_map/ppermute | solution.py:250
  40.8 6.8 %collective-permute-start.13 = (bf16[256,512]{1,0:T(8,128)(2,1)S(1)}, bf16[256,512]{1,0:T(8,128)(2,1)S(1)}, u32[]{:S(2)}, u32[]{:S(2)}) collective-permute-start(bf16[256,512]{1,0:T(8,128)(2,1)S(1)} %add_convert_fusion.7), channel_id=1, source_target_pairs={{0,16},{4,20},{8,24},{12,28},{16,0},{20,4},{24,8},{28,12},{1,17},{... | collective-permute-start | bytes 786440 | tf_op jit(solution)/shard_map/ppermute | solution.py:250
  47.9 6.4 %collective-permute-start.17 = (bf16[256,512]{1,0:T(8,128)(2,1)S(1)}, bf16[256,512]{1,0:T(8,128)(2,1)S(1)}, u32[]{:S(2)}, u32[]{:S(2)}) collective-permute-start(bf16[256,512]{1,0:T(8,128)(2,1)S(1)} %select_convert_fusion.1), channel_id=1, source_target_pairs={{0,1},{1,0},{2,3},{3,2},{4,5},{5,4},{6,7},{7,6},{8,9},{9,8},{10,11... | collective-permute-start | bytes 786440 | tf_op jit(solution)/shard_map/ppermute | solution.py:290
  49.6 11.3 %collective-permute-start.11 = (bf16[512,512]{1,0:T(8,128)(2,1)S(1)}, bf16[512,512]{1,0:T(8,128)(2,1)S(1)}, u32[]{:S(2)}, u32[]{:S(2)}) collective-permute-start(bf16[512,512]{1,0:T(8,128)(2,1)S(1)} %get-tuple-element.112), channel_id=1, source_target_pairs={{0,8},{4,12},{8,0},{12,4},{16,24},{20,28},{24,16},{28,20},{1,9},{5... | collective-permute-start | bytes 1572872 | tf_op jit(solution)/shard_map/ppermute | solution.py:250
  51.1 11.4 %collective-permute-start.12 = (bf16[512,512]{1,0:T(8,128)(2,1)S(1)}, bf16[512,512]{1,0:T(8,128)(2,1)S(1)}, u32[]{:S(2)}, u32[]{:S(2)}) collective-permute-start(bf16[512,512]{1,0:T(8,128)(2,1)S(1)} %get-tuple-element.113), channel_id=1, source_target_pairs={{0,16},{4,20},{8,24},{12,28},{16,0},{20,4},{24,8},{28,12},{1,17},{... | collective-permute-start | bytes 1572872 | tf_op jit(solution)/shard_map/ppermute | solution.py:250
  54.6 11.3 %collective-permute-start.18 = (bf16[256,512]{1,0:T(8,128)(2,1)S(1)}, bf16[256,512]{1,0:T(8,128)(2,1)S(1)}, u32[]{:S(2)}, u32[]{:S(2)}) collective-permute-start(bf16[256,512]{1,0:T(8,128)(2,1)S(1)} %add_convert_fusion.3), channel_id=1, source_target_pairs={{0,2},{1,3},{2,0},{3,1},{4,6},{5,7},{6,4},{7,5},{8,10},{9,11},{10,... | collective-permute-start | bytes 786440 | tf_op jit(solution)/shard_map/ppermute | solution.py:290
  62.7 6.4 %collective-permute-start.16 = (bf16[256,512]{1,0:T(8,128)(2,1)S(1)}, bf16[256,512]{1,0:T(8,128)(2,1)S(1)}, u32[]{:S(2)}, u32[]{:S(2)}) collective-permute-start(bf16[256,512]{1,0:T(8,128)(2,1)S(1)} %add_convert_fusion.4), channel_id=1, source_target_pairs={{0,8},{4,12},{8,0},{12,4},{16,24},{20,28},{24,16},{28,20},{1,9},{5... | collective-permute-start | bytes 786440 | tf_op jit(solution)/shard_map/ppermute | solution.py:250
  63.0 7.6 %collective-permute-start.15 = (bf16[256,512]{1,0:T(8,128)(2,1)S(1)}, bf16[256,512]{1,0:T(8,128)(2,1)S(1)}, u32[]{:S(2)}, u32[]{:S(2)}) collective-permute-start(bf16[256,512]{1,0:T(8,128)(2,1)S(1)} %add_convert_fusion.5), channel_id=1, source_target_pairs={{0,16},{4,20},{8,24},{12,28},{16,0},{20,4},{24,8},{28,12},{1,17},{... | collective-permute-start | bytes 786440 | tf_op jit(solution)/shard_map/ppermute | solution.py:250
  70.9 9.4 %collective-permute-start.19 = (bf16[256,512]{1,0:T(8,128)(2,1)S(1)}, bf16[256,512]{1,0:T(8,128)(2,1)S(1)}, u32[]{:S(2)}, u32[]{:S(2)}) collective-permute-start(bf16[256,512]{1,0:T(8,128)(2,1)S(1)} %select_convert_fusion), channel_id=1, source_target_pairs={{0,1},{1,0},{2,3},{3,2},{4,5},{5,4},{6,7},{7,6},{8,9},{9,8},{10,11... | collective-permute-start | bytes 786440 | tf_op jit(solution)/shard_map/ppermute | solution.py:290
  71.0 1.0 %slice-start = ((bf16[784,512]{1,0:T(8,128)(2,1)}), bf16[512,512]{1,0:T(8,128)(2,1)S(1)}, s32[]{:S(2)}) async-start(bf16[784,512]{1,0:T(8,128)(2,1)} %copy-done.1), calls=%async_computation | async-start | bytes 1048576 | tf_op jit(solution)/shard_map/slice | solution.py:338
  71.2 20.8 %collective-permute-start.26 = (bf16[752,512]{1,0:T(8,128)(2,1)S(1)}, bf16[752,512]{1,0:T(8,128)(2,1)S(1)}, u32[]{:S(2)}, u32[]{:S(2)}) collective-permute-start(bf16[752,512]{1,0:T(8,128)(2,1)S(1)} %pad_maximum_fusion.1), channel_id=1, source_target_pairs={{0,16},{4,20},{8,24},{12,28},{16,0},{20,4},{24,8},{28,12},{1,17},{... | collective-permute-start | bytes 2310152 | tf_op jit(solution)/shard_map/ppermute | solution.py:250
  72.1 19.9 %collective-permute-start.25 = (bf16[752,512]{1,0:T(8,128)(2,1)S(1)}, bf16[752,512]{1,0:T(8,128)(2,1)S(1)}, u32[]{:S(2)}, u32[]{:S(2)}) collective-permute-start(bf16[752,512]{1,0:T(8,128)(2,1)S(1)} %pad_maximum_fusion), channel_id=1, source_target_pairs={{0,8},{4,12},{8,0},{12,4},{16,24},{20,28},{24,16},{28,20},{1,9},{5... | collective-permute-start | bytes 2310152 | tf_op jit(solution)/shard_map/ppermute | solution.py:250
  75.1 20.7 %copy-start.2 = (bf16[784,512]{1,0:T(8,128)(2,1)S(1)}, bf16[784,512]{1,0:T(8,128)(2,1)}, u32[]{:S(2)}) copy-start(bf16[784,512]{1,0:T(8,128)(2,1)} %copy-done.1) | copy-start | bytes 2408452
  75.2 5.2 %collective-permute-start.20 = (f32[12,128]{1,0:T(8,128)S(1)}, f32[12,128]{1,0:T(8,128)S(1)}, u32[]{:S(2)}, u32[]{:S(2)}) collective-permute-start(f32[12,128]{1,0:T(8,128)S(1)} %maximum_bitcast_fusion), channel_id=1, source_target_pairs={{0,1},{1,0},{2,3},{3,2},{4,5},{5,4},{6,7},{7,6},{8,9},{9,8},{10,11... | collective-permute-start | bytes 18440 | tf_op jit(solution)/shard_map/ppermute | solution.py:290
  77.2 13.6 %collective-permute-start.22 = (bf16[256,512]{1,0:T(8,128)(2,1)S(1)}, bf16[256,512]{1,0:T(8,128)(2,1)S(1)}, u32[]{:S(2)}, u32[]{:S(2)}) collective-permute-start(bf16[256,512]{1,0:T(8,128)(2,1)S(1)} %add_convert_fusion.2), channel_id=1, source_target_pairs={{0,1},{1,0},{2,3},{3,2},{4,5},{5,4},{6,7},{7,6},{8,9},{9,8},{10,11... | collective-permute-start | bytes 786440 | tf_op jit(solution)/shard_map/ppermute | solution.py:290
  80.5 11.5 %collective-permute-start.21 = (bf16[256,512]{1,0:T(8,128)(2,1)S(1)}, bf16[256,512]{1,0:T(8,128)(2,1)S(1)}, u32[]{:S(2)}, u32[]{:S(2)}) collective-permute-start(bf16[256,512]{1,0:T(8,128)(2,1)S(1)} %add_convert_fusion.1), channel_id=1, source_target_pairs={{0,2},{1,3},{2,0},{3,1},{4,6},{5,7},{6,4},{7,5},{8,10},{9,11},{10,... | collective-permute-start | bytes 786440 | tf_op jit(solution)/shard_map/ppermute | solution.py:290
  82.6 8.2 %collective-permute-start.23 = (f32[12,128]{1,0:T(8,128)S(1)}, f32[12,128]{1,0:T(8,128)S(1)}, u32[]{:S(2)}, u32[]{:S(2)}) collective-permute-start(f32[12,128]{1,0:T(8,128)S(1)} %fusion), channel_id=1, source_target_pairs={{0,2},{1,3},{2,0},{3,1},{4,6},{5,7},{6,4},{7,5},{8,10},{9,11},{10,... | collective-permute-start | bytes 18440 | tf_op jit(solution)/shard_map/ppermute | solution.py:290
  90.8 1.2 %collective-permute-start.24 = (f32[8,128]{1,0:T(8,128)S(1)}, f32[8,128]{1,0:T(8,128)S(1)}, u32[]{:S(2)}, u32[]{:S(2)}) collective-permute-start(f32[8,128]{1,0:T(8,128)S(1)} %slice.104), channel_id=1, source_target_pairs={{0,4},{4,0},{8,12},{12,8},{16,20},{20,16},{24,28},{28,24},{1,5},{5... | collective-permute-start | bytes 12296 | tf_op jit(solution)/shard_map/ppermute | solution.py:250
  92.1 9.3 %collective-permute-start.27 = (bf16[256,512]{1,0:T(8,128)(2,1)S(1)}, bf16[256,512]{1,0:T(8,128)(2,1)S(1)}, u32[]{:S(2)}, u32[]{:S(2)}) collective-permute-start(bf16[256,512]{1,0:T(8,128)(2,1)S(1)} %add_convert_fusion), channel_id=1, source_target_pairs={{0,1},{1,0},{2,3},{3,2},{4,5},{5,4},{6,7},{7,6},{8,9},{9,8},{10,11... | collective-permute-start | bytes 786440 | tf_op jit(solution)/shard_map/ppermute | solution.py:290
  92.3 7.9 %copy-start.3 = (f32[512]{0:T(512)S(1)}, f32[512]{0:T(512)}, u32[]{:S(2)}) copy-start(f32[512]{0:T(512)} %param.10) | copy-start | bytes 6148
  92.3 5.9 %collective-permute-start.33 = (f32[20,128]{1,0:T(8,128)S(1)}, f32[20,128]{1,0:T(8,128)S(1)}, u32[]{:S(2)}, u32[]{:S(2)}) collective-permute-start(f32[20,128]{1,0:T(8,128)S(1)} %constant_dynamic-update-slice_fusion.here), channel_id=1, source_target_pairs={{0,24},{4,28},{8,16},{12,20},{16,8},{20,12},{24,0},{28,4},{1,25},{... | collective-permute-start | bytes 30728 | tf_op jit(solution)/shard_map/ppermute | solution.py:250
  93.8 5.0 %collective-permute-start.32 = (f32[20,128]{1,0:T(8,128)S(1)}, f32[20,128]{1,0:T(8,128)S(1)}, u32[]{:S(2)}, u32[]{:S(2)}) collective-permute-start(f32[20,128]{1,0:T(8,128)S(1)} %constant_dynamic-update-slice_fusion.here), channel_id=1, source_target_pairs={{0,16},{4,20},{8,24},{12,28},{16,0},{20,4},{24,8},{28,12},{1,17},{... | collective-permute-start | bytes 30728 | tf_op jit(solution)/shard_map/ppermute | solution.py:250
  95.1 3.8 %collective-permute-start.31 = (f32[20,128]{1,0:T(8,128)S(1)}, f32[20,128]{1,0:T(8,128)S(1)}, u32[]{:S(2)}, u32[]{:S(2)}) collective-permute-start(f32[20,128]{1,0:T(8,128)S(1)} %constant_dynamic-update-slice_fusion.here), channel_id=1, source_target_pairs={{0,8},{4,12},{8,0},{12,4},{16,24},{20,28},{24,16},{28,20},{1,9},{5... | collective-permute-start | bytes 30728 | tf_op jit(solution)/shard_map/ppermute | solution.py:250
  98.2 1.5 %collective-permute-start.28 = (bf16[160,512]{1,0:T(8,128)(2,1)S(1)}, bf16[160,512]{1,0:T(8,128)(2,1)S(1)}, u32[]{:S(2)}, u32[]{:S(2)}) collective-permute-start(bf16[160,512]{1,0:T(8,128)(2,1)S(1)} %get-tuple-element.131), channel_id=1, source_target_pairs={{0,4},{4,0},{8,12},{12,8},{16,20},{20,16},{24,28},{28,24},{1,5},{5... | collective-permute-start | bytes 491528 | tf_op jit(solution)/shard_map/ppermute | solution.py:250
  98.3 1.6 %collective-permute-start.29 = (bf16[160,512]{1,0:T(8,128)(2,1)S(1)}, bf16[160,512]{1,0:T(8,128)(2,1)S(1)}, u32[]{:S(2)}, u32[]{:S(2)}) collective-permute-start(bf16[160,512]{1,0:T(8,128)(2,1)S(1)} %get-tuple-element.132), channel_id=1, source_target_pairs={{0,4},{4,0},{8,12},{12,8},{16,20},{20,16},{24,28},{28,24},{1,5},{5... | collective-permute-start | bytes 491528 | tf_op jit(solution)/shard_map/ppermute | solution.py:250
  98.8 1.4 %collective-permute-start.30 = (bf16[192,512]{1,0:T(8,128)(2,1)S(1)}, bf16[192,512]{1,0:T(8,128)(2,1)S(1)}, u32[]{:S(2)}, u32[]{:S(2)}) collective-permute-start(bf16[192,512]{1,0:T(8,128)(2,1)S(1)} %get-tuple-element.133), channel_id=1, source_target_pairs={{0,4},{4,0},{8,12},{12,8},{16,20},{20,16},{24,28},{28,24},{1,5},{5... | collective-permute-start | bytes 589832 | tf_op jit(solution)/shard_map/ppermute | solution.py:250

commit v7 on v6

--- a/solution.py
+++ b/solution.py
@@ -173,14 +173,14 @@
         ref[at : at + half] = part.astype(ref.dtype)
 
 
-def first_grad_body(m1, m2, m3, s1, s2, s3, dproj, upper, lower, *outs):
-    dproj_sib = jnp.concatenate([upper[...], lower[...]], axis=0)
+def first_grad_body(m1, m2, m3, s1, s2, s3, dproj, upper, middle, lower, *outs):
+    dproj_sib = jnp.concatenate([upper[...], middle[...], lower[...]], axis=0)
     for chip, mine, sib in ((3, m3, s3), (1, m1, s1), (2, m2, s2)):
         spread(product(mine[...], sib[...], dproj[...], dproj_sib), chip, outs)
 
 
-def second_grad_body(m_a0, m0, m1, m2, m3, s3, rest, dproj, upper, lower, own_a, own_b, *outs):
-    dproj_sib = jnp.concatenate([upper[...], lower[...]], axis=0)
+def second_grad_body(m_a0, m0, m1, m2, m3, s3, rest, dproj, upper, middle, lower, own_a, own_b, *outs):
+    dproj_sib = jnp.concatenate([upper[...], middle[...], lower[...]], axis=0)
     half = m0.shape[1]
     own_a[...] = product(m_a0[...], rest[:, :half], dproj[...], dproj_sib)
     for chip, mine in ((3, m3), (1, m1), (2, m2), (0, m0)):
@@ -259,7 +259,7 @@
     odd, at, key_weight, hidden_in, key_cotangent, segment_ids = after(
         (odd, at, key_weight, hidden_in, key_cotangent, segment_ids)
     )
-    early = half + own*17//64
+    early = half + own * 3 // 16
     late = own - early
     w_x, w_y = px(key_weight[late:]), py(key_weight[:early])
 
@@ -267,8 +267,9 @@
     mine_a, mine_b, (s_a3, s_a1, s_a2, s_b3, rest) = parts[:4], parts[4:8], parts[8:13]
     cosine, sine, dproj, my_gain = parts[13:]
     my_gain = my_gain.reshape(own)
-    n = tok // 2
-    dproj_sib = core(dproj[:n]), core(dproj[n:])
+    third = tok // 48 * 16
+    cuts = (0, third, 2 * third, tok)
+    dproj_sib = [core(dproj[i:j]) for i, j in zip(cuts[:-1], cuts[1:], strict=True)]
     s_a3, s_a1, s_a2 = core(s_a3), core(s_a1), core(s_a2)
 
     def part_shapes(h):

time: 103 us -> 102 us (level)
  waiting for transfers between devices: 48 us -> 45.3 us
    ppermute x26 -> x27, waiting for transfers between devices: 32.7 us -> 22 us  [over(): return lambda v: lax.ppermute(v, 'blk', [(i, i ^ bit) for i in range(8)])]
    ppermute x8, waiting for transfers between devices: 15.3 us -> 23.3 us  [over_z(): return lambda v: lax.ppermute(v, 'dp', [(i, i ^ bit) for i in range(4)])]
    ppermute x26 -> x27, starting transfers between devices: 19 us -> 19.5 us  [over(): return lambda v: lax.ppermute(v, 'blk', [(i, i ^ bit) for i in range(8)])]
  transfers between devices with their start and end apart: 34 -> 35, of which waited for: 24 -> 19; matrix products, arithmetic and copies ran while one was open for 2% -> 2% of each run, Pallas kernels for 18% -> 19%
where the time goes in v7:
time: 102 us
  waiting for transfers between devices  45.3 us (44%)
  starting transfers between devices  30 us (29%)
  Pallas kernels  19 us (19%)
  other arithmetic  3.88 us (4%)
  local copies, waits for them, and re-layouts  2.57 us (3%)
    ppermute x8, waiting for transfers between devices, over_z(): return lambda v: lax.ppermute(v, 'dp', [(i, i ^ bit) for i in range(4)])  23.3 us
    ppermute x27, waiting for transfers between devices, over(): return lambda v: lax.ppermute(v, 'blk', [(i, i ^ bit) for i in range(8)])  22 us
    ppermute x27, starting transfers between devices, over(): return lambda v: lax.ppermute(v, 'blk', [(i, i ^ bit) for i in range(8)])  19.5 us
    ppermute x8, starting transfers between devices, over_z(): return lambda v: lax.ppermute(v, 'dp', [(i, i ^ bit) for i in range(4)])  10.4 us
    pallas_call x1, Pallas kernels, prepared(): pl.pallas_call(functools.partial(prepare_body, segs.shape[1] // step), gr...  7.75 us
    pallas_call x2, Pallas kernels, forward(): call(functools.partial(forward_body, places, len(acts), len(init)), [shap...  4.66 us
    pallas_call x1, Pallas kernels, by_permutes(): call(second_grad_body, [own_shape, own_shape, *part_shapes(quarter)], 'gr...  2.93 us
  transfers between devices with their start and end apart: 35, of which 19 were waited for; matrix products, arithmetic and copies ran while one was open for 2% of the time, Pallas kernels for 19%

profile of v7, /device:TPU:0, one launch (start us, length us, event | category | flops | bytes accessed | tf_op | source)
XLA Modules:
  0.0 101.6 jit_solution(9413629677281480883)
XLA Ops:
  0.6 1.4 %fusion.2 = (bf16[704,512]{1,0:T(8,128)(2,1)S(1)}, bf16[704,512]{1,0:T(8,128)(2,1)S(1)}) fusion(bf16[1024,512]{1,0:T(8,128)(2,1)} %refs_6_), kind=kLoop, calls=%fused_computation.37 | loop fusion | bytes 2883584 | tf_op jit(solution)/shard_map/slice | solution.py:264
  2.1 3.0 %collective-permute-start.7 = (bf16[704,512]{1,0:T(8,128)(2,1)S(1)}, bf16[704,512]{1,0:T(8,128)(2,1)S(1)}, u32[]{:S(2)}, u32[]{:S(2)}) collective-permute-start(bf16[704,512]{1,0:T(8,128)(2,1)S(1)} %get-tuple-element.152), channel_id=1, source_target_pairs={{0,16},{4,20},{8,24},{12,28},{16,0},{20,4},{24,8},{28,12},{1,17},{... | collective-permute-start | bytes 2162696 | tf_op jit(solution)/shard_map/ppermute | solution.py:250
  5.1 1.5 %collective-permute-start.6 = (bf16[704,512]{1,0:T(8,128)(2,1)S(1)}, bf16[704,512]{1,0:T(8,128)(2,1)S(1)}, u32[]{:S(2)}, u32[]{:S(2)}) collective-permute-start(bf16[704,512]{1,0:T(8,128)(2,1)S(1)} %get-tuple-element.153), channel_id=1, source_target_pairs={{0,8},{4,12},{8,0},{12,4},{16,24},{20,28},{24,16},{28,20},{1,9},{5... | collective-permute-start | bytes 2162696 | tf_op jit(solution)/shard_map/ppermute | solution.py:250
  6.6 7.7 %prepare.1 = (bf16[512,512]{1,0:T(8,128)(2,1)S(1)}, bf16[512,512]{1,0:T(8,128)(2,1)S(1)}, bf16[512,512]{1,0:T(8,128)(2,1)S(1)}, bf16[512,512]{1,0:T(8,128)(2,1)S...) custom-call(s32[1]{0:T(128)} %bitcast.at_ref, ...), custom_call_target="tpu_custom_call" | custom-call | flops 1 | bytes 1 | tf_op jit(solution)/shard_map/prepare/pallas_call | solution.py:131
  14.5 0.6 collective-permute-start.4
  15.1 1.0 collective-permute-done.4.middle
  16.9 1.1 %collective-permute-done.s1.refs_6_ = bf16[512,512]{1,0:T(8,128)(2,1)S(1)} collective-permute-done((bf16[512,512]{1,0:T(8,128)(2,1)S(1)}, bf16[512,512]{1,0:T(8,128)(2,1)S(1)}, u32[]{:S(2)}, u32[]{:S(2)}) %collective-permute-start) | collective-permute-done | bytes 524320 | tf_op jit(solution)/shard_map/ppermute | solution.py:250
  18.0 0.7 collective-permute-done.1.s2.refs_4_
  18.8 0.7 collective-permute-done.2.s3.refs_4_
  19.5 1.8 %grad_a.1 = (bf16[512,512]{1,0:T(8,128)(2,1)S(1)}, bf16[512,512]{1,0:T(8,128)(2,1)S(1)}, bf16[256,512]{1,0:T(8,128)(2,1)S(1)}, bf16[256,512]{1,0:T(8,128)(2,1)S(1)}) custom-call(bf16[512,512]{1,0:T(8,128)(2,1)S(1)} %get-tuple-element.86.m1.refs_2_, bf16[512,512]{1,0:T(8,128)(2,1)S(1)} %get-tuple-element.87.m2.refs_2_, ...), custom_call_target="tpu_custom_call" | custom-call | flops 1 | bytes 1 | tf_op jit(solution)/shard_map/grad_a/pallas_call | solution.py:306
  21.4 1.3 %collective-permute-done.6.refs_8_.refs_13_ = bf16[704,512]{1,0:T(8,128)(2,1)S(1)} collective-permute-done((bf16[704,512]{1,0:T(8,128)(2,1)S(1)}, bf16[704,512]{1,0:T(8,128)(2,1)S(1)}, u32[]{:S(2)}, u32[]{:S(2)}) %collective-permute-start.6) | collective-permute-done | bytes 720928 | tf_op jit(solution)/shard_map/ppermute | solution.py:250
  22.7 0.5 collective-permute-start.8
  23.2 1.5 %collective-permute-start.10 = (bf16[512,512]{1,0:T(8,128)(2,1)S(1)}, bf16[512,512]{1,0:T(8,128)(2,1)S(1)}, u32[]{:S(2)}, u32[]{:S(2)}) collective-permute-start(bf16[512,512]{1,0:T(8,128)(2,1)S(1)} %get-tuple-element.103), channel_id=1, source_target_pairs={{0,8},{4,12},{8,0},{12,4},{16,24},{20,28},{24,16},{28,20},{1,9},{5... | collective-permute-start | bytes 1572872 | tf_op jit(solution)/shard_map/ppermute | solution.py:250
  24.7 0.5 collective-permute-start.11
  25.2 2.4 %collective-permute-done.8.s3.refs_5_ = bf16[512,512]{1,0:T(8,128)(2,1)S(1)} collective-permute-done((bf16[512,512]{1,0:T(8,128)(2,1)S(1)}, bf16[512,512]{1,0:T(8,128)(2,1)S(1)}, u32[]{:S(2)}, u32[]{:S(2)}) %collective-permute-start.8) | collective-permute-done | bytes 524320 | tf_op jit(solution)/shard_map/ppermute | solution.py:250
  27.6 2.9 %grad_b.1 = (f32[512,512]{1,0:T(8,128)S(1)}, f32[512,512]{1,0:T(8,128)S(1)}, bf16[512,512]{1,0:T(8,128)(2,1)S(1)}, bf16[512,512]{1,0:T(8,128)(2,1)S(1)}, bf16[25...) custom-call(bf16[512,512]{1,0:T(8,128)(2,1)S(1)} %get-tuple-element.79.m_a0.refs_0_, ...), custom_call_target="tpu_custom_call" | custom-call | flops 1 | bytes 1 | tf_op jit(solution)/shard_map/grad_b/pallas_call | solution.py:314
  30.6 2.3 %forward.2 = (f32[512,512]{1,0:T(8,128)S(1)}, f32[512,512]{1,0:T(8,128)S(1)}) custom-call(bf16[512,512]{1,0:T(8,128)(2,1)S(1)} %get-tuple-element.79.m_a0.refs_0_, bf16[512,512]{1,0:T(8,128)(2,1)S(1)} %get-tuple-element.80.m0.refs_1_, bf16[512,512]{1,0:T(8,128)(2,1)S(1)} %get-tuple-element.87.m2.refs_2_, bf16[512,512]{1,0:T(8,128)(2,1)S(1)} %get-tuple-element.81.m1.refs_3_, ...), custom_call_target="tpu_custom_call" | custom-call | flops 1 | bytes 1 | tf_op jit(solution)/shard_map/forward/pallas_call | solution.py:223
  32.9 4.2 %collective-permute-done.10 = bf16[512,512]{1,0:T(8,128)(2,1)S(1)} collective-permute-done((bf16[512,512]{1,0:T(8,128)(2,1)S(1)}, bf16[512,512]{1,0:T(8,128)(2,1)S(1)}, u32[]{:S(2)}, u32[]{:S(2)}) %collective-permute-start.10) | collective-permute-done | bytes 524320 | tf_op jit(solution)/shard_map/ppermute | solution.py:250
  37.0 1.2 %collective-permute-done.11 = bf16[512,512]{1,0:T(8,128)(2,1)S(1)} collective-permute-done((bf16[512,512]{1,0:T(8,128)(2,1)S(1)}, bf16[512,512]{1,0:T(8,128)(2,1)S(1)}, u32[]{:S(2)}, u32[]{:S(2)}) %collective-permute-start.11) | collective-permute-done | bytes 524320 | tf_op jit(solution)/shard_map/ppermute | solution.py:250
  38.4 0.6 collective-permute-start.15
  39.5 1.6 %collective-permute-start.12 = (bf16[512,512]{1,0:T(8,128)(2,1)S(1)}, bf16[512,512]{1,0:T(8,128)(2,1)S(1)}, u32[]{:S(2)}, u32[]{:S(2)}) collective-permute-start(bf16[512,512]{1,0:T(8,128)(2,1)S(1)} %get-tuple-element.112), channel_id=1, source_target_pairs={{0,8},{4,12},{8,0},{12,4},{16,24},{20,28},{24,16},{28,20},{1,9},{5... | collective-permute-start | bytes 1572872 | tf_op jit(solution)/shard_map/ppermute | solution.py:250
  41.2 1.5 %collective-permute-start.13 = (bf16[512,512]{1,0:T(8,128)(2,1)S(1)}, bf16[512,512]{1,0:T(8,128)(2,1)S(1)}, u32[]{:S(2)}, u32[]{:S(2)}) collective-permute-start(bf16[512,512]{1,0:T(8,128)(2,1)S(1)} %get-tuple-element.113), channel_id=1, source_target_pairs={{0,16},{4,20},{8,24},{12,28},{16,0},{20,4},{24,8},{28,12},{1,17},{... | collective-permute-start | bytes 1572872 | tf_op jit(solution)/shard_map/ppermute | solution.py:250
  42.7 5.0 %collective-permute-done.15 = bf16[256,512]{1,0:T(8,128)(2,1)S(1)} collective-permute-done((bf16[256,512]{1,0:T(8,128)(2,1)S(1)}, bf16[256,512]{1,0:T(8,128)(2,1)S(1)}, u32[]{:S(2)}, u32[]{:S(2)}) %collective-permute-start.15) | collective-permute-done | bytes 262176 | tf_op jit(solution)/shard_map/ppermute | solution.py:250
  47.7 0.5 collective-permute-done.14
  48.5 1.6 %collective-permute-start.18 = (bf16[256,512]{1,0:T(8,128)(2,1)S(1)}, bf16[256,512]{1,0:T(8,128)(2,1)S(1)}, u32[]{:S(2)}, u32[]{:S(2)}) collective-permute-start(bf16[256,512]{1,0:T(8,128)(2,1)S(1)} %select_convert_fusion.1), channel_id=1, source_target_pairs={{0,1},{1,0},{2,3},{3,2},{4,5},{5,4},{6,7},{7,6},{8,9},{9,8},{10,11... | collective-permute-start | bytes 786440 | tf_op jit(solution)/shard_map/ppermute | solution.py:291
  50.3 7.3 %collective-permute-done.18 = bf16[256,512]{1,0:T(8,128)(2,1)S(1)} collective-permute-done((bf16[256,512]{1,0:T(8,128)(2,1)S(1)}, bf16[256,512]{1,0:T(8,128)(2,1)S(1)}, u32[]{:S(2)}, u32[]{:S(2)}) %collective-permute-start.18) | collective-permute-done | bytes 262176 | tf_op jit(solution)/shard_map/ppermute | solution.py:291
  57.9 2.7 %collective-permute-start.19 = (bf16[256,512]{1,0:T(8,128)(2,1)S(1)}, bf16[256,512]{1,0:T(8,128)(2,1)S(1)}, u32[]{:S(2)}, u32[]{:S(2)}) collective-permute-start(bf16[256,512]{1,0:T(8,128)(2,1)S(1)} %add_convert_fusion.3), channel_id=1, source_target_pairs={{0,2},{1,3},{2,0},{3,1},{4,6},{5,7},{6,4},{7,5},{8,10},{9,11},{10,... | collective-permute-start | bytes 786440 | tf_op jit(solution)/shard_map/ppermute | solution.py:291
  60.7 1.5 %collective-permute-start.17 = (bf16[256,512]{1,0:T(8,128)(2,1)S(1)}, bf16[256,512]{1,0:T(8,128)(2,1)S(1)}, u32[]{:S(2)}, u32[]{:S(2)}) collective-permute-start(bf16[256,512]{1,0:T(8,128)(2,1)S(1)} %add_convert_fusion.4), channel_id=1, source_target_pairs={{0,8},{4,12},{8,0},{12,4},{16,24},{20,28},{24,16},{28,20},{1,9},{5... | collective-permute-start | bytes 786440 | tf_op jit(solution)/shard_map/ppermute | solution.py:250
  62.3 0.5 collective-permute-start.16
  62.8 5.3 %collective-permute-done.19 = bf16[256,512]{1,0:T(8,128)(2,1)S(1)} collective-permute-done((bf16[256,512]{1,0:T(8,128)(2,1)S(1)}, bf16[256,512]{1,0:T(8,128)(2,1)S(1)}, u32[]{:S(2)}, u32[]{:S(2)}) %collective-permute-start.19) | collective-permute-done | bytes 262176 | tf_op jit(solution)/shard_map/ppermute | solution.py:291
  68.1 1.9 %collective-permute-done.16 = bf16[256,512]{1,0:T(8,128)(2,1)S(1)} collective-permute-done((bf16[256,512]{1,0:T(8,128)(2,1)S(1)}, bf16[256,512]{1,0:T(8,128)(2,1)S(1)}, u32[]{:S(2)}, u32[]{:S(2)}) %collective-permute-start.16) | collective-permute-done | bytes 262176 | tf_op jit(solution)/shard_map/ppermute | solution.py:250
  70.4 0.9 collective-permute-start.20
  71.3 1.0 slice-done
  72.5 0.5 collective-permute-start.27
  73.5 1.3 %collective-permute-start.21 = (f32[12,128]{1,0:T(8,128)S(1)}, f32[12,128]{1,0:T(8,128)S(1)}, u32[]{:S(2)}, u32[]{:S(2)}) collective-permute-start(f32[12,128]{1,0:T(8,128)S(1)} %maximum_bitcast_fusion), channel_id=1, source_target_pairs={{0,1},{1,0},{2,3},{3,2},{4,5},{5,4},{6,7},{7,6},{8,9},{9,8},{10,11... | collective-permute-start | bytes 18440 | tf_op jit(solution)/shard_map/ppermute | solution.py:291
  74.9 0.7 collective-permute-start.23
  75.6 4.1 %collective-permute-done.21 = f32[12,128]{1,0:T(8,128)S(1)} collective-permute-done((f32[12,128]{1,0:T(8,128)S(1)}, f32[12,128]{1,0:T(8,128)S(1)}, u32[]{:S(2)}, u32[]{:S(2)}) %collective-permute-start.21) | collective-permute-done | bytes 6176 | tf_op jit(solution)/shard_map/ppermute | solution.py:291
  79.9 2.9 %collective-permute-start.24 = (f32[12,128]{1,0:T(8,128)S(1)}, f32[12,128]{1,0:T(8,128)S(1)}, u32[]{:S(2)}, u32[]{:S(2)}) collective-permute-start(f32[12,128]{1,0:T(8,128)S(1)} %fusion), channel_id=1, source_target_pairs={{0,2},{1,3},{2,0},{3,1},{4,6},{5,7},{6,4},{7,5},{8,10},{9,11},{10,... | collective-permute-start | bytes 18440 | tf_op jit(solution)/shard_map/ppermute | solution.py:291
  82.8 6.6 %collective-permute-done.24 = f32[12,128]{1,0:T(8,128)S(1)} collective-permute-done((f32[12,128]{1,0:T(8,128)S(1)}, f32[12,128]{1,0:T(8,128)S(1)}, u32[]{:S(2)}, u32[]{:S(2)}) %collective-permute-start.24) | collective-permute-done | bytes 6176 | tf_op jit(solution)/shard_map/ppermute | solution.py:291
  89.5 1.1 %collective-permute-done.25 = f32[8,128]{1,0:T(8,128)S(1)} collective-permute-done((f32[8,128]{1,0:T(8,128)S(1)}, f32[8,128]{1,0:T(8,128)S(1)}, u32[]{:S(2)}, u32[]{:S(2)}) %collective-permute-start.25) | collective-permute-done | bytes 4128 | tf_op jit(solution)/shard_map/ppermute | solution.py:250
  90.8 1.4 %collective-permute-start.34 = (f32[20,128]{1,0:T(8,128)S(1)}, f32[20,128]{1,0:T(8,128)S(1)}, u32[]{:S(2)}, u32[]{:S(2)}) collective-permute-start(f32[20,128]{1,0:T(8,128)S(1)} %constant_dynamic-update-slice_fusion.here), channel_id=1, source_target_pairs={{0,24},{4,28},{8,16},{12,20},{16,8},{20,12},{24,0},{28,4},{1,25},{... | collective-permute-start | bytes 30728 | tf_op jit(solution)/shard_map/ppermute | solution.py:250
  92.2 0.8 collective-permute-start.33
  93.0 1.4 %collective-permute-start.32 = (f32[20,128]{1,0:T(8,128)S(1)}, f32[20,128]{1,0:T(8,128)S(1)}, u32[]{:S(2)}, u32[]{:S(2)}) collective-permute-start(f32[20,128]{1,0:T(8,128)S(1)} %constant_dynamic-update-slice_fusion.here), channel_id=1, source_target_pairs={{0,8},{4,12},{8,0},{12,4},{16,24},{20,28},{24,16},{28,20},{1,9},{5... | collective-permute-start | bytes 30728 | tf_op jit(solution)/shard_map/ppermute | solution.py:250
  94.4 2.3 %forward.3 = (f32[512,512]{1,0:T(8,128)S(1)}, bf16[160,512]{1,0:T(8,128)(2,1)S(1)}, bf16[160,512]{1,0:T(8,128)(2,1)S(1)}, bf16[192,512]{1,0:T(8,128)(2,1)S(1)}) custom-call(bf16[512,512]{1,0:T(8,128)(2,1)S(1)} %get-tuple-element.88.m3.refs_0_, bf16[512,512]{1,0:T(8,128)(2,1)S(1)} %get-tuple-element.83.m3.refs_1_, ...), custom_call_target="tpu_custom_call" | custom-call | flops 1 | bytes 1 | tf_op jit(solution)/shard_map/forward/pallas_call | solution.py:223
  96.8 0.5 collective-permute-start.30
  97.5 0.6 collect.1
  98.8 1.2 %keys.1 = bf16[512,512]{1,0:T(8,128)(2,1)} custom-call(f32[512,512]{1,0:T(8,128)S(1)} %get-tuple-element.130.here, bf16[160,512]{1,0:T(8,128)(2,1)S(1)} %collective-permute-done.29.upper, bf16[160,512]{1,0:T(8,128)(2,1)S(1)} %collective-permute-done.30.middle, bf16[192,512]{1,0:T(8,128)(2,1)S(1)} %collective-permute-done.31.lower, f32[1,512]{1,0:T(1,128)S(1)} %bitcast.11, ...), custom_call_target="tpu_custom_call" | custom-call | flops 1 | bytes 1 | tf_op jit(solution)/shard_map/keys/pallas_call | solution.py:377
  100.0 1.6 %convert_multiply_fusion = f32[1024,512]{1,0:T(8,128)} fusion(bf16[256,512]{1,0:T(8,128)(2,1)S(1)} %get-tuple-element.157, bf16[256,512]{1,0:T(8,128)(2,1)S(1)} %get-tuple-element.156, bf16[256,512]{1,0:T(8,128)(2,1)S(1)} %get-tuple-element.155, bf16[256,512]{1,0:T(8,128)(2,1)S(1)} %get-tuple-element.154), kind=kLoop, calls=%fused_computation | loop fusion | flops 4718592 | bytes 3145728 | tf_op jit(solution)/shard_map/mul | solution.py:395
  (80 shorter events, 4.9 us)
Async XLA Ops:
  2.1 19.3 %collective-permute-start.7 = (bf16[704,512]{1,0:T(8,128)(2,1)S(1)}, bf16[704,512]{1,0:T(8,128)(2,1)S(1)}, u32[]{:S(2)}, u32[]{:S(2)}) collective-permute-start(bf16[704,512]{1,0:T(8,128)(2,1)S(1)} %get-tuple-element.152), channel_id=1, source_target_pairs={{0,16},{4,20},{8,24},{12,28},{16,0},{20,4},{24,8},{28,12},{1,17},{... | collective-permute-start | bytes 2162696 | tf_op jit(solution)/shard_map/ppermute | solution.py:250
  5.1 17.6 %collective-permute-start.6 = (bf16[704,512]{1,0:T(8,128)(2,1)S(1)}, bf16[704,512]{1,0:T(8,128)(2,1)S(1)}, u32[]{:S(2)}, u32[]{:S(2)}) collective-permute-start(bf16[704,512]{1,0:T(8,128)(2,1)S(1)} %get-tuple-element.153), channel_id=1, source_target_pairs={{0,8},{4,12},{8,0},{12,4},{16,24},{20,28},{24,16},{28,20},{1,9},{5... | collective-permute-start | bytes 2162696 | tf_op jit(solution)/shard_map/ppermute | solution.py:250
  14.4 2.3 %collective-permute-start.5 = (bf16[192,512]{1,0:T(8,128)(2,1)S(1)}, bf16[192,512]{1,0:T(8,128)(2,1)S(1)}, u32[]{:S(2)}, u32[]{:S(2)}) collective-permute-start(bf16[192,512]{1,0:T(8,128)(2,1)S(1)} %slice.83), channel_id=1, source_target_pairs={{0,4},{4,0},{8,12},{12,8},{16,20},{20,16},{24,28},{28,24},{1,5},{5... | collective-permute-start | bytes 589832 | tf_op jit(solution)/shard_map/ppermute | solution.py:250
  14.5 1.6 %collective-permute-start.4 = (bf16[160,512]{1,0:T(8,128)(2,1)S(1)}, bf16[160,512]{1,0:T(8,128)(2,1)S(1)}, u32[]{:S(2)}, u32[]{:S(2)}) collective-permute-start(bf16[160,512]{1,0:T(8,128)(2,1)S(1)} %get-tuple-element.158), channel_id=1, source_target_pairs={{0,4},{4,0},{8,12},{12,8},{16,20},{20,16},{24,28},{28,24},{1,5},{5... | collective-permute-start | bytes 491528 | tf_op jit(solution)/shard_map/ppermute | solution.py:250
  15.0 1.4 %collective-permute-start.3 = (bf16[160,512]{1,0:T(8,128)(2,1)S(1)}, bf16[160,512]{1,0:T(8,128)(2,1)S(1)}, u32[]{:S(2)}, u32[]{:S(2)}) collective-permute-start(bf16[160,512]{1,0:T(8,128)(2,1)S(1)} %get-tuple-element.159), channel_id=1, source_target_pairs={{0,4},{4,0},{8,12},{12,8},{16,20},{20,16},{24,28},{28,24},{1,5},{5... | collective-permute-start | bytes 491528 | tf_op jit(solution)/shard_map/ppermute | solution.py:250
  16.1 1.9 %collective-permute-start = (bf16[512,512]{1,0:T(8,128)(2,1)S(1)}, bf16[512,512]{1,0:T(8,128)(2,1)S(1)}, u32[]{:S(2)}, u32[]{:S(2)}) collective-permute-start(bf16[512,512]{1,0:T(8,128)(2,1)S(1)} %get-tuple-element.89), channel_id=1, source_target_pairs={{0,4},{4,0},{8,12},{12,8},{16,20},{20,16},{24,28},{28,24},{1,5},{5... | collective-permute-start | bytes 1572872 | tf_op jit(solution)/shard_map/ppermute | solution.py:250
  16.4 2.3 %collective-permute-start.1 = (bf16[512,512]{1,0:T(8,128)(2,1)S(1)}, bf16[512,512]{1,0:T(8,128)(2,1)S(1)}, u32[]{:S(2)}, u32[]{:S(2)}) collective-permute-start(bf16[512,512]{1,0:T(8,128)(2,1)S(1)} %get-tuple-element.90), channel_id=1, source_target_pairs={{0,4},{4,0},{8,12},{12,8},{16,20},{20,16},{24,28},{28,24},{1,5},{5... | collective-permute-start | bytes 1572872 | tf_op jit(solution)/shard_map/ppermute | solution.py:250
  16.7 2.9 %collective-permute-start.2 = (bf16[512,512]{1,0:T(8,128)(2,1)S(1)}, bf16[512,512]{1,0:T(8,128)(2,1)S(1)}, u32[]{:S(2)}, u32[]{:S(2)}) collective-permute-start(bf16[512,512]{1,0:T(8,128)(2,1)S(1)} %get-tuple-element.91), channel_id=1, source_target_pairs={{0,4},{4,0},{8,12},{12,8},{16,20},{20,16},{24,28},{28,24},{1,5},{5... | collective-permute-start | bytes 1572872 | tf_op jit(solution)/shard_map/ppermute | solution.py:250
  21.4 49.9 %copy-start.1 = (bf16[704,512]{1,0:T(8,128)(2,1)}, bf16[704,512]{1,0:T(8,128)(2,1)S(1)}, u32[]{:S(2)}) copy-start(bf16[704,512]{1,0:T(8,128)(2,1)S(1)} %collective-permute-done.7.refs_7_.refs_12_) | copy-start | bytes 2162692
  22.7 48.6 %copy-start.3 = (bf16[704,512]{1,0:T(8,128)(2,1)}, bf16[704,512]{1,0:T(8,128)(2,1)S(1)}, u32[]{:S(2)}) copy-start(bf16[704,512]{1,0:T(8,128)(2,1)S(1)} %collective-permute-done.6.refs_8_.refs_13_) | copy-start | bytes 2162692
  22.7 4.9 %collective-permute-start.9 = (bf16[512,2048]{1,0:T(8,128)(2,1)S(1)}, bf16[512,2048]{1,0:T(8,128)(2,1)S(1)}, u32[]{:S(2)}, u32[]{:S(2)}) collective-permute-start(bf16[512,2048]{1,0:T(8,128)(2,1)S(1)} %get-tuple-element.99), channel_id=1, source_target_pairs={{0,4},{4,0},{8,12},{12,8},{16,20},{20,16},{24,28},{28,24},{1,5},{5... | collective-permute-start | bytes 6291464 | tf_op jit(solution)/shard_map/ppermute | solution.py:250
  22.7 4.9 %collective-permute-start.8 = (bf16[512,512]{1,0:T(8,128)(2,1)S(1)}, bf16[512,512]{1,0:T(8,128)(2,1)S(1)}, u32[]{:S(2)}, u32[]{:S(2)}) collective-permute-start(bf16[512,512]{1,0:T(8,128)(2,1)S(1)} %get-tuple-element.98), channel_id=1, source_target_pairs={{0,4},{4,0},{8,12},{12,8},{16,20},{20,16},{24,28},{28,24},{1,5},{5... | collective-permute-start | bytes 1572872 | tf_op jit(solution)/shard_map/ppermute | solution.py:250
  23.2 13.8 %collective-permute-start.10 = (bf16[512,512]{1,0:T(8,128)(2,1)S(1)}, bf16[512,512]{1,0:T(8,128)(2,1)S(1)}, u32[]{:S(2)}, u32[]{:S(2)}) collective-permute-start(bf16[512,512]{1,0:T(8,128)(2,1)S(1)} %get-tuple-element.103), channel_id=1, source_target_pairs={{0,8},{4,12},{8,0},{12,4},{16,24},{20,28},{24,16},{28,20},{1,9},{5... | collective-permute-start | bytes 1572872 | tf_op jit(solution)/shard_map/ppermute | solution.py:250
  24.7 13.6 %collective-permute-start.11 = (bf16[512,512]{1,0:T(8,128)(2,1)S(1)}, bf16[512,512]{1,0:T(8,128)(2,1)S(1)}, u32[]{:S(2)}, u32[]{:S(2)}) collective-permute-start(bf16[512,512]{1,0:T(8,128)(2,1)S(1)} %get-tuple-element.104), channel_id=1, source_target_pairs={{0,16},{4,20},{8,24},{12,28},{16,0},{20,4},{24,8},{28,12},{1,17},{... | collective-permute-start | bytes 1572872 | tf_op jit(solution)/shard_map/ppermute | solution.py:250
  27.6 2.9 %copy-start = (bf16[1024,512]{1,0:T(8,128)(2,1)S(1)}, bf16[1024,512]{1,0:T(8,128)(2,1)}, u32[]{:S(2)}) copy-start(bf16[1024,512]{1,0:T(8,128)(2,1)} %refs_6_) | copy-start | bytes 3145732
  38.4 9.3 %collective-permute-start.15 = (bf16[256,512]{1,0:T(8,128)(2,1)S(1)}, bf16[256,512]{1,0:T(8,128)(2,1)S(1)}, u32[]{:S(2)}, u32[]{:S(2)}) collective-permute-start(bf16[256,512]{1,0:T(8,128)(2,1)S(1)} %add_convert_fusion.6), channel_id=1, source_target_pairs={{0,8},{4,12},{8,0},{12,4},{16,24},{20,28},{24,16},{28,20},{1,9},{5... | collective-permute-start | bytes 786440 | tf_op jit(solution)/shard_map/ppermute | solution.py:250
  39.0 9.2 %collective-permute-start.14 = (bf16[256,512]{1,0:T(8,128)(2,1)S(1)}, bf16[256,512]{1,0:T(8,128)(2,1)S(1)}, u32[]{:S(2)}, u32[]{:S(2)}) collective-permute-start(bf16[256,512]{1,0:T(8,128)(2,1)S(1)} %add_convert_fusion.7), channel_id=1, source_target_pairs={{0,16},{4,20},{8,24},{12,28},{16,0},{20,4},{24,8},{28,12},{1,17},{... | collective-permute-start | bytes 786440 | tf_op jit(solution)/shard_map/ppermute | solution.py:250
  39.5 21.1 %collective-permute-start.12 = (bf16[512,512]{1,0:T(8,128)(2,1)S(1)}, bf16[512,512]{1,0:T(8,128)(2,1)S(1)}, u32[]{:S(2)}, u32[]{:S(2)}) collective-permute-start(bf16[512,512]{1,0:T(8,128)(2,1)S(1)} %get-tuple-element.112), channel_id=1, source_target_pairs={{0,8},{4,12},{8,0},{12,4},{16,24},{20,28},{24,16},{28,20},{1,9},{5... | collective-permute-start | bytes 1572872 | tf_op jit(solution)/shard_map/ppermute | solution.py:250
  41.2 19.4 %collective-permute-start.13 = (bf16[512,512]{1,0:T(8,128)(2,1)S(1)}, bf16[512,512]{1,0:T(8,128)(2,1)S(1)}, u32[]{:S(2)}, u32[]{:S(2)}) collective-permute-start(bf16[512,512]{1,0:T(8,128)(2,1)S(1)} %get-tuple-element.113), channel_id=1, source_target_pairs={{0,16},{4,20},{8,24},{12,28},{16,0},{20,4},{24,8},{28,12},{1,17},{... | collective-permute-start | bytes 1572872 | tf_op jit(solution)/shard_map/ppermute | solution.py:250
  48.5 9.1 %collective-permute-start.18 = (bf16[256,512]{1,0:T(8,128)(2,1)S(1)}, bf16[256,512]{1,0:T(8,128)(2,1)S(1)}, u32[]{:S(2)}, u32[]{:S(2)}) collective-permute-start(bf16[256,512]{1,0:T(8,128)(2,1)S(1)} %select_convert_fusion.1), channel_id=1, source_target_pairs={{0,1},{1,0},{2,3},{3,2},{4,5},{5,4},{6,7},{7,6},{8,9},{9,8},{10,11... | collective-permute-start | bytes 786440 | tf_op jit(solution)/shard_map/ppermute | solution.py:291
  57.9 10.2 %collective-permute-start.19 = (bf16[256,512]{1,0:T(8,128)(2,1)S(1)}, bf16[256,512]{1,0:T(8,128)(2,1)S(1)}, u32[]{:S(2)}, u32[]{:S(2)}) collective-permute-start(bf16[256,512]{1,0:T(8,128)(2,1)S(1)} %add_convert_fusion.3), channel_id=1, source_target_pairs={{0,2},{1,3},{2,0},{3,1},{4,6},{5,7},{6,4},{7,5},{8,10},{9,11},{10,... | collective-permute-start | bytes 786440 | tf_op jit(solution)/shard_map/ppermute | solution.py:291
  60.7 7.4 %collective-permute-start.17 = (bf16[256,512]{1,0:T(8,128)(2,1)S(1)}, bf16[256,512]{1,0:T(8,128)(2,1)S(1)}, u32[]{:S(2)}, u32[]{:S(2)}) collective-permute-start(bf16[256,512]{1,0:T(8,128)(2,1)S(1)} %add_convert_fusion.4), channel_id=1, source_target_pairs={{0,8},{4,12},{8,0},{12,4},{16,24},{20,28},{24,16},{28,20},{1,9},{5... | collective-permute-start | bytes 786440 | tf_op jit(solution)/shard_map/ppermute | solution.py:250
  62.3 7.8 %collective-permute-start.16 = (bf16[256,512]{1,0:T(8,128)(2,1)S(1)}, bf16[256,512]{1,0:T(8,128)(2,1)S(1)}, u32[]{:S(2)}, u32[]{:S(2)}) collective-permute-start(bf16[256,512]{1,0:T(8,128)(2,1)S(1)} %add_convert_fusion.5), channel_id=1, source_target_pairs={{0,16},{4,20},{8,24},{12,28},{16,0},{20,4},{24,8},{28,12},{1,17},{... | collective-permute-start | bytes 786440 | tf_op jit(solution)/shard_map/ppermute | solution.py:250
  70.4 9.3 %collective-permute-start.20 = (bf16[256,512]{1,0:T(8,128)(2,1)S(1)}, bf16[256,512]{1,0:T(8,128)(2,1)S(1)}, u32[]{:S(2)}, u32[]{:S(2)}) collective-permute-start(bf16[256,512]{1,0:T(8,128)(2,1)S(1)} %select_convert_fusion), channel_id=1, source_target_pairs={{0,1},{1,0},{2,3},{3,2},{4,5},{5,4},{6,7},{7,6},{8,9},{9,8},{10,11... | collective-permute-start | bytes 786440 | tf_op jit(solution)/shard_map/ppermute | solution.py:291
  71.3 1.0 %slice-start = ((bf16[704,512]{1,0:T(8,128)(2,1)}), bf16[512,512]{1,0:T(8,128)(2,1)S(1)}, s32[]{:S(2)}) async-start(bf16[704,512]{1,0:T(8,128)(2,1)} %copy-done.1), calls=%async_computation | async-start | bytes 1048576 | tf_op jit(solution)/shard_map/slice | solution.py:339
  71.3 1.2 %slice-start.1 = ((bf16[704,512]{1,0:T(8,128)(2,1)}), bf16[512,512]{1,0:T(8,128)(2,1)S(1)}, s32[]{:S(2)}) async-start(bf16[704,512]{1,0:T(8,128)(2,1)} %copy-done.3), calls=%async_computation.1 | async-start | bytes 1048576 | tf_op jit(solution)/shard_map/slice | solution.py:340
  72.4 18.2 %collective-permute-start.26 = (bf16[832,512]{1,0:T(8,128)(2,1)S(1)}, bf16[832,512]{1,0:T(8,128)(2,1)S(1)}, u32[]{:S(2)}, u32[]{:S(2)}) collective-permute-start(bf16[832,512]{1,0:T(8,128)(2,1)S(1)} %pad_maximum_fusion), channel_id=1, source_target_pairs={{0,8},{4,12},{8,0},{12,4},{16,24},{20,28},{24,16},{28,20},{1,9},{5... | collective-permute-start | bytes 2555912 | tf_op jit(solution)/shard_map/ppermute | solution.py:250
  72.5 18.1 %collective-permute-start.27 = (bf16[832,512]{1,0:T(8,128)(2,1)S(1)}, bf16[832,512]{1,0:T(8,128)(2,1)S(1)}, u32[]{:S(2)}, u32[]{:S(2)}) collective-permute-start(bf16[832,512]{1,0:T(8,128)(2,1)S(1)} %pad_maximum_fusion.1), channel_id=1, source_target_pairs={{0,16},{4,20},{8,24},{12,28},{16,0},{20,4},{24,8},{28,12},{1,17},{... | collective-permute-start | bytes 2555912 | tf_op jit(solution)/shard_map/ppermute | solution.py:250
  73.5 20.9 %copy-start.2 = (bf16[704,512]{1,0:T(8,128)(2,1)S(1)}, bf16[704,512]{1,0:T(8,128)(2,1)}, u32[]{:S(2)}) copy-start(bf16[704,512]{1,0:T(8,128)(2,1)} %copy-done.1) | copy-start | bytes 2162692
  73.5 20.9 %copy-start.4 = (bf16[704,512]{1,0:T(8,128)(2,1)S(1)}, bf16[704,512]{1,0:T(8,128)(2,1)}, u32[]{:S(2)}) copy-start(bf16[704,512]{1,0:T(8,128)(2,1)} %copy-done.3) | copy-start | bytes 2162692
  73.5 6.2 %collective-permute-start.21 = (f32[12,128]{1,0:T(8,128)S(1)}, f32[12,128]{1,0:T(8,128)S(1)}, u32[]{:S(2)}, u32[]{:S(2)}) collective-permute-start(f32[12,128]{1,0:T(8,128)S(1)} %maximum_bitcast_fusion), channel_id=1, source_target_pairs={{0,1},{1,0},{2,3},{3,2},{4,5},{5,4},{6,7},{7,6},{8,9},{9,8},{10,11... | collective-permute-start | bytes 18440 | tf_op jit(solution)/shard_map/ppermute | solution.py:291
  74.9 14.6 %collective-permute-start.23 = (bf16[256,512]{1,0:T(8,128)(2,1)S(1)}, bf16[256,512]{1,0:T(8,128)(2,1)S(1)}, u32[]{:S(2)}, u32[]{:S(2)}) collective-permute-start(bf16[256,512]{1,0:T(8,128)(2,1)S(1)} %add_convert_fusion.2), channel_id=1, source_target_pairs={{0,1},{1,0},{2,3},{3,2},{4,5},{5,4},{6,7},{7,6},{8,9},{9,8},{10,11... | collective-permute-start | bytes 786440 | tf_op jit(solution)/shard_map/ppermute | solution.py:291
  79.9 10.8 %collective-permute-start.22 = (bf16[256,512]{1,0:T(8,128)(2,1)S(1)}, bf16[256,512]{1,0:T(8,128)(2,1)S(1)}, u32[]{:S(2)}, u32[]{:S(2)}) collective-permute-start(bf16[256,512]{1,0:T(8,128)(2,1)S(1)} %add_convert_fusion.1), channel_id=1, source_target_pairs={{0,2},{1,3},{2,0},{3,1},{4,6},{5,7},{6,4},{7,5},{8,10},{9,11},{10,... | collective-permute-start | bytes 786440 | tf_op jit(solution)/shard_map/ppermute | solution.py:291
  79.9 9.5 %collective-permute-start.24 = (f32[12,128]{1,0:T(8,128)S(1)}, f32[12,128]{1,0:T(8,128)S(1)}, u32[]{:S(2)}, u32[]{:S(2)}) collective-permute-start(f32[12,128]{1,0:T(8,128)S(1)} %fusion), channel_id=1, source_target_pairs={{0,2},{1,3},{2,0},{3,1},{4,6},{5,7},{6,4},{7,5},{8,10},{9,11},{10,... | collective-permute-start | bytes 18440 | tf_op jit(solution)/shard_map/ppermute | solution.py:291
  89.5 1.2 %collective-permute-start.25 = (f32[8,128]{1,0:T(8,128)S(1)}, f32[8,128]{1,0:T(8,128)S(1)}, u32[]{:S(2)}, u32[]{:S(2)}) collective-permute-start(f32[8,128]{1,0:T(8,128)S(1)} %slice.108), channel_id=1, source_target_pairs={{0,4},{4,0},{8,12},{12,8},{16,20},{20,16},{24,28},{28,24},{1,5},{5... | collective-permute-start | bytes 12296 | tf_op jit(solution)/shard_map/ppermute | solution.py:250
  90.7 9.2 %collective-permute-start.28 = (bf16[256,512]{1,0:T(8,128)(2,1)S(1)}, bf16[256,512]{1,0:T(8,128)(2,1)S(1)}, u32[]{:S(2)}, u32[]{:S(2)}) collective-permute-start(bf16[256,512]{1,0:T(8,128)(2,1)S(1)} %add_convert_fusion), channel_id=1, source_target_pairs={{0,1},{1,0},{2,3},{3,2},{4,5},{5,4},{6,7},{7,6},{8,9},{9,8},{10,11... | collective-permute-start | bytes 786440 | tf_op jit(solution)/shard_map/ppermute | solution.py:291
  90.8 7.9 %copy-start.5 = (f32[512]{0:T(512)S(1)}, f32[512]{0:T(512)}, u32[]{:S(2)}) copy-start(f32[512]{0:T(512)} %param.10) | copy-start | bytes 6148
  90.8 6.0 %collective-permute-start.34 = (f32[20,128]{1,0:T(8,128)S(1)}, f32[20,128]{1,0:T(8,128)S(1)}, u32[]{:S(2)}, u32[]{:S(2)}) collective-permute-start(f32[20,128]{1,0:T(8,128)S(1)} %constant_dynamic-update-slice_fusion.here), channel_id=1, source_target_pairs={{0,24},{4,28},{8,16},{12,20},{16,8},{20,12},{24,0},{28,4},{1,25},{... | collective-permute-start | bytes 30728 | tf_op jit(solution)/shard_map/ppermute | solution.py:250
  92.2 5.1 %collective-permute-start.33 = (f32[20,128]{1,0:T(8,128)S(1)}, f32[20,128]{1,0:T(8,128)S(1)}, u32[]{:S(2)}, u32[]{:S(2)}) collective-permute-start(f32[20,128]{1,0:T(8,128)S(1)} %constant_dynamic-update-slice_fusion.here), channel_id=1, source_target_pairs={{0,16},{4,20},{8,24},{12,28},{16,0},{20,4},{24,8},{28,12},{1,17},{... | collective-permute-start | bytes 30728 | tf_op jit(solution)/shard_map/ppermute | solution.py:250
  93.0 4.4 %collective-permute-start.32 = (f32[20,128]{1,0:T(8,128)S(1)}, f32[20,128]{1,0:T(8,128)S(1)}, u32[]{:S(2)}, u32[]{:S(2)}) collective-permute-start(f32[20,128]{1,0:T(8,128)S(1)} %constant_dynamic-update-slice_fusion.here), channel_id=1, source_target_pairs={{0,8},{4,12},{8,0},{12,4},{16,24},{20,28},{24,16},{28,20},{1,9},{5... | collective-permute-start | bytes 30728 | tf_op jit(solution)/shard_map/ppermute | solution.py:250
  96.7 1.5 %collective-permute-start.29 = (bf16[160,512]{1,0:T(8,128)(2,1)S(1)}, bf16[160,512]{1,0:T(8,128)(2,1)S(1)}, u32[]{:S(2)}, u32[]{:S(2)}) collective-permute-start(bf16[160,512]{1,0:T(8,128)(2,1)S(1)} %get-tuple-element.131), channel_id=1, source_target_pairs={{0,4},{4,0},{8,12},{12,8},{16,20},{20,16},{24,28},{28,24},{1,5},{5... | collective-permute-start | bytes 491528 | tf_op jit(solution)/shard_map/ppermute | solution.py:250
  96.8 1.6 %collective-permute-start.30 = (bf16[160,512]{1,0:T(8,128)(2,1)S(1)}, bf16[160,512]{1,0:T(8,128)(2,1)S(1)}, u32[]{:S(2)}, u32[]{:S(2)}) collective-permute-start(bf16[160,512]{1,0:T(8,128)(2,1)S(1)} %get-tuple-element.132), channel_id=1, source_target_pairs={{0,4},{4,0},{8,12},{12,8},{16,20},{20,16},{24,28},{28,24},{1,5},{5... | collective-permute-start | bytes 491528 | tf_op jit(solution)/shard_map/ppermute | solution.py:250
  97.3 1.4 %collective-permute-start.31 = (bf16[192,512]{1,0:T(8,128)(2,1)S(1)}, bf16[192,512]{1,0:T(8,128)(2,1)S(1)}, u32[]{:S(2)}, u32[]{:S(2)}) collective-permute-start(bf16[192,512]{1,0:T(8,128)(2,1)S(1)} %get-tuple-element.133), channel_id=1, source_target_pairs={{0,4},{4,0},{8,12},{12,8},{16,20},{20,16},{24,28},{28,24},{1,5},{5... | collective-permute-start | bytes 589832 | tf_op jit(solution)/shard_map/ppermute | solution.py:250

commit v8 on v7

--- a/solution.py
+++ b/solution.py
@@ -115,7 +115,7 @@
 
 def prepared(x, gain, segs, cotangent, at):
     rows, wide = x.shape
-    step = 128
+    step = 256
     half = wide // 16
     outs = [(half, BF16)] * 12 + [(4 * half, BF16), (HEAD, F32), (HEAD, F32), (KW, BF16)]
     def whole(v):
@@ -144,7 +144,7 @@
             jax.ShapeDtypeStruct((1, 2 * half), F32),
         ],
         cost_estimate=pl.CostEstimate(flops=1, bytes_accessed=1, transcendentals=0),
-        compiler_params=pltpu.CompilerParams(vmem_limit_bytes=14 * 1024 * 1024),
+        compiler_params=pltpu.CompilerParams(vmem_limit_bytes=30 * 1024 * 1024),
         name="prepare",
     )(at, x, gain, segs, cotangent)
 

time: 102 us -> 101 us (level)
  waiting for transfers between devices: 45.3 us -> 42.9 us
  Pallas kernels: 19 us -> 20.2 us
    ppermute x27, waiting for transfers between devices: 22 us -> 20.3 us  [over(): return lambda v: lax.ppermute(v, 'blk', [(i, i ^ bit) for i in range(8)])]
    pallas_call x1, Pallas kernels: 7.75 us -> 8.97 us  [prepared(): pl.pallas_call(functools.partial(prepare_body, segs.shape[1] // step), gr...]
  transfers between devices with their start and end apart: 35 -> 35, of which waited for: 19 -> 19; matrix products, arithmetic and copies ran while one was open for 2% -> 2% of each run, Pallas kernels for 19% -> 20%
where the time goes in v8:
time: 101 us
  waiting for transfers between devices  42.9 us (42%)
  starting transfers between devices  30.4 us (30%)
  Pallas kernels  20.2 us (20%)
  other arithmetic  3.93 us (4%)
  local copies, waits for them, and re-layouts  2.55 us (3%)
    ppermute x8, waiting for transfers between devices, over_z(): return lambda v: lax.ppermute(v, 'dp', [(i, i ^ bit) for i in range(4)])  22.6 us
    ppermute x27, waiting for transfers between devices, over(): return lambda v: lax.ppermute(v, 'blk', [(i, i ^ bit) for i in range(8)])  20.3 us
    ppermute x27, starting transfers between devices, over(): return lambda v: lax.ppermute(v, 'blk', [(i, i ^ bit) for i in range(8)])  20 us
    ppermute x8, starting transfers between devices, over_z(): return lambda v: lax.ppermute(v, 'dp', [(i, i ^ bit) for i in range(4)])  10.5 us
    pallas_call x1, Pallas kernels, prepared(): pl.pallas_call(functools.partial(prepare_body, segs.shape[1] // step), gr...  8.97 us
    pallas_call x2, Pallas kernels, forward(): call(functools.partial(forward_body, places, len(acts), len(init)), [shap...  4.66 us
    pallas_call x1, Pallas kernels, by_permutes(): call(second_grad_body, [own_shape, own_shape, *part_shapes(quarter)], 'gr...  2.91 us
  transfers between devices with their start and end apart: 35, of which 19 were waited for; matrix products, arithmetic and copies ran while one was open for 2% of the time, Pallas kernels for 20%

profile of v8, /device:TPU:0, one launch (start us, length us, event | category | flops | bytes accessed | tf_op | source)
XLA Modules:
  0.0 100.9 jit_solution(14280748646899444797)
XLA Ops:
  0.6 1.4 %fusion.2 = (bf16[704,512]{1,0:T(8,128)(2,1)S(1)}, bf16[704,512]{1,0:T(8,128)(2,1)S(1)}) fusion(bf16[1024,512]{1,0:T(8,128)(2,1)} %refs_6_), kind=kLoop, calls=%fused_computation.37 | loop fusion | bytes 2883584 | tf_op jit(solution)/shard_map/slice | solution.py:264
  2.1 3.0 %collective-permute-start.7 = (bf16[704,512]{1,0:T(8,128)(2,1)S(1)}, bf16[704,512]{1,0:T(8,128)(2,1)S(1)}, u32[]{:S(2)}, u32[]{:S(2)}) collective-permute-start(bf16[704,512]{1,0:T(8,128)(2,1)S(1)} %get-tuple-element.152), channel_id=1, source_target_pairs={{0,16},{4,20},{8,24},{12,28},{16,0},{20,4},{24,8},{28,12},{1,17},{... | collective-permute-start | bytes 2162696 | tf_op jit(solution)/shard_map/ppermute | solution.py:250
  5.1 1.5 %collective-permute-start.6 = (bf16[704,512]{1,0:T(8,128)(2,1)S(1)}, bf16[704,512]{1,0:T(8,128)(2,1)S(1)}, u32[]{:S(2)}, u32[]{:S(2)}) collective-permute-start(bf16[704,512]{1,0:T(8,128)(2,1)S(1)} %get-tuple-element.153), channel_id=1, source_target_pairs={{0,8},{4,12},{8,0},{12,4},{16,24},{20,28},{24,16},{28,20},{1,9},{5... | collective-permute-start | bytes 2162696 | tf_op jit(solution)/shard_map/ppermute | solution.py:250
  6.6 9.0 %prepare.1 = (bf16[512,512]{1,0:T(8,128)(2,1)S(1)}, bf16[512,512]{1,0:T(8,128)(2,1)S(1)}, bf16[512,512]{1,0:T(8,128)(2,1)S(1)}, bf16[512,512]{1,0:T(8,128)(2,1)S...) custom-call(s32[1]{0:T(128)} %bitcast.at_ref, ...), custom_call_target="tpu_custom_call" | custom-call | flops 1 | bytes 1 | tf_op jit(solution)/shard_map/prepare/pallas_call | solution.py:131
  15.7 0.6 collective-permute-start.4
  16.3 1.0 collective-permute-done.4.middle
  18.2 1.1 %collective-permute-done.s1.refs_6_ = bf16[512,512]{1,0:T(8,128)(2,1)S(1)} collective-permute-done((bf16[512,512]{1,0:T(8,128)(2,1)S(1)}, bf16[512,512]{1,0:T(8,128)(2,1)S(1)}, u32[]{:S(2)}, u32[]{:S(2)}) %collective-permute-start) | collective-permute-done | bytes 524320 | tf_op jit(solution)/shard_map/ppermute | solution.py:250
  19.2 0.7 collective-permute-done.1.s2.refs_4_
  20.0 0.7 collective-permute-done.2.s3.refs_4_
  20.7 1.8 %grad_a.1 = (bf16[512,512]{1,0:T(8,128)(2,1)S(1)}, bf16[512,512]{1,0:T(8,128)(2,1)S(1)}, bf16[256,512]{1,0:T(8,128)(2,1)S(1)}, bf16[256,512]{1,0:T(8,128)(2,1)S(1)}) custom-call(bf16[512,512]{1,0:T(8,128)(2,1)S(1)} %get-tuple-element.86.m1.refs_2_, bf16[512,512]{1,0:T(8,128)(2,1)S(1)} %get-tuple-element.87.m2.refs_2_, ...), custom_call_target="tpu_custom_call" | custom-call | flops 1 | bytes 1 | tf_op jit(solution)/shard_map/grad_a/pallas_call | solution.py:306
  23.2 1.5 %collective-permute-start.10 = (bf16[512,512]{1,0:T(8,128)(2,1)S(1)}, bf16[512,512]{1,0:T(8,128)(2,1)S(1)}, u32[]{:S(2)}, u32[]{:S(2)}) collective-permute-start(bf16[512,512]{1,0:T(8,128)(2,1)S(1)} %get-tuple-element.103), channel_id=1, source_target_pairs={{0,8},{4,12},{8,0},{12,4},{16,24},{20,28},{24,16},{28,20},{1,9},{5... | collective-permute-start | bytes 1572872 | tf_op jit(solution)/shard_map/ppermute | solution.py:250
  24.7 0.5 collective-permute-start.11
  25.2 2.4 %collective-permute-done.8.s3.refs_5_ = bf16[512,512]{1,0:T(8,128)(2,1)S(1)} collective-permute-done((bf16[512,512]{1,0:T(8,128)(2,1)S(1)}, bf16[512,512]{1,0:T(8,128)(2,1)S(1)}, u32[]{:S(2)}, u32[]{:S(2)}) %collective-permute-start.8) | collective-permute-done | bytes 524320 | tf_op jit(solution)/shard_map/ppermute | solution.py:250
  27.6 2.9 %grad_b.1 = (f32[512,512]{1,0:T(8,128)S(1)}, f32[512,512]{1,0:T(8,128)S(1)}, bf16[512,512]{1,0:T(8,128)(2,1)S(1)}, bf16[512,512]{1,0:T(8,128)(2,1)S(1)}, bf16[25...) custom-call(bf16[512,512]{1,0:T(8,128)(2,1)S(1)} %get-tuple-element.79.m_a0.refs_0_, ...), custom_call_target="tpu_custom_call" | custom-call | flops 1 | bytes 1 | tf_op jit(solution)/shard_map/grad_b/pallas_call | solution.py:314
  30.5 2.3 %forward.2 = (f32[512,512]{1,0:T(8,128)S(1)}, f32[512,512]{1,0:T(8,128)S(1)}) custom-call(bf16[512,512]{1,0:T(8,128)(2,1)S(1)} %get-tuple-element.79.m_a0.refs_0_, bf16[512,512]{1,0:T(8,128)(2,1)S(1)} %get-tuple-element.80.m0.refs_1_, bf16[512,512]{1,0:T(8,128)(2,1)S(1)} %get-tuple-element.87.m2.refs_2_, bf16[512,512]{1,0:T(8,128)(2,1)S(1)} %get-tuple-element.81.m1.refs_3_, ...), custom_call_target="tpu_custom_call" | custom-call | flops 1 | bytes 1 | tf_op jit(solution)/shard_map/forward/pallas_call | solution.py:223
  32.9 4.5 %collective-permute-done.10 = bf16[512,512]{1,0:T(8,128)(2,1)S(1)} collective-permute-done((bf16[512,512]{1,0:T(8,128)(2,1)S(1)}, bf16[512,512]{1,0:T(8,128)(2,1)S(1)}, u32[]{:S(2)}, u32[]{:S(2)}) %collective-permute-start.10) | collective-permute-done | bytes 524320 | tf_op jit(solution)/shard_map/ppermute | solution.py:250
  37.3 0.9 collective-permute-done.11
  38.4 0.9 collective-permute-start.15
  39.3 0.5 collective-permute-start.14
  39.9 1.2 %collective-permute-start.12 = (bf16[512,512]{1,0:T(8,128)(2,1)S(1)}, bf16[512,512]{1,0:T(8,128)(2,1)S(1)}, u32[]{:S(2)}, u32[]{:S(2)}) collective-permute-start(bf16[512,512]{1,0:T(8,128)(2,1)S(1)} %get-tuple-element.112), channel_id=1, source_target_pairs={{0,8},{4,12},{8,0},{12,4},{16,24},{20,28},{24,16},{28,20},{1,9},{5... | collective-permute-start | bytes 1572872 | tf_op jit(solution)/shard_map/ppermute | solution.py:250
  41.2 1.5 %collective-permute-start.13 = (bf16[512,512]{1,0:T(8,128)(2,1)S(1)}, bf16[512,512]{1,0:T(8,128)(2,1)S(1)}, u32[]{:S(2)}, u32[]{:S(2)}) collective-permute-start(bf16[512,512]{1,0:T(8,128)(2,1)S(1)} %get-tuple-element.113), channel_id=1, source_target_pairs={{0,16},{4,20},{8,24},{12,28},{16,0},{20,4},{24,8},{28,12},{1,17},{... | collective-permute-start | bytes 1572872 | tf_op jit(solution)/shard_map/ppermute | solution.py:250
  42.7 5.0 %collective-permute-done.15 = bf16[256,512]{1,0:T(8,128)(2,1)S(1)} collective-permute-done((bf16[256,512]{1,0:T(8,128)(2,1)S(1)}, bf16[256,512]{1,0:T(8,128)(2,1)S(1)}, u32[]{:S(2)}, u32[]{:S(2)}) %collective-permute-start.15) | collective-permute-done | bytes 262176 | tf_op jit(solution)/shard_map/ppermute | solution.py:250
  47.7 0.8 collective-permute-done.14
  48.8 1.6 %collective-permute-start.18 = (bf16[256,512]{1,0:T(8,128)(2,1)S(1)}, bf16[256,512]{1,0:T(8,128)(2,1)S(1)}, u32[]{:S(2)}, u32[]{:S(2)}) collective-permute-start(bf16[256,512]{1,0:T(8,128)(2,1)S(1)} %select_convert_fusion.1), channel_id=1, source_target_pairs={{0,1},{1,0},{2,3},{3,2},{4,5},{5,4},{6,7},{7,6},{8,9},{9,8},{10,11... | collective-permute-start | bytes 786440 | tf_op jit(solution)/shard_map/ppermute | solution.py:291
  50.6 6.7 %collective-permute-done.18 = bf16[256,512]{1,0:T(8,128)(2,1)S(1)} collective-permute-done((bf16[256,512]{1,0:T(8,128)(2,1)S(1)}, bf16[256,512]{1,0:T(8,128)(2,1)S(1)}, u32[]{:S(2)}, u32[]{:S(2)}) %collective-permute-start.18) | collective-permute-done | bytes 262176 | tf_op jit(solution)/shard_map/ppermute | solution.py:291
  57.5 2.8 %collective-permute-start.19 = (bf16[256,512]{1,0:T(8,128)(2,1)S(1)}, bf16[256,512]{1,0:T(8,128)(2,1)S(1)}, u32[]{:S(2)}, u32[]{:S(2)}) collective-permute-start(bf16[256,512]{1,0:T(8,128)(2,1)S(1)} %add_convert_fusion.3), channel_id=1, source_target_pairs={{0,2},{1,3},{2,0},{3,1},{4,6},{5,7},{6,4},{7,5},{8,10},{9,11},{10,... | collective-permute-start | bytes 786440 | tf_op jit(solution)/shard_map/ppermute | solution.py:291
  60.5 1.8 %collective-permute-start.17 = (bf16[256,512]{1,0:T(8,128)(2,1)S(1)}, bf16[256,512]{1,0:T(8,128)(2,1)S(1)}, u32[]{:S(2)}, u32[]{:S(2)}) collective-permute-start(bf16[256,512]{1,0:T(8,128)(2,1)S(1)} %add_convert_fusion.4), channel_id=1, source_target_pairs={{0,8},{4,12},{8,0},{12,4},{16,24},{20,28},{24,16},{28,20},{1,9},{5... | collective-permute-start | bytes 786440 | tf_op jit(solution)/shard_map/ppermute | solution.py:250
  62.4 0.5 collective-permute-start.16
  62.9 4.9 %collective-permute-done.19 = bf16[256,512]{1,0:T(8,128)(2,1)S(1)} collective-permute-done((bf16[256,512]{1,0:T(8,128)(2,1)S(1)}, bf16[256,512]{1,0:T(8,128)(2,1)S(1)}, u32[]{:S(2)}, u32[]{:S(2)}) %collective-permute-start.19) | collective-permute-done | bytes 262176 | tf_op jit(solution)/shard_map/ppermute | solution.py:291
  67.8 1.1 %collective-permute-done.16 = bf16[256,512]{1,0:T(8,128)(2,1)S(1)} collective-permute-done((bf16[256,512]{1,0:T(8,128)(2,1)S(1)}, bf16[256,512]{1,0:T(8,128)(2,1)S(1)}, u32[]{:S(2)}, u32[]{:S(2)}) %collective-permute-start.16) | collective-permute-done | bytes 262176 | tf_op jit(solution)/shard_map/ppermute | solution.py:250
  69.3 0.8 collective-permute-start.20
  70.2 1.0 slice-done
  71.4 0.6 collective-permute-start.27
  72.0 0.4 multiply_reduce_fusion.3
  72.5 2.1 %collective-permute-start.21 = (f32[12,128]{1,0:T(8,128)S(1)}, f32[12,128]{1,0:T(8,128)S(1)}, u32[]{:S(2)}, u32[]{:S(2)}) collective-permute-start(f32[12,128]{1,0:T(8,128)S(1)} %maximum_bitcast_fusion), channel_id=1, source_target_pairs={{0,1},{1,0},{2,3},{3,2},{4,5},{5,4},{6,7},{7,6},{8,9},{9,8},{10,11... | collective-permute-start | bytes 18440 | tf_op jit(solution)/shard_map/ppermute | solution.py:291
  74.6 4.1 %collective-permute-done.21 = f32[12,128]{1,0:T(8,128)S(1)} collective-permute-done((f32[12,128]{1,0:T(8,128)S(1)}, f32[12,128]{1,0:T(8,128)S(1)}, u32[]{:S(2)}, u32[]{:S(2)}) %collective-permute-start.21) | collective-permute-done | bytes 6176 | tf_op jit(solution)/shard_map/ppermute | solution.py:291
  78.9 0.8 collective-permute-start.22
  79.7 2.2 %collective-permute-start.24 = (f32[12,128]{1,0:T(8,128)S(1)}, f32[12,128]{1,0:T(8,128)S(1)}, u32[]{:S(2)}, u32[]{:S(2)}) collective-permute-start(f32[12,128]{1,0:T(8,128)S(1)} %fusion), channel_id=1, source_target_pairs={{0,2},{1,3},{2,0},{3,1},{4,6},{5,7},{6,4},{7,5},{8,10},{9,11},{10,... | collective-permute-start | bytes 18440 | tf_op jit(solution)/shard_map/ppermute | solution.py:291
  81.9 6.8 %collective-permute-done.24 = f32[12,128]{1,0:T(8,128)S(1)} collective-permute-done((f32[12,128]{1,0:T(8,128)S(1)}, f32[12,128]{1,0:T(8,128)S(1)}, u32[]{:S(2)}, u32[]{:S(2)}) %collective-permute-start.24) | collective-permute-done | bytes 6176 | tf_op jit(solution)/shard_map/ppermute | solution.py:291
  88.8 1.1 %collective-permute-done.25 = f32[8,128]{1,0:T(8,128)S(1)} collective-permute-done((f32[8,128]{1,0:T(8,128)S(1)}, f32[8,128]{1,0:T(8,128)S(1)}, u32[]{:S(2)}, u32[]{:S(2)}) %collective-permute-start.25) | collective-permute-done | bytes 4128 | tf_op jit(solution)/shard_map/ppermute | solution.py:250
  90.1 1.8 %collective-permute-start.34 = (f32[20,128]{1,0:T(8,128)S(1)}, f32[20,128]{1,0:T(8,128)S(1)}, u32[]{:S(2)}, u32[]{:S(2)}) collective-permute-start(f32[20,128]{1,0:T(8,128)S(1)} %constant_dynamic-update-slice_fusion.here), channel_id=1, source_target_pairs={{0,24},{4,28},{8,16},{12,20},{16,8},{20,12},{24,0},{28,4},{1,25},{... | collective-permute-start | bytes 30728 | tf_op jit(solution)/shard_map/ppermute | solution.py:250
  91.9 0.5 collective-permute-start.33
  92.4 1.2 %collective-permute-start.32 = (f32[20,128]{1,0:T(8,128)S(1)}, f32[20,128]{1,0:T(8,128)S(1)}, u32[]{:S(2)}, u32[]{:S(2)}) collective-permute-start(f32[20,128]{1,0:T(8,128)S(1)} %constant_dynamic-update-slice_fusion.here), channel_id=1, source_target_pairs={{0,8},{4,12},{8,0},{12,4},{16,24},{20,28},{24,16},{28,20},{1,9},{5... | collective-permute-start | bytes 30728 | tf_op jit(solution)/shard_map/ppermute | solution.py:250
  93.7 2.3 %forward.3 = (f32[512,512]{1,0:T(8,128)S(1)}, bf16[160,512]{1,0:T(8,128)(2,1)S(1)}, bf16[160,512]{1,0:T(8,128)(2,1)S(1)}, bf16[192,512]{1,0:T(8,128)(2,1)S(1)}) custom-call(bf16[512,512]{1,0:T(8,128)(2,1)S(1)} %get-tuple-element.88.m3.refs_0_, bf16[512,512]{1,0:T(8,128)(2,1)S(1)} %get-tuple-element.83.m3.refs_1_, ...), custom_call_target="tpu_custom_call" | custom-call | flops 1 | bytes 1 | tf_op jit(solution)/shard_map/forward/pallas_call | solution.py:223
  96.1 0.5 collective-permute-start.30
  96.7 0.6 collect.1
  98.0 1.2 %keys.1 = bf16[512,512]{1,0:T(8,128)(2,1)} custom-call(f32[512,512]{1,0:T(8,128)S(1)} %get-tuple-element.130.here, bf16[160,512]{1,0:T(8,128)(2,1)S(1)} %collective-permute-done.29.upper, bf16[160,512]{1,0:T(8,128)(2,1)S(1)} %collective-permute-done.30.middle, bf16[192,512]{1,0:T(8,128)(2,1)S(1)} %collective-permute-done.31.lower, f32[1,512]{1,0:T(1,128)S(1)} %bitcast.11, ...), custom_call_target="tpu_custom_call" | custom-call | flops 1 | bytes 1 | tf_op jit(solution)/shard_map/keys/pallas_call | solution.py:377
  99.3 1.6 %convert_multiply_fusion = f32[1024,512]{1,0:T(8,128)} fusion(bf16[256,512]{1,0:T(8,128)(2,1)S(1)} %get-tuple-element.157, bf16[256,512]{1,0:T(8,128)(2,1)S(1)} %get-tuple-element.156, bf16[256,512]{1,0:T(8,128)(2,1)S(1)} %get-tuple-element.155, bf16[256,512]{1,0:T(8,128)(2,1)S(1)} %get-tuple-element.154), kind=kLoop, calls=%fused_computation | loop fusion | flops 4718592 | bytes 3145728 | tf_op jit(solution)/shard_map/mul | solution.py:395
  (80 shorter events, 4.7 us)
Async XLA Ops:
  2.1 20.5 %collective-permute-start.7 = (bf16[704,512]{1,0:T(8,128)(2,1)S(1)}, bf16[704,512]{1,0:T(8,128)(2,1)S(1)}, u32[]{:S(2)}, u32[]{:S(2)}) collective-permute-start(bf16[704,512]{1,0:T(8,128)(2,1)S(1)} %get-tuple-element.152), channel_id=1, source_target_pairs={{0,16},{4,20},{8,24},{12,28},{16,0},{20,4},{24,8},{28,12},{1,17},{... | collective-permute-start | bytes 2162696 | tf_op jit(solution)/shard_map/ppermute | solution.py:250
  5.1 17.6 %collective-permute-start.6 = (bf16[704,512]{1,0:T(8,128)(2,1)S(1)}, bf16[704,512]{1,0:T(8,128)(2,1)S(1)}, u32[]{:S(2)}, u32[]{:S(2)}) collective-permute-start(bf16[704,512]{1,0:T(8,128)(2,1)S(1)} %get-tuple-element.153), channel_id=1, source_target_pairs={{0,8},{4,12},{8,0},{12,4},{16,24},{20,28},{24,16},{28,20},{1,9},{5... | collective-permute-start | bytes 2162696 | tf_op jit(solution)/shard_map/ppermute | solution.py:250
  15.6 2.3 %collective-permute-start.5 = (bf16[192,512]{1,0:T(8,128)(2,1)S(1)}, bf16[192,512]{1,0:T(8,128)(2,1)S(1)}, u32[]{:S(2)}, u32[]{:S(2)}) collective-permute-start(bf16[192,512]{1,0:T(8,128)(2,1)S(1)} %slice.83), channel_id=1, source_target_pairs={{0,4},{4,0},{8,12},{12,8},{16,20},{20,16},{24,28},{28,24},{1,5},{5... | collective-permute-start | bytes 589832 | tf_op jit(solution)/shard_map/ppermute | solution.py:250
  15.7 1.6 %collective-permute-start.4 = (bf16[160,512]{1,0:T(8,128)(2,1)S(1)}, bf16[160,512]{1,0:T(8,128)(2,1)S(1)}, u32[]{:S(2)}, u32[]{:S(2)}) collective-permute-start(bf16[160,512]{1,0:T(8,128)(2,1)S(1)} %get-tuple-element.158), channel_id=1, source_target_pairs={{0,4},{4,0},{8,12},{12,8},{16,20},{20,16},{24,28},{28,24},{1,5},{5... | collective-permute-start | bytes 491528 | tf_op jit(solution)/shard_map/ppermute | solution.py:250
  16.3 1.4 %collective-permute-start.3 = (bf16[160,512]{1,0:T(8,128)(2,1)S(1)}, bf16[160,512]{1,0:T(8,128)(2,1)S(1)}, u32[]{:S(2)}, u32[]{:S(2)}) collective-permute-start(bf16[160,512]{1,0:T(8,128)(2,1)S(1)} %get-tuple-element.159), channel_id=1, source_target_pairs={{0,4},{4,0},{8,12},{12,8},{16,20},{20,16},{24,28},{28,24},{1,5},{5... | collective-permute-start | bytes 491528 | tf_op jit(solution)/shard_map/ppermute | solution.py:250
  17.3 1.9 %collective-permute-start = (bf16[512,512]{1,0:T(8,128)(2,1)S(1)}, bf16[512,512]{1,0:T(8,128)(2,1)S(1)}, u32[]{:S(2)}, u32[]{:S(2)}) collective-permute-start(bf16[512,512]{1,0:T(8,128)(2,1)S(1)} %get-tuple-element.89), channel_id=1, source_target_pairs={{0,4},{4,0},{8,12},{12,8},{16,20},{20,16},{24,28},{28,24},{1,5},{5... | collective-permute-start | bytes 1572872 | tf_op jit(solution)/shard_map/ppermute | solution.py:250
  17.7 2.3 %collective-permute-start.1 = (bf16[512,512]{1,0:T(8,128)(2,1)S(1)}, bf16[512,512]{1,0:T(8,128)(2,1)S(1)}, u32[]{:S(2)}, u32[]{:S(2)}) collective-permute-start(bf16[512,512]{1,0:T(8,128)(2,1)S(1)} %get-tuple-element.90), channel_id=1, source_target_pairs={{0,4},{4,0},{8,12},{12,8},{16,20},{20,16},{24,28},{28,24},{1,5},{5... | collective-permute-start | bytes 1572872 | tf_op jit(solution)/shard_map/ppermute | solution.py:250
  17.9 2.9 %collective-permute-start.2 = (bf16[512,512]{1,0:T(8,128)(2,1)S(1)}, bf16[512,512]{1,0:T(8,128)(2,1)S(1)}, u32[]{:S(2)}, u32[]{:S(2)}) collective-permute-start(bf16[512,512]{1,0:T(8,128)(2,1)S(1)} %get-tuple-element.91), channel_id=1, source_target_pairs={{0,4},{4,0},{8,12},{12,8},{16,20},{20,16},{24,28},{28,24},{1,5},{5... | collective-permute-start | bytes 1572872 | tf_op jit(solution)/shard_map/ppermute | solution.py:250
  22.6 47.5 %copy-start.1 = (bf16[704,512]{1,0:T(8,128)(2,1)}, bf16[704,512]{1,0:T(8,128)(2,1)S(1)}, u32[]{:S(2)}) copy-start(bf16[704,512]{1,0:T(8,128)(2,1)S(1)} %collective-permute-done.7.refs_7_.refs_12_) | copy-start | bytes 2162692
  22.7 47.4 %copy-start.3 = (bf16[704,512]{1,0:T(8,128)(2,1)}, bf16[704,512]{1,0:T(8,128)(2,1)S(1)}, u32[]{:S(2)}) copy-start(bf16[704,512]{1,0:T(8,128)(2,1)S(1)} %collective-permute-done.6.refs_8_.refs_13_) | copy-start | bytes 2162692
  22.7 4.9 %collective-permute-start.9 = (bf16[512,2048]{1,0:T(8,128)(2,1)S(1)}, bf16[512,2048]{1,0:T(8,128)(2,1)S(1)}, u32[]{:S(2)}, u32[]{:S(2)}) collective-permute-start(bf16[512,2048]{1,0:T(8,128)(2,1)S(1)} %get-tuple-element.99), channel_id=1, source_target_pairs={{0,4},{4,0},{8,12},{12,8},{16,20},{20,16},{24,28},{28,24},{1,5},{5... | collective-permute-start | bytes 6291464 | tf_op jit(solution)/shard_map/ppermute | solution.py:250
  23.0 4.6 %collective-permute-start.8 = (bf16[512,512]{1,0:T(8,128)(2,1)S(1)}, bf16[512,512]{1,0:T(8,128)(2,1)S(1)}, u32[]{:S(2)}, u32[]{:S(2)}) collective-permute-start(bf16[512,512]{1,0:T(8,128)(2,1)S(1)} %get-tuple-element.98), channel_id=1, source_target_pairs={{0,4},{4,0},{8,12},{12,8},{16,20},{20,16},{24,28},{28,24},{1,5},{5... | collective-permute-start | bytes 1572872 | tf_op jit(solution)/shard_map/ppermute | solution.py:250
  23.2 14.1 %collective-permute-start.10 = (bf16[512,512]{1,0:T(8,128)(2,1)S(1)}, bf16[512,512]{1,0:T(8,128)(2,1)S(1)}, u32[]{:S(2)}, u32[]{:S(2)}) collective-permute-start(bf16[512,512]{1,0:T(8,128)(2,1)S(1)} %get-tuple-element.103), channel_id=1, source_target_pairs={{0,8},{4,12},{8,0},{12,4},{16,24},{20,28},{24,16},{28,20},{1,9},{5... | collective-permute-start | bytes 1572872 | tf_op jit(solution)/shard_map/ppermute | solution.py:250
  24.7 13.6 %collective-permute-start.11 = (bf16[512,512]{1,0:T(8,128)(2,1)S(1)}, bf16[512,512]{1,0:T(8,128)(2,1)S(1)}, u32[]{:S(2)}, u32[]{:S(2)}) collective-permute-start(bf16[512,512]{1,0:T(8,128)(2,1)S(1)} %get-tuple-element.104), channel_id=1, source_target_pairs={{0,16},{4,20},{8,24},{12,28},{16,0},{20,4},{24,8},{28,12},{1,17},{... | collective-permute-start | bytes 1572872 | tf_op jit(solution)/shard_map/ppermute | solution.py:250
  27.6 2.9 %copy-start = (bf16[1024,512]{1,0:T(8,128)(2,1)S(1)}, bf16[1024,512]{1,0:T(8,128)(2,1)}, u32[]{:S(2)}) copy-start(bf16[1024,512]{1,0:T(8,128)(2,1)} %refs_6_) | copy-start | bytes 3145732
  38.4 9.3 %collective-permute-start.15 = (bf16[256,512]{1,0:T(8,128)(2,1)S(1)}, bf16[256,512]{1,0:T(8,128)(2,1)S(1)}, u32[]{:S(2)}, u32[]{:S(2)}) collective-permute-start(bf16[256,512]{1,0:T(8,128)(2,1)S(1)} %add_convert_fusion.6), channel_id=1, source_target_pairs={{0,8},{4,12},{8,0},{12,4},{16,24},{20,28},{24,16},{28,20},{1,9},{5... | collective-permute-start | bytes 786440 | tf_op jit(solution)/shard_map/ppermute | solution.py:250
  39.3 9.2 %collective-permute-start.14 = (bf16[256,512]{1,0:T(8,128)(2,1)S(1)}, bf16[256,512]{1,0:T(8,128)(2,1)S(1)}, u32[]{:S(2)}, u32[]{:S(2)}) collective-permute-start(bf16[256,512]{1,0:T(8,128)(2,1)S(1)} %add_convert_fusion.7), channel_id=1, source_target_pairs={{0,16},{4,20},{8,24},{12,28},{16,0},{20,4},{24,8},{28,12},{1,17},{... | collective-permute-start | bytes 786440 | tf_op jit(solution)/shard_map/ppermute | solution.py:250
  39.9 20.5 %collective-permute-start.12 = (bf16[512,512]{1,0:T(8,128)(2,1)S(1)}, bf16[512,512]{1,0:T(8,128)(2,1)S(1)}, u32[]{:S(2)}, u32[]{:S(2)}) collective-permute-start(bf16[512,512]{1,0:T(8,128)(2,1)S(1)} %get-tuple-element.112), channel_id=1, source_target_pairs={{0,8},{4,12},{8,0},{12,4},{16,24},{20,28},{24,16},{28,20},{1,9},{5... | collective-permute-start | bytes 1572872 | tf_op jit(solution)/shard_map/ppermute | solution.py:250
  41.2 19.2 %collective-permute-start.13 = (bf16[512,512]{1,0:T(8,128)(2,1)S(1)}, bf16[512,512]{1,0:T(8,128)(2,1)S(1)}, u32[]{:S(2)}, u32[]{:S(2)}) collective-permute-start(bf16[512,512]{1,0:T(8,128)(2,1)S(1)} %get-tuple-element.113), channel_id=1, source_target_pairs={{0,16},{4,20},{8,24},{12,28},{16,0},{20,4},{24,8},{28,12},{1,17},{... | collective-permute-start | bytes 1572872 | tf_op jit(solution)/shard_map/ppermute | solution.py:250
  48.8 8.5 %collective-permute-start.18 = (bf16[256,512]{1,0:T(8,128)(2,1)S(1)}, bf16[256,512]{1,0:T(8,128)(2,1)S(1)}, u32[]{:S(2)}, u32[]{:S(2)}) collective-permute-start(bf16[256,512]{1,0:T(8,128)(2,1)S(1)} %select_convert_fusion.1), channel_id=1, source_target_pairs={{0,1},{1,0},{2,3},{3,2},{4,5},{5,4},{6,7},{7,6},{8,9},{9,8},{10,11... | collective-permute-start | bytes 786440 | tf_op jit(solution)/shard_map/ppermute | solution.py:291
  57.5 10.2 %collective-permute-start.19 = (bf16[256,512]{1,0:T(8,128)(2,1)S(1)}, bf16[256,512]{1,0:T(8,128)(2,1)S(1)}, u32[]{:S(2)}, u32[]{:S(2)}) collective-permute-start(bf16[256,512]{1,0:T(8,128)(2,1)S(1)} %add_convert_fusion.3), channel_id=1, source_target_pairs={{0,2},{1,3},{2,0},{3,1},{4,6},{5,7},{6,4},{7,5},{8,10},{9,11},{10,... | collective-permute-start | bytes 786440 | tf_op jit(solution)/shard_map/ppermute | solution.py:291
  60.5 7.3 %collective-permute-start.17 = (bf16[256,512]{1,0:T(8,128)(2,1)S(1)}, bf16[256,512]{1,0:T(8,128)(2,1)S(1)}, u32[]{:S(2)}, u32[]{:S(2)}) collective-permute-start(bf16[256,512]{1,0:T(8,128)(2,1)S(1)} %add_convert_fusion.4), channel_id=1, source_target_pairs={{0,8},{4,12},{8,0},{12,4},{16,24},{20,28},{24,16},{28,20},{1,9},{5... | collective-permute-start | bytes 786440 | tf_op jit(solution)/shard_map/ppermute | solution.py:250
  62.4 6.6 %collective-permute-start.16 = (bf16[256,512]{1,0:T(8,128)(2,1)S(1)}, bf16[256,512]{1,0:T(8,128)(2,1)S(1)}, u32[]{:S(2)}, u32[]{:S(2)}) collective-permute-start(bf16[256,512]{1,0:T(8,128)(2,1)S(1)} %add_convert_fusion.5), channel_id=1, source_target_pairs={{0,16},{4,20},{8,24},{12,28},{16,0},{20,4},{24,8},{28,12},{1,17},{... | collective-permute-start | bytes 786440 | tf_op jit(solution)/shard_map/ppermute | solution.py:250
  69.3 9.4 %collective-permute-start.20 = (bf16[256,512]{1,0:T(8,128)(2,1)S(1)}, bf16[256,512]{1,0:T(8,128)(2,1)S(1)}, u32[]{:S(2)}, u32[]{:S(2)}) collective-permute-start(bf16[256,512]{1,0:T(8,128)(2,1)S(1)} %select_convert_fusion), channel_id=1, source_target_pairs={{0,1},{1,0},{2,3},{3,2},{4,5},{5,4},{6,7},{7,6},{8,9},{9,8},{10,11... | collective-permute-start | bytes 786440 | tf_op jit(solution)/shard_map/ppermute | solution.py:291
  70.1 1.0 %slice-start = ((bf16[704,512]{1,0:T(8,128)(2,1)}), bf16[512,512]{1,0:T(8,128)(2,1)S(1)}, s32[]{:S(2)}) async-start(bf16[704,512]{1,0:T(8,128)(2,1)} %copy-done.1), calls=%async_computation | async-start | bytes 1048576 | tf_op jit(solution)/shard_map/slice | solution.py:339
  70.1 1.2 %slice-start.1 = ((bf16[704,512]{1,0:T(8,128)(2,1)}), bf16[512,512]{1,0:T(8,128)(2,1)S(1)}, s32[]{:S(2)}) async-start(bf16[704,512]{1,0:T(8,128)(2,1)} %copy-done.3), calls=%async_computation.1 | async-start | bytes 1048576 | tf_op jit(solution)/shard_map/slice | solution.py:340
  71.2 18.7 %collective-permute-start.26 = (bf16[832,512]{1,0:T(8,128)(2,1)S(1)}, bf16[832,512]{1,0:T(8,128)(2,1)S(1)}, u32[]{:S(2)}, u32[]{:S(2)}) collective-permute-start(bf16[832,512]{1,0:T(8,128)(2,1)S(1)} %pad_maximum_fusion), channel_id=1, source_target_pairs={{0,8},{4,12},{8,0},{12,4},{16,24},{20,28},{24,16},{28,20},{1,9},{5... | collective-permute-start | bytes 2555912 | tf_op jit(solution)/shard_map/ppermute | solution.py:250
  71.4 18.5 %collective-permute-start.27 = (bf16[832,512]{1,0:T(8,128)(2,1)S(1)}, bf16[832,512]{1,0:T(8,128)(2,1)S(1)}, u32[]{:S(2)}, u32[]{:S(2)}) collective-permute-start(bf16[832,512]{1,0:T(8,128)(2,1)S(1)} %pad_maximum_fusion.1), channel_id=1, source_target_pairs={{0,16},{4,20},{8,24},{12,28},{16,0},{20,4},{24,8},{28,12},{1,17},{... | collective-permute-start | bytes 2555912 | tf_op jit(solution)/shard_map/ppermute | solution.py:250
  72.4 21.2 %copy-start.2 = (bf16[704,512]{1,0:T(8,128)(2,1)S(1)}, bf16[704,512]{1,0:T(8,128)(2,1)}, u32[]{:S(2)}) copy-start(bf16[704,512]{1,0:T(8,128)(2,1)} %copy-done.1) | copy-start | bytes 2162692
  72.4 21.2 %copy-start.4 = (bf16[704,512]{1,0:T(8,128)(2,1)S(1)}, bf16[704,512]{1,0:T(8,128)(2,1)}, u32[]{:S(2)}) copy-start(bf16[704,512]{1,0:T(8,128)(2,1)} %copy-done.3) | copy-start | bytes 2162692
  72.5 6.3 %collective-permute-start.21 = (f32[12,128]{1,0:T(8,128)S(1)}, f32[12,128]{1,0:T(8,128)S(1)}, u32[]{:S(2)}, u32[]{:S(2)}) collective-permute-start(f32[12,128]{1,0:T(8,128)S(1)} %maximum_bitcast_fusion), channel_id=1, source_target_pairs={{0,1},{1,0},{2,3},{3,2},{4,5},{5,4},{6,7},{7,6},{8,9},{9,8},{10,11... | collective-permute-start | bytes 18440 | tf_op jit(solution)/shard_map/ppermute | solution.py:291
  74.5 14.2 %collective-permute-start.23 = (bf16[256,512]{1,0:T(8,128)(2,1)S(1)}, bf16[256,512]{1,0:T(8,128)(2,1)S(1)}, u32[]{:S(2)}, u32[]{:S(2)}) collective-permute-start(bf16[256,512]{1,0:T(8,128)(2,1)S(1)} %add_convert_fusion.2), channel_id=1, source_target_pairs={{0,1},{1,0},{2,3},{3,2},{4,5},{5,4},{6,7},{7,6},{8,9},{9,8},{10,11... | collective-permute-start | bytes 786440 | tf_op jit(solution)/shard_map/ppermute | solution.py:291
  78.9 11.0 %collective-permute-start.22 = (bf16[256,512]{1,0:T(8,128)(2,1)S(1)}, bf16[256,512]{1,0:T(8,128)(2,1)S(1)}, u32[]{:S(2)}, u32[]{:S(2)}) collective-permute-start(bf16[256,512]{1,0:T(8,128)(2,1)S(1)} %add_convert_fusion.1), channel_id=1, source_target_pairs={{0,2},{1,3},{2,0},{3,1},{4,6},{5,7},{6,4},{7,5},{8,10},{9,11},{10,... | collective-permute-start | bytes 786440 | tf_op jit(solution)/shard_map/ppermute | solution.py:291
  79.7 9.0 %collective-permute-start.24 = (f32[12,128]{1,0:T(8,128)S(1)}, f32[12,128]{1,0:T(8,128)S(1)}, u32[]{:S(2)}, u32[]{:S(2)}) collective-permute-start(f32[12,128]{1,0:T(8,128)S(1)} %fusion), channel_id=1, source_target_pairs={{0,2},{1,3},{2,0},{3,1},{4,6},{5,7},{6,4},{7,5},{8,10},{9,11},{10,... | collective-permute-start | bytes 18440 | tf_op jit(solution)/shard_map/ppermute | solution.py:291
  88.7 1.2 %collective-permute-start.25 = (f32[8,128]{1,0:T(8,128)S(1)}, f32[8,128]{1,0:T(8,128)S(1)}, u32[]{:S(2)}, u32[]{:S(2)}) collective-permute-start(f32[8,128]{1,0:T(8,128)S(1)} %slice.108), channel_id=1, source_target_pairs={{0,4},{4,0},{8,12},{12,8},{16,20},{20,16},{24,28},{28,24},{1,5},{5... | collective-permute-start | bytes 12296 | tf_op jit(solution)/shard_map/ppermute | solution.py:250
  90.0 9.2 %collective-permute-start.28 = (bf16[256,512]{1,0:T(8,128)(2,1)S(1)}, bf16[256,512]{1,0:T(8,128)(2,1)S(1)}, u32[]{:S(2)}, u32[]{:S(2)}) collective-permute-start(bf16[256,512]{1,0:T(8,128)(2,1)S(1)} %add_convert_fusion), channel_id=1, source_target_pairs={{0,1},{1,0},{2,3},{3,2},{4,5},{5,4},{6,7},{7,6},{8,9},{9,8},{10,11... | collective-permute-start | bytes 786440 | tf_op jit(solution)/shard_map/ppermute | solution.py:291
  90.1 7.9 %copy-start.5 = (f32[512]{0:T(512)S(1)}, f32[512]{0:T(512)}, u32[]{:S(2)}) copy-start(f32[512]{0:T(512)} %param.10) | copy-start | bytes 6148
  90.1 6.0 %collective-permute-start.34 = (f32[20,128]{1,0:T(8,128)S(1)}, f32[20,128]{1,0:T(8,128)S(1)}, u32[]{:S(2)}, u32[]{:S(2)}) collective-permute-start(f32[20,128]{1,0:T(8,128)S(1)} %constant_dynamic-update-slice_fusion.here), channel_id=1, source_target_pairs={{0,24},{4,28},{8,16},{12,20},{16,8},{20,12},{24,0},{28,4},{1,25},{... | collective-permute-start | bytes 30728 | tf_op jit(solution)/shard_map/ppermute | solution.py:250
  91.9 4.6 %collective-permute-start.33 = (f32[20,128]{1,0:T(8,128)S(1)}, f32[20,128]{1,0:T(8,128)S(1)}, u32[]{:S(2)}, u32[]{:S(2)}) collective-permute-start(f32[20,128]{1,0:T(8,128)S(1)} %constant_dynamic-update-slice_fusion.here), channel_id=1, source_target_pairs={{0,16},{4,20},{8,24},{12,28},{16,0},{20,4},{24,8},{28,12},{1,17},{... | collective-permute-start | bytes 30728 | tf_op jit(solution)/shard_map/ppermute | solution.py:250
  92.4 4.3 %collective-permute-start.32 = (f32[20,128]{1,0:T(8,128)S(1)}, f32[20,128]{1,0:T(8,128)S(1)}, u32[]{:S(2)}, u32[]{:S(2)}) collective-permute-start(f32[20,128]{1,0:T(8,128)S(1)} %constant_dynamic-update-slice_fusion.here), channel_id=1, source_target_pairs={{0,8},{4,12},{8,0},{12,4},{16,24},{20,28},{24,16},{28,20},{1,9},{5... | collective-permute-start | bytes 30728 | tf_op jit(solution)/shard_map/ppermute | solution.py:250
  96.0 1.5 %collective-permute-start.29 = (bf16[160,512]{1,0:T(8,128)(2,1)S(1)}, bf16[160,512]{1,0:T(8,128)(2,1)S(1)}, u32[]{:S(2)}, u32[]{:S(2)}) collective-permute-start(bf16[160,512]{1,0:T(8,128)(2,1)S(1)} %get-tuple-element.131), channel_id=1, source_target_pairs={{0,4},{4,0},{8,12},{12,8},{16,20},{20,16},{24,28},{28,24},{1,5},{5... | collective-permute-start | bytes 491528 | tf_op jit(solution)/shard_map/ppermute | solution.py:250
  96.1 1.6 %collective-permute-start.30 = (bf16[160,512]{1,0:T(8,128)(2,1)S(1)}, bf16[160,512]{1,0:T(8,128)(2,1)S(1)}, u32[]{:S(2)}, u32[]{:S(2)}) collective-permute-start(bf16[160,512]{1,0:T(8,128)(2,1)S(1)} %get-tuple-element.132), channel_id=1, source_target_pairs={{0,4},{4,0},{8,12},{12,8},{16,20},{20,16},{24,28},{28,24},{1,5},{5... | collective-permute-start | bytes 491528 | tf_op jit(solution)/shard_map/ppermute | solution.py:250
  96.6 1.4 %collective-permute-start.31 = (bf16[192,512]{1,0:T(8,128)(2,1)S(1)}, bf16[192,512]{1,0:T(8,128)(2,1)S(1)}, u32[]{:S(2)}, u32[]{:S(2)}) collective-permute-start(bf16[192,512]{1,0:T(8,128)(2,1)S(1)} %get-tuple-element.133), channel_id=1, source_target_pairs={{0,4},{4,0},{8,12},{12,8},{16,20},{20,16},{24,28},{28,24},{1,5},{5... | collective-permute-start | bytes 589832 | tf_op jit(solution)/shard_map/ppermute | solution.py:250
